TPU v7x, 32 devices: a whole 2x2x4 slice. The times are simulated.
32 devices in a mesh: groups: 2 (over y), row: 4 (over x, core), col: 4 (over z).
Axes of the slice: x: 2, y: 2, z: 4, core: 2. Of those that a mesh axis runs over, the one named last changes fastest.
Arguments:
- corpus: float32 [65536, 256], P(('groups', 'row', 'col')), parts along dimension 0, may hold values from -20 to 20
- sample_rows: int32 [8192], P(('groups', 'row', 'col')), parts along dimension 0, may hold values from 0 to 2047
- initial: float32 [64, 8192], P(None, ('groups', 'row', 'col')), parts along dimension 1, may hold values from -6 to 6
Outputs:
- vectors: float32 [64, 8192], P(None, ('groups', 'row', 'col')), parts along dimension 1
There are 2 independent parts, one for each index of `groups`. A program takes and returns all parts, laid end to end along the dimension named above; each array names one. Nothing has to cross between parts.
Inputs may be any that keep to these rules, and one draw needn't show every extreme that they name: Every device samples its landmarks from its own block of corpus rows: landmark i is corpus row (i // 256) * 2048 + sample_rows[i]; repeats may occur.
All inputs are finite; a program needn't handle non-finite values.
Results may differ from a plain program's by a relative error of at most 0.0044.
Values may be sent and summed in bfloat16 or wider, within the bound.
No kernel may reach another device: no remote copies, remote signals or barrier semaphores. Data moves between devices by JAX's collectives and lax.ppermute only.
A program may use at most 128 MiB of HBM per device.

v0:
```python
import math

import jax
import jax.numpy as jnp
from jax import lax
from jax.sharding import PartitionSpec as P

ITERS = 2


def kernel_block(row_block, col_embeds, col_norms):
    embed_dim = row_block.shape[1]
    products = jnp.dot(
        row_block, col_embeds, precision=lax.Precision.HIGHEST, preferred_element_type=jnp.float32
    )
    row_norms = jnp.sum(row_block * row_block, axis=1)
    distance = row_norms[:, None] + col_norms[None, :] - 2.0 * products
    return jnp.exp(-distance / (2.0 * embed_dim)).astype(jnp.bfloat16)


def build_tile(row_panel, col_embeds):
    panel_rows, embed_dim = row_panel.shape
    col_count = col_embeds.shape[1]
    col_norms = jnp.sum(col_embeds * col_embeds, axis=0)
    block_rows = math.gcd(panel_rows, 512)
    blocks = row_panel.reshape(panel_rows // block_rows, block_rows, embed_dim)
    blocks_out = lax.map(lambda row_block: kernel_block(row_block, col_embeds, col_norms), blocks)
    return blocks_out.reshape(panel_rows, col_count)


def apply_cols(rounded, kernel_cols):
    return lax.dot_general(
        rounded, kernel_cols, (((1,), (1,)), ((), ())), preferred_element_type=jnp.float32
    )


def local(corpus, sample_rows, initial):
    landmarks = corpus[sample_rows]
    local_cols = landmarks.T
    row_panel = lax.all_gather(landmarks, "col", axis=0, tiled=True)
    col_panel = lax.all_gather(local_cols, "row", axis=1, tiled=True)
    landmark_count = float(initial.shape[1] * lax.axis_size("row") * lax.axis_size("col"))
    offset_mean = lax.psum(jnp.sum(initial, axis=1), ("row", "col")) / landmark_count
    vectors = initial - offset_mean[:, None]
    kernel_tile = build_tile(row_panel, col_panel)
    for sweep in range(ITERS):
        rounded = vectors.astype(jnp.bfloat16)
        partial_value = apply_cols(lax.all_gather(rounded, "row", axis=1, tiled=True), kernel_tile)
        image_rows = lax.psum_scatter(partial_value, "col", scatter_dimension=1, tiled=True)
        row_mean = lax.psum(jnp.sum(image_rows, axis=1), ("row", "col")) / landmark_count
        centered = image_rows - row_mean[:, None]
        local_gram = jnp.dot(centered, centered.T, precision=lax.Precision.HIGHEST)
        gram_matrix = lax.psum(local_gram, ("row", "col"))
        factor = jnp.linalg.cholesky(gram_matrix)
        vectors = math.sqrt(landmark_count) * jax.scipy.linalg.solve_triangular(
            factor, centered, lower=True
        )
    return vectors


def solution(mesh):
    return jax.shard_map(
        local,
        mesh=mesh,
        in_specs=(
            P(("groups", "row", "col"), None),
            P(("groups", "row", "col")),
            P(None, ("groups", "row", "col")),
        ),
        out_specs=P(None, ("groups", "row", "col")),
        check_vma=False,
    )
```

profile of v0, /device:TPU:0, one launch (start us, length us, event | category | flops | bytes accessed | tf_op | source)
XLA Modules:
  0.0 337.2 jit_solution(10541468101713872107)
XLA Ops:
  6.5 0.0 copy-start
  6.5 0.0 copy-start.2
  6.5 0.0 all-gather.4.cloned.1.call-start
  6.5 0.8 compare_select_fusion
  7.4 0.8 copy-done
  8.1 1.7 gather_fusion
  9.8 0.0 all-gather.4.cloned.1.call-update
  9.8 0.0 all-gather.6.cloned.1.call-start
  9.9 0.7 all-gather.6.cloned.1.call-update
  10.6 0.0 reduce-scatter.3.cloned.1.call-start
  10.6 0.0 copy-done.2
  10.7 0.1 reduce_sum.45
  10.8 35.4 %psum.35 = f32[64]{0:T(128)S(1)} all-reduce(f32[64]{0:T(128)S(1)} %reduce_sum.45), channel_id=1, replica_groups=mesh['groups'=2,'row'=4,'col'=4] {'row','col'}, use_global_device_ids=true, to_apply=%region_1.0 | all-reduce | flops 64 | bytes 512 | tf_op jit(solution)/shard_map/psum | solution.py:43
  46.2 0.1 subtract_convert_fusion
  46.3 5.4 %all_gather.12 = bf16[64,1024]{1,0:T(8,128)(2,1)S(1)} all-gather(bf16[64,256]{1,0:T(8,128)(2,1)S(1)} %subtract_convert_fusion), channel_id=1, replica_groups=mesh['groups'=2,'row'=4,'col'=4] {'row'}, dimensions={1}, use_global_device_ids=true | all-gather | bytes 163840 | tf_op jit(solution)/shard_map/all_gather | solution.py:48
  51.7 0.0 all-gather.4.cloned.1.call-done
  51.7 0.0 copy-start.1
  51.7 2.6 copy.4
  54.3 0.0 copy-done.1
  54.3 0.2 multiply_reduce_fusion
  54.5 4.6 %all-gather.6.cloned.1.call-done = f32[1024,256]{1,0:T(8,128)} async-done(((f32[256,256]{1,0:T(8,128)}), f32[1024,256]{1,0:T(8,128)}) %all-gather.6.cloned.1.call-update) | async-done | bytes 1048592 | tf_op jit(solution)/shard_map/all_gather | solution.py:40
  59.2 11.6 %while.10 = (s32[]{:T(128)}, bf16[2,512,1024]{2,1,0:T(8,128)(2,1)}, f32[2,512,256]{2,1,0:T(8,128)}, f32[1024]{0:T(1024)S(1)}, f32[256,1024]{1,0:T(8,128)}, /*index=5*/s32[]{:T(128)}) while((s32[]{:T(128)}, bf16[2,512,1024]{2,1,0:T(8,128)(2,1)}, f32[2,512,256]{2,1,0:T(8,128)}, f32[1024]{0:T(1024)S(1)}, f32[256,1024]{1,0:T(8,128)}, ...), condition=%wide.region_5.6_spmd, body=%wide.region_3.5_spmd.sunk | while | flops 1614020096 | bytes 3155017 | solution.py:27
  59.2 1.2 fusion.38
  60.4 4.6 %fusion.39 = bf16[2,512,1024]{2,1,0:T(8,128)(2,1)} fusion(bf16[2,512,1024]{2,1,0:T(8,128)(2,1)} %get-tuple-element.88, s32[]{:T(128)} %get-tuple-element.87, f32[256,1024]{1,0:T(8,128)} %get-tuple-element.97, f32[1024]{0:T(1024)S(1)} %get-tuple-element.96, f32[512]{0:T(512)S(1)} %fusion.38, f32[2,512,256]{2,1,0:T(8,128)} %get-tuple-element.95), kind=kOutput, calls=%fused_computation.3.clone.1 | convolution fusion | flops 1613758464 | bytes 2628608 | tf_op jit(solution)/shard_map/while/body/eval_jaxpr/dot_general | solution.py:13
  65.0 1.2 fusion.38
  66.2 4.6 %fusion.39 = bf16[2,512,1024]{2,1,0:T(8,128)(2,1)} fusion(bf16[2,512,1024]{2,1,0:T(8,128)(2,1)} %get-tuple-element.88, s32[]{:T(128)} %get-tuple-element.87, f32[256,1024]{1,0:T(8,128)} %get-tuple-element.97, f32[1024]{0:T(1024)S(1)} %get-tuple-element.96, f32[512]{0:T(512)S(1)} %fusion.38, f32[2,512,256]{2,1,0:T(8,128)} %get-tuple-element.95), kind=kOutput, calls=%fused_computation.3.clone.1 | convolution fusion | flops 1613758464 | bytes 2628608 | tf_op jit(solution)/shard_map/while/body/eval_jaxpr/dot_general | solution.py:13
  70.8 3.1 fusion.25
  73.9 0.0 reduce-scatter.3.cloned.1.call-update
  73.9 0.0 reduce-scatter.5.cloned.1.call-start
  73.9 19.2 %reduce-scatter.3.cloned.1.call-done = f32[64,256]{1,0:T(8,128)} async-done(((f32[64,1024]{1,0:T(8,128)}), f32[64,256]{1,0:T(8,128)}) %reduce-scatter.3.cloned.1.call-update) | async-done | bytes 65552 | tf_op jit(solution)/shard_map/reduce_scatter | solution.py:49
  93.1 0.9 reduce_sum.47
  94.0 29.7 %psum.36 = f32[64]{0:T(128)S(1)} all-reduce(f32[64]{0:T(128)S(1)} %reduce_sum.47), channel_id=1, replica_groups=mesh['groups'=2,'row'=4,'col'=4] {'row','col'}, use_global_device_ids=true, to_apply=%region_8.9 | all-reduce | flops 64 | bytes 512 | tf_op jit(solution)/shard_map/psum | solution.py:50
  123.7 1.2 fusion.11
  124.9 60.2 %psum.37 = f32[64,64]{0,1:T(8,128)S(1)} all-reduce(f32[64,64]{0,1:T(8,128)S(1)} %fusion.11), channel_id=1, replica_groups=mesh['groups'=2,'row'=4,'col'=4] {'row','col'}, use_global_device_ids=true, to_apply=%region_9.10 | all-reduce | flops 4096 | bytes 32768 | tf_op jit(solution)/shard_map/psum | solution.py:53
  185.1 0.1 copy.6
  185.2 5.8 %cholesky.44 = f32[64,64]{1,0:T(8,128)S(1)} custom-call(f32[64,64]{1,0:T(8,128)S(1)} %fusion.18), custom_call_target="Cholesky" | custom-call | tf_op jit(solution)/shard_map/jit(cholesky)/cholesky | solution.py:54
  191.1 0.6 compare_reduce_fusion.1
  191.8 0.7 fusion.13
  192.4 4.9 %custom-call.6 = f32[1,64,64]{1,2,0:T(8,128)S(1)} custom-call(f32[1,64,64]{2,1,0:T(8,128)S(1)} %fusion.13), custom_call_target="InvertDiagBlocksLowerTriangular" | custom-call | tf_op jit(solution)/shard_map/jit(_solve_triangular)/triangular_solve | solution.py:55
  197.3 1.1 fusion.6
  198.5 5.4 %all_gather.15 = bf16[64,1024]{1,0:T(8,128)(2,1)S(1)} all-gather(bf16[64,256]{1,0:T(8,128)(2,1)S(1)} %fusion.6), channel_id=1, replica_groups=mesh['groups'=2,'row'=4,'col'=4] {'row'}, dimensions={1}, use_global_device_ids=true | all-gather | bytes 163840 | tf_op jit(solution)/shard_map/all_gather | solution.py:48
  203.9 3.1 fusion.26
  207.0 0.0 reduce-scatter.5.cloned.1.call-update
  207.0 17.9 %reduce-scatter.5.cloned.1.call-done = f32[64,256]{1,0:T(8,128)} async-done(((f32[64,1024]{1,0:T(8,128)}), f32[64,256]{1,0:T(8,128)}) %reduce-scatter.5.cloned.1.call-update) | async-done | bytes 65552 | tf_op jit(solution)/shard_map/reduce_scatter | solution.py:49
  224.8 0.9 reduce_sum.48
  225.8 29.7 %psum.38 = f32[64]{0:T(128)S(1)} all-reduce(f32[64]{0:T(128)S(1)} %reduce_sum.48), channel_id=1, replica_groups=mesh['groups'=2,'row'=4,'col'=4] {'row','col'}, use_global_device_ids=true, to_apply=%region_14.17 | all-reduce | flops 64 | bytes 512 | tf_op jit(solution)/shard_map/psum | solution.py:50
  255.5 1.2 fusion.8
  256.7 60.0 %psum.39 = f32[64,64]{0,1:T(8,128)S(1)} all-reduce(f32[64,64]{0,1:T(8,128)S(1)} %fusion.8), channel_id=1, replica_groups=mesh['groups'=2,'row'=4,'col'=4] {'row','col'}, use_global_device_ids=true, to_apply=%region_15.18 | all-reduce | flops 4096 | bytes 32768 | tf_op jit(solution)/shard_map/psum | solution.py:53
  316.7 0.1 copy.8
  316.8 5.8 %cholesky.55 = f32[64,64]{1,0:T(8,128)S(1)} custom-call(f32[64,64]{1,0:T(8,128)S(1)} %fusion.16), custom_call_target="Cholesky" | custom-call | tf_op jit(solution)/shard_map/jit(cholesky)/cholesky | solution.py:54
  322.7 0.6 compare_reduce_fusion
  323.3 0.7 fusion.14
  324.0 4.9 %custom-call.7 = f32[1,64,64]{1,2,0:T(8,128)S(1)} custom-call(f32[1,64,64]{2,1,0:T(8,128)S(1)} %fusion.14), custom_call_target="InvertDiagBlocksLowerTriangular" | custom-call | tf_op jit(solution)/shard_map/jit(_solve_triangular)/triangular_solve | solution.py:55
  328.9 1.8 convolution_multiply_fusion
  (9 shorter events, 0.1 us)
Async XLA Ops:
  6.5 1.6 copy-start
  6.5 4.1 %copy-start.2 = (f32[64,256]{1,0:T(8,128)S(1)}, f32[64,256]{1,0:T(8,128)}, u32[]{:S(2)}) copy-start(f32[64,256]{1,0:T(8,128)} %param.10) | copy-start | bytes 196612
  6.5 45.2 %all-gather.4.cloned.1.call-start = ((), (), s32[]{:S(2)}) async-start(), calls=%async_computation.2 | async-start | bytes 1310720 | tf_op jit(solution)/shard_map/all_gather | solution.py:41
  9.8 49.4 %all-gather.6.cloned.1.call-start = ((), (), s32[]{:S(2)}) async-start(), calls=%async_computation.5 | async-start | bytes 1310720 | tf_op jit(solution)/shard_map/all_gather | solution.py:40
  10.6 82.5 %reduce-scatter.3.cloned.1.call-start = ((), (), s32[]{:S(2)}) async-start(), calls=%async_computation.3 | async-start | bytes 327680 | tf_op jit(solution)/shard_map/reduce_scatter | solution.py:49
  51.7 2.6 copy-start.1
  73.9 151.0 %reduce-scatter.5.cloned.1.call-start = ((), (), s32[]{:S(2)}) async-start(), calls=%async_computation.4 | async-start | bytes 327680 | tf_op jit(solution)/shard_map/reduce_scatter | solution.py:49
Sparse Core Ops, SparseCore 0:
  10.0 19.5 all-gather.3
  31.1 28.0 all-gather.5
  74.0 19.0 reduce-scatter.2
  207.1 17.6 reduce-scatter.4
where the time goes:
time: 338 us; the launch traced here: 337 us
  blocking collectives  226 us (67%)
  waiting for transfers between devices  42.4 us (13%)
  other arithmetic  29.7 us (9%)
  matrix products  20.6 us (6%)
  between operations  13.2 us (4%)
  local copies, waits for them, and re-layouts  5.23 us (2%)
    psum x2, blocking collectives, local(): gram_matrix = lax.psum(local_gram, ('row', 'col'))  120 us
    psum x2, blocking collectives, local(): lax.psum(jnp.sum(image_rows, axis=1), ('row', 'col')) / landmark_count  59.4 us
    reduce_scatter x2, waiting for transfers between devices, local(): lax.psum_scatter(partial_value, 'col', scatter_dimension=1, tiled=True)  37 us
    psum x1, blocking collectives, local(): lax.psum(jnp.sum(initial, axis=1), ('row', 'col')) / landmark_count  35.4 us
    another operation x6, other arithmetic, local(): factor = jnp.linalg.cholesky(gram_matrix)  13 us
    another operation x4, other arithmetic, local(): jax.scipy.linalg.solve_triangular(factor, centered, lower=True)  11.1 us
    all_gather x2, blocking collectives, local(): lax.all_gather(rounded, 'row', axis=1, tiled=True)  10.9 us
    dot_general x2, matrix products, kernel_block(): jnp.dot(row_block, col_embeds, precision=lax.Precision.HIGHEST, preferred...  9.21 us
  transfers between devices with their start and end apart: 4, of which 3 were waited for; matrix products, arithmetic and copies ran while one was open for 1% of the time, Pallas kernels for 0%

commit v1 on v0

v1 whole, which is shorter than its diff:
```python
import functools
import math

import jax
import jax.numpy as jnp
from jax import lax
from jax.experimental import pallas as pl
from jax.experimental.pallas import tpu as pltpu
from jax.sharding import PartitionSpec as P

ITERS = 2
REACH = 20.0
UNIT = REACH / 32767.0
FIXED = 2.0**28
HIGHEST = lax.Precision.HIGHEST
BF16, F32 = jnp.bfloat16, jnp.float32
VMEM = pl.BlockSpec(memory_space=pltpu.VMEM)


def matmul(a, b, contract, precision=None):
    return lax.dot_general(a, b, ((contract[:1], contract[1:]), ((), ())), precision=precision, preferred_element_type=F32)


def encode(landmarks, initial):
    half = landmarks.shape[0] // 2
    code = jnp.round(landmarks * (1.0 / UNIT)).astype(jnp.int32)
    packed = (code[:half] << 16) | (code[half:] & 0xFFFF)
    return jnp.concatenate([packed, jnp.round(initial * FIXED).astype(jnp.int32)], axis=0)


def split_codes(words):
    code = jnp.concatenate([words >> 16, (words << 16) >> 16], axis=0)
    high = ((code + 128) >> 8) << 8
    return high.astype(F32).astype(BF16), (code - high).astype(F32).astype(BF16)


def kernel_rows(words, own_high, own_low, own_norms, scale):
    high, low = split_codes(words)
    wide = high.astype(F32) + low.astype(F32)
    norms = scale * jnp.sum(wide * wide, axis=1, keepdims=True)
    dots = matmul(high, own_high, (1, 1)) + (matmul(high, own_low, (1, 1)) + matmul(low, own_high, (1, 1))) + matmul(low, own_low, (1, 1))
    return jnp.exp((2.0 * scale) * dots - (norms + own_norms)).astype(BF16)


def own_side(words, scale):
    high, low = split_codes(words)
    wide = high.astype(F32) + low.astype(F32)
    norms = matmul(jnp.ones((8, wide.shape[1]), F32), wide * wide, (1, 1), HIGHEST)[:1]
    return high, low, scale * norms


def build_kernel(count, half, scale, own_ref, *refs):
    blocks, out_ref = refs[:count], refs[count]
    own_high, own_low, own_norms = own_side(own_ref[:half], scale)
    for b, block in enumerate(blocks):
        out_ref[pl.ds(b * 2 * half, 2 * half), :] = kernel_rows(block[:half], own_high, own_low, own_norms, scale)


def first_kernel(count, last, half, scale, total, own_ref, *refs):
    blocks = refs[:count]
    parts = refs[count : count + (count // last) - 1]
    out_ref, tile_ref = refs[-2:]
    size = 2 * half
    own_high, own_low, own_norms = own_side(own_ref[:half], scale)
    for b, block in enumerate(blocks[count - last :]):
        tile_ref[pl.ds(b * size, size), :] = kernel_rows(block[:half], own_high, own_low, own_norms, scale)
    starts = [block[half:].astype(F32) * (1.0 / FIXED) for block in blocks]
    sums = starts[0]
    for start in starts[1:]:
        sums = sums + start
    mean = jnp.sum(sums, axis=1, keepdims=True) / total
    images = None
    for b, start in enumerate(starts):
        part, inner = divmod(b, last)
        ref = parts[part] if part < len(parts) else tile_ref
        term = matmul((start - mean).astype(BF16), ref[pl.ds(inner * size, size), :], (1, 0))
        images = term if images is None else images + term
    out_ref[...] = images


def inverse_factor(gram):
    n = gram.shape[0]
    row_id = lax.broadcasted_iota(jnp.int32, (n, 2 * n), 0)
    col_id = lax.broadcasted_iota(jnp.int32, (n, 2 * n), 1)
    eye = (row_id[:, :n] == col_id[:, :n]).astype(F32)
    work = jnp.concatenate([gram, eye], axis=1)
    done = []
    for top in range(0, n, 8):
        rows = n - top
        local = lax.broadcasted_iota(jnp.int32, (rows, 2 * n), 0)
        columns = [jnp.broadcast_to(work[:, top + k : top + k + 1], (rows, 2 * n)) for k in range(8)]
        for k in range(8):
            column = columns[k]
            factor = jnp.where(local > k, column * (1.0 / column[k : k + 1]), 0.0)
            work = work - factor * work[k : k + 1]
            for later in range(k + 1, 8):
                columns[later] = columns[later] - factor * columns[later][k : k + 1]
        done.append(work[:8])
        work = work[8:]
    upper = jnp.concatenate(done, axis=0)
    pivots = jnp.sum(jnp.where(row_id == col_id, upper, 0.0), axis=1, keepdims=True)
    return upper[:, n:] * lax.rsqrt(pivots)


def second_kernel(count, last, total, copies, *refs):
    images = refs[:count]
    tiles = refs[count : count + count // last]
    out_ref, share_ref = refs[-2:]
    size = images[0].shape[1]
    values = [image[...] for image in images]
    sums = values[0]
    for value in values[1:]:
        sums = sums + value
    mean = jnp.sum(sums, axis=1, keepdims=True) / total
    gram = None
    centered = []
    for value in values:
        centered.append(value - mean)
        term = matmul(centered[-1], centered[-1], (1, 1), HIGHEST)
        gram = term if gram is None else gram + term
    solve = math.sqrt(total) * inverse_factor(gram)
    result = None
    for b, value in enumerate(centered):
        part, inner = divmod(b, last)
        vectors = matmul(solve, value, (1, 0), HIGHEST).astype(BF16)
        term = matmul(vectors, tiles[part][pl.ds(inner * size, size), :], (1, 0))
        result = term if result is None else result + term
    out_ref[...] = result
    local_mean = jnp.sum(result, axis=1, keepdims=True) / size
    local = result - local_mean
    local_gram = matmul(local, local, (1, 1), HIGHEST)
    h = local_gram.shape[0] // 2
    share = jnp.concatenate(
        [local_gram[:h], local_gram[h:, h:], local_mean[:h], local_mean[h:], jnp.zeros((h, h - 2), F32)], axis=1
    )
    for c in range(copies):
        share_ref[c] = share


def last_kernel(total, shares_ref, images_ref, out_ref):
    copies, h, _ = shares_ref.shape
    size = images_ref.shape[1]
    shares = [shares_ref[c] for c in range(copies)]
    summed = shares[0]
    for share in shares[1:]:
        summed = summed + share
    means = jnp.concatenate([jnp.concatenate([s[:, 3 * h : 3 * h + 1], s[:, 3 * h + 1 : 3 * h + 2]], axis=0) for s in shares], axis=1)
    mean = jnp.sum(means, axis=1, keepdims=True) / copies
    apart = means - mean
    top = summed[:, : 2 * h]
    bottom = jnp.concatenate([top[:, h:].T, summed[:, 2 * h : 3 * h]], axis=1)
    gram = jnp.concatenate([top, bottom], axis=0) + size * matmul(apart, apart, (1, 1), HIGHEST)
    solve = math.sqrt(total) * inverse_factor(gram)
    out_ref[...] = matmul(solve, images_ref[...] - mean, (1, 0), HIGHEST)


def call(kernel, args, out_shape):
    return pl.pallas_call(
        kernel,
        out_shape=out_shape,
        in_specs=[VMEM] * len(args),
        out_specs=jax.tree.map(lambda _: VMEM, out_shape),
        compiler_params=pltpu.CompilerParams(vmem_limit_bytes=48 * 2**20),
    )(*args)


def gather_blocks(block):
    rows, cols = lax.axis_size("row"), lax.axis_size("col")

    def swap(value, axis, size, offset):
        return lax.ppermute(value, axis, [(i, i ^ offset) for i in range(size)]) if offset else value

    out = []
    for c in range(cols):
        along = swap(block, "col", cols, c)
        for r in range(0, rows, 2):
            chip = swap(along, "row", rows, r)
            out += [chip, swap(chip, "row", rows, 1)]
    return out


def local(corpus, sample_rows, initial):
    vecs, size = initial.shape
    half = size // 2
    rows, cols = lax.axis_size("row"), lax.axis_size("col")
    count = rows * cols
    last = rows
    total = float(size * count)
    scale = UNIT * UNIT / (2.0 * corpus.shape[1])
    landmarks = corpus.at[sample_rows].get(mode="promise_in_bounds")
    own = encode(landmarks, initial)
    blocks = gather_blocks(own)
    tiles = []
    for g in range(0, count - last, last):
        group = blocks[g : g + last]
        tiles.append(
            call(functools.partial(build_kernel, last, half, scale), [own] + group, jax.ShapeDtypeStruct((last * size, size), BF16))
        )
    images, tile = call(
        functools.partial(first_kernel, count, last, half, scale, total),
        [own] + blocks + tiles,
        (jax.ShapeDtypeStruct((vecs, size), F32), jax.ShapeDtypeStruct((last * size, size), BF16)),
    )
    tiles.append(tile)
    gathered = gather_blocks(images)
    images, share = call(
        functools.partial(second_kernel, count, last, total, count),
        gathered + tiles,
        (jax.ShapeDtypeStruct((vecs, size), F32), jax.ShapeDtypeStruct((count, vecs // 2, 2 * vecs), F32)),
    )
    shares = lax.all_to_all(share, ("row", "col"), split_axis=0, concat_axis=0)
    return call(functools.partial(last_kernel, total), [shares, images], jax.ShapeDtypeStruct((vecs, size), F32))


def local_large(corpus, sample_rows, initial):
    both = ("row", "col")
    landmarks = corpus[sample_rows]
    everyone = lax.all_gather(landmarks, both, axis=0, tiled=True)
    total = float(everyone.shape[0])
    norms = jnp.sum(everyone * everyone, axis=1)
    own_norms = jnp.sum(landmarks * landmarks, axis=1)
    products = jnp.dot(everyone, landmarks.T, precision=HIGHEST, preferred_element_type=F32)
    tile = jnp.exp(-(norms[:, None] + own_norms[None, :] - 2.0 * products) / (2.0 * corpus.shape[1])).astype(BF16)
    starts = lax.all_gather(initial, both, axis=1, tiled=True)
    rounded = (starts - jnp.mean(starts, axis=1, keepdims=True)).astype(BF16)
    vectors = None
    for _ in range(ITERS):
        images = jnp.dot(rounded, tile, preferred_element_type=F32)
        gathered = lax.all_gather(images, both, axis=1, tiled=True)
        mean = jnp.mean(gathered, axis=1, keepdims=True)
        centered = gathered - mean
        factor = jnp.linalg.cholesky(jnp.dot(centered, centered.T, precision=HIGHEST))
        rounded = (math.sqrt(total) * jax.scipy.linalg.solve_triangular(factor, centered, lower=True)).astype(BF16)
        vectors = math.sqrt(total) * jax.scipy.linalg.solve_triangular(factor, images - mean, lower=True)
    return vectors


def solution(mesh):
    shape = mesh.shape
    whole = P(("groups", "row", "col"))
    return jax.shard_map(
        local if shape["row"] * shape["col"] <= 16 else local_large,
        mesh=mesh,
        in_specs=(P(("groups", "row", "col"), None), whole, P(None, ("groups", "row", "col"))),
        out_specs=P(None, ("groups", "row", "col")),
        check_vma=False,
    )
```

time: 338 us -> 77.6 us (0.23)
  blocking collectives: 226 us -> 14.3 us
  other arithmetic: 29.7 us -> 1.74 us
  starting transfers between devices: 0.12 us -> 24.3 us
  waiting for transfers between devices: 42.4 us -> 20.4 us
  matrix products: 20.6 us -> 0 us
  Pallas kernels: 0 us -> 15.5 us
  between operations: 13.2 us -> 0.16 us
  local copies, waits for them, and re-layouts: 5.23 us -> 0.97 us
    psum x5 -> x0, blocking collectives: 215 us -> none  [the longest x2 120 us: local(): gram_matrix = lax.psum(local_gram, ('row', 'col'))]
    reduce_scatter x2 -> x0, waiting for transfers between devices: 37 us -> none  [local(): lax.psum_scatter(partial_value, 'col', scatter_dimension=1, tiled=True)]
    ppermute x0 -> x30, starting transfers between devices: none -> 24.3 us  [swap(): lax.ppermute(value, axis, [(i, i ^ offset) for i in range(size)])]
    another operation x10 -> x0, other arithmetic: 24.1 us -> none  [the longest x6 13 us: local(): factor = jnp.linalg.cholesky(gram_matrix)]
    ppermute x0 -> x30, waiting for transfers between devices: none -> 20.4 us  [swap(): lax.ppermute(value, axis, [(i, i ^ offset) for i in range(size)])]
    dot_general x6 -> x0, matrix products: 17.7 us -> none  [the longest x2 9.21 us: kernel_block(): jnp.dot(row_block, col_embeds, precision=lax.Precision.HIGHEST, preferred...]
    pallas_call x0 -> x6, Pallas kernels: none -> 15.5 us  [call(): pl.pallas_call(kernel, out_shape=out_shape, in_specs=[VMEM] * len(args),...]
    all_to_all x0 -> x1, blocking collectives: none -> 14.3 us  [local(): shares = lax.all_to_all(share, ('row', 'col'), split_axis=0, concat_axis=0)]
  transfers between devices with their start and end apart: 4 -> 30, of which waited for: 3 -> 9; matrix products, arithmetic and copies ran while one was open for 1% -> 0% of each run, Pallas kernels for 0% -> 4%
where the time goes in v1:
time: 77.6 us; the launch traced here: 77.4 us
  starting transfers between devices  24.3 us (31%)
  waiting for transfers between devices  20.4 us (26%)
  Pallas kernels  15.5 us (20%)
  blocking collectives  14.3 us (18%)
  other arithmetic  1.74 us (2%)
  local copies, waits for them, and re-layouts  0.97 us (1%)
    ppermute x30, starting transfers between devices, swap(): lax.ppermute(value, axis, [(i, i ^ offset) for i in range(size)])  24.3 us
    ppermute x30, waiting for transfers between devices, swap(): lax.ppermute(value, axis, [(i, i ^ offset) for i in range(size)])  20.4 us
    pallas_call x6, Pallas kernels, call(): pl.pallas_call(kernel, out_shape=out_shape, in_specs=[VMEM] * len(args),...  15.5 us
    all_to_all x1, blocking collectives, local(): shares = lax.all_to_all(share, ('row', 'col'), split_axis=0, concat_axis=0)  14.3 us
  transfers between devices with their start and end apart: 30, of which 9 were waited for; matrix products, arithmetic and copies ran while one was open for 0% of the time, Pallas kernels for 4%

profile of v1, /device:TPU:0, one launch (start us, length us, event | category | flops | bytes accessed | tf_op | source)
XLA Modules:
  0.0 77.4 jit_solution(17493722094980469951)
XLA Ops:
  0.0 0.8 %compare_select_fusion = s32[256]{0:T(256)S(1)} fusion(s32[256]{0:T(256)} %param.4), kind=kLoop, calls=%fused_computation.8 | loop fusion | flops 768 | bytes 2048 | tf_op jit(solution)/shard_map/select_n | solution.py:190
  0.8 0.8 %round-nearest-even_convert_fusion.1 = s32[64,256]{1,0:T(8,128)S(1)} fusion(f32[64,256]{1,0:T(8,128)} %param.5), kind=kLoop, calls=%fused_computation.6 | loop fusion | flops 49152 | bytes 131072 | tf_op jit(solution)/shard_map/convert_element_type | solution.py:28
  1.7 1.0 %gather_fusion = f32[256,256]{1,0:T(8,128)S(1)} fusion(f32[2048,256]{1,0:T(8,128)S(1)} %copy-done, s32[1024]{0:T(1024)S(1)} %pad_clamp_fusion), kind=kCustom, calls=%fused_computation | custom fusion | bytes 525312 | tf_op jit(solution)/shard_map/gather | solution.py:190
  2.7 5.1 %collective-permute-start.11 = (s32[192,256]{1,0:T(8,128)S(1)}, s32[192,256]{1,0:T(8,128)S(1)}, u32[]{:S(2)}, u32[]{:S(2)}) collective-permute-start(s32[192,256]{1,0:T(8,128)S(1)} %pad_add_fusion.own_ref.refs_0_), channel_id=1, source_target_pairs={{0,3},{1,2},{2,1},{3,0},{4,7},{5,6},{6,5},{7,4},{8,11},{9,10},{10,... | collective-permute-start | bytes 589832 | tf_op jit(solution)/shard_map/ppermute | solution.py:171
  7.9 0.0 collective-permute-start.3
  7.9 0.6 collective-permute-start.7
  8.5 1.6 %collective-permute-start.1 = (s32[192,256]{1,0:T(8,128)S(1)}, s32[192,256]{1,0:T(8,128)S(1)}, u32[]{:S(2)}, u32[]{:S(2)}) collective-permute-start(s32[192,256]{1,0:T(8,128)S(1)} %pad_add_fusion.own_ref.refs_0_), channel_id=1, source_target_pairs={{0,8},{4,12},{8,0},{12,4},{1,9},{5,13},{9,1},{13,5},{2,10},{6,14},... | collective-permute-start | bytes 589832 | tf_op jit(solution)/shard_map/ppermute | solution.py:171
  10.1 0.0 collective-permute-start
  10.1 3.5 %collective-permute-done.11.refs_12_ = s32[192,256]{1,0:T(8,128)S(1)} collective-permute-done((s32[192,256]{1,0:T(8,128)S(1)}, s32[192,256]{1,0:T(8,128)S(1)}, u32[]{:S(2)}, u32[]{:S(2)}) %collective-permute-start.11) | collective-permute-done | bytes 196640 | tf_op jit(solution)/shard_map/ppermute | solution.py:171
  13.6 1.7 %collective-permute-start.13 = (s32[192,256]{1,0:T(8,128)S(1)}, s32[192,256]{1,0:T(8,128)S(1)}, u32[]{:S(2)}, u32[]{:S(2)}) collective-permute-start(s32[192,256]{1,0:T(8,128)S(1)} %collective-permute-done.11.refs_12_), channel_id=1, source_target_pairs={{0,8},{4,12},{8,0},{12,4},{1,9},{5,13},{9,1},{13,5},{2,10},{6,14},... | collective-permute-start | bytes 589832 | tf_op jit(solution)/shard_map/ppermute | solution.py:171
  15.3 2.7 %collective-permute-done.3.refs_0_.refs_4_ = s32[192,256]{1,0:T(8,128)S(1)} collective-permute-done((s32[192,256]{1,0:T(8,128)S(1)}, s32[192,256]{1,0:T(8,128)S(1)}, u32[]{:S(2)}, u32[]{:S(2)}) %collective-permute-start.3) | collective-permute-done | bytes 196640 | tf_op jit(solution)/shard_map/ppermute | solution.py:171
  18.1 1.4 %collective-permute-start.5 = (s32[192,256]{1,0:T(8,128)S(1)}, s32[192,256]{1,0:T(8,128)S(1)}, u32[]{:S(2)}, u32[]{:S(2)}) collective-permute-start(s32[192,256]{1,0:T(8,128)S(1)} %collective-permute-done.3.refs_0_.refs_4_), channel_id=1, source_target_pairs={{0,8},{4,12},{8,0},{12,4},{1,9},{5,13},{9,1},{13,5},{2,10},{6,14},... | collective-permute-start | bytes 589832 | tf_op jit(solution)/shard_map/ppermute | solution.py:171
  19.5 5.1 %collective-permute-done.7.refs_0_.refs_8_ = s32[192,256]{1,0:T(8,128)S(1)} collective-permute-done((s32[192,256]{1,0:T(8,128)S(1)}, s32[192,256]{1,0:T(8,128)S(1)}, u32[]{:S(2)}, u32[]{:S(2)}) %collective-permute-start.7) | collective-permute-done | bytes 196640 | tf_op jit(solution)/shard_map/ppermute | solution.py:171
  24.6 1.5 %collective-permute-start.9 = (s32[192,256]{1,0:T(8,128)S(1)}, s32[192,256]{1,0:T(8,128)S(1)}, u32[]{:S(2)}, u32[]{:S(2)}) collective-permute-start(s32[192,256]{1,0:T(8,128)S(1)} %collective-permute-done.7.refs_0_.refs_8_), channel_id=1, source_target_pairs={{0,8},{4,12},{8,0},{12,4},{1,9},{5,13},{9,1},{13,5},{2,10},{6,14},... | collective-permute-start | bytes 589832 | tf_op jit(solution)/shard_map/ppermute | solution.py:171
  26.0 0.0 collective-permute-done.1.refs_2_
  26.1 0.0 collective-permute-start.4
  26.1 0.0 collective-permute-done.refs_1_
  26.1 0.5 collective-permute-start.2
  26.6 0.0 collective-permute-done.13.refs_14_
  26.6 0.1 collective-permute-start.8
  26.6 0.0 collective-permute-done.5.refs_2_.refs_6_
  26.6 0.4 collective-permute-start.6
  27.1 3.4 %collective-permute-done.9.refs_2_.refs_10_ = s32[192,256]{1,0:T(8,128)S(1)} collective-permute-done((s32[192,256]{1,0:T(8,128)S(1)}, s32[192,256]{1,0:T(8,128)S(1)}, u32[]{:S(2)}, u32[]{:S(2)}) %collective-permute-start.9) | collective-permute-done | bytes 196640 | tf_op jit(solution)/shard_map/ppermute | solution.py:171
  30.5 0.0 collective-permute-start.10
  30.5 0.0 collective-permute-done.4.refs_1_.refs_5_
  30.5 0.5 collective-permute-start.12
  31.0 0.0 collective-permute-done.2.refs_3_
  31.0 0.1 collective-permute-start.14
  31.1 1.1 %shard_map.37.refs_16_ = bf16[1024,256]{1,0:T(8,128)(2,1)S(1)} custom-call(s32[192,256]{1,0:T(8,128)S(1)} %pad_add_fusion.own_ref.refs_0_, s32[192,256]{1,0:T(8,128)S(1)} %pad_add_fusion.own_ref.refs_0_, s32[192,256]{1,0:T(8,128)S(1)} %collective-permute-done.refs_1_, s32[192,256]{1,0:T(8,128)S(1)} %collective-permute-done.1.refs_2_, ...), custom_call_target="tpu_custom_call" | custom-call | tf_op jit(solution)/shard_map/pallas_call | solution.py:158
  32.2 0.0 collective-permute-done.6.refs_3_.refs_7_
  32.2 1.1 %shard_map.38.refs_17_ = bf16[1024,256]{1,0:T(8,128)(2,1)S(1)} custom-call(s32[192,256]{1,0:T(8,128)S(1)} %pad_add_fusion.own_ref.refs_0_, s32[192,256]{1,0:T(8,128)S(1)} %collective-permute-done.3.refs_0_.refs_4_, s32[192,256]{1,0:T(8,128)S(1)} %collective-permute-done.4.refs_1_.refs_5_, s32[192,256]{1,0:T(8,128)S(1)} %collective-permute-done.5.refs_2_.refs_6_, ...), custom_call_target="tpu_custom_call" | custom-call | tf_op jit(solution)/shard_map/pallas_call | solution.py:158
  33.2 0.0 collective-permute-done.8.refs_1_.refs_9_
  33.3 1.1 %shard_map.39.refs_18_ = bf16[1024,256]{1,0:T(8,128)(2,1)S(1)} custom-call(s32[192,256]{1,0:T(8,128)S(1)} %pad_add_fusion.own_ref.refs_0_, s32[192,256]{1,0:T(8,128)S(1)} %collective-permute-done.7.refs_0_.refs_8_, s32[192,256]{1,0:T(8,128)S(1)} %collective-permute-done.8.refs_1_.refs_9_, s32[192,256]{1,0:T(8,128)S(1)} %collective-permute-done.9.refs_2_.refs_10_, ...), custom_call_target="tpu_custom_call" | custom-call | tf_op jit(solution)/shard_map/pallas_call | solution.py:158
  34.3 0.0 collective-permute-done.12.refs_13_
  34.4 1.8 %shard_map.40 = (f32[64,256]{1,0:T(8,128)S(1)}, bf16[1024,256]{1,0:T(8,128)(2,1)S(1)}) custom-call(s32[192,256]{1,0:T(8,128)S(1)} %pad_add_fusion.own_ref.refs_0_, s32[192,256]{1,0:T(8,128)S(1)} %pad_add_fusion.own_ref.refs_0_, s32[192,256]{1,0:T(8,128)S(1)} %collective-permute-done.refs_1_, s32[192,256]{1,0:T(8,128)S(1)} %collective-permute-done.1.refs_2_, ...), custom_call_target="tpu_custom_call" | custom-call | tf_op jit(solution)/shard_map/pallas_call | solution.py:158
  36.1 2.4 %collective-permute-start.26 = (f32[64,256]{1,0:T(8,128)S(1)}, f32[64,256]{1,0:T(8,128)S(1)}, u32[]{:S(2)}, u32[]{:S(2)}) collective-permute-start(f32[64,256]{1,0:T(8,128)S(1)} %get-tuple-element.9.refs_0_), channel_id=1, source_target_pairs={{0,3},{1,2},{2,1},{3,0},{4,7},{5,6},{6,5},{7,4},{8,11},{9,10},{10,... | collective-permute-start | bytes 196616 | tf_op jit(solution)/shard_map/ppermute | solution.py:171
  38.5 2.1 %collective-permute-start.18 = (f32[64,256]{1,0:T(8,128)S(1)}, f32[64,256]{1,0:T(8,128)S(1)}, u32[]{:S(2)}, u32[]{:S(2)}) collective-permute-start(f32[64,256]{1,0:T(8,128)S(1)} %get-tuple-element.9.refs_0_), channel_id=1, source_target_pairs={{0,1},{1,0},{2,3},{3,2},{4,5},{5,4},{6,7},{7,6},{8,9},{9,8},{10,11... | collective-permute-start | bytes 196616 | tf_op jit(solution)/shard_map/ppermute | solution.py:171
  40.6 1.5 %collective-permute-start.16 = (f32[64,256]{1,0:T(8,128)S(1)}, f32[64,256]{1,0:T(8,128)S(1)}, u32[]{:S(2)}, u32[]{:S(2)}) collective-permute-start(f32[64,256]{1,0:T(8,128)S(1)} %get-tuple-element.9.refs_0_), channel_id=1, source_target_pairs={{0,8},{4,12},{8,0},{12,4},{1,9},{5,13},{9,1},{13,5},{2,10},{6,14},... | collective-permute-start | bytes 196616 | tf_op jit(solution)/shard_map/ppermute | solution.py:171
  42.1 0.0 collective-permute-start.15
  42.1 0.9 %collective-permute-done.26.refs_12_ = f32[64,256]{1,0:T(8,128)S(1)} collective-permute-done((f32[64,256]{1,0:T(8,128)S(1)}, f32[64,256]{1,0:T(8,128)S(1)}, u32[]{:S(2)}, u32[]{:S(2)}) %collective-permute-start.26) | collective-permute-done | bytes 65568 | tf_op jit(solution)/shard_map/ppermute | solution.py:171
  43.0 1.5 %collective-permute-start.28 = (f32[64,256]{1,0:T(8,128)S(1)}, f32[64,256]{1,0:T(8,128)S(1)}, u32[]{:S(2)}, u32[]{:S(2)}) collective-permute-start(f32[64,256]{1,0:T(8,128)S(1)} %collective-permute-done.26.refs_12_), channel_id=1, source_target_pairs={{0,8},{4,12},{8,0},{12,4},{1,9},{5,13},{9,1},{13,5},{2,10},{6,14},... | collective-permute-start | bytes 196616 | tf_op jit(solution)/shard_map/ppermute | solution.py:171
  44.5 0.8 %collective-permute-done.22.refs_8_ = f32[64,256]{1,0:T(8,128)S(1)} collective-permute-done((f32[64,256]{1,0:T(8,128)S(1)}, f32[64,256]{1,0:T(8,128)S(1)}, u32[]{:S(2)}, u32[]{:S(2)}) %collective-permute-start.22) | collective-permute-done | bytes 65568 | tf_op jit(solution)/shard_map/ppermute | solution.py:171
  45.3 0.0 collective-permute-start.27
  45.3 0.0 collective-permute-done.18.refs_4_
  45.3 1.5 %collective-permute-start.24 = (f32[64,256]{1,0:T(8,128)S(1)}, f32[64,256]{1,0:T(8,128)S(1)}, u32[]{:S(2)}, u32[]{:S(2)}) collective-permute-start(f32[64,256]{1,0:T(8,128)S(1)} %collective-permute-done.22.refs_8_), channel_id=1, source_target_pairs={{0,8},{4,12},{8,0},{12,4},{1,9},{5,13},{9,1},{13,5},{2,10},{6,14},... | collective-permute-start | bytes 196616 | tf_op jit(solution)/shard_map/ppermute | solution.py:171
  46.8 0.2 collective-permute-start.23
  47.0 0.0 collective-permute-done.15.refs_1_
  47.0 0.5 collective-permute-start.20
  47.5 0.0 collective-permute-done.28.refs_14_
  47.5 0.0 collective-permute-start.19
  47.6 0.5 collective-permute-start.17
  48.0 1.7 %collective-permute-done.24.refs_10_ = f32[64,256]{1,0:T(8,128)S(1)} collective-permute-done((f32[64,256]{1,0:T(8,128)S(1)}, f32[64,256]{1,0:T(8,128)S(1)}, u32[]{:S(2)}, u32[]{:S(2)}) %collective-permute-start.24) | collective-permute-done | bytes 65568 | tf_op jit(solution)/shard_map/ppermute | solution.py:171
  49.8 0.0 collective-permute-done.23.refs_9_
  49.8 0.5 collective-permute-start.25
  50.3 1.0 %collective-permute-done.20.refs_6_ = f32[64,256]{1,0:T(8,128)S(1)} collective-permute-done((f32[64,256]{1,0:T(8,128)S(1)}, f32[64,256]{1,0:T(8,128)S(1)}, u32[]{:S(2)}, u32[]{:S(2)}) %collective-permute-start.20) | collective-permute-done | bytes 65568 | tf_op jit(solution)/shard_map/ppermute | solution.py:171
  51.3 0.0 collective-permute-start.21
  51.3 0.0 collective-permute-done.19.refs_5_
  51.3 0.0 collective-permute-done.17.refs_3_
  51.3 0.0 collective-permute-done.29.refs_15_
  51.3 0.0 collective-permute-done.25.refs_11_
  51.3 1.2 %collective-permute-done.21.refs_7_ = f32[64,256]{1,0:T(8,128)S(1)} collective-permute-done((f32[64,256]{1,0:T(8,128)S(1)}, f32[64,256]{1,0:T(8,128)S(1)}, u32[]{:S(2)}, u32[]{:S(2)}) %collective-permute-start.21) | collective-permute-done | bytes 65568 | tf_op jit(solution)/shard_map/ppermute | solution.py:171
  52.6 7.3 %shard_map.41 = (f32[64,256]{1,0:T(8,128)S(1)}, f32[16,32,128]{2,1,0:T(8,128)S(1)}) custom-call(f32[64,256]{1,0:T(8,128)S(1)} %get-tuple-element.9.refs_0_, f32[64,256]{1,0:T(8,128)S(1)} %collective-permute-done.15.refs_1_, f32[64,256]{1,0:T(8,128)S(1)} %collective-permute-done.16.refs_2_, f32[64,256]{1,0:T(8,128)S(1)} %collective-permute-done.17.refs_3_, ...), custom_call_target="tpu_custom_call" | custom-call | tf_op jit(solution)/shard_map/pallas_call | solution.py:158
  59.8 14.3 %all_to_all.5.shares_ref = f32[16,32,128]{2,1,0:T(8,128)S(1)} all-to-all(f32[16,32,128]{2,1,0:T(8,128)S(1)} %get-tuple-element.11), channel_id=1, replica_groups=mesh['groups'=2,'row'=4,'col'=4] {'row','col'}, dimensions={0} | all-to-all | bytes 524288 | tf_op jit(solution)/shard_map/all_to_all | solution.py:211
  74.2 3.3 %shard_map.42 = f32[64,256]{1,0:T(8,128)} custom-call(f32[16,32,128]{2,1,0:T(8,128)S(1)} %all_to_all.5.shares_ref, f32[64,256]{1,0:T(8,128)S(1)} %get-tuple-element.12.images_ref), custom_call_target="tpu_custom_call" | custom-call | tf_op jit(solution)/shard_map/pallas_call | solution.py:158
  (12 shorter events, 0.1 us)
Async XLA Ops:
  0.0 1.7 %copy-start = (f32[2048,256]{1,0:T(8,128)S(1)}, f32[2048,256]{1,0:T(8,128)}, u32[]{:S(2)}) copy-start(f32[2048,256]{1,0:T(8,128)} %param.3) | copy-start | bytes 6291460
  2.7 10.9 %collective-permute-start.11 = (s32[192,256]{1,0:T(8,128)S(1)}, s32[192,256]{1,0:T(8,128)S(1)}, u32[]{:S(2)}, u32[]{:S(2)}) collective-permute-start(s32[192,256]{1,0:T(8,128)S(1)} %pad_add_fusion.own_ref.refs_0_), channel_id=1, source_target_pairs={{0,3},{1,2},{2,1},{3,0},{4,7},{5,6},{6,5},{7,4},{8,11},{9,10},{10,... | collective-permute-start | bytes 589832 | tf_op jit(solution)/shard_map/ppermute | solution.py:171
  7.9 10.2 %collective-permute-start.3 = (s32[192,256]{1,0:T(8,128)S(1)}, s32[192,256]{1,0:T(8,128)S(1)}, u32[]{:S(2)}, u32[]{:S(2)}) collective-permute-start(s32[192,256]{1,0:T(8,128)S(1)} %pad_add_fusion.own_ref.refs_0_), channel_id=1, source_target_pairs={{0,1},{1,0},{2,3},{3,2},{4,5},{5,4},{6,7},{7,6},{8,9},{9,8},{10,11... | collective-permute-start | bytes 589832 | tf_op jit(solution)/shard_map/ppermute | solution.py:171
  7.9 16.7 %collective-permute-start.7 = (s32[192,256]{1,0:T(8,128)S(1)}, s32[192,256]{1,0:T(8,128)S(1)}, u32[]{:S(2)}, u32[]{:S(2)}) collective-permute-start(s32[192,256]{1,0:T(8,128)S(1)} %pad_add_fusion.own_ref.refs_0_), channel_id=1, source_target_pairs={{0,2},{1,3},{2,0},{3,1},{4,6},{5,7},{6,4},{7,5},{8,10},{9,11},{10,... | collective-permute-start | bytes 589832 | tf_op jit(solution)/shard_map/ppermute | solution.py:171
  8.5 17.5 %collective-permute-start.1 = (s32[192,256]{1,0:T(8,128)S(1)}, s32[192,256]{1,0:T(8,128)S(1)}, u32[]{:S(2)}, u32[]{:S(2)}) collective-permute-start(s32[192,256]{1,0:T(8,128)S(1)} %pad_add_fusion.own_ref.refs_0_), channel_id=1, source_target_pairs={{0,8},{4,12},{8,0},{12,4},{1,9},{5,13},{9,1},{13,5},{2,10},{6,14},... | collective-permute-start | bytes 589832 | tf_op jit(solution)/shard_map/ppermute | solution.py:171
  10.1 15.9 %collective-permute-start = (s32[192,256]{1,0:T(8,128)S(1)}, s32[192,256]{1,0:T(8,128)S(1)}, u32[]{:S(2)}, u32[]{:S(2)}) collective-permute-start(s32[192,256]{1,0:T(8,128)S(1)} %pad_add_fusion.own_ref.refs_0_), channel_id=1, source_target_pairs={{0,4},{4,0},{8,12},{12,8},{1,5},{5,1},{9,13},{13,9},{2,6},{6,2},{1... | collective-permute-start | bytes 589832 | tf_op jit(solution)/shard_map/ppermute | solution.py:171
  13.6 12.9 %collective-permute-start.13 = (s32[192,256]{1,0:T(8,128)S(1)}, s32[192,256]{1,0:T(8,128)S(1)}, u32[]{:S(2)}, u32[]{:S(2)}) collective-permute-start(s32[192,256]{1,0:T(8,128)S(1)} %collective-permute-done.11.refs_12_), channel_id=1, source_target_pairs={{0,8},{4,12},{8,0},{12,4},{1,9},{5,13},{9,1},{13,5},{2,10},{6,14},... | collective-permute-start | bytes 589832 | tf_op jit(solution)/shard_map/ppermute | solution.py:171
  18.1 8.6 %collective-permute-start.5 = (s32[192,256]{1,0:T(8,128)S(1)}, s32[192,256]{1,0:T(8,128)S(1)}, u32[]{:S(2)}, u32[]{:S(2)}) collective-permute-start(s32[192,256]{1,0:T(8,128)S(1)} %collective-permute-done.3.refs_0_.refs_4_), channel_id=1, source_target_pairs={{0,8},{4,12},{8,0},{12,4},{1,9},{5,13},{9,1},{13,5},{2,10},{6,14},... | collective-permute-start | bytes 589832 | tf_op jit(solution)/shard_map/ppermute | solution.py:171
  24.6 6.0 %collective-permute-start.9 = (s32[192,256]{1,0:T(8,128)S(1)}, s32[192,256]{1,0:T(8,128)S(1)}, u32[]{:S(2)}, u32[]{:S(2)}) collective-permute-start(s32[192,256]{1,0:T(8,128)S(1)} %collective-permute-done.7.refs_0_.refs_8_), channel_id=1, source_target_pairs={{0,8},{4,12},{8,0},{12,4},{1,9},{5,13},{9,1},{13,5},{2,10},{6,14},... | collective-permute-start | bytes 589832 | tf_op jit(solution)/shard_map/ppermute | solution.py:171
  26.1 4.5 %collective-permute-start.4 = (s32[192,256]{1,0:T(8,128)S(1)}, s32[192,256]{1,0:T(8,128)S(1)}, u32[]{:S(2)}, u32[]{:S(2)}) collective-permute-start(s32[192,256]{1,0:T(8,128)S(1)} %collective-permute-done.3.refs_0_.refs_4_), channel_id=1, source_target_pairs={{0,4},{4,0},{8,12},{12,8},{1,5},{5,1},{9,13},{13,9},{2,6},{6,2},{1... | collective-permute-start | bytes 589832 | tf_op jit(solution)/shard_map/ppermute | solution.py:171
  26.1 5.0 %collective-permute-start.2 = (s32[192,256]{1,0:T(8,128)S(1)}, s32[192,256]{1,0:T(8,128)S(1)}, u32[]{:S(2)}, u32[]{:S(2)}) collective-permute-start(s32[192,256]{1,0:T(8,128)S(1)} %collective-permute-done.1.refs_2_), channel_id=1, source_target_pairs={{0,4},{4,0},{8,12},{12,8},{1,5},{5,1},{9,13},{13,9},{2,6},{6,2},{1... | collective-permute-start | bytes 589832 | tf_op jit(solution)/shard_map/ppermute | solution.py:171
  26.6 6.7 %collective-permute-start.8 = (s32[192,256]{1,0:T(8,128)S(1)}, s32[192,256]{1,0:T(8,128)S(1)}, u32[]{:S(2)}, u32[]{:S(2)}) collective-permute-start(s32[192,256]{1,0:T(8,128)S(1)} %collective-permute-done.7.refs_0_.refs_8_), channel_id=1, source_target_pairs={{0,4},{4,0},{8,12},{12,8},{1,5},{5,1},{9,13},{13,9},{2,6},{6,2},{1... | collective-permute-start | bytes 589832 | tf_op jit(solution)/shard_map/ppermute | solution.py:171
  26.6 5.5 %collective-permute-start.6 = (s32[192,256]{1,0:T(8,128)S(1)}, s32[192,256]{1,0:T(8,128)S(1)}, u32[]{:S(2)}, u32[]{:S(2)}) collective-permute-start(s32[192,256]{1,0:T(8,128)S(1)} %collective-permute-done.5.refs_2_.refs_6_), channel_id=1, source_target_pairs={{0,4},{4,0},{8,12},{12,8},{1,5},{5,1},{9,13},{13,9},{2,6},{6,2},{1... | collective-permute-start | bytes 589832 | tf_op jit(solution)/shard_map/ppermute | solution.py:171
  30.5 2.7 %collective-permute-start.10 = (s32[192,256]{1,0:T(8,128)S(1)}, s32[192,256]{1,0:T(8,128)S(1)}, u32[]{:S(2)}, u32[]{:S(2)}) collective-permute-start(s32[192,256]{1,0:T(8,128)S(1)} %collective-permute-done.9.refs_2_.refs_10_), channel_id=1, source_target_pairs={{0,4},{4,0},{8,12},{12,8},{1,5},{5,1},{9,13},{13,9},{2,6},{6,2},{1... | collective-permute-start | bytes 589832 | tf_op jit(solution)/shard_map/ppermute | solution.py:171
  30.5 3.8 %collective-permute-start.12 = (s32[192,256]{1,0:T(8,128)S(1)}, s32[192,256]{1,0:T(8,128)S(1)}, u32[]{:S(2)}, u32[]{:S(2)}) collective-permute-start(s32[192,256]{1,0:T(8,128)S(1)} %collective-permute-done.11.refs_12_), channel_id=1, source_target_pairs={{0,4},{4,0},{8,12},{12,8},{1,5},{5,1},{9,13},{13,9},{2,6},{6,2},{1... | collective-permute-start | bytes 589832 | tf_op jit(solution)/shard_map/ppermute | solution.py:171
  31.0 3.3 %collective-permute-start.14 = (s32[192,256]{1,0:T(8,128)S(1)}, s32[192,256]{1,0:T(8,128)S(1)}, u32[]{:S(2)}, u32[]{:S(2)}) collective-permute-start(s32[192,256]{1,0:T(8,128)S(1)} %collective-permute-done.13.refs_14_), channel_id=1, source_target_pairs={{0,4},{4,0},{8,12},{12,8},{1,5},{5,1},{9,13},{13,9},{2,6},{6,2},{1... | collective-permute-start | bytes 589832 | tf_op jit(solution)/shard_map/ppermute | solution.py:171
  36.1 6.8 %collective-permute-start.26 = (f32[64,256]{1,0:T(8,128)S(1)}, f32[64,256]{1,0:T(8,128)S(1)}, u32[]{:S(2)}, u32[]{:S(2)}) collective-permute-start(f32[64,256]{1,0:T(8,128)S(1)} %get-tuple-element.9.refs_0_), channel_id=1, source_target_pairs={{0,3},{1,2},{2,1},{3,0},{4,7},{5,6},{6,5},{7,4},{8,11},{9,10},{10,... | collective-permute-start | bytes 196616 | tf_op jit(solution)/shard_map/ppermute | solution.py:171
  38.5 6.8 %collective-permute-start.22 = (f32[64,256]{1,0:T(8,128)S(1)}, f32[64,256]{1,0:T(8,128)S(1)}, u32[]{:S(2)}, u32[]{:S(2)}) collective-permute-start(f32[64,256]{1,0:T(8,128)S(1)} %get-tuple-element.9.refs_0_), channel_id=1, source_target_pairs={{0,2},{1,3},{2,0},{3,1},{4,6},{5,7},{6,4},{7,5},{8,10},{9,11},{10,... | collective-permute-start | bytes 196616 | tf_op jit(solution)/shard_map/ppermute | solution.py:171
  38.5 6.8 %collective-permute-start.18 = (f32[64,256]{1,0:T(8,128)S(1)}, f32[64,256]{1,0:T(8,128)S(1)}, u32[]{:S(2)}, u32[]{:S(2)}) collective-permute-start(f32[64,256]{1,0:T(8,128)S(1)} %get-tuple-element.9.refs_0_), channel_id=1, source_target_pairs={{0,1},{1,0},{2,3},{3,2},{4,5},{5,4},{6,7},{7,6},{8,9},{9,8},{10,11... | collective-permute-start | bytes 196616 | tf_op jit(solution)/shard_map/ppermute | solution.py:171
  40.6 6.2 %collective-permute-start.16 = (f32[64,256]{1,0:T(8,128)S(1)}, f32[64,256]{1,0:T(8,128)S(1)}, u32[]{:S(2)}, u32[]{:S(2)}) collective-permute-start(f32[64,256]{1,0:T(8,128)S(1)} %get-tuple-element.9.refs_0_), channel_id=1, source_target_pairs={{0,8},{4,12},{8,0},{12,4},{1,9},{5,13},{9,1},{13,5},{2,10},{6,14},... | collective-permute-start | bytes 196616 | tf_op jit(solution)/shard_map/ppermute | solution.py:171
  42.1 4.9 %collective-permute-start.15 = (f32[64,256]{1,0:T(8,128)S(1)}, f32[64,256]{1,0:T(8,128)S(1)}, u32[]{:S(2)}, u32[]{:S(2)}) collective-permute-start(f32[64,256]{1,0:T(8,128)S(1)} %get-tuple-element.9.refs_0_), channel_id=1, source_target_pairs={{0,4},{4,0},{8,12},{12,8},{1,5},{5,1},{9,13},{13,9},{2,6},{6,2},{1... | collective-permute-start | bytes 196616 | tf_op jit(solution)/shard_map/ppermute | solution.py:171
  43.0 4.5 %collective-permute-start.28 = (f32[64,256]{1,0:T(8,128)S(1)}, f32[64,256]{1,0:T(8,128)S(1)}, u32[]{:S(2)}, u32[]{:S(2)}) collective-permute-start(f32[64,256]{1,0:T(8,128)S(1)} %collective-permute-done.26.refs_12_), channel_id=1, source_target_pairs={{0,8},{4,12},{8,0},{12,4},{1,9},{5,13},{9,1},{13,5},{2,10},{6,14},... | collective-permute-start | bytes 196616 | tf_op jit(solution)/shard_map/ppermute | solution.py:171
  45.3 2.3 %collective-permute-start.27 = (f32[64,256]{1,0:T(8,128)S(1)}, f32[64,256]{1,0:T(8,128)S(1)}, u32[]{:S(2)}, u32[]{:S(2)}) collective-permute-start(f32[64,256]{1,0:T(8,128)S(1)} %collective-permute-done.26.refs_12_), channel_id=1, source_target_pairs={{0,4},{4,0},{8,12},{12,8},{1,5},{5,1},{9,13},{13,9},{2,6},{6,2},{1... | collective-permute-start | bytes 196616 | tf_op jit(solution)/shard_map/ppermute | solution.py:171
  45.3 4.5 %collective-permute-start.24 = (f32[64,256]{1,0:T(8,128)S(1)}, f32[64,256]{1,0:T(8,128)S(1)}, u32[]{:S(2)}, u32[]{:S(2)}) collective-permute-start(f32[64,256]{1,0:T(8,128)S(1)} %collective-permute-done.22.refs_8_), channel_id=1, source_target_pairs={{0,8},{4,12},{8,0},{12,4},{1,9},{5,13},{9,1},{13,5},{2,10},{6,14},... | collective-permute-start | bytes 196616 | tf_op jit(solution)/shard_map/ppermute | solution.py:171
  46.8 3.0 %collective-permute-start.23 = (f32[64,256]{1,0:T(8,128)S(1)}, f32[64,256]{1,0:T(8,128)S(1)}, u32[]{:S(2)}, u32[]{:S(2)}) collective-permute-start(f32[64,256]{1,0:T(8,128)S(1)} %collective-permute-done.22.refs_8_), channel_id=1, source_target_pairs={{0,4},{4,0},{8,12},{12,8},{1,5},{5,1},{9,13},{13,9},{2,6},{6,2},{1... | collective-permute-start | bytes 196616 | tf_op jit(solution)/shard_map/ppermute | solution.py:171
  47.0 4.3 %collective-permute-start.20 = (f32[64,256]{1,0:T(8,128)S(1)}, f32[64,256]{1,0:T(8,128)S(1)}, u32[]{:S(2)}, u32[]{:S(2)}) collective-permute-start(f32[64,256]{1,0:T(8,128)S(1)} %collective-permute-done.18.refs_4_), channel_id=1, source_target_pairs={{0,8},{4,12},{8,0},{12,4},{1,9},{5,13},{9,1},{13,5},{2,10},{6,14},... | collective-permute-start | bytes 196616 | tf_op jit(solution)/shard_map/ppermute | solution.py:171
  47.5 3.8 %collective-permute-start.19 = (f32[64,256]{1,0:T(8,128)S(1)}, f32[64,256]{1,0:T(8,128)S(1)}, u32[]{:S(2)}, u32[]{:S(2)}) collective-permute-start(f32[64,256]{1,0:T(8,128)S(1)} %collective-permute-done.18.refs_4_), channel_id=1, source_target_pairs={{0,4},{4,0},{8,12},{12,8},{1,5},{5,1},{9,13},{13,9},{2,6},{6,2},{1... | collective-permute-start | bytes 196616 | tf_op jit(solution)/shard_map/ppermute | solution.py:171
  47.6 3.7 %collective-permute-start.17 = (f32[64,256]{1,0:T(8,128)S(1)}, f32[64,256]{1,0:T(8,128)S(1)}, u32[]{:S(2)}, u32[]{:S(2)}) collective-permute-start(f32[64,256]{1,0:T(8,128)S(1)} %collective-permute-done.16.refs_2_), channel_id=1, source_target_pairs={{0,4},{4,0},{8,12},{12,8},{1,5},{5,1},{9,13},{13,9},{2,6},{6,2},{1... | collective-permute-start | bytes 196616 | tf_op jit(solution)/shard_map/ppermute | solution.py:171
  49.8 1.5 %collective-permute-start.29 = (f32[64,256]{1,0:T(8,128)S(1)}, f32[64,256]{1,0:T(8,128)S(1)}, u32[]{:S(2)}, u32[]{:S(2)}) collective-permute-start(f32[64,256]{1,0:T(8,128)S(1)} %collective-permute-done.28.refs_14_), channel_id=1, source_target_pairs={{0,4},{4,0},{8,12},{12,8},{1,5},{5,1},{9,13},{13,9},{2,6},{6,2},{1... | collective-permute-start | bytes 196616 | tf_op jit(solution)/shard_map/ppermute | solution.py:171
  49.8 1.6 %collective-permute-start.25 = (f32[64,256]{1,0:T(8,128)S(1)}, f32[64,256]{1,0:T(8,128)S(1)}, u32[]{:S(2)}, u32[]{:S(2)}) collective-permute-start(f32[64,256]{1,0:T(8,128)S(1)} %collective-permute-done.24.refs_10_), channel_id=1, source_target_pairs={{0,4},{4,0},{8,12},{12,8},{1,5},{5,1},{9,13},{13,9},{2,6},{6,2},{1... | collective-permute-start | bytes 196616 | tf_op jit(solution)/shard_map/ppermute | solution.py:171
  51.3 1.3 %collective-permute-start.21 = (f32[64,256]{1,0:T(8,128)S(1)}, f32[64,256]{1,0:T(8,128)S(1)}, u32[]{:S(2)}, u32[]{:S(2)}) collective-permute-start(f32[64,256]{1,0:T(8,128)S(1)} %collective-permute-done.20.refs_6_), channel_id=1, source_target_pairs={{0,4},{4,0},{8,12},{12,8},{1,5},{5,1},{9,13},{13,9},{2,6},{6,2},{1... | collective-permute-start | bytes 196616 | tf_op jit(solution)/shard_map/ppermute | solution.py:171

commit v2 on v1

--- a/solution.py
+++ b/solution.py
@@ -102,6 +102,27 @@
     return upper[:, n:] * lax.rsqrt(pivots)
 
 
+def thirds(value):
+    high = value.astype(BF16)
+    rest = value - high.astype(F32)
+    middle = rest.astype(BF16)
+    return jnp.concatenate([high, middle, (rest - middle.astype(F32)).astype(BF16)], axis=0)
+
+
+def gram_of(stack):
+    n = stack.shape[0] // 3
+    p = matmul(stack, stack, (1, 1))
+    middle = p[n : 2 * n, n : 2 * n] + (p[:n, 2 * n :] + p[2 * n :, :n])
+    return p[:n, :n] + ((p[:n, n : 2 * n] + p[n : 2 * n, :n]) + middle)
+
+
+def times(matrix, stack):
+    n = matrix.shape[0]
+    parts = thirds(matrix)
+    p = matmul(jnp.concatenate([parts, parts, parts], axis=1), stack, (1, 0))
+    return p[:n] + (p[n : 2 * n] + p[2 * n :])
+
+
 def second_kernel(count, last, total, copies, *refs):
     images = refs[:count]
     tiles = refs[count : count + count // last]
@@ -112,23 +133,17 @@
     for value in values[1:]:
         sums = sums + value
     mean = jnp.sum(sums, axis=1, keepdims=True) / total
-    gram = None
-    centered = []
-    for value in values:
-        centered.append(value - mean)
-        term = matmul(centered[-1], centered[-1], (1, 1), HIGHEST)
-        gram = term if gram is None else gram + term
-    solve = math.sqrt(total) * inverse_factor(gram)
+    stack = thirds(jnp.concatenate([value - mean for value in values], axis=1))
+    solve = math.sqrt(total) * inverse_factor(gram_of(stack))
+    vectors = times(solve, stack).astype(BF16)
     result = None
-    for b, value in enumerate(centered):
-        part, inner = divmod(b, last)
-        vectors = matmul(solve, value, (1, 0), HIGHEST).astype(BF16)
-        term = matmul(vectors, tiles[part][pl.ds(inner * size, size), :], (1, 0))
+    for t, tile in enumerate(tiles):
+        depth = tile.shape[0]
+        term = matmul(vectors[:, t * depth : (t + 1) * depth], tile[...], (1, 0))
         result = term if result is None else result + term
     out_ref[...] = result
     local_mean = jnp.sum(result, axis=1, keepdims=True) / size
-    local = result - local_mean
-    local_gram = matmul(local, local, (1, 1), HIGHEST)
+    local_gram = gram_of(thirds(result - local_mean))
     h = local_gram.shape[0] // 2
     share = jnp.concatenate(
         [local_gram[:h], local_gram[h:, h:], local_mean[:h], local_mean[h:], jnp.zeros((h, h - 2), F32)], axis=1
@@ -154,29 +169,38 @@
     out_ref[...] = matmul(solve, images_ref[...] - mean, (1, 0), HIGHEST)
 
 
-def call(kernel, args, out_shape):
+def call(kernel, args, out_shape, flops=0):
     return pl.pallas_call(
         kernel,
         out_shape=out_shape,
         in_specs=[VMEM] * len(args),
         out_specs=jax.tree.map(lambda _: VMEM, out_shape),
         compiler_params=pltpu.CompilerParams(vmem_limit_bytes=48 * 2**20),
+        cost_estimate=pl.CostEstimate(flops=flops, bytes_accessed=flops // 300, transcendentals=0) if flops else None,
     )(*args)
 
 
-def gather_blocks(block):
+def after(value, *others):
+    return lax.optimization_barrier((value, *others))[0]
+
+
+def gather_blocks(block, work=None):
     rows, cols = lax.axis_size("row"), lax.axis_size("col")
 
     def swap(value, axis, size, offset):
-        return lax.ppermute(value, axis, [(i, i ^ offset) for i in range(size)]) if offset else value
-
-    out = []
+        return lax.ppermute(value, axis, [(i, i ^ offset) for i in range(size)])
+
+    along = [block] + [swap(block, "col", cols, c) for c in range(1, cols)]
+    groups, done = [], []
     for c in range(cols):
-        along = swap(block, "col", cols, c)
-        for r in range(0, rows, 2):
-            chip = swap(along, "row", rows, r)
-            out += [chip, swap(chip, "row", rows, 1)]
-    return out
+        chips = [along[c]]
+        chips += [swap(along[c], "row", rows, r) for r in range(2, rows, 2)]
+        if work and 1 <= c < cols:
+            done.append(work(groups[c - 1]))
+        if work and c == cols - 1:
+            chips[-1] = after(chips[-1], *done[:-1])
+        groups.append([b for chip in chips for b in (chip, swap(chip, "row", rows, 1))])
+    return groups, done
 
 
 def local(corpus, sample_rows, initial):
@@ -187,22 +211,27 @@
     last = rows
     total = float(size * count)
     scale = UNIT * UNIT / (2.0 * corpus.shape[1])
-    landmarks = corpus.at[sample_rows].get(mode="promise_in_bounds")
+    landmarks = lax.gather(
+        corpus,
+        sample_rows[:, None],
+        lax.GatherDimensionNumbers(offset_dims=(1,), collapsed_slice_dims=(0,), start_index_map=(0,)),
+        (1, corpus.shape[1]),
+        mode="promise_in_bounds",
+    )
     own = encode(landmarks, initial)
-    blocks = gather_blocks(own)
-    tiles = []
-    for g in range(0, count - last, last):
-        group = blocks[g : g + last]
-        tiles.append(
-            call(functools.partial(build_kernel, last, half, scale), [own] + group, jax.ShapeDtypeStruct((last * size, size), BF16))
-        )
+
+    def build(group):
+        return call(functools.partial(build_kernel, last, half, scale), [own] + group, jax.ShapeDtypeStruct((last * size, size), BF16), 10**9)
+
+    groups, tiles = gather_blocks(own, build)
+    blocks = [block for group in groups for block in group]
     images, tile = call(
         functools.partial(first_kernel, count, last, half, scale, total),
         [own] + blocks + tiles,
         (jax.ShapeDtypeStruct((vecs, size), F32), jax.ShapeDtypeStruct((last * size, size), BF16)),
     )
     tiles.append(tile)
-    gathered = gather_blocks(images)
+    gathered = [block for group in gather_blocks(images)[0] for block in group]
     images, share = call(
         functools.partial(second_kernel, count, last, total, count),
         gathered + tiles,

time: 77.6 us -> 75.8 us (0.977)
  waiting for transfers between devices: 20.4 us -> 23.6 us
  Pallas kernels: 15.5 us -> 13.3 us
  starting transfers between devices: 24.3 us -> 22.3 us
    ppermute x30, waiting for transfers between devices: 20.4 us -> 23.6 us  [swap(): return lax.ppermute(value, axis, [(i, i ^ offset) for i in range(size)])]
    pallas_call x6, Pallas kernels: 15.5 us -> 13.3 us  [call(): pl.pallas_call(kernel, out_shape=out_shape, in_specs=[VMEM] * len(args),...]
    ppermute x30, starting transfers between devices: 24.3 us -> 22.3 us  [swap(): return lax.ppermute(value, axis, [(i, i ^ offset) for i in range(size)])]
    select_n x1 -> x0, other arithmetic: 0.83 us -> none  [local(): landmarks = corpus.at[sample_rows].get(mode='promise_in_bounds')]
    gather x1, other arithmetic: 0.01 us -> 0.83 us  [local(): lax.gather(corpus, sample_rows[:, None], lax.GatherDimensionNumbers(offse...]
  transfers between devices with their start and end apart: 30 -> 30, of which waited for: 9 -> 12; matrix products, arithmetic and copies ran while one was open for 0% -> 0% of each run, Pallas kernels for 4% -> 4%
where the time goes in v2:
time: 75.8 us; the launch traced here: 75.6 us
  waiting for transfers between devices  23.6 us (31%)
  starting transfers between devices  22.3 us (29%)
  blocking collectives  13.6 us (18%)
  Pallas kernels  13.3 us (18%)
  other arithmetic  1.74 us (2%)
  local copies, waits for them, and re-layouts  0.97 us (1%)
    ppermute x30, waiting for transfers between devices, swap(): return lax.ppermute(value, axis, [(i, i ^ offset) for i in range(size)])  23.6 us
    ppermute x30, starting transfers between devices, swap(): return lax.ppermute(value, axis, [(i, i ^ offset) for i in range(size)])  22.3 us
    all_to_all x1, blocking collectives, local(): shares = lax.all_to_all(share, ('row', 'col'), split_axis=0, concat_axis=0)  13.6 us
    pallas_call x6, Pallas kernels, call(): pl.pallas_call(kernel, out_shape=out_shape, in_specs=[VMEM] * len(args),...  13.3 us
  transfers between devices with their start and end apart: 30, of which 12 were waited for; matrix products, arithmetic and copies ran while one was open for 0% of the time, Pallas kernels for 4%

profile of v2, /device:TPU:0, one launch (start us, length us, event | category | flops | bytes accessed | tf_op | source)
XLA Modules:
  0.0 75.6 jit_solution(8208188367453911303)
XLA Ops:
  0.0 0.8 %pad_clamp_fusion = s32[1024]{0:T(1024)S(1)} fusion(s32[256]{0:T(256)} %param.4), kind=kLoop, calls=%fused_computation.7 | loop fusion | flops 1024 | bytes 5120 | tf_op jit(solution)/shard_map/gather | solution.py:214
  0.8 0.8 %round-nearest-even_convert_fusion.1 = s32[64,256]{1,0:T(8,128)S(1)} fusion(f32[64,256]{1,0:T(8,128)} %param.5), kind=kLoop, calls=%fused_computation.6 | loop fusion | flops 49152 | bytes 131072 | tf_op jit(solution)/shard_map/convert_element_type | solution.py:28
  1.7 1.0 %gather_fusion = f32[256,256]{1,0:T(8,128)S(1)} fusion(f32[2048,256]{1,0:T(8,128)S(1)} %copy-done, s32[1024]{0:T(1024)S(1)} %pad_clamp_fusion), kind=kCustom, calls=%fused_computation | custom fusion | bytes 525312 | tf_op jit(solution)/shard_map/gather | solution.py:214
  2.7 3.1 %collective-permute-start.3 = (s32[192,256]{1,0:T(8,128)S(1)}, s32[192,256]{1,0:T(8,128)S(1)}, u32[]{:S(2)}, u32[]{:S(2)}) collective-permute-start(s32[192,256]{1,0:T(8,128)S(1)} %pad_add_fusion.own_ref.refs_0_), channel_id=1, source_target_pairs={{0,1},{1,0},{2,3},{3,2},{4,5},{5,4},{6,7},{7,6},{8,9},{9,8},{10,11... | collective-permute-start | bytes 589832 | tf_op jit(solution)/shard_map/ppermute | solution.py:191
  5.8 1.5 %collective-permute-start.1 = (s32[192,256]{1,0:T(8,128)S(1)}, s32[192,256]{1,0:T(8,128)S(1)}, u32[]{:S(2)}, u32[]{:S(2)}) collective-permute-start(s32[192,256]{1,0:T(8,128)S(1)} %pad_add_fusion.own_ref.refs_0_), channel_id=1, source_target_pairs={{0,8},{4,12},{8,0},{12,4},{1,9},{5,13},{9,1},{13,5},{2,10},{6,14},... | collective-permute-start | bytes 589832 | tf_op jit(solution)/shard_map/ppermute | solution.py:191
  7.3 2.6 %collective-permute-start.7 = (s32[192,256]{1,0:T(8,128)S(1)}, s32[192,256]{1,0:T(8,128)S(1)}, u32[]{:S(2)}, u32[]{:S(2)}) collective-permute-start(s32[192,256]{1,0:T(8,128)S(1)} %pad_add_fusion.own_ref.refs_0_), channel_id=1, source_target_pairs={{0,2},{1,3},{2,0},{3,1},{4,6},{5,7},{6,4},{7,5},{8,10},{9,11},{10,... | collective-permute-start | bytes 589832 | tf_op jit(solution)/shard_map/ppermute | solution.py:191
  9.9 0.2 collective-permute-start.11
  10.1 2.8 %collective-permute-done.3.refs_0_.refs_4_ = s32[192,256]{1,0:T(8,128)S(1)} collective-permute-done((s32[192,256]{1,0:T(8,128)S(1)}, s32[192,256]{1,0:T(8,128)S(1)}, u32[]{:S(2)}, u32[]{:S(2)}) %collective-permute-start.3) | collective-permute-done | bytes 196640 | tf_op jit(solution)/shard_map/ppermute | solution.py:191
  13.0 2.5 %collective-permute-start.5 = (s32[192,256]{1,0:T(8,128)S(1)}, s32[192,256]{1,0:T(8,128)S(1)}, u32[]{:S(2)}, u32[]{:S(2)}) collective-permute-start(s32[192,256]{1,0:T(8,128)S(1)} %collective-permute-done.3.refs_0_.refs_4_), channel_id=1, source_target_pairs={{0,8},{4,12},{8,0},{12,4},{1,9},{5,13},{9,1},{13,5},{2,10},{6,14},... | collective-permute-start | bytes 589832 | tf_op jit(solution)/shard_map/ppermute | solution.py:191
  15.5 0.0 collective-permute-start
  15.5 0.0 collective-permute-done.1.refs_2_
  15.5 0.5 collective-permute-start.2
  16.0 8.5 %collective-permute-done.7.refs_0_.refs_8_ = s32[192,256]{1,0:T(8,128)S(1)} collective-permute-done((s32[192,256]{1,0:T(8,128)S(1)}, s32[192,256]{1,0:T(8,128)S(1)}, u32[]{:S(2)}, u32[]{:S(2)}) %collective-permute-start.7) | collective-permute-done | bytes 196640 | tf_op jit(solution)/shard_map/ppermute | solution.py:191
  24.5 0.5 collective-permute-start.9
  25.0 0.0 collective-permute-done.11.refs_12_
  25.0 0.0 collective-permute-start.4
  25.0 0.0 collective-permute-done.5.refs_2_.refs_6_
  25.0 0.5 collective-permute-start.6
  25.5 0.0 collective-permute-done.refs_1_
  25.5 1.5 %collective-permute-start.13 = (s32[192,256]{1,0:T(8,128)S(1)}, s32[192,256]{1,0:T(8,128)S(1)}, u32[]{:S(2)}, u32[]{:S(2)}) collective-permute-start(s32[192,256]{1,0:T(8,128)S(1)} %collective-permute-done.11.refs_12_), channel_id=1, source_target_pairs={{0,8},{4,12},{8,0},{12,4},{1,9},{5,13},{9,1},{13,5},{2,10},{6,14},... | collective-permute-start | bytes 589832 | tf_op jit(solution)/shard_map/ppermute | solution.py:191
  27.0 0.0 collective-permute-done.2.refs_3_
  27.0 0.0 collective-permute-start.12
  27.0 1.1 %shard_map.37.refs_16_ = bf16[1024,256]{1,0:T(8,128)(2,1)S(1)} custom-call(s32[192,256]{1,0:T(8,128)S(1)} %pad_add_fusion.own_ref.refs_0_, s32[192,256]{1,0:T(8,128)S(1)} %pad_add_fusion.own_ref.refs_0_, s32[192,256]{1,0:T(8,128)S(1)} %collective-permute-done.refs_1_, s32[192,256]{1,0:T(8,128)S(1)} %collective-permute-done.1.refs_2_, ...), custom_call_target="tpu_custom_call" | custom-call | flops 1000000000 | bytes 3333333 | tf_op jit(solution)/shard_map/pallas_call | solution.py:173
  28.1 4.0 %collective-permute-done.9.refs_2_.refs_10_ = s32[192,256]{1,0:T(8,128)S(1)} collective-permute-done((s32[192,256]{1,0:T(8,128)S(1)}, s32[192,256]{1,0:T(8,128)S(1)}, u32[]{:S(2)}, u32[]{:S(2)}) %collective-permute-start.9) | collective-permute-done | bytes 196640 | tf_op jit(solution)/shard_map/ppermute | solution.py:191
  32.1 0.0 collective-permute-start.8
  32.1 0.0 collective-permute-done.4.refs_1_.refs_5_
  32.1 0.5 collective-permute-start.10
  32.6 0.0 collective-permute-done.6.refs_3_.refs_7_
  32.6 1.1 %shard_map.38.refs_17_ = bf16[1024,256]{1,0:T(8,128)(2,1)S(1)} custom-call(s32[192,256]{1,0:T(8,128)S(1)} %pad_add_fusion.own_ref.refs_0_, s32[192,256]{1,0:T(8,128)S(1)} %collective-permute-done.3.refs_0_.refs_4_, s32[192,256]{1,0:T(8,128)S(1)} %collective-permute-done.4.refs_1_.refs_5_, s32[192,256]{1,0:T(8,128)S(1)} %collective-permute-done.5.refs_2_.refs_6_, ...), custom_call_target="tpu_custom_call" | custom-call | flops 1000000000 | bytes 3333333 | tf_op jit(solution)/shard_map/pallas_call | solution.py:173
  33.7 0.7 collective-permute-done.13.refs_14_
  34.4 0.0 collective-permute-start.14
  34.4 0.0 collective-permute-done.8.refs_1_.refs_9_
  34.4 0.0 collective-permute-done.10.refs_3_.refs_11_
  34.4 1.1 %shard_map.39.refs_18_ = bf16[1024,256]{1,0:T(8,128)(2,1)S(1)} custom-call(s32[192,256]{1,0:T(8,128)S(1)} %pad_add_fusion.own_ref.refs_0_, s32[192,256]{1,0:T(8,128)S(1)} %collective-permute-done.7.refs_0_.refs_8_, s32[192,256]{1,0:T(8,128)S(1)} %collective-permute-done.8.refs_1_.refs_9_, s32[192,256]{1,0:T(8,128)S(1)} %collective-permute-done.9.refs_2_.refs_10_, ...), custom_call_target="tpu_custom_call" | custom-call | flops 1000000000 | bytes 3333333 | tf_op jit(solution)/shard_map/pallas_call | solution.py:173
  35.5 0.0 collective-permute-done.12.refs_13_
  35.5 0.4 collective-permute-done.14.refs_15_
  35.8 1.8 %shard_map.40 = (f32[64,256]{1,0:T(8,128)S(1)}, bf16[1024,256]{1,0:T(8,128)(2,1)S(1)}) custom-call(s32[192,256]{1,0:T(8,128)S(1)} %pad_add_fusion.own_ref.refs_0_, s32[192,256]{1,0:T(8,128)S(1)} %pad_add_fusion.own_ref.refs_0_, s32[192,256]{1,0:T(8,128)S(1)} %collective-permute-done.refs_1_, s32[192,256]{1,0:T(8,128)S(1)} %collective-permute-done.1.refs_2_, ...), custom_call_target="tpu_custom_call" | custom-call | tf_op jit(solution)/shard_map/pallas_call | solution.py:173
  37.6 2.2 %collective-permute-start.26 = (f32[64,256]{1,0:T(8,128)S(1)}, f32[64,256]{1,0:T(8,128)S(1)}, u32[]{:S(2)}, u32[]{:S(2)}) collective-permute-start(f32[64,256]{1,0:T(8,128)S(1)} %get-tuple-element.11.refs_0_), channel_id=1, source_target_pairs={{0,3},{1,2},{2,1},{3,0},{4,7},{5,6},{6,5},{7,4},{8,11},{9,10},{10,... | collective-permute-start | bytes 196616 | tf_op jit(solution)/shard_map/ppermute | solution.py:191
  39.8 0.0 collective-permute-start.22
  39.8 2.2 %collective-permute-start.18 = (f32[64,256]{1,0:T(8,128)S(1)}, f32[64,256]{1,0:T(8,128)S(1)}, u32[]{:S(2)}, u32[]{:S(2)}) collective-permute-start(f32[64,256]{1,0:T(8,128)S(1)} %get-tuple-element.11.refs_0_), channel_id=1, source_target_pairs={{0,1},{1,0},{2,3},{3,2},{4,5},{5,4},{6,7},{7,6},{8,9},{9,8},{10,11... | collective-permute-start | bytes 196616 | tf_op jit(solution)/shard_map/ppermute | solution.py:191
  42.0 0.5 collective-permute-start.16
  42.6 0.0 collective-permute-start.15
  42.6 1.8 %collective-permute-done.26.refs_12_ = f32[64,256]{1,0:T(8,128)S(1)} collective-permute-done((f32[64,256]{1,0:T(8,128)S(1)}, f32[64,256]{1,0:T(8,128)S(1)}, u32[]{:S(2)}, u32[]{:S(2)}) %collective-permute-start.26) | collective-permute-done | bytes 65568 | tf_op jit(solution)/shard_map/ppermute | solution.py:191
  44.4 0.5 collective-permute-start.28
  45.0 1.5 %collective-permute-done.22.refs_8_ = f32[64,256]{1,0:T(8,128)S(1)} collective-permute-done((f32[64,256]{1,0:T(8,128)S(1)}, f32[64,256]{1,0:T(8,128)S(1)}, u32[]{:S(2)}, u32[]{:S(2)}) %collective-permute-start.22) | collective-permute-done | bytes 65568 | tf_op jit(solution)/shard_map/ppermute | solution.py:191
  46.4 0.0 collective-permute-start.27
  46.4 0.5 collective-permute-start.24
  47.0 0.2 collective-permute-start.23
  47.2 1.5 %collective-permute-start.20 = (f32[64,256]{1,0:T(8,128)S(1)}, f32[64,256]{1,0:T(8,128)S(1)}, u32[]{:S(2)}, u32[]{:S(2)}) collective-permute-start(f32[64,256]{1,0:T(8,128)S(1)} %collective-permute-done.18.refs_4_), channel_id=1, source_target_pairs={{0,8},{4,12},{8,0},{12,4},{1,9},{5,13},{9,1},{13,5},{2,10},{6,14},... | collective-permute-start | bytes 196616 | tf_op jit(solution)/shard_map/ppermute | solution.py:191
  48.7 0.0 collective-permute-done.28.refs_14_
  48.7 0.0 collective-permute-start.19
  48.7 0.0 collective-permute-done.27.refs_13_
  48.7 0.5 collective-permute-start.17
  49.2 2.1 %collective-permute-done.24.refs_10_ = f32[64,256]{1,0:T(8,128)S(1)} collective-permute-done((f32[64,256]{1,0:T(8,128)S(1)}, f32[64,256]{1,0:T(8,128)S(1)}, u32[]{:S(2)}, u32[]{:S(2)}) %collective-permute-start.24) | collective-permute-done | bytes 65568 | tf_op jit(solution)/shard_map/ppermute | solution.py:191
  51.3 0.0 collective-permute-start.29
  51.3 0.0 collective-permute-done.23.refs_9_
  51.3 0.5 collective-permute-start.25
  51.8 0.5 collective-permute-done.20.refs_6_
  52.4 0.2 collective-permute-done.29.refs_15_
  52.6 0.2 collective-permute-done.25.refs_11_
  52.8 0.8 %collective-permute-done.21.refs_7_ = f32[64,256]{1,0:T(8,128)S(1)} collective-permute-done((f32[64,256]{1,0:T(8,128)S(1)}, f32[64,256]{1,0:T(8,128)S(1)}, u32[]{:S(2)}, u32[]{:S(2)}) %collective-permute-start.21) | collective-permute-done | bytes 65568 | tf_op jit(solution)/shard_map/ppermute | solution.py:191
  53.6 5.1 %shard_map.41 = (f32[64,256]{1,0:T(8,128)S(1)}, f32[16,32,128]{2,1,0:T(8,128)S(1)}) custom-call(f32[64,256]{1,0:T(8,128)S(1)} %get-tuple-element.11.refs_0_, f32[64,256]{1,0:T(8,128)S(1)} %collective-permute-done.15.refs_1_, f32[64,256]{1,0:T(8,128)S(1)} %collective-permute-done.16.refs_2_, f32[64,256]{1,0:T(8,128)S(1)} %collective-permute-done.17.refs_3_, ...), custom_call_target="tpu_custom_call" | custom-call | tf_op jit(solution)/shard_map/pallas_call | solution.py:173
  58.7 13.6 %all_to_all.5.shares_ref = f32[16,32,128]{2,1,0:T(8,128)S(1)} all-to-all(f32[16,32,128]{2,1,0:T(8,128)S(1)} %get-tuple-element.13), channel_id=1, replica_groups=mesh['groups'=2,'row'=4,'col'=4] {'row','col'}, dimensions={0} | all-to-all | bytes 524288 | tf_op jit(solution)/shard_map/all_to_all | solution.py:240
  72.3 3.3 %shard_map.42 = f32[64,256]{1,0:T(8,128)} custom-call(f32[16,32,128]{2,1,0:T(8,128)S(1)} %all_to_all.5.shares_ref, f32[64,256]{1,0:T(8,128)S(1)} %get-tuple-element.14.images_ref), custom_call_target="tpu_custom_call" | custom-call | tf_op jit(solution)/shard_map/pallas_call | solution.py:173
  (11 shorter events, 0.1 us)
Async XLA Ops:
  0.0 1.7 %copy-start = (f32[2048,256]{1,0:T(8,128)S(1)}, f32[2048,256]{1,0:T(8,128)}, u32[]{:S(2)}) copy-start(f32[2048,256]{1,0:T(8,128)} %param.3) | copy-start | bytes 6291460
  2.7 10.2 %collective-permute-start.3 = (s32[192,256]{1,0:T(8,128)S(1)}, s32[192,256]{1,0:T(8,128)S(1)}, u32[]{:S(2)}, u32[]{:S(2)}) collective-permute-start(s32[192,256]{1,0:T(8,128)S(1)} %pad_add_fusion.own_ref.refs_0_), channel_id=1, source_target_pairs={{0,1},{1,0},{2,3},{3,2},{4,5},{5,4},{6,7},{7,6},{8,9},{9,8},{10,11... | collective-permute-start | bytes 589832 | tf_op jit(solution)/shard_map/ppermute | solution.py:191
  5.8 9.7 %collective-permute-start.1 = (s32[192,256]{1,0:T(8,128)S(1)}, s32[192,256]{1,0:T(8,128)S(1)}, u32[]{:S(2)}, u32[]{:S(2)}) collective-permute-start(s32[192,256]{1,0:T(8,128)S(1)} %pad_add_fusion.own_ref.refs_0_), channel_id=1, source_target_pairs={{0,8},{4,12},{8,0},{12,4},{1,9},{5,13},{9,1},{13,5},{2,10},{6,14},... | collective-permute-start | bytes 589832 | tf_op jit(solution)/shard_map/ppermute | solution.py:191
  7.3 17.2 %collective-permute-start.7 = (s32[192,256]{1,0:T(8,128)S(1)}, s32[192,256]{1,0:T(8,128)S(1)}, u32[]{:S(2)}, u32[]{:S(2)}) collective-permute-start(s32[192,256]{1,0:T(8,128)S(1)} %pad_add_fusion.own_ref.refs_0_), channel_id=1, source_target_pairs={{0,2},{1,3},{2,0},{3,1},{4,6},{5,7},{6,4},{7,5},{8,10},{9,11},{10,... | collective-permute-start | bytes 589832 | tf_op jit(solution)/shard_map/ppermute | solution.py:191
  9.9 15.1 %collective-permute-start.11 = (s32[192,256]{1,0:T(8,128)S(1)}, s32[192,256]{1,0:T(8,128)S(1)}, u32[]{:S(2)}, u32[]{:S(2)}) collective-permute-start(s32[192,256]{1,0:T(8,128)S(1)} %pad_add_fusion.own_ref.refs_0_), channel_id=1, source_target_pairs={{0,3},{1,2},{2,1},{3,0},{4,7},{5,6},{6,5},{7,4},{8,11},{9,10},{10,... | collective-permute-start | bytes 589832 | tf_op jit(solution)/shard_map/ppermute | solution.py:191
  13.0 12.1 %collective-permute-start.5 = (s32[192,256]{1,0:T(8,128)S(1)}, s32[192,256]{1,0:T(8,128)S(1)}, u32[]{:S(2)}, u32[]{:S(2)}) collective-permute-start(s32[192,256]{1,0:T(8,128)S(1)} %collective-permute-done.3.refs_0_.refs_4_), channel_id=1, source_target_pairs={{0,8},{4,12},{8,0},{12,4},{1,9},{5,13},{9,1},{13,5},{2,10},{6,14},... | collective-permute-start | bytes 589832 | tf_op jit(solution)/shard_map/ppermute | solution.py:191
  15.5 10.0 %collective-permute-start = (s32[192,256]{1,0:T(8,128)S(1)}, s32[192,256]{1,0:T(8,128)S(1)}, u32[]{:S(2)}, u32[]{:S(2)}) collective-permute-start(s32[192,256]{1,0:T(8,128)S(1)} %pad_add_fusion.own_ref.refs_0_), channel_id=1, source_target_pairs={{0,4},{4,0},{8,12},{12,8},{1,5},{5,1},{9,13},{13,9},{2,6},{6,2},{1... | collective-permute-start | bytes 589832 | tf_op jit(solution)/shard_map/ppermute | solution.py:191
  15.5 11.5 %collective-permute-start.2 = (s32[192,256]{1,0:T(8,128)S(1)}, s32[192,256]{1,0:T(8,128)S(1)}, u32[]{:S(2)}, u32[]{:S(2)}) collective-permute-start(s32[192,256]{1,0:T(8,128)S(1)} %collective-permute-done.1.refs_2_), channel_id=1, source_target_pairs={{0,4},{4,0},{8,12},{12,8},{1,5},{5,1},{9,13},{13,9},{2,6},{6,2},{1... | collective-permute-start | bytes 589832 | tf_op jit(solution)/shard_map/ppermute | solution.py:191
  24.5 7.6 %collective-permute-start.9 = (s32[192,256]{1,0:T(8,128)S(1)}, s32[192,256]{1,0:T(8,128)S(1)}, u32[]{:S(2)}, u32[]{:S(2)}) collective-permute-start(s32[192,256]{1,0:T(8,128)S(1)} %collective-permute-done.7.refs_0_.refs_8_), channel_id=1, source_target_pairs={{0,8},{4,12},{8,0},{12,4},{1,9},{5,13},{9,1},{13,5},{2,10},{6,14},... | collective-permute-start | bytes 589832 | tf_op jit(solution)/shard_map/ppermute | solution.py:191
  25.0 7.1 %collective-permute-start.4 = (s32[192,256]{1,0:T(8,128)S(1)}, s32[192,256]{1,0:T(8,128)S(1)}, u32[]{:S(2)}, u32[]{:S(2)}) collective-permute-start(s32[192,256]{1,0:T(8,128)S(1)} %collective-permute-done.3.refs_0_.refs_4_), channel_id=1, source_target_pairs={{0,4},{4,0},{8,12},{12,8},{1,5},{5,1},{9,13},{13,9},{2,6},{6,2},{1... | collective-permute-start | bytes 589832 | tf_op jit(solution)/shard_map/ppermute | solution.py:191
  25.0 7.6 %collective-permute-start.6 = (s32[192,256]{1,0:T(8,128)S(1)}, s32[192,256]{1,0:T(8,128)S(1)}, u32[]{:S(2)}, u32[]{:S(2)}) collective-permute-start(s32[192,256]{1,0:T(8,128)S(1)} %collective-permute-done.5.refs_2_.refs_6_), channel_id=1, source_target_pairs={{0,4},{4,0},{8,12},{12,8},{1,5},{5,1},{9,13},{13,9},{2,6},{6,2},{1... | collective-permute-start | bytes 589832 | tf_op jit(solution)/shard_map/ppermute | solution.py:191
  25.5 8.8 %collective-permute-start.13 = (s32[192,256]{1,0:T(8,128)S(1)}, s32[192,256]{1,0:T(8,128)S(1)}, u32[]{:S(2)}, u32[]{:S(2)}) collective-permute-start(s32[192,256]{1,0:T(8,128)S(1)} %collective-permute-done.11.refs_12_), channel_id=1, source_target_pairs={{0,8},{4,12},{8,0},{12,4},{1,9},{5,13},{9,1},{13,5},{2,10},{6,14},... | collective-permute-start | bytes 589832 | tf_op jit(solution)/shard_map/ppermute | solution.py:191
  27.0 8.4 %collective-permute-start.12 = (s32[192,256]{1,0:T(8,128)S(1)}, s32[192,256]{1,0:T(8,128)S(1)}, u32[]{:S(2)}, u32[]{:S(2)}) collective-permute-start(s32[192,256]{1,0:T(8,128)S(1)} %collective-permute-done.11.refs_12_), channel_id=1, source_target_pairs={{0,4},{4,0},{8,12},{12,8},{1,5},{5,1},{9,13},{13,9},{2,6},{6,2},{1... | collective-permute-start | bytes 589832 | tf_op jit(solution)/shard_map/ppermute | solution.py:191
  32.1 2.3 %collective-permute-start.8 = (s32[192,256]{1,0:T(8,128)S(1)}, s32[192,256]{1,0:T(8,128)S(1)}, u32[]{:S(2)}, u32[]{:S(2)}) collective-permute-start(s32[192,256]{1,0:T(8,128)S(1)} %collective-permute-done.7.refs_0_.refs_8_), channel_id=1, source_target_pairs={{0,4},{4,0},{8,12},{12,8},{1,5},{5,1},{9,13},{13,9},{2,6},{6,2},{1... | collective-permute-start | bytes 589832 | tf_op jit(solution)/shard_map/ppermute | solution.py:191
  32.1 2.3 %collective-permute-start.10 = (s32[192,256]{1,0:T(8,128)S(1)}, s32[192,256]{1,0:T(8,128)S(1)}, u32[]{:S(2)}, u32[]{:S(2)}) collective-permute-start(s32[192,256]{1,0:T(8,128)S(1)} %collective-permute-done.9.refs_2_.refs_10_), channel_id=1, source_target_pairs={{0,4},{4,0},{8,12},{12,8},{1,5},{5,1},{9,13},{13,9},{2,6},{6,2},{1... | collective-permute-start | bytes 589832 | tf_op jit(solution)/shard_map/ppermute | solution.py:191
  34.4 1.4 %collective-permute-start.14 = (s32[192,256]{1,0:T(8,128)S(1)}, s32[192,256]{1,0:T(8,128)S(1)}, u32[]{:S(2)}, u32[]{:S(2)}) collective-permute-start(s32[192,256]{1,0:T(8,128)S(1)} %collective-permute-done.13.refs_14_), channel_id=1, source_target_pairs={{0,4},{4,0},{8,12},{12,8},{1,5},{5,1},{9,13},{13,9},{2,6},{6,2},{1... | collective-permute-start | bytes 589832 | tf_op jit(solution)/shard_map/ppermute | solution.py:191
  37.6 6.8 %collective-permute-start.26 = (f32[64,256]{1,0:T(8,128)S(1)}, f32[64,256]{1,0:T(8,128)S(1)}, u32[]{:S(2)}, u32[]{:S(2)}) collective-permute-start(f32[64,256]{1,0:T(8,128)S(1)} %get-tuple-element.11.refs_0_), channel_id=1, source_target_pairs={{0,3},{1,2},{2,1},{3,0},{4,7},{5,6},{6,5},{7,4},{8,11},{9,10},{10,... | collective-permute-start | bytes 196616 | tf_op jit(solution)/shard_map/ppermute | solution.py:191
  39.8 6.6 %collective-permute-start.22 = (f32[64,256]{1,0:T(8,128)S(1)}, f32[64,256]{1,0:T(8,128)S(1)}, u32[]{:S(2)}, u32[]{:S(2)}) collective-permute-start(f32[64,256]{1,0:T(8,128)S(1)} %get-tuple-element.11.refs_0_), channel_id=1, source_target_pairs={{0,2},{1,3},{2,0},{3,1},{4,6},{5,7},{6,4},{7,5},{8,10},{9,11},{10,... | collective-permute-start | bytes 196616 | tf_op jit(solution)/shard_map/ppermute | solution.py:191
  39.8 6.6 %collective-permute-start.18 = (f32[64,256]{1,0:T(8,128)S(1)}, f32[64,256]{1,0:T(8,128)S(1)}, u32[]{:S(2)}, u32[]{:S(2)}) collective-permute-start(f32[64,256]{1,0:T(8,128)S(1)} %get-tuple-element.11.refs_0_), channel_id=1, source_target_pairs={{0,1},{1,0},{2,3},{3,2},{4,5},{5,4},{6,7},{7,6},{8,9},{9,8},{10,11... | collective-permute-start | bytes 196616 | tf_op jit(solution)/shard_map/ppermute | solution.py:191
  42.0 4.9 %collective-permute-start.16 = (f32[64,256]{1,0:T(8,128)S(1)}, f32[64,256]{1,0:T(8,128)S(1)}, u32[]{:S(2)}, u32[]{:S(2)}) collective-permute-start(f32[64,256]{1,0:T(8,128)S(1)} %get-tuple-element.11.refs_0_), channel_id=1, source_target_pairs={{0,8},{4,12},{8,0},{12,4},{1,9},{5,13},{9,1},{13,5},{2,10},{6,14},... | collective-permute-start | bytes 196616 | tf_op jit(solution)/shard_map/ppermute | solution.py:191
  42.6 4.6 %collective-permute-start.15 = (f32[64,256]{1,0:T(8,128)S(1)}, f32[64,256]{1,0:T(8,128)S(1)}, u32[]{:S(2)}, u32[]{:S(2)}) collective-permute-start(f32[64,256]{1,0:T(8,128)S(1)} %get-tuple-element.11.refs_0_), channel_id=1, source_target_pairs={{0,4},{4,0},{8,12},{12,8},{1,5},{5,1},{9,13},{13,9},{2,6},{6,2},{1... | collective-permute-start | bytes 196616 | tf_op jit(solution)/shard_map/ppermute | solution.py:191
  44.4 4.3 %collective-permute-start.28 = (f32[64,256]{1,0:T(8,128)S(1)}, f32[64,256]{1,0:T(8,128)S(1)}, u32[]{:S(2)}, u32[]{:S(2)}) collective-permute-start(f32[64,256]{1,0:T(8,128)S(1)} %collective-permute-done.26.refs_12_), channel_id=1, source_target_pairs={{0,8},{4,12},{8,0},{12,4},{1,9},{5,13},{9,1},{13,5},{2,10},{6,14},... | collective-permute-start | bytes 196616 | tf_op jit(solution)/shard_map/ppermute | solution.py:191
  46.4 2.3 %collective-permute-start.27 = (f32[64,256]{1,0:T(8,128)S(1)}, f32[64,256]{1,0:T(8,128)S(1)}, u32[]{:S(2)}, u32[]{:S(2)}) collective-permute-start(f32[64,256]{1,0:T(8,128)S(1)} %collective-permute-done.26.refs_12_), channel_id=1, source_target_pairs={{0,4},{4,0},{8,12},{12,8},{1,5},{5,1},{9,13},{13,9},{2,6},{6,2},{1... | collective-permute-start | bytes 196616 | tf_op jit(solution)/shard_map/ppermute | solution.py:191
  46.4 4.9 %collective-permute-start.24 = (f32[64,256]{1,0:T(8,128)S(1)}, f32[64,256]{1,0:T(8,128)S(1)}, u32[]{:S(2)}, u32[]{:S(2)}) collective-permute-start(f32[64,256]{1,0:T(8,128)S(1)} %collective-permute-done.22.refs_8_), channel_id=1, source_target_pairs={{0,8},{4,12},{8,0},{12,4},{1,9},{5,13},{9,1},{13,5},{2,10},{6,14},... | collective-permute-start | bytes 196616 | tf_op jit(solution)/shard_map/ppermute | solution.py:191
  47.0 4.4 %collective-permute-start.23 = (f32[64,256]{1,0:T(8,128)S(1)}, f32[64,256]{1,0:T(8,128)S(1)}, u32[]{:S(2)}, u32[]{:S(2)}) collective-permute-start(f32[64,256]{1,0:T(8,128)S(1)} %collective-permute-done.22.refs_8_), channel_id=1, source_target_pairs={{0,4},{4,0},{8,12},{12,8},{1,5},{5,1},{9,13},{13,9},{2,6},{6,2},{1... | collective-permute-start | bytes 196616 | tf_op jit(solution)/shard_map/ppermute | solution.py:191
  47.2 5.1 %collective-permute-start.20 = (f32[64,256]{1,0:T(8,128)S(1)}, f32[64,256]{1,0:T(8,128)S(1)}, u32[]{:S(2)}, u32[]{:S(2)}) collective-permute-start(f32[64,256]{1,0:T(8,128)S(1)} %collective-permute-done.18.refs_4_), channel_id=1, source_target_pairs={{0,8},{4,12},{8,0},{12,4},{1,9},{5,13},{9,1},{13,5},{2,10},{6,14},... | collective-permute-start | bytes 196616 | tf_op jit(solution)/shard_map/ppermute | solution.py:191
  48.7 3.7 %collective-permute-start.19 = (f32[64,256]{1,0:T(8,128)S(1)}, f32[64,256]{1,0:T(8,128)S(1)}, u32[]{:S(2)}, u32[]{:S(2)}) collective-permute-start(f32[64,256]{1,0:T(8,128)S(1)} %collective-permute-done.18.refs_4_), channel_id=1, source_target_pairs={{0,4},{4,0},{8,12},{12,8},{1,5},{5,1},{9,13},{13,9},{2,6},{6,2},{1... | collective-permute-start | bytes 196616 | tf_op jit(solution)/shard_map/ppermute | solution.py:191
  48.7 3.6 %collective-permute-start.17 = (f32[64,256]{1,0:T(8,128)S(1)}, f32[64,256]{1,0:T(8,128)S(1)}, u32[]{:S(2)}, u32[]{:S(2)}) collective-permute-start(f32[64,256]{1,0:T(8,128)S(1)} %collective-permute-done.16.refs_2_), channel_id=1, source_target_pairs={{0,4},{4,0},{8,12},{12,8},{1,5},{5,1},{9,13},{13,9},{2,6},{6,2},{1... | collective-permute-start | bytes 196616 | tf_op jit(solution)/shard_map/ppermute | solution.py:191
  51.3 1.3 %collective-permute-start.29 = (f32[64,256]{1,0:T(8,128)S(1)}, f32[64,256]{1,0:T(8,128)S(1)}, u32[]{:S(2)}, u32[]{:S(2)}) collective-permute-start(f32[64,256]{1,0:T(8,128)S(1)} %collective-permute-done.28.refs_14_), channel_id=1, source_target_pairs={{0,4},{4,0},{8,12},{12,8},{1,5},{5,1},{9,13},{13,9},{2,6},{6,2},{1... | collective-permute-start | bytes 196616 | tf_op jit(solution)/shard_map/ppermute | solution.py:191
  51.3 1.4 %collective-permute-start.25 = (f32[64,256]{1,0:T(8,128)S(1)}, f32[64,256]{1,0:T(8,128)S(1)}, u32[]{:S(2)}, u32[]{:S(2)}) collective-permute-start(f32[64,256]{1,0:T(8,128)S(1)} %collective-permute-done.24.refs_10_), channel_id=1, source_target_pairs={{0,4},{4,0},{8,12},{12,8},{1,5},{5,1},{9,13},{13,9},{2,6},{6,2},{1... | collective-permute-start | bytes 196616 | tf_op jit(solution)/shard_map/ppermute | solution.py:191
  52.3 1.3 %collective-permute-start.21 = (f32[64,256]{1,0:T(8,128)S(1)}, f32[64,256]{1,0:T(8,128)S(1)}, u32[]{:S(2)}, u32[]{:S(2)}) collective-permute-start(f32[64,256]{1,0:T(8,128)S(1)} %collective-permute-done.20.refs_6_), channel_id=1, source_target_pairs={{0,4},{4,0},{8,12},{12,8},{1,5},{5,1},{9,13},{13,9},{2,6},{6,2},{1... | collective-permute-start | bytes 196616 | tf_op jit(solution)/shard_map/ppermute | solution.py:191

commit v3 on v2

v3 whole, which is shorter than its diff:
```python
import functools
import math

import jax
import jax.numpy as jnp
from jax import lax
from jax.experimental import pallas as pl
from jax.experimental.pallas import tpu as pltpu
from jax.sharding import PartitionSpec as P

ITERS = 2
REACH = 20.0
UNIT = REACH / 32767.0
FIXED = 2.0**28
HIGHEST = lax.Precision.HIGHEST
BF16, F32 = jnp.bfloat16, jnp.float32
VMEM = pl.BlockSpec(memory_space=pltpu.VMEM)


def matmul(a, b, contract, precision=None):
    return lax.dot_general(a, b, ((contract[:1], contract[1:]), ((), ())), precision=precision, preferred_element_type=F32)


def encode(landmarks, initial):
    half = landmarks.shape[0] // 2
    code = jnp.round(landmarks * (1.0 / UNIT)).astype(jnp.int32)
    packed = (code[:half] << 16) | (code[half:] & 0xFFFF)
    return jnp.concatenate([packed, jnp.round(initial * FIXED).astype(jnp.int32)], axis=0)


def split_codes(words):
    code = jnp.concatenate([words >> 16, (words << 16) >> 16], axis=0)
    high = ((code + 128) >> 8) << 8
    return high.astype(F32).astype(BF16), (code - high).astype(F32).astype(BF16)


def kernel_rows(words, own_high, own_low, own_norms, scale):
    high, low = split_codes(words)
    wide = high.astype(F32) + low.astype(F32)
    norms = scale * jnp.sum(wide * wide, axis=1, keepdims=True)
    dots = matmul(high, own_high, (1, 1)) + (matmul(high, own_low, (1, 1)) + matmul(low, own_high, (1, 1))) + matmul(low, own_low, (1, 1))
    return jnp.exp((2.0 * scale) * dots - (norms + own_norms)).astype(BF16)


def own_side(refs, half, scale):
    parts = [split_codes(ref[:half]) for ref in refs]
    high = jnp.concatenate([part[0] for part in parts], axis=0)
    low = jnp.concatenate([part[1] for part in parts], axis=0)
    wide = high.astype(F32) + low.astype(F32)
    norms = matmul(jnp.ones((8, wide.shape[1]), F32), wide * wide, (1, 1), HIGHEST)[:1]
    return high, low, scale * norms


def build_kernel(half, scale, *refs):
    own, blocks, out_ref = refs[:2], refs[2:-1], refs[-1]
    own_high, own_low, own_norms = own_side(own, half, scale)
    for b, block in enumerate(blocks):
        out_ref[pl.ds(b * 2 * half, 2 * half), :] = kernel_rows(block[:half], own_high, own_low, own_norms, scale)


def first_kernel(counts, half, scale, total, *refs):
    count = sum(counts)
    own, blocks, parts = refs[:2], refs[2 : 2 + count], refs[2 + count : -2]
    out_ref, tile_ref = refs[-2:]
    size = 2 * half
    own_high, own_low, own_norms = own_side(own, half, scale)
    for b, block in enumerate(blocks[count - counts[-1] :]):
        tile_ref[pl.ds(b * size, size), :] = kernel_rows(block[:half], own_high, own_low, own_norms, scale)
    starts = [block[half:].astype(F32) * (1.0 / FIXED) for block in blocks]
    sums = starts[0]
    for start in starts[1:]:
        sums = sums + start
    mean = jnp.sum(sums, axis=1, keepdims=True) / total
    rounded = [(start - mean).astype(BF16) for start in starts]
    images = None
    for tile in (*parts, tile_ref):
        group, rounded = rounded[: tile.shape[0] // size], rounded[tile.shape[0] // size :]
        term = matmul(jnp.concatenate(group, axis=1), tile[...], (1, 0))
        images = term if images is None else images + term
    out_ref[...] = images


def inverse_factor(gram):
    n = gram.shape[0]
    row_id = lax.broadcasted_iota(jnp.int32, (n, 2 * n), 0)
    col_id = lax.broadcasted_iota(jnp.int32, (n, 2 * n), 1)
    eye = (row_id[:, :n] == col_id[:, :n]).astype(F32)
    work = jnp.concatenate([gram, eye], axis=1)
    done = []
    for top in range(0, n, 8):
        rows = n - top
        local = lax.broadcasted_iota(jnp.int32, (rows, 2 * n), 0)
        columns = [jnp.broadcast_to(work[:, top + k : top + k + 1], (rows, 2 * n)) for k in range(8)]
        for k in range(8):
            column = columns[k]
            factor = jnp.where(local > k, column * (1.0 / column[k : k + 1]), 0.0)
            work = work - factor * work[k : k + 1]
            for later in range(k + 1, 8):
                columns[later] = columns[later] - factor * columns[later][k : k + 1]
        done.append(work[:8])
        work = work[8:]
    upper = jnp.concatenate(done, axis=0)
    pivots = jnp.sum(jnp.where(row_id == col_id, upper, 0.0), axis=1, keepdims=True)
    return upper[:, n:] * lax.rsqrt(pivots)


def thirds(value):
    high = value.astype(BF16)
    rest = value - high.astype(F32)
    middle = rest.astype(BF16)
    return jnp.concatenate([high, middle, (rest - middle.astype(F32)).astype(BF16)], axis=0)


def gram_of(stack):
    n = stack.shape[0] // 3
    p = matmul(stack, stack, (1, 1))
    middle = p[n : 2 * n, n : 2 * n] + (p[:n, 2 * n :] + p[2 * n :, :n])
    return p[:n, :n] + ((p[:n, n : 2 * n] + p[n : 2 * n, :n]) + middle)


def times(matrix, stack):
    n = matrix.shape[0]
    parts = thirds(matrix)
    p = matmul(jnp.concatenate([parts, parts, parts], axis=1), stack, (1, 0))
    return p[:n] + (p[n : 2 * n] + p[2 * n :])


def second_kernel(pieces, total, *refs):
    count = 1 + max(piece[0] for piece in pieces)
    images, tiles = refs[:count], refs[count:-3]
    own_ref, other_ref, share_ref = refs[-3:]
    size = own_ref.shape[1]
    values = [images[i][:, b * size : (b + 1) * size] for i, b in pieces]
    sums = values[0]
    for value in values[1:]:
        sums = sums + value
    mean = jnp.sum(sums, axis=1, keepdims=True) / total
    stack = thirds(jnp.concatenate([value - mean for value in values], axis=1))
    solve = math.sqrt(total) * inverse_factor(gram_of(stack))
    vectors = times(solve, stack).astype(BF16)
    result, begin = None, 0
    for tile in tiles:
        end = begin + tile.shape[0]
        term = matmul(vectors[:, begin:end], tile[...], (1, 0))
        result, begin = term if result is None else result + term, end
    own_ref[...] = result[:, :size]
    other_ref[...] = result[:, size:]
    local_mean = jnp.sum(result, axis=1, keepdims=True) / (2 * size)
    gram = gram_of(thirds(result - local_mean))
    n = gram.shape[0]
    h = n // 2
    eye = lax.broadcasted_iota(jnp.int32, (n, n), 0) == lax.broadcasted_iota(jnp.int32, (n, n), 1)
    across = jnp.sum(jnp.where(eye, local_mean, 0.0), axis=0, keepdims=True)
    share_ref[:h] = jnp.concatenate([gram[:h], gram[h:, h:], local_mean[:h], local_mean[h:], jnp.zeros((h, h - 2), F32)], axis=1)
    share_ref[h:] = jnp.broadcast_to(jnp.concatenate([across, across[:, h:], jnp.zeros((1, h), F32)], axis=1), (8, 4 * h))


def merge(a, b, each):
    h = a.shape[0] - 8
    apart = a - b
    lane = lax.broadcasted_iota(jnp.int32, (h, 4 * h), 1)
    down = jnp.where(lane < 2 * h, apart[:h, 3 * h : 3 * h + 1], apart[:h, 3 * h + 1 : 3 * h + 2])
    both = a + b
    top = jnp.where(lane < 3 * h, both[:h] + (0.5 * each) * (down * apart[h : h + 1]), 0.5 * both[:h])
    return jnp.concatenate([top, 0.5 * both[h:]], axis=0)


def merge_kernel(each, a_ref, b_ref, out_ref):
    out_ref[...] = merge(a_ref[...], b_ref[...], each)


def last_kernel(total, outer_ref, share_ref, near_ref, far_ref, across_ref, own_ref, given_ref, out_ref):
    outer = outer_ref[0] == 1
    first = jnp.where(outer, near_ref[...], share_ref[...])
    second = jnp.where(outer, far_ref[...], across_ref[...])
    images = jnp.where(outer, given_ref[...], own_ref[...])
    share = merge(first, second, 0.5 * total)
    h = share.shape[0] - 8
    mean = jnp.concatenate([share[:h, 3 * h : 3 * h + 1], share[:h, 3 * h + 1 : 3 * h + 2]], axis=0)
    top = share[:h, : 2 * h]
    bottom = jnp.concatenate([top[:, h:].T, share[:h, 2 * h : 3 * h]], axis=1)
    solve = math.sqrt(total) * inverse_factor(jnp.concatenate([top, bottom], axis=0))
    out_ref[...] = times(solve, thirds(images - mean))


def call(kernel, args, out_shape, in_specs=None):
    return pl.pallas_call(
        kernel,
        out_shape=out_shape,
        in_specs=in_specs or [VMEM] * len(args),
        out_specs=jax.tree.map(lambda _: VMEM, out_shape),
        compiler_params=pltpu.CompilerParams(vmem_limit_bytes=24 * 2**20),
    )(*args)


def after(value, *others):
    return lax.optimization_barrier((value, *others))[0]


def exchange(axis, offset, size=4):
    return lambda value: lax.ppermute(value, axis, [(i, i ^ offset) for i in range(size)])


CORE, CHIP = exchange("row", 1), exchange("row", 2)
NEAR, FAR, OPPOSITE = exchange("col", 1), exchange("col", 2), exchange("col", 3)


def middle(value):
    return lax.ppermute(value, "col", MIDDLE)


MIDDLE = [(1, 2), (2, 1)]


def local(corpus, sample_rows, initial):
    vecs, size = initial.shape
    half = size // 2
    count = 16
    total = float(size * count)
    scale = UNIT * UNIT / (2.0 * corpus.shape[1])
    landmarks = lax.gather(
        corpus,
        sample_rows[:, None],
        lax.GatherDimensionNumbers(offset_dims=(1,), collapsed_slice_dims=(0,), start_index_map=(0,)),
        (1, corpus.shape[1]),
        mode="promise_in_bounds",
    )
    own = encode(landmarks, initial)

    def build(*blocks):
        shape = jax.ShapeDtypeStruct((len(blocks) * size, 2 * size), BF16)
        return call(functools.partial(build_kernel, half, scale), [own, outer, *blocks], shape)

    outer, partner, chip = NEAR(own), middle(own), CHIP(own)
    groups = [[own, outer, CORE(own), CORE(outer)]]
    tiles = [build(*groups[0])]
    partner_outer, chip_outer, chip_partner = middle(outer), NEAR(chip), CHIP(partner)
    groups.append([partner, CORE(partner), chip, CORE(chip)])
    tiles.append(build(*groups[1]))
    chip_partner_outer = CHIP(after(partner_outer, tiles[0]))
    groups.append([partner_outer, CORE(partner_outer), chip_outer, CORE(chip_outer)])
    tiles.append(build(*groups[2]))
    groups.append([chip_partner, CORE(chip_partner)])
    tiles.append(build(*groups[3]))
    groups.append([chip_partner_outer, CORE(after(chip_partner_outer, *tiles[1:4]))])
    images, tile = call(
        functools.partial(first_kernel, [len(group) for group in groups], half, scale, total),
        [own, outer] + [block for group in groups for block in group] + tiles,
        (jax.ShapeDtypeStruct((vecs, 2 * size), F32), jax.ShapeDtypeStruct((2 * size, 2 * size), BF16)),
    )
    tiles.append(tile)
    there, beside = middle(images), CHIP(images)
    beyond = CHIP(there)
    gathered = [images, there, beside, beyond]
    gathered += [CORE(value) for value in gathered]
    here, part, chip, far = 0, 1, 2, 3
    pieces = [(here, 0), (here, 1), (here + 4, 0), (here + 4, 1), (part, 0), (part + 4, 0), (chip, 0), (chip + 4, 0)]
    pieces += [(part, 1), (part + 4, 1), (chip, 1), (chip + 4, 1), (far, 0), (far + 4, 0), (far, 1), (far + 4, 1)]
    block = jax.ShapeDtypeStruct((vecs, size), F32)
    packed = jax.ShapeDtypeStruct((vecs // 2 + 8, 2 * vecs), F32)
    images, other, share = call(functools.partial(second_kernel, pieces, total), gathered + tiles, (block, block, packed))
    given = NEAR(other)
    for step, swap in enumerate((CORE, CHIP)):
        share = call(functools.partial(merge_kernel, 2.0 * size * 2**step), [share, swap(share)], packed)
    place = lax.axis_index("col")
    flag = ((place == 0) | (place == 3)).astype(jnp.int32).reshape(1)
    return call(
        functools.partial(last_kernel, total),
        [flag, share, NEAR(share), FAR(share), OPPOSITE(share), images, given],
        block,
        [pl.BlockSpec(memory_space=pltpu.SMEM)] + [VMEM] * 6,
    )


def local_large(corpus, sample_rows, initial):
    both = ("row", "col")
    landmarks = corpus[sample_rows]
    everyone = lax.all_gather(landmarks, both, axis=0, tiled=True)
    total = float(everyone.shape[0])
    norms = jnp.sum(everyone * everyone, axis=1)
    own_norms = jnp.sum(landmarks * landmarks, axis=1)
    products = jnp.dot(everyone, landmarks.T, precision=HIGHEST, preferred_element_type=F32)
    tile = jnp.exp(-(norms[:, None] + own_norms[None, :] - 2.0 * products) / (2.0 * corpus.shape[1])).astype(BF16)
    starts = lax.all_gather(initial, both, axis=1, tiled=True)
    rounded = (starts - jnp.mean(starts, axis=1, keepdims=True)).astype(BF16)
    vectors = None
    for _ in range(ITERS):
        images = jnp.dot(rounded, tile, preferred_element_type=F32)
        gathered = lax.all_gather(images, both, axis=1, tiled=True)
        mean = jnp.mean(gathered, axis=1, keepdims=True)
        centered = gathered - mean
        factor = jnp.linalg.cholesky(jnp.dot(centered, centered.T, precision=HIGHEST))
        rounded = (math.sqrt(total) * jax.scipy.linalg.solve_triangular(factor, centered, lower=True)).astype(BF16)
        vectors = math.sqrt(total) * jax.scipy.linalg.solve_triangular(factor, images - mean, lower=True)
    return vectors


def solution(mesh):
    shape = mesh.shape
    whole = P(("groups", "row", "col"))
    return jax.shard_map(
        local if (shape["row"], shape["col"]) == (4, 4) else local_large,
        mesh=mesh,
        in_specs=(P(("groups", "row", "col"), None), whole, P(None, ("groups", "row", "col"))),
        out_specs=P(None, ("groups", "row", "col")),
        check_vma=False,
    )
```

time: 75.8 us -> 69.9 us (0.922)
  blocking collectives: 13.6 us -> 0 us
  Pallas kernels: 13.3 us -> 18 us
  starting transfers between devices: 22.3 us -> 27 us
  waiting for transfers between devices: 23.6 us -> 21.8 us
  other arithmetic: 1.74 us -> 0.9 us
  local copies, waits for them, and re-layouts: 0.97 us -> 1.74 us
    all_to_all x1 -> x0, blocking collectives: 13.6 us -> none  [local(): shares = lax.all_to_all(share, ('row', 'col'), split_axis=0, concat_axis=0)]
    ppermute x30 -> x28, starting transfers between devices: 22.3 us -> 27 us  [the longest x25 24.9 us: exchange(): lax.ppermute(value, axis, [(i, i ^ offset) for i in range(size)])]
    pallas_call x6 -> x9, Pallas kernels: 13.3 us -> 18 us  [call(): pl.pallas_call(kernel, out_shape=out_shape, in_specs=in_specs or [VMEM] *...]
    ppermute x30 -> x28, waiting for transfers between devices: 23.6 us -> 21.8 us  [the longest x25 21.8 us: exchange(): lax.ppermute(value, axis, [(i, i ^ offset) for i in range(size)])]
    convert_element_type x1, other arithmetic: 0.85 us -> 0.01 us  [encode(): jnp.round(initial * FIXED).astype(jnp.int32)]
    unnamed x2 -> x4, local copies, waits for them, and re-layouts: 0.01 us -> 0.77 us
  transfers between devices with their start and end apart: 30 -> 28, of which waited for: 12 -> 11; matrix products, arithmetic and copies ran while one was open for 0% -> 0% of each run, Pallas kernels for 4% -> 11%
where the time goes in v3:
time: 69.9 us; the launch traced here: 69.7 us
  starting transfers between devices  27 us (39%)
  waiting for transfers between devices  21.8 us (31%)
  Pallas kernels  18 us (26%)
  local copies, waits for them, and re-layouts  1.74 us (2%)
  other arithmetic  0.9 us (1%)
    ppermute x25, starting transfers between devices, exchange(): lax.ppermute(value, axis, [(i, i ^ offset) for i in range(size)])  24.9 us
    ppermute x25, waiting for transfers between devices, exchange(): lax.ppermute(value, axis, [(i, i ^ offset) for i in range(size)])  21.8 us
    pallas_call x9, Pallas kernels, call(): pl.pallas_call(kernel, out_shape=out_shape, in_specs=in_specs or [VMEM] *...  18 us
    ppermute x3, starting transfers between devices, middle(): return lax.ppermute(value, 'col', MIDDLE)  2.17 us
  transfers between devices with their start and end apart: 28, of which 11 were waited for; matrix products, arithmetic and copies ran while one was open for 0% of the time, Pallas kernels for 11%

profile of v3, /device:TPU:0, one launch (start us, length us, event | category | flops | bytes accessed | tf_op | source)
XLA Modules:
  0.0 69.7 jit_solution(16434292795118893075)
XLA Ops:
  0.0 0.8 %pad_clamp_fusion = s32[1024]{0:T(1024)S(1)} fusion(s32[256]{0:T(256)} %param.4), kind=kLoop, calls=%fused_computation.7 | loop fusion | flops 1024 | bytes 5120 | tf_op jit(solution)/shard_map/gather | solution.py:221
  0.8 0.8 %copy-done = f32[2048,256]{1,0:T(8,128)S(1)} copy-done((f32[2048,256]{1,0:T(8,128)S(1)}, f32[2048,256]{1,0:T(8,128)}, u32[]{:S(2)}) %copy-start) | copy-done | bytes 2097176
  1.6 1.0 %gather_fusion = f32[256,256]{1,0:T(8,128)S(1)} fusion(f32[2048,256]{1,0:T(8,128)S(1)} %copy-done, s32[1024]{0:T(1024)S(1)} %pad_clamp_fusion), kind=kCustom, calls=%fused_computation | custom fusion | bytes 525312 | tf_op jit(solution)/shard_map/gather | solution.py:221
  2.7 3.1 %collective-permute-start = (s32[192,256]{1,0:T(8,128)S(1)}, s32[192,256]{1,0:T(8,128)S(1)}, u32[]{:S(2)}, u32[]{:S(2)}) collective-permute-start(s32[192,256]{1,0:T(8,128)S(1)} %pad_add_fusion.refs_0_.refs_2_), channel_id=1, source_target_pairs={{0,1},{1,0},{2,3},{3,2},{4,5},{5,4},{6,7},{7,6},{8,9},{9,8},{10,11... | collective-permute-start | bytes 589832 | tf_op jit(solution)/shard_map/ppermute | solution.py:201
  5.8 0.7 collective-permute-start.3
  6.4 1.6 %collective-permute-start.5 = (s32[192,256]{1,0:T(8,128)S(1)}, s32[192,256]{1,0:T(8,128)S(1)}, u32[]{:S(2)}, u32[]{:S(2)}) collective-permute-start(s32[192,256]{1,0:T(8,128)S(1)} %pad_add_fusion.refs_0_.refs_2_), channel_id=1, source_target_pairs={{0,8},{4,12},{8,0},{12,4},{1,9},{5,13},{9,1},{13,5},{2,10},{6,14},... | collective-permute-start | bytes 589832 | tf_op jit(solution)/shard_map/ppermute | solution.py:201
  8.0 0.0 collective-permute-start.1
  8.0 2.7 %collective-permute-done.refs_1_.refs_3_ = s32[192,256]{1,0:T(8,128)S(1)} collective-permute-done((s32[192,256]{1,0:T(8,128)S(1)}, s32[192,256]{1,0:T(8,128)S(1)}, u32[]{:S(2)}, u32[]{:S(2)}) %collective-permute-start) | collective-permute-done | bytes 196640 | tf_op jit(solution)/shard_map/ppermute | solution.py:201
  10.7 0.0 collective-permute-start.2
  10.7 0.7 collective-permute-start.7
  11.4 0.0 collective-permute-done.3.refs_2_.refs_6_
  11.4 1.7 %collective-permute-start.11 = (s32[192,256]{1,0:T(8,128)S(1)}, s32[192,256]{1,0:T(8,128)S(1)}, u32[]{:S(2)}, u32[]{:S(2)}) collective-permute-start(s32[192,256]{1,0:T(8,128)S(1)} %collective-permute-done.3.refs_2_.refs_6_), channel_id=1, source_target_pairs={{0,8},{4,12},{8,0},{12,4},{1,9},{5,13},{9,1},{13,5},{2,10},{6,14},... | collective-permute-start | bytes 589832 | tf_op jit(solution)/shard_map/ppermute | solution.py:201
  13.1 0.0 collective-permute-done.5.refs_4_.refs_8_
  13.1 4.4 %collective-permute-start.9 = (s32[192,256]{1,0:T(8,128)S(1)}, s32[192,256]{1,0:T(8,128)S(1)}, u32[]{:S(2)}, u32[]{:S(2)}) collective-permute-start(s32[192,256]{1,0:T(8,128)S(1)} %collective-permute-done.5.refs_4_.refs_8_), channel_id=1, source_target_pairs={{0,1},{1,0},{2,3},{3,2},{4,5},{5,4},{6,7},{7,6},{8,9},{9,8},{10,11... | collective-permute-start | bytes 589832 | tf_op jit(solution)/shard_map/ppermute | solution.py:201
  17.5 0.0 collective-permute-done.1.refs_4_
  17.5 0.0 collective-permute-start.4
  17.5 0.0 collective-permute-done.2.refs_5_
  17.5 0.5 collective-permute-start.6
  18.0 2.1 %shard_map.37.refs_18_.refs_8_ = bf16[1024,512]{1,0:T(8,128)(2,1)S(1)} custom-call(s32[192,256]{1,0:T(8,128)S(1)} %pad_add_fusion.refs_0_.refs_2_, s32[192,256]{1,0:T(8,128)S(1)} %collective-permute-done.refs_1_.refs_3_, s32[192,256]{1,0:T(8,128)S(1)} %pad_add_fusion.refs_0_.refs_2_, s32[192,256]{1,0:T(8,128)S(1)} %collective-permute-done.refs_1_.refs_3_, ...), custom_call_target="tpu_custom_call" | custom-call | tf_op jit(solution)/shard_map/pallas_call | solution.py:187
  20.1 0.0 collective-permute-done.7.refs_2_.refs_10_
  20.1 0.1 collective-permute-start.8
  20.2 0.0 collective-permute-done.11.refs_2_.refs_14_
  20.2 0.4 collective-permute-start.12
  20.7 1.8 %collective-permute-done.9.refs_4_.refs_12_ = s32[192,256]{1,0:T(8,128)S(1)} collective-permute-done((s32[192,256]{1,0:T(8,128)S(1)}, s32[192,256]{1,0:T(8,128)S(1)}, u32[]{:S(2)}, u32[]{:S(2)}) %collective-permute-start.9) | collective-permute-done | bytes 196640 | tf_op jit(solution)/shard_map/ppermute | solution.py:201
  22.5 0.0 collective-permute-start.10
  22.5 0.0 collective-permute-done.4.refs_3_.refs_7_
  22.5 0.5 collective-permute-start.13
  23.0 0.0 collective-permute-done.6.refs_5_.refs_9_
  23.0 2.1 %shard_map.38.refs_19_.refs_9_ = bf16[1024,512]{1,0:T(8,128)(2,1)S(1)} custom-call(s32[192,256]{1,0:T(8,128)S(1)} %pad_add_fusion.refs_0_.refs_2_, s32[192,256]{1,0:T(8,128)S(1)} %collective-permute-done.refs_1_.refs_3_, s32[192,256]{1,0:T(8,128)S(1)} %collective-permute-done.3.refs_2_.refs_6_, s32[192,256]{1,0:T(8,128)S(1)} %collective-permute-done.4.refs_3_.refs_7_, ...), custom_call_target="tpu_custom_call" | custom-call | tf_op jit(solution)/shard_map/pallas_call | solution.py:187
  25.1 0.0 collective-permute-done.12.refs_3_.refs_15_
  25.1 1.4 %shard_map.40.refs_21_.refs_11_ = bf16[512,512]{1,0:T(8,128)(2,1)S(1)} custom-call(s32[192,256]{1,0:T(8,128)S(1)} %pad_add_fusion.refs_0_.refs_2_, s32[192,256]{1,0:T(8,128)S(1)} %collective-permute-done.refs_1_.refs_3_, s32[192,256]{1,0:T(8,128)S(1)} %collective-permute-done.11.refs_2_.refs_14_, s32[192,256]{1,0:T(8,128)S(1)} %collective-permute-done.12.refs_3_.refs_15_), custom_call_target="tpu_custom_call" | custom-call | tf_op jit(solution)/shard_map/pallas_call | solution.py:187
  26.5 0.0 collective-permute-done.8.refs_3_.refs_11_
  26.6 0.0 collective-permute-done.10.refs_5_.refs_13_
  26.6 2.1 %shard_map.39.refs_20_.refs_10_ = bf16[1024,512]{1,0:T(8,128)(2,1)S(1)} custom-call(s32[192,256]{1,0:T(8,128)S(1)} %pad_add_fusion.refs_0_.refs_2_, s32[192,256]{1,0:T(8,128)S(1)} %collective-permute-done.refs_1_.refs_3_, s32[192,256]{1,0:T(8,128)S(1)} %collective-permute-done.7.refs_2_.refs_10_, s32[192,256]{1,0:T(8,128)S(1)} %collective-permute-done.8.refs_3_.refs_11_, ...), custom_call_target="tpu_custom_call" | custom-call | tf_op jit(solution)/shard_map/pallas_call | solution.py:187
  28.6 1.2 %collective-permute-done.13.refs_16_ = s32[192,256]{1,0:T(8,128)S(1)} collective-permute-done((s32[192,256]{1,0:T(8,128)S(1)}, s32[192,256]{1,0:T(8,128)S(1)}, u32[]{:S(2)}, u32[]{:S(2)}) %collective-permute-start.13) | collective-permute-done | bytes 196640 | tf_op jit(solution)/shard_map/ppermute | solution.py:201
  29.8 0.0 collective-permute-start.14
  29.8 1.4 %collective-permute-done.14.refs_17_ = s32[192,256]{1,0:T(8,128)S(1)} collective-permute-done((s32[192,256]{1,0:T(8,128)S(1)}, s32[192,256]{1,0:T(8,128)S(1)}, u32[]{:S(2)}, u32[]{:S(2)}) %collective-permute-start.14) | collective-permute-done | bytes 196640 | tf_op jit(solution)/shard_map/ppermute | solution.py:201
  31.2 2.1 %shard_map.41 = (f32[64,512]{1,0:T(8,128)S(1)}, bf16[512,512]{1,0:T(8,128)(2,1)S(1)}) custom-call(s32[192,256]{1,0:T(8,128)S(1)} %pad_add_fusion.refs_0_.refs_2_, s32[192,256]{1,0:T(8,128)S(1)} %collective-permute-done.refs_1_.refs_3_, s32[192,256]{1,0:T(8,128)S(1)} %pad_add_fusion.refs_0_.refs_2_, s32[192,256]{1,0:T(8,128)S(1)} %collective-permute-done.refs_1_.refs_3_, ...), custom_call_target="tpu_custom_call" | custom-call | tf_op jit(solution)/shard_map/pallas_call | solution.py:187
  33.4 0.8 %collective-permute-start.15 = (f32[64,512]{1,0:T(8,128)S(1)}, f32[64,512]{1,0:T(8,128)S(1)}, u32[]{:S(2)}, u32[]{:S(2)}) collective-permute-start(f32[64,512]{1,0:T(8,128)S(1)} %get-tuple-element.14.refs_0_), channel_id=1, source_target_pairs={{1,2},{2,1},{5,6},{6,5},{9,10},{10,9},{13,14},{14,13},{17,18},{18,... | collective-permute-start | bytes 393224 | tf_op jit(solution)/shard_map/ppermute | solution.py:209
  34.2 0.6 collective-permute-start.16
  34.8 0.0 collective-permute-done.15.refs_1_
  34.8 1.5 %collective-permute-start.17 = (f32[64,512]{1,0:T(8,128)S(1)}, f32[64,512]{1,0:T(8,128)S(1)}, u32[]{:S(2)}, u32[]{:S(2)}) collective-permute-start(f32[64,512]{1,0:T(8,128)S(1)} %collective-permute-done.15.refs_1_), channel_id=1, source_target_pairs={{0,8},{4,12},{8,0},{12,4},{1,9},{5,13},{9,1},{13,5},{2,10},{6,14},... | collective-permute-start | bytes 393224 | tf_op jit(solution)/shard_map/ppermute | solution.py:201
  36.3 0.0 collective-permute-start.18
  36.3 0.5 collective-permute-start.19
  36.8 3.8 %collective-permute-done.16.refs_2_ = f32[64,512]{1,0:T(8,128)S(1)} collective-permute-done((f32[64,512]{1,0:T(8,128)S(1)}, f32[64,512]{1,0:T(8,128)S(1)}, u32[]{:S(2)}, u32[]{:S(2)}) %collective-permute-start.16) | collective-permute-done | bytes 131104 | tf_op jit(solution)/shard_map/ppermute | solution.py:201
  40.6 0.0 collective-permute-start.20
  40.6 2.0 %collective-permute-done.17.refs_3_ = f32[64,512]{1,0:T(8,128)S(1)} collective-permute-done((f32[64,512]{1,0:T(8,128)S(1)}, f32[64,512]{1,0:T(8,128)S(1)}, u32[]{:S(2)}, u32[]{:S(2)}) %collective-permute-start.17) | collective-permute-done | bytes 131104 | tf_op jit(solution)/shard_map/ppermute | solution.py:201
  42.6 0.0 collective-permute-done.20.refs_6_
  42.7 1.3 %collective-permute-done.21.refs_7_ = f32[64,512]{1,0:T(8,128)S(1)} collective-permute-done((f32[64,512]{1,0:T(8,128)S(1)}, f32[64,512]{1,0:T(8,128)S(1)}, u32[]{:S(2)}, u32[]{:S(2)}) %collective-permute-start.21) | collective-permute-done | bytes 131104 | tf_op jit(solution)/shard_map/ppermute | solution.py:201
  44.0 5.4 %shard_map.42 = (f32[64,256]{1,0:T(8,128)S(1)}, f32[64,256]{1,0:T(8,128)S(1)}, f32[40,128]{1,0:T(8,128)S(1)}) custom-call(f32[64,512]{1,0:T(8,128)S(1)} %get-tuple-element.14.refs_0_, f32[64,512]{1,0:T(8,128)S(1)} %collective-permute-done.15.refs_1_, f32[64,512]{1,0:T(8,128)S(1)} %collective-permute-done.16.refs_2_, ...), custom_call_target="tpu_custom_call" | custom-call | tf_op jit(solution)/shard_map/pallas_call | solution.py:187
  49.3 4.9 %collective-permute-start.27 = (f32[64,256]{1,0:T(8,128)S(1)}, f32[64,256]{1,0:T(8,128)S(1)}, u32[]{:S(2)}, u32[]{:S(2)}) collective-permute-start(f32[64,256]{1,0:T(8,128)S(1)} %get-tuple-element.18), channel_id=1, source_target_pairs={{0,1},{1,0},{2,3},{3,2},{4,5},{5,4},{6,7},{7,6},{8,9},{9,8},{10,11... | collective-permute-start | bytes 196616 | tf_op jit(solution)/shard_map/ppermute | solution.py:201
  54.3 0.0 collective-permute-start.22
  54.3 1.2 %collective-permute-done.22.b_ref = f32[40,128]{1,0:T(8,128)S(1)} collective-permute-done((f32[40,128]{1,0:T(8,128)S(1)}, f32[40,128]{1,0:T(8,128)S(1)}, u32[]{:S(2)}, u32[]{:S(2)}) %collective-permute-start.22) | collective-permute-done | bytes 20512 | tf_op jit(solution)/shard_map/ppermute | solution.py:201
  55.5 0.1 shard_map.43.a_ref
  55.6 0.5 collective-permute-start.23
  56.1 3.2 %collective-permute-done.23.b_ref = f32[40,128]{1,0:T(8,128)S(1)} collective-permute-done((f32[40,128]{1,0:T(8,128)S(1)}, f32[40,128]{1,0:T(8,128)S(1)}, u32[]{:S(2)}, u32[]{:S(2)}) %collective-permute-start.23) | collective-permute-done | bytes 20512 | tf_op jit(solution)/shard_map/ppermute | solution.py:201
  59.3 0.1 shard_map.44.share_ref
  59.4 0.1 collective-permute-start.24
  59.5 1.8 %collective-permute-start.25 = (f32[40,128]{1,0:T(8,128)S(1)}, f32[40,128]{1,0:T(8,128)S(1)}, u32[]{:S(2)}, u32[]{:S(2)}) collective-permute-start(f32[40,128]{1,0:T(8,128)S(1)} %shard_map.44.share_ref), channel_id=1, source_target_pairs={{0,2},{1,3},{2,0},{3,1},{4,6},{5,7},{6,4},{7,5},{8,10},{9,11},{10,... | collective-permute-start | bytes 61448 | tf_op jit(solution)/shard_map/ppermute | solution.py:201
  61.3 2.5 %collective-permute-start.26 = (f32[40,128]{1,0:T(8,128)S(1)}, f32[40,128]{1,0:T(8,128)S(1)}, u32[]{:S(2)}, u32[]{:S(2)}) collective-permute-start(f32[40,128]{1,0:T(8,128)S(1)} %shard_map.44.share_ref), channel_id=1, source_target_pairs={{0,3},{1,2},{2,1},{3,0},{4,7},{5,6},{6,5},{7,4},{8,11},{9,10},{10,... | collective-permute-start | bytes 61448 | tf_op jit(solution)/shard_map/ppermute | solution.py:201
  63.8 0.0 collective-permute-done.24.near_ref
  63.8 0.4 collective-permute-done.25.far_ref
  64.2 2.7 %collective-permute-done.26.across_ref = f32[40,128]{1,0:T(8,128)S(1)} collective-permute-done((f32[40,128]{1,0:T(8,128)S(1)}, f32[40,128]{1,0:T(8,128)S(1)}, u32[]{:S(2)}, u32[]{:S(2)}) %collective-permute-start.26) | collective-permute-done | bytes 20512 | tf_op jit(solution)/shard_map/ppermute | solution.py:201
  66.9 2.8 %shard_map.45 = f32[64,256]{1,0:T(8,128)} custom-call(s32[1]{0:T(128)} %bitcast.outer_ref, f32[40,128]{1,0:T(8,128)S(1)} %shard_map.44.share_ref, f32[40,128]{1,0:T(8,128)S(1)} %collective-permute-done.24.near_ref, f32[40,128]{1,0:T(8,128)S(1)} %collective-permute-done.25.far_ref, f32[40,128]{1,0:T(8,128)S(1)} %collective-permute-done.26.across_ref, ...), custom_call_target="tpu_custom_call" | custom-call | tf_op jit(solution)/shard_map/pallas_call | solution.py:187
  (11 shorter events, 0.1 us)
Async XLA Ops:
  0.0 1.6 %copy-start = (f32[2048,256]{1,0:T(8,128)S(1)}, f32[2048,256]{1,0:T(8,128)}, u32[]{:S(2)}) copy-start(f32[2048,256]{1,0:T(8,128)} %param.3) | copy-start | bytes 6291460
  0.0 2.6 %copy-start.1 = (f32[64,256]{1,0:T(8,128)S(1)}, f32[64,256]{1,0:T(8,128)}, u32[]{:S(2)}) copy-start(f32[64,256]{1,0:T(8,128)} %param.5) | copy-start | bytes 196612
  2.7 8.0 %collective-permute-start = (s32[192,256]{1,0:T(8,128)S(1)}, s32[192,256]{1,0:T(8,128)S(1)}, u32[]{:S(2)}, u32[]{:S(2)}) collective-permute-start(s32[192,256]{1,0:T(8,128)S(1)} %pad_add_fusion.refs_0_.refs_2_), channel_id=1, source_target_pairs={{0,1},{1,0},{2,3},{3,2},{4,5},{5,4},{6,7},{7,6},{8,9},{9,8},{10,11... | collective-permute-start | bytes 589832 | tf_op jit(solution)/shard_map/ppermute | solution.py:201
  5.8 5.6 %collective-permute-start.3 = (s32[192,256]{1,0:T(8,128)S(1)}, s32[192,256]{1,0:T(8,128)S(1)}, u32[]{:S(2)}, u32[]{:S(2)}) collective-permute-start(s32[192,256]{1,0:T(8,128)S(1)} %pad_add_fusion.refs_0_.refs_2_), channel_id=1, source_target_pairs={{1,2},{2,1},{5,6},{6,5},{9,10},{10,9},{13,14},{14,13},{17,18},{18,... | collective-permute-start | bytes 589832 | tf_op jit(solution)/shard_map/ppermute | solution.py:209
  6.4 6.6 %collective-permute-start.5 = (s32[192,256]{1,0:T(8,128)S(1)}, s32[192,256]{1,0:T(8,128)S(1)}, u32[]{:S(2)}, u32[]{:S(2)}) collective-permute-start(s32[192,256]{1,0:T(8,128)S(1)} %pad_add_fusion.refs_0_.refs_2_), channel_id=1, source_target_pairs={{0,8},{4,12},{8,0},{12,4},{1,9},{5,13},{9,1},{13,5},{2,10},{6,14},... | collective-permute-start | bytes 589832 | tf_op jit(solution)/shard_map/ppermute | solution.py:201
  8.0 9.5 %collective-permute-start.1 = (s32[192,256]{1,0:T(8,128)S(1)}, s32[192,256]{1,0:T(8,128)S(1)}, u32[]{:S(2)}, u32[]{:S(2)}) collective-permute-start(s32[192,256]{1,0:T(8,128)S(1)} %pad_add_fusion.refs_0_.refs_2_), channel_id=1, source_target_pairs={{0,4},{4,0},{8,12},{12,8},{1,5},{5,1},{9,13},{13,9},{2,6},{6,2},{1... | collective-permute-start | bytes 589832 | tf_op jit(solution)/shard_map/ppermute | solution.py:201
  10.7 6.8 %collective-permute-start.2 = (s32[192,256]{1,0:T(8,128)S(1)}, s32[192,256]{1,0:T(8,128)S(1)}, u32[]{:S(2)}, u32[]{:S(2)}) collective-permute-start(s32[192,256]{1,0:T(8,128)S(1)} %collective-permute-done.refs_1_.refs_3_), channel_id=1, source_target_pairs={{0,4},{4,0},{8,12},{12,8},{1,5},{5,1},{9,13},{13,9},{2,6},{6,2},{1... | collective-permute-start | bytes 589832 | tf_op jit(solution)/shard_map/ppermute | solution.py:201
  10.7 9.4 %collective-permute-start.7 = (s32[192,256]{1,0:T(8,128)S(1)}, s32[192,256]{1,0:T(8,128)S(1)}, u32[]{:S(2)}, u32[]{:S(2)}) collective-permute-start(s32[192,256]{1,0:T(8,128)S(1)} %collective-permute-done.refs_1_.refs_3_), channel_id=1, source_target_pairs={{1,2},{2,1},{5,6},{6,5},{9,10},{10,9},{13,14},{14,13},{17,18},{18,... | collective-permute-start | bytes 589832 | tf_op jit(solution)/shard_map/ppermute | solution.py:209
  11.4 8.8 %collective-permute-start.11 = (s32[192,256]{1,0:T(8,128)S(1)}, s32[192,256]{1,0:T(8,128)S(1)}, u32[]{:S(2)}, u32[]{:S(2)}) collective-permute-start(s32[192,256]{1,0:T(8,128)S(1)} %collective-permute-done.3.refs_2_.refs_6_), channel_id=1, source_target_pairs={{0,8},{4,12},{8,0},{12,4},{1,9},{5,13},{9,1},{13,5},{2,10},{6,14},... | collective-permute-start | bytes 589832 | tf_op jit(solution)/shard_map/ppermute | solution.py:201
  13.1 9.4 %collective-permute-start.9 = (s32[192,256]{1,0:T(8,128)S(1)}, s32[192,256]{1,0:T(8,128)S(1)}, u32[]{:S(2)}, u32[]{:S(2)}) collective-permute-start(s32[192,256]{1,0:T(8,128)S(1)} %collective-permute-done.5.refs_4_.refs_8_), channel_id=1, source_target_pairs={{0,1},{1,0},{2,3},{3,2},{4,5},{5,4},{6,7},{7,6},{8,9},{9,8},{10,11... | collective-permute-start | bytes 589832 | tf_op jit(solution)/shard_map/ppermute | solution.py:201
  17.5 5.0 %collective-permute-start.4 = (s32[192,256]{1,0:T(8,128)S(1)}, s32[192,256]{1,0:T(8,128)S(1)}, u32[]{:S(2)}, u32[]{:S(2)}) collective-permute-start(s32[192,256]{1,0:T(8,128)S(1)} %collective-permute-done.3.refs_2_.refs_6_), channel_id=1, source_target_pairs={{0,4},{4,0},{8,12},{12,8},{1,5},{5,1},{9,13},{13,9},{2,6},{6,2},{1... | collective-permute-start | bytes 589832 | tf_op jit(solution)/shard_map/ppermute | solution.py:201
  17.5 5.5 %collective-permute-start.6 = (s32[192,256]{1,0:T(8,128)S(1)}, s32[192,256]{1,0:T(8,128)S(1)}, u32[]{:S(2)}, u32[]{:S(2)}) collective-permute-start(s32[192,256]{1,0:T(8,128)S(1)} %collective-permute-done.5.refs_4_.refs_8_), channel_id=1, source_target_pairs={{0,4},{4,0},{8,12},{12,8},{1,5},{5,1},{9,13},{13,9},{2,6},{6,2},{1... | collective-permute-start | bytes 589832 | tf_op jit(solution)/shard_map/ppermute | solution.py:201
  20.1 6.5 %collective-permute-start.8 = (s32[192,256]{1,0:T(8,128)S(1)}, s32[192,256]{1,0:T(8,128)S(1)}, u32[]{:S(2)}, u32[]{:S(2)}) collective-permute-start(s32[192,256]{1,0:T(8,128)S(1)} %collective-permute-done.7.refs_2_.refs_10_), channel_id=1, source_target_pairs={{0,4},{4,0},{8,12},{12,8},{1,5},{5,1},{9,13},{13,9},{2,6},{6,2},{1... | collective-permute-start | bytes 589832 | tf_op jit(solution)/shard_map/ppermute | solution.py:201
  20.2 4.9 %collective-permute-start.12 = (s32[192,256]{1,0:T(8,128)S(1)}, s32[192,256]{1,0:T(8,128)S(1)}, u32[]{:S(2)}, u32[]{:S(2)}) collective-permute-start(s32[192,256]{1,0:T(8,128)S(1)} %collective-permute-done.11.refs_2_.refs_14_), channel_id=1, source_target_pairs={{0,4},{4,0},{8,12},{12,8},{1,5},{5,1},{9,13},{13,9},{2,6},{6,2},{1... | collective-permute-start | bytes 589832 | tf_op jit(solution)/shard_map/ppermute | solution.py:201
  22.5 4.1 %collective-permute-start.10 = (s32[192,256]{1,0:T(8,128)S(1)}, s32[192,256]{1,0:T(8,128)S(1)}, u32[]{:S(2)}, u32[]{:S(2)}) collective-permute-start(s32[192,256]{1,0:T(8,128)S(1)} %collective-permute-done.9.refs_4_.refs_12_), channel_id=1, source_target_pairs={{0,4},{4,0},{8,12},{12,8},{1,5},{5,1},{9,13},{13,9},{2,6},{6,2},{1... | collective-permute-start | bytes 589832 | tf_op jit(solution)/shard_map/ppermute | solution.py:201
  22.5 7.3 %collective-permute-start.13 = (s32[192,256]{1,0:T(8,128)S(1)}, s32[192,256]{1,0:T(8,128)S(1)}, u32[]{:S(2)}, u32[]{:S(2)}) collective-permute-start(s32[192,256]{1,0:T(8,128)S(1)} %collective-permute-done.7.refs_2_.refs_10_), channel_id=1, source_target_pairs={{0,8},{4,12},{8,0},{12,4},{1,9},{5,13},{9,1},{13,5},{2,10},{6,14},... | collective-permute-start | bytes 589832 | tf_op jit(solution)/shard_map/ppermute | solution.py:201
  29.8 1.4 %collective-permute-start.14 = (s32[192,256]{1,0:T(8,128)S(1)}, s32[192,256]{1,0:T(8,128)S(1)}, u32[]{:S(2)}, u32[]{:S(2)}) collective-permute-start(s32[192,256]{1,0:T(8,128)S(1)} %collective-permute-done.13.refs_16_), channel_id=1, source_target_pairs={{0,4},{4,0},{8,12},{12,8},{1,5},{5,1},{9,13},{13,9},{2,6},{6,2},{1... | collective-permute-start | bytes 589832 | tf_op jit(solution)/shard_map/ppermute | solution.py:201
  33.4 1.5 %collective-permute-start.15 = (f32[64,512]{1,0:T(8,128)S(1)}, f32[64,512]{1,0:T(8,128)S(1)}, u32[]{:S(2)}, u32[]{:S(2)}) collective-permute-start(f32[64,512]{1,0:T(8,128)S(1)} %get-tuple-element.14.refs_0_), channel_id=1, source_target_pairs={{1,2},{2,1},{5,6},{6,5},{9,10},{10,9},{13,14},{14,13},{17,18},{18,... | collective-permute-start | bytes 393224 | tf_op jit(solution)/shard_map/ppermute | solution.py:209
  34.2 6.4 %collective-permute-start.16 = (f32[64,512]{1,0:T(8,128)S(1)}, f32[64,512]{1,0:T(8,128)S(1)}, u32[]{:S(2)}, u32[]{:S(2)}) collective-permute-start(f32[64,512]{1,0:T(8,128)S(1)} %get-tuple-element.14.refs_0_), channel_id=1, source_target_pairs={{0,8},{4,12},{8,0},{12,4},{1,9},{5,13},{9,1},{13,5},{2,10},{6,14},... | collective-permute-start | bytes 393224 | tf_op jit(solution)/shard_map/ppermute | solution.py:201
  34.8 7.8 %collective-permute-start.17 = (f32[64,512]{1,0:T(8,128)S(1)}, f32[64,512]{1,0:T(8,128)S(1)}, u32[]{:S(2)}, u32[]{:S(2)}) collective-permute-start(f32[64,512]{1,0:T(8,128)S(1)} %collective-permute-done.15.refs_1_), channel_id=1, source_target_pairs={{0,8},{4,12},{8,0},{12,4},{1,9},{5,13},{9,1},{13,5},{2,10},{6,14},... | collective-permute-start | bytes 393224 | tf_op jit(solution)/shard_map/ppermute | solution.py:201
  36.3 6.3 %collective-permute-start.18 = (f32[64,512]{1,0:T(8,128)S(1)}, f32[64,512]{1,0:T(8,128)S(1)}, u32[]{:S(2)}, u32[]{:S(2)}) collective-permute-start(f32[64,512]{1,0:T(8,128)S(1)} %get-tuple-element.14.refs_0_), channel_id=1, source_target_pairs={{0,4},{4,0},{8,12},{12,8},{1,5},{5,1},{9,13},{13,9},{2,6},{6,2},{1... | collective-permute-start | bytes 393224 | tf_op jit(solution)/shard_map/ppermute | solution.py:201
  36.3 6.3 %collective-permute-start.19 = (f32[64,512]{1,0:T(8,128)S(1)}, f32[64,512]{1,0:T(8,128)S(1)}, u32[]{:S(2)}, u32[]{:S(2)}) collective-permute-start(f32[64,512]{1,0:T(8,128)S(1)} %collective-permute-done.15.refs_1_), channel_id=1, source_target_pairs={{0,4},{4,0},{8,12},{12,8},{1,5},{5,1},{9,13},{13,9},{2,6},{6,2},{1... | collective-permute-start | bytes 393224 | tf_op jit(solution)/shard_map/ppermute | solution.py:201
  40.6 2.0 %collective-permute-start.20 = (f32[64,512]{1,0:T(8,128)S(1)}, f32[64,512]{1,0:T(8,128)S(1)}, u32[]{:S(2)}, u32[]{:S(2)}) collective-permute-start(f32[64,512]{1,0:T(8,128)S(1)} %collective-permute-done.16.refs_2_), channel_id=1, source_target_pairs={{0,4},{4,0},{8,12},{12,8},{1,5},{5,1},{9,13},{13,9},{2,6},{6,2},{1... | collective-permute-start | bytes 393224 | tf_op jit(solution)/shard_map/ppermute | solution.py:201
  42.6 1.3 %collective-permute-start.21 = (f32[64,512]{1,0:T(8,128)S(1)}, f32[64,512]{1,0:T(8,128)S(1)}, u32[]{:S(2)}, u32[]{:S(2)}) collective-permute-start(f32[64,512]{1,0:T(8,128)S(1)} %collective-permute-done.17.refs_3_), channel_id=1, source_target_pairs={{0,4},{4,0},{8,12},{12,8},{1,5},{5,1},{9,13},{13,9},{2,6},{6,2},{1... | collective-permute-start | bytes 393224 | tf_op jit(solution)/shard_map/ppermute | solution.py:201
  49.3 17.6 %collective-permute-start.27 = (f32[64,256]{1,0:T(8,128)S(1)}, f32[64,256]{1,0:T(8,128)S(1)}, u32[]{:S(2)}, u32[]{:S(2)}) collective-permute-start(f32[64,256]{1,0:T(8,128)S(1)} %get-tuple-element.18), channel_id=1, source_target_pairs={{0,1},{1,0},{2,3},{3,2},{4,5},{5,4},{6,7},{7,6},{8,9},{9,8},{10,11... | collective-permute-start | bytes 196616 | tf_op jit(solution)/shard_map/ppermute | solution.py:201
  54.3 1.2 %collective-permute-start.22 = (f32[40,128]{1,0:T(8,128)S(1)}, f32[40,128]{1,0:T(8,128)S(1)}, u32[]{:S(2)}, u32[]{:S(2)}) collective-permute-start(f32[40,128]{1,0:T(8,128)S(1)} %get-tuple-element.16.a_ref), channel_id=1, source_target_pairs={{0,4},{4,0},{8,12},{12,8},{1,5},{5,1},{9,13},{13,9},{2,6},{6,2},{1... | collective-permute-start | bytes 61448 | tf_op jit(solution)/shard_map/ppermute | solution.py:201
  55.6 3.8 %collective-permute-start.23 = (f32[40,128]{1,0:T(8,128)S(1)}, f32[40,128]{1,0:T(8,128)S(1)}, u32[]{:S(2)}, u32[]{:S(2)}) collective-permute-start(f32[40,128]{1,0:T(8,128)S(1)} %shard_map.43.a_ref), channel_id=1, source_target_pairs={{0,8},{4,12},{8,0},{12,4},{1,9},{5,13},{9,1},{13,5},{2,10},{6,14},... | collective-permute-start | bytes 61448 | tf_op jit(solution)/shard_map/ppermute | solution.py:201
  59.4 4.4 %collective-permute-start.24 = (f32[40,128]{1,0:T(8,128)S(1)}, f32[40,128]{1,0:T(8,128)S(1)}, u32[]{:S(2)}, u32[]{:S(2)}) collective-permute-start(f32[40,128]{1,0:T(8,128)S(1)} %shard_map.44.share_ref), channel_id=1, source_target_pairs={{0,1},{1,0},{2,3},{3,2},{4,5},{5,4},{6,7},{7,6},{8,9},{9,8},{10,11... | collective-permute-start | bytes 61448 | tf_op jit(solution)/shard_map/ppermute | solution.py:201
  59.5 4.7 %collective-permute-start.25 = (f32[40,128]{1,0:T(8,128)S(1)}, f32[40,128]{1,0:T(8,128)S(1)}, u32[]{:S(2)}, u32[]{:S(2)}) collective-permute-start(f32[40,128]{1,0:T(8,128)S(1)} %shard_map.44.share_ref), channel_id=1, source_target_pairs={{0,2},{1,3},{2,0},{3,1},{4,6},{5,7},{6,4},{7,5},{8,10},{9,11},{10,... | collective-permute-start | bytes 61448 | tf_op jit(solution)/shard_map/ppermute | solution.py:201
  61.3 5.6 %collective-permute-start.26 = (f32[40,128]{1,0:T(8,128)S(1)}, f32[40,128]{1,0:T(8,128)S(1)}, u32[]{:S(2)}, u32[]{:S(2)}) collective-permute-start(f32[40,128]{1,0:T(8,128)S(1)} %shard_map.44.share_ref), channel_id=1, source_target_pairs={{0,3},{1,2},{2,1},{3,0},{4,7},{5,6},{6,5},{7,4},{8,11},{9,10},{10,... | collective-permute-start | bytes 61448 | tf_op jit(solution)/shard_map/ppermute | solution.py:201

commit v4 on v3

--- a/solution.py
+++ b/solution.py
@@ -89,14 +89,22 @@
     done = []
     for top in range(0, n, 8):
         rows = n - top
-        local = lax.broadcasted_iota(jnp.int32, (rows, 2 * n), 0)
+        place = lax.broadcasted_iota(jnp.int32, (rows, 2 * n), 0)
         columns = [jnp.broadcast_to(work[:, top + k : top + k + 1], (rows, 2 * n)) for k in range(8)]
-        for k in range(8):
-            column = columns[k]
-            factor = jnp.where(local > k, column * (1.0 / column[k : k + 1]), 0.0)
-            work = work - factor * work[k : k + 1]
-            for later in range(k + 1, 8):
-                columns[later] = columns[later] - factor * columns[later][k : k + 1]
+        for k in range(0, 8, 2):
+            one, two = columns[k], columns[k + 1]
+            a, b, d = one[k : k + 1], one[k + 1 : k + 2], two[k + 1 : k + 2]
+            inverse = 1.0 / a
+            slope = b * inverse
+            second = jnp.where(place > k + 1, (two * a - one * b) * (1.0 / (a * d - b * b)), 0.0)
+            first = jnp.where(place > k, one, 0.0)
+
+            def eliminate(value):
+                upper = value[k : k + 1]
+                return value - first * (upper * inverse) - second * (value[k + 1 : k + 2] - slope * upper)
+
+            work = eliminate(work)
+            columns = columns[: k + 2] + [eliminate(column) for column in columns[k + 2 :]]
         done.append(work[:8])
         work = work[8:]
     upper = jnp.concatenate(done, axis=0)
@@ -209,6 +217,10 @@
     return lax.ppermute(value, "col", MIDDLE)
 
 
+def diagonal(value):
+    return lax.ppermute(value, ("row", "col"), [(4 * r + c, 4 * (r ^ 2) + 3 - c) for r in range(4) for c in (1, 2)])
+
+
 MIDDLE = [(1, 2), (2, 1)]
 
 
@@ -242,15 +254,18 @@
     tiles.append(build(*groups[2]))
     groups.append([chip_partner, CORE(chip_partner)])
     tiles.append(build(*groups[3]))
-    groups.append([chip_partner_outer, CORE(after(chip_partner_outer, *tiles[1:4]))])
+    final = CORE(after(chip_partner_outer, *tiles[1:4]))
+    groups.append([chip_partner_outer])
+    tiles.append(build(*groups[4]))
+    groups.append([final])
     images, tile = call(
         functools.partial(first_kernel, [len(group) for group in groups], half, scale, total),
         [own, outer] + [block for group in groups for block in group] + tiles,
-        (jax.ShapeDtypeStruct((vecs, 2 * size), F32), jax.ShapeDtypeStruct((2 * size, 2 * size), BF16)),
+        (jax.ShapeDtypeStruct((vecs, 2 * size), F32), jax.ShapeDtypeStruct((size, 2 * size), BF16)),
     )
     tiles.append(tile)
     there, beside = middle(images), CHIP(images)
-    beyond = CHIP(there)
+    beyond = diagonal(images)
     gathered = [images, there, beside, beyond]
     gathered += [CORE(value) for value in gathered]
     here, part, chip, far = 0, 1, 2, 3

time: 69.9 us -> 68.6 us (0.981)
  waiting for transfers between devices: 21.8 us -> 18.4 us
  starting transfers between devices: 27 us -> 28.8 us
    ppermute x25 -> x24, waiting for transfers between devices: 21.8 us -> 18.4 us  [exchange(): lax.ppermute(value, axis, [(i, i ^ offset) for i in range(size)])]
    ppermute x25 -> x24, starting transfers between devices: 24.9 us -> 26 us  [exchange(): lax.ppermute(value, axis, [(i, i ^ offset) for i in range(size)])]
    ppermute x0 -> x1, starting transfers between devices: none -> 0.84 us  [diagonal(): lax.ppermute(value, ('row', 'col'), [(4 * r + c, 4 * (r ^ 2) + 3 - c) for...]
    pallas_call x9 -> x10, Pallas kernels: 18 us -> 18.3 us  [call(): pl.pallas_call(kernel, out_shape=out_shape, in_specs=in_specs or [VMEM] *...]
  transfers between devices with their start and end apart: 28 -> 28, of which waited for: 11 -> 11; matrix products, arithmetic and copies ran while one was open for 0% -> 0% of each run, Pallas kernels for 11% -> 13%
where the time goes in v4:
time: 68.6 us; the launch traced here: 68.4 us
  starting transfers between devices  28.8 us (42%)
  waiting for transfers between devices  18.4 us (27%)
  Pallas kernels  18.3 us (27%)
  local copies, waits for them, and re-layouts  1.74 us (3%)
  other arithmetic  0.9 us (1%)
    ppermute x24, starting transfers between devices, exchange(): lax.ppermute(value, axis, [(i, i ^ offset) for i in range(size)])  26 us
    ppermute x24, waiting for transfers between devices, exchange(): lax.ppermute(value, axis, [(i, i ^ offset) for i in range(size)])  18.4 us
    pallas_call x10, Pallas kernels, call(): pl.pallas_call(kernel, out_shape=out_shape, in_specs=in_specs or [VMEM] *...  18.3 us
    ppermute x3, starting transfers between devices, middle(): return lax.ppermute(value, 'col', MIDDLE)  1.99 us
  transfers between devices with their start and end apart: 28, of which 11 were waited for; matrix products, arithmetic and copies ran while one was open for 0% of the time, Pallas kernels for 13%

profile of v4, /device:TPU:0, one launch (start us, length us, event | category | flops | bytes accessed | tf_op | source)
XLA Modules:
  0.0 68.4 jit_solution(17480288228298517233)
XLA Ops:
  0.0 0.8 %pad_clamp_fusion = s32[1024]{0:T(1024)S(1)} fusion(s32[256]{0:T(256)} %param.4), kind=kLoop, calls=%fused_computation.7 | loop fusion | flops 1024 | bytes 5120 | tf_op jit(solution)/shard_map/gather | solution.py:233
  0.8 0.8 %copy-done = f32[2048,256]{1,0:T(8,128)S(1)} copy-done((f32[2048,256]{1,0:T(8,128)S(1)}, f32[2048,256]{1,0:T(8,128)}, u32[]{:S(2)}) %copy-start) | copy-done | bytes 2097176
  1.6 1.0 %gather_fusion = f32[256,256]{1,0:T(8,128)S(1)} fusion(f32[2048,256]{1,0:T(8,128)S(1)} %copy-done, s32[1024]{0:T(1024)S(1)} %pad_clamp_fusion), kind=kCustom, calls=%fused_computation | custom fusion | bytes 525312 | tf_op jit(solution)/shard_map/gather | solution.py:233
  2.7 3.1 %collective-permute-start = (s32[192,256]{1,0:T(8,128)S(1)}, s32[192,256]{1,0:T(8,128)S(1)}, u32[]{:S(2)}, u32[]{:S(2)}) collective-permute-start(s32[192,256]{1,0:T(8,128)S(1)} %pad_add_fusion.refs_0_.refs_2_), channel_id=1, source_target_pairs={{0,1},{1,0},{2,3},{3,2},{4,5},{5,4},{6,7},{7,6},{8,9},{9,8},{10,11... | collective-permute-start | bytes 589832 | tf_op jit(solution)/shard_map/ppermute | solution.py:209
  5.8 0.7 collective-permute-start.3
  6.4 1.6 %collective-permute-start.5 = (s32[192,256]{1,0:T(8,128)S(1)}, s32[192,256]{1,0:T(8,128)S(1)}, u32[]{:S(2)}, u32[]{:S(2)}) collective-permute-start(s32[192,256]{1,0:T(8,128)S(1)} %pad_add_fusion.refs_0_.refs_2_), channel_id=1, source_target_pairs={{0,8},{4,12},{8,0},{12,4},{1,9},{5,13},{9,1},{13,5},{2,10},{6,14},... | collective-permute-start | bytes 589832 | tf_op jit(solution)/shard_map/ppermute | solution.py:209
  8.0 0.0 collective-permute-start.1
  8.0 2.7 %collective-permute-done.refs_1_.refs_3_ = s32[192,256]{1,0:T(8,128)S(1)} collective-permute-done((s32[192,256]{1,0:T(8,128)S(1)}, s32[192,256]{1,0:T(8,128)S(1)}, u32[]{:S(2)}, u32[]{:S(2)}) %collective-permute-start) | collective-permute-done | bytes 196640 | tf_op jit(solution)/shard_map/ppermute | solution.py:209
  10.7 0.0 collective-permute-start.2
  10.7 0.7 collective-permute-start.7
  11.4 0.0 collective-permute-done.3.refs_2_.refs_6_
  11.4 1.7 %collective-permute-start.11 = (s32[192,256]{1,0:T(8,128)S(1)}, s32[192,256]{1,0:T(8,128)S(1)}, u32[]{:S(2)}, u32[]{:S(2)}) collective-permute-start(s32[192,256]{1,0:T(8,128)S(1)} %collective-permute-done.3.refs_2_.refs_6_), channel_id=1, source_target_pairs={{0,8},{4,12},{8,0},{12,4},{1,9},{5,13},{9,1},{13,5},{2,10},{6,14},... | collective-permute-start | bytes 589832 | tf_op jit(solution)/shard_map/ppermute | solution.py:209
  13.1 0.0 collective-permute-done.5.refs_4_.refs_8_
  13.1 4.4 %collective-permute-start.9 = (s32[192,256]{1,0:T(8,128)S(1)}, s32[192,256]{1,0:T(8,128)S(1)}, u32[]{:S(2)}, u32[]{:S(2)}) collective-permute-start(s32[192,256]{1,0:T(8,128)S(1)} %collective-permute-done.5.refs_4_.refs_8_), channel_id=1, source_target_pairs={{0,1},{1,0},{2,3},{3,2},{4,5},{5,4},{6,7},{7,6},{8,9},{9,8},{10,11... | collective-permute-start | bytes 589832 | tf_op jit(solution)/shard_map/ppermute | solution.py:209
  17.5 0.0 collective-permute-done.1.refs_4_
  17.5 0.0 collective-permute-start.4
  17.5 0.0 collective-permute-done.2.refs_5_
  17.5 0.5 collective-permute-start.6
  18.0 2.1 %shard_map.37.refs_18_.refs_8_ = bf16[1024,512]{1,0:T(8,128)(2,1)S(1)} custom-call(s32[192,256]{1,0:T(8,128)S(1)} %pad_add_fusion.refs_0_.refs_2_, s32[192,256]{1,0:T(8,128)S(1)} %collective-permute-done.refs_1_.refs_3_, s32[192,256]{1,0:T(8,128)S(1)} %pad_add_fusion.refs_0_.refs_2_, s32[192,256]{1,0:T(8,128)S(1)} %collective-permute-done.refs_1_.refs_3_, ...), custom_call_target="tpu_custom_call" | custom-call | tf_op jit(solution)/shard_map/pallas_call | solution.py:195
  20.1 0.0 collective-permute-done.7.refs_2_.refs_10_
  20.1 0.1 collective-permute-start.8
  20.2 0.0 collective-permute-done.11.refs_2_.refs_14_
  20.2 0.4 collective-permute-start.12
  20.7 1.8 %collective-permute-done.9.refs_4_.refs_12_ = s32[192,256]{1,0:T(8,128)S(1)} collective-permute-done((s32[192,256]{1,0:T(8,128)S(1)}, s32[192,256]{1,0:T(8,128)S(1)}, u32[]{:S(2)}, u32[]{:S(2)}) %collective-permute-start.9) | collective-permute-done | bytes 196640 | tf_op jit(solution)/shard_map/ppermute | solution.py:209
  22.5 0.0 collective-permute-start.10
  22.5 0.0 collective-permute-done.4.refs_3_.refs_7_
  22.5 0.5 collective-permute-start.13
  23.0 0.0 collective-permute-done.6.refs_5_.refs_9_
  23.0 2.1 %shard_map.38.refs_19_.refs_9_ = bf16[1024,512]{1,0:T(8,128)(2,1)S(1)} custom-call(s32[192,256]{1,0:T(8,128)S(1)} %pad_add_fusion.refs_0_.refs_2_, s32[192,256]{1,0:T(8,128)S(1)} %collective-permute-done.refs_1_.refs_3_, s32[192,256]{1,0:T(8,128)S(1)} %collective-permute-done.3.refs_2_.refs_6_, s32[192,256]{1,0:T(8,128)S(1)} %collective-permute-done.4.refs_3_.refs_7_, ...), custom_call_target="tpu_custom_call" | custom-call | tf_op jit(solution)/shard_map/pallas_call | solution.py:195
  25.1 1.4 %shard_map.40.refs_21_.refs_11_ = bf16[512,512]{1,0:T(8,128)(2,1)S(1)} custom-call(s32[192,256]{1,0:T(8,128)S(1)} %pad_add_fusion.refs_0_.refs_2_, s32[192,256]{1,0:T(8,128)S(1)} %collective-permute-done.refs_1_.refs_3_, s32[192,256]{1,0:T(8,128)S(1)} %collective-permute-done.11.refs_2_.refs_14_, s32[192,256]{1,0:T(8,128)S(1)} %collective-permute-done.12.refs_3_.refs_15_), custom_call_target="tpu_custom_call" | custom-call | tf_op jit(solution)/shard_map/pallas_call | solution.py:195
  26.6 2.1 %shard_map.39.refs_20_.refs_10_ = bf16[1024,512]{1,0:T(8,128)(2,1)S(1)} custom-call(s32[192,256]{1,0:T(8,128)S(1)} %pad_add_fusion.refs_0_.refs_2_, s32[192,256]{1,0:T(8,128)S(1)} %collective-permute-done.refs_1_.refs_3_, s32[192,256]{1,0:T(8,128)S(1)} %collective-permute-done.7.refs_2_.refs_10_, s32[192,256]{1,0:T(8,128)S(1)} %collective-permute-done.8.refs_3_.refs_11_, ...), custom_call_target="tpu_custom_call" | custom-call | tf_op jit(solution)/shard_map/pallas_call | solution.py:195
  28.6 1.2 %collective-permute-done.13.refs_2_.refs_16_ = s32[192,256]{1,0:T(8,128)S(1)} collective-permute-done((s32[192,256]{1,0:T(8,128)S(1)}, s32[192,256]{1,0:T(8,128)S(1)}, u32[]{:S(2)}, u32[]{:S(2)}) %collective-permute-start.13) | collective-permute-done | bytes 196640 | tf_op jit(solution)/shard_map/ppermute | solution.py:209
  29.8 0.0 collective-permute-start.14
  29.8 1.1 %shard_map.41.refs_22_.refs_12_ = bf16[256,512]{1,0:T(8,128)(2,1)S(1)} custom-call(s32[192,256]{1,0:T(8,128)S(1)} %pad_add_fusion.refs_0_.refs_2_, s32[192,256]{1,0:T(8,128)S(1)} %collective-permute-done.refs_1_.refs_3_, s32[192,256]{1,0:T(8,128)S(1)} %collective-permute-done.13.refs_2_.refs_16_), custom_call_target="tpu_custom_call" | custom-call | tf_op jit(solution)/shard_map/pallas_call | solution.py:195
  30.9 0.3 collective-permute-done.14.refs_17_
  31.2 1.8 %shard_map.42 = (f32[64,512]{1,0:T(8,128)S(1)}, bf16[256,512]{1,0:T(8,128)(2,1)S(1)}) custom-call(s32[192,256]{1,0:T(8,128)S(1)} %pad_add_fusion.refs_0_.refs_2_, s32[192,256]{1,0:T(8,128)S(1)} %collective-permute-done.refs_1_.refs_3_, s32[192,256]{1,0:T(8,128)S(1)} %pad_add_fusion.refs_0_.refs_2_, s32[192,256]{1,0:T(8,128)S(1)} %collective-permute-done.refs_1_.refs_3_, ...), custom_call_target="tpu_custom_call" | custom-call | tf_op jit(solution)/shard_map/pallas_call | solution.py:195
  33.0 0.7 collective-permute-start.15
  33.7 0.6 collective-permute-start.16
  34.3 0.8 %collective-permute-start.17 = (f32[64,512]{1,0:T(8,128)S(1)}, f32[64,512]{1,0:T(8,128)S(1)}, u32[]{:S(2)}, u32[]{:S(2)}) collective-permute-start(f32[64,512]{1,0:T(8,128)S(1)} %get-tuple-element.14.refs_0_), channel_id=1, source_target_pairs={{1,10},{2,9},{5,14},{6,13},{9,2},{10,1},{13,6},{14,5},{17,26},{18,... | collective-permute-start | bytes 393224 | tf_op jit(solution)/shard_map/ppermute | solution.py:221
  35.2 0.1 collective-permute-start.18
  35.2 0.0 collective-permute-done.15.refs_1_
  35.3 0.5 collective-permute-start.19
  35.7 3.6 %collective-permute-done.16.refs_2_ = f32[64,512]{1,0:T(8,128)S(1)} collective-permute-done((f32[64,512]{1,0:T(8,128)S(1)}, f32[64,512]{1,0:T(8,128)S(1)}, u32[]{:S(2)}, u32[]{:S(2)}) %collective-permute-start.16) | collective-permute-done | bytes 131104 | tf_op jit(solution)/shard_map/ppermute | solution.py:209
  39.4 0.0 collective-permute-start.20
  39.4 0.0 collective-permute-done.17.refs_3_
  39.4 0.5 collective-permute-start.21
  39.9 0.0 collective-permute-done.18.refs_4_
  39.9 0.0 collective-permute-done.19.refs_5_
  39.9 0.8 %collective-permute-done.20.refs_6_ = f32[64,512]{1,0:T(8,128)S(1)} collective-permute-done((f32[64,512]{1,0:T(8,128)S(1)}, f32[64,512]{1,0:T(8,128)S(1)}, u32[]{:S(2)}, u32[]{:S(2)}) %collective-permute-start.20) | collective-permute-done | bytes 131104 | tf_op jit(solution)/shard_map/ppermute | solution.py:209
  40.7 0.2 collective-permute-done.21.refs_7_
  40.9 5.1 %shard_map.43 = (f32[64,256]{1,0:T(8,128)S(1)}, f32[64,256]{1,0:T(8,128)S(1)}, f32[40,128]{1,0:T(8,128)S(1)}) custom-call(f32[64,512]{1,0:T(8,128)S(1)} %get-tuple-element.14.refs_0_, f32[64,512]{1,0:T(8,128)S(1)} %collective-permute-done.15.refs_1_, f32[64,512]{1,0:T(8,128)S(1)} %collective-permute-done.16.refs_2_, ...), custom_call_target="tpu_custom_call" | custom-call | tf_op jit(solution)/shard_map/pallas_call | solution.py:195
  46.0 6.1 %collective-permute-start.27 = (f32[64,256]{1,0:T(8,128)S(1)}, f32[64,256]{1,0:T(8,128)S(1)}, u32[]{:S(2)}, u32[]{:S(2)}) collective-permute-start(f32[64,256]{1,0:T(8,128)S(1)} %get-tuple-element.18), channel_id=1, source_target_pairs={{0,1},{1,0},{2,3},{3,2},{4,5},{5,4},{6,7},{7,6},{8,9},{9,8},{10,11... | collective-permute-start | bytes 196616 | tf_op jit(solution)/shard_map/ppermute | solution.py:209
  52.0 1.2 %collective-permute-done.22.b_ref = f32[40,128]{1,0:T(8,128)S(1)} collective-permute-done((f32[40,128]{1,0:T(8,128)S(1)}, f32[40,128]{1,0:T(8,128)S(1)}, u32[]{:S(2)}, u32[]{:S(2)}) %collective-permute-start.22) | collective-permute-done | bytes 20512 | tf_op jit(solution)/shard_map/ppermute | solution.py:209
  53.2 0.1 shard_map.44.a_ref
  53.3 1.5 %collective-permute-start.23 = (f32[40,128]{1,0:T(8,128)S(1)}, f32[40,128]{1,0:T(8,128)S(1)}, u32[]{:S(2)}, u32[]{:S(2)}) collective-permute-start(f32[40,128]{1,0:T(8,128)S(1)} %shard_map.44.a_ref), channel_id=1, source_target_pairs={{0,8},{4,12},{8,0},{12,4},{1,9},{5,13},{9,1},{13,5},{2,10},{6,14},... | collective-permute-start | bytes 61448 | tf_op jit(solution)/shard_map/ppermute | solution.py:209
  54.8 2.3 %collective-permute-done.23.b_ref = f32[40,128]{1,0:T(8,128)S(1)} collective-permute-done((f32[40,128]{1,0:T(8,128)S(1)}, f32[40,128]{1,0:T(8,128)S(1)}, u32[]{:S(2)}, u32[]{:S(2)}) %collective-permute-start.23) | collective-permute-done | bytes 20512 | tf_op jit(solution)/shard_map/ppermute | solution.py:209
  57.1 0.1 shard_map.45.share_ref
  57.2 0.1 collective-permute-start.24
  57.3 3.0 %collective-permute-start.25 = (f32[40,128]{1,0:T(8,128)S(1)}, f32[40,128]{1,0:T(8,128)S(1)}, u32[]{:S(2)}, u32[]{:S(2)}) collective-permute-start(f32[40,128]{1,0:T(8,128)S(1)} %shard_map.45.share_ref), channel_id=1, source_target_pairs={{0,2},{1,3},{2,0},{3,1},{4,6},{5,7},{6,4},{7,5},{8,10},{9,11},{10,... | collective-permute-start | bytes 61448 | tf_op jit(solution)/shard_map/ppermute | solution.py:209
  60.2 1.3 %collective-permute-start.26 = (f32[40,128]{1,0:T(8,128)S(1)}, f32[40,128]{1,0:T(8,128)S(1)}, u32[]{:S(2)}, u32[]{:S(2)}) collective-permute-start(f32[40,128]{1,0:T(8,128)S(1)} %shard_map.45.share_ref), channel_id=1, source_target_pairs={{0,3},{1,2},{2,1},{3,0},{4,7},{5,6},{6,5},{7,4},{8,11},{9,10},{10,... | collective-permute-start | bytes 61448 | tf_op jit(solution)/shard_map/ppermute | solution.py:209
  61.6 0.4 collective-permute-done.25.far_ref
  62.0 3.8 %collective-permute-done.26.across_ref = f32[40,128]{1,0:T(8,128)S(1)} collective-permute-done((f32[40,128]{1,0:T(8,128)S(1)}, f32[40,128]{1,0:T(8,128)S(1)}, u32[]{:S(2)}, u32[]{:S(2)}) %collective-permute-start.26) | collective-permute-done | bytes 20512 | tf_op jit(solution)/shard_map/ppermute | solution.py:209
  65.8 0.0 collective-permute-done.27.given_ref
  65.8 2.6 %shard_map.46 = f32[64,256]{1,0:T(8,128)} custom-call(s32[1]{0:T(128)} %bitcast.outer_ref, f32[40,128]{1,0:T(8,128)S(1)} %shard_map.45.share_ref, f32[40,128]{1,0:T(8,128)S(1)} %collective-permute-done.24.near_ref, f32[40,128]{1,0:T(8,128)S(1)} %collective-permute-done.25.far_ref, f32[40,128]{1,0:T(8,128)S(1)} %collective-permute-done.26.across_ref, ...), custom_call_target="tpu_custom_call" | custom-call | tf_op jit(solution)/shard_map/pallas_call | solution.py:195
  (12 shorter events, 0.1 us)
Async XLA Ops:
  0.0 1.6 %copy-start = (f32[2048,256]{1,0:T(8,128)S(1)}, f32[2048,256]{1,0:T(8,128)}, u32[]{:S(2)}) copy-start(f32[2048,256]{1,0:T(8,128)} %param.3) | copy-start | bytes 6291460
  0.0 2.6 %copy-start.1 = (f32[64,256]{1,0:T(8,128)S(1)}, f32[64,256]{1,0:T(8,128)}, u32[]{:S(2)}) copy-start(f32[64,256]{1,0:T(8,128)} %param.5) | copy-start | bytes 196612
  2.7 8.0 %collective-permute-start = (s32[192,256]{1,0:T(8,128)S(1)}, s32[192,256]{1,0:T(8,128)S(1)}, u32[]{:S(2)}, u32[]{:S(2)}) collective-permute-start(s32[192,256]{1,0:T(8,128)S(1)} %pad_add_fusion.refs_0_.refs_2_), channel_id=1, source_target_pairs={{0,1},{1,0},{2,3},{3,2},{4,5},{5,4},{6,7},{7,6},{8,9},{9,8},{10,11... | collective-permute-start | bytes 589832 | tf_op jit(solution)/shard_map/ppermute | solution.py:209
  5.8 5.6 %collective-permute-start.3 = (s32[192,256]{1,0:T(8,128)S(1)}, s32[192,256]{1,0:T(8,128)S(1)}, u32[]{:S(2)}, u32[]{:S(2)}) collective-permute-start(s32[192,256]{1,0:T(8,128)S(1)} %pad_add_fusion.refs_0_.refs_2_), channel_id=1, source_target_pairs={{1,2},{2,1},{5,6},{6,5},{9,10},{10,9},{13,14},{14,13},{17,18},{18,... | collective-permute-start | bytes 589832 | tf_op jit(solution)/shard_map/ppermute | solution.py:217
  6.4 6.6 %collective-permute-start.5 = (s32[192,256]{1,0:T(8,128)S(1)}, s32[192,256]{1,0:T(8,128)S(1)}, u32[]{:S(2)}, u32[]{:S(2)}) collective-permute-start(s32[192,256]{1,0:T(8,128)S(1)} %pad_add_fusion.refs_0_.refs_2_), channel_id=1, source_target_pairs={{0,8},{4,12},{8,0},{12,4},{1,9},{5,13},{9,1},{13,5},{2,10},{6,14},... | collective-permute-start | bytes 589832 | tf_op jit(solution)/shard_map/ppermute | solution.py:209
  8.0 9.5 %collective-permute-start.1 = (s32[192,256]{1,0:T(8,128)S(1)}, s32[192,256]{1,0:T(8,128)S(1)}, u32[]{:S(2)}, u32[]{:S(2)}) collective-permute-start(s32[192,256]{1,0:T(8,128)S(1)} %pad_add_fusion.refs_0_.refs_2_), channel_id=1, source_target_pairs={{0,4},{4,0},{8,12},{12,8},{1,5},{5,1},{9,13},{13,9},{2,6},{6,2},{1... | collective-permute-start | bytes 589832 | tf_op jit(solution)/shard_map/ppermute | solution.py:209
  10.7 6.8 %collective-permute-start.2 = (s32[192,256]{1,0:T(8,128)S(1)}, s32[192,256]{1,0:T(8,128)S(1)}, u32[]{:S(2)}, u32[]{:S(2)}) collective-permute-start(s32[192,256]{1,0:T(8,128)S(1)} %collective-permute-done.refs_1_.refs_3_), channel_id=1, source_target_pairs={{0,4},{4,0},{8,12},{12,8},{1,5},{5,1},{9,13},{13,9},{2,6},{6,2},{1... | collective-permute-start | bytes 589832 | tf_op jit(solution)/shard_map/ppermute | solution.py:209
  10.7 9.4 %collective-permute-start.7 = (s32[192,256]{1,0:T(8,128)S(1)}, s32[192,256]{1,0:T(8,128)S(1)}, u32[]{:S(2)}, u32[]{:S(2)}) collective-permute-start(s32[192,256]{1,0:T(8,128)S(1)} %collective-permute-done.refs_1_.refs_3_), channel_id=1, source_target_pairs={{1,2},{2,1},{5,6},{6,5},{9,10},{10,9},{13,14},{14,13},{17,18},{18,... | collective-permute-start | bytes 589832 | tf_op jit(solution)/shard_map/ppermute | solution.py:217
  11.4 8.8 %collective-permute-start.11 = (s32[192,256]{1,0:T(8,128)S(1)}, s32[192,256]{1,0:T(8,128)S(1)}, u32[]{:S(2)}, u32[]{:S(2)}) collective-permute-start(s32[192,256]{1,0:T(8,128)S(1)} %collective-permute-done.3.refs_2_.refs_6_), channel_id=1, source_target_pairs={{0,8},{4,12},{8,0},{12,4},{1,9},{5,13},{9,1},{13,5},{2,10},{6,14},... | collective-permute-start | bytes 589832 | tf_op jit(solution)/shard_map/ppermute | solution.py:209
  13.1 9.4 %collective-permute-start.9 = (s32[192,256]{1,0:T(8,128)S(1)}, s32[192,256]{1,0:T(8,128)S(1)}, u32[]{:S(2)}, u32[]{:S(2)}) collective-permute-start(s32[192,256]{1,0:T(8,128)S(1)} %collective-permute-done.5.refs_4_.refs_8_), channel_id=1, source_target_pairs={{0,1},{1,0},{2,3},{3,2},{4,5},{5,4},{6,7},{7,6},{8,9},{9,8},{10,11... | collective-permute-start | bytes 589832 | tf_op jit(solution)/shard_map/ppermute | solution.py:209
  17.5 5.0 %collective-permute-start.4 = (s32[192,256]{1,0:T(8,128)S(1)}, s32[192,256]{1,0:T(8,128)S(1)}, u32[]{:S(2)}, u32[]{:S(2)}) collective-permute-start(s32[192,256]{1,0:T(8,128)S(1)} %collective-permute-done.3.refs_2_.refs_6_), channel_id=1, source_target_pairs={{0,4},{4,0},{8,12},{12,8},{1,5},{5,1},{9,13},{13,9},{2,6},{6,2},{1... | collective-permute-start | bytes 589832 | tf_op jit(solution)/shard_map/ppermute | solution.py:209
  17.5 5.5 %collective-permute-start.6 = (s32[192,256]{1,0:T(8,128)S(1)}, s32[192,256]{1,0:T(8,128)S(1)}, u32[]{:S(2)}, u32[]{:S(2)}) collective-permute-start(s32[192,256]{1,0:T(8,128)S(1)} %collective-permute-done.5.refs_4_.refs_8_), channel_id=1, source_target_pairs={{0,4},{4,0},{8,12},{12,8},{1,5},{5,1},{9,13},{13,9},{2,6},{6,2},{1... | collective-permute-start | bytes 589832 | tf_op jit(solution)/shard_map/ppermute | solution.py:209
  20.1 6.5 %collective-permute-start.8 = (s32[192,256]{1,0:T(8,128)S(1)}, s32[192,256]{1,0:T(8,128)S(1)}, u32[]{:S(2)}, u32[]{:S(2)}) collective-permute-start(s32[192,256]{1,0:T(8,128)S(1)} %collective-permute-done.7.refs_2_.refs_10_), channel_id=1, source_target_pairs={{0,4},{4,0},{8,12},{12,8},{1,5},{5,1},{9,13},{13,9},{2,6},{6,2},{1... | collective-permute-start | bytes 589832 | tf_op jit(solution)/shard_map/ppermute | solution.py:209
  20.2 4.9 %collective-permute-start.12 = (s32[192,256]{1,0:T(8,128)S(1)}, s32[192,256]{1,0:T(8,128)S(1)}, u32[]{:S(2)}, u32[]{:S(2)}) collective-permute-start(s32[192,256]{1,0:T(8,128)S(1)} %collective-permute-done.11.refs_2_.refs_14_), channel_id=1, source_target_pairs={{0,4},{4,0},{8,12},{12,8},{1,5},{5,1},{9,13},{13,9},{2,6},{6,2},{1... | collective-permute-start | bytes 589832 | tf_op jit(solution)/shard_map/ppermute | solution.py:209
  22.5 4.1 %collective-permute-start.10 = (s32[192,256]{1,0:T(8,128)S(1)}, s32[192,256]{1,0:T(8,128)S(1)}, u32[]{:S(2)}, u32[]{:S(2)}) collective-permute-start(s32[192,256]{1,0:T(8,128)S(1)} %collective-permute-done.9.refs_4_.refs_12_), channel_id=1, source_target_pairs={{0,4},{4,0},{8,12},{12,8},{1,5},{5,1},{9,13},{13,9},{2,6},{6,2},{1... | collective-permute-start | bytes 589832 | tf_op jit(solution)/shard_map/ppermute | solution.py:209
  22.5 7.3 %collective-permute-start.13 = (s32[192,256]{1,0:T(8,128)S(1)}, s32[192,256]{1,0:T(8,128)S(1)}, u32[]{:S(2)}, u32[]{:S(2)}) collective-permute-start(s32[192,256]{1,0:T(8,128)S(1)} %collective-permute-done.7.refs_2_.refs_10_), channel_id=1, source_target_pairs={{0,8},{4,12},{8,0},{12,4},{1,9},{5,13},{9,1},{13,5},{2,10},{6,14},... | collective-permute-start | bytes 589832 | tf_op jit(solution)/shard_map/ppermute | solution.py:209
  29.8 1.4 %collective-permute-start.14 = (s32[192,256]{1,0:T(8,128)S(1)}, s32[192,256]{1,0:T(8,128)S(1)}, u32[]{:S(2)}, u32[]{:S(2)}) collective-permute-start(s32[192,256]{1,0:T(8,128)S(1)} %collective-permute-done.13.refs_2_.refs_16_), channel_id=1, source_target_pairs={{0,4},{4,0},{8,12},{12,8},{1,5},{5,1},{9,13},{13,9},{2,6},{6,2},{1... | collective-permute-start | bytes 589832 | tf_op jit(solution)/shard_map/ppermute | solution.py:209
  33.0 2.2 %collective-permute-start.15 = (f32[64,512]{1,0:T(8,128)S(1)}, f32[64,512]{1,0:T(8,128)S(1)}, u32[]{:S(2)}, u32[]{:S(2)}) collective-permute-start(f32[64,512]{1,0:T(8,128)S(1)} %get-tuple-element.14.refs_0_), channel_id=1, source_target_pairs={{1,2},{2,1},{5,6},{6,5},{9,10},{10,9},{13,14},{14,13},{17,18},{18,... | collective-permute-start | bytes 393224 | tf_op jit(solution)/shard_map/ppermute | solution.py:217
  33.7 5.7 %collective-permute-start.16 = (f32[64,512]{1,0:T(8,128)S(1)}, f32[64,512]{1,0:T(8,128)S(1)}, u32[]{:S(2)}, u32[]{:S(2)}) collective-permute-start(f32[64,512]{1,0:T(8,128)S(1)} %get-tuple-element.14.refs_0_), channel_id=1, source_target_pairs={{0,8},{4,12},{8,0},{12,4},{1,9},{5,13},{9,1},{13,5},{2,10},{6,14},... | collective-permute-start | bytes 393224 | tf_op jit(solution)/shard_map/ppermute | solution.py:209
  34.3 5.1 %collective-permute-start.17 = (f32[64,512]{1,0:T(8,128)S(1)}, f32[64,512]{1,0:T(8,128)S(1)}, u32[]{:S(2)}, u32[]{:S(2)}) collective-permute-start(f32[64,512]{1,0:T(8,128)S(1)} %get-tuple-element.14.refs_0_), channel_id=1, source_target_pairs={{1,10},{2,9},{5,14},{6,13},{9,2},{10,1},{13,6},{14,5},{17,26},{18,... | collective-permute-start | bytes 393224 | tf_op jit(solution)/shard_map/ppermute | solution.py:221
  35.2 4.7 %collective-permute-start.18 = (f32[64,512]{1,0:T(8,128)S(1)}, f32[64,512]{1,0:T(8,128)S(1)}, u32[]{:S(2)}, u32[]{:S(2)}) collective-permute-start(f32[64,512]{1,0:T(8,128)S(1)} %get-tuple-element.14.refs_0_), channel_id=1, source_target_pairs={{0,4},{4,0},{8,12},{12,8},{1,5},{5,1},{9,13},{13,9},{2,6},{6,2},{1... | collective-permute-start | bytes 393224 | tf_op jit(solution)/shard_map/ppermute | solution.py:209
  35.3 4.6 %collective-permute-start.19 = (f32[64,512]{1,0:T(8,128)S(1)}, f32[64,512]{1,0:T(8,128)S(1)}, u32[]{:S(2)}, u32[]{:S(2)}) collective-permute-start(f32[64,512]{1,0:T(8,128)S(1)} %collective-permute-done.15.refs_1_), channel_id=1, source_target_pairs={{0,4},{4,0},{8,12},{12,8},{1,5},{5,1},{9,13},{13,9},{2,6},{6,2},{1... | collective-permute-start | bytes 393224 | tf_op jit(solution)/shard_map/ppermute | solution.py:209
  39.4 1.3 %collective-permute-start.20 = (f32[64,512]{1,0:T(8,128)S(1)}, f32[64,512]{1,0:T(8,128)S(1)}, u32[]{:S(2)}, u32[]{:S(2)}) collective-permute-start(f32[64,512]{1,0:T(8,128)S(1)} %collective-permute-done.16.refs_2_), channel_id=1, source_target_pairs={{0,4},{4,0},{8,12},{12,8},{1,5},{5,1},{9,13},{13,9},{2,6},{6,2},{1... | collective-permute-start | bytes 393224 | tf_op jit(solution)/shard_map/ppermute | solution.py:209
  39.4 1.5 %collective-permute-start.21 = (f32[64,512]{1,0:T(8,128)S(1)}, f32[64,512]{1,0:T(8,128)S(1)}, u32[]{:S(2)}, u32[]{:S(2)}) collective-permute-start(f32[64,512]{1,0:T(8,128)S(1)} %collective-permute-done.17.refs_3_), channel_id=1, source_target_pairs={{0,4},{4,0},{8,12},{12,8},{1,5},{5,1},{9,13},{13,9},{2,6},{6,2},{1... | collective-permute-start | bytes 393224 | tf_op jit(solution)/shard_map/ppermute | solution.py:209
  46.0 19.8 %collective-permute-start.27 = (f32[64,256]{1,0:T(8,128)S(1)}, f32[64,256]{1,0:T(8,128)S(1)}, u32[]{:S(2)}, u32[]{:S(2)}) collective-permute-start(f32[64,256]{1,0:T(8,128)S(1)} %get-tuple-element.18), channel_id=1, source_target_pairs={{0,1},{1,0},{2,3},{3,2},{4,5},{5,4},{6,7},{7,6},{8,9},{9,8},{10,11... | collective-permute-start | bytes 196616 | tf_op jit(solution)/shard_map/ppermute | solution.py:209
  52.0 1.2 %collective-permute-start.22 = (f32[40,128]{1,0:T(8,128)S(1)}, f32[40,128]{1,0:T(8,128)S(1)}, u32[]{:S(2)}, u32[]{:S(2)}) collective-permute-start(f32[40,128]{1,0:T(8,128)S(1)} %get-tuple-element.16.a_ref), channel_id=1, source_target_pairs={{0,4},{4,0},{8,12},{12,8},{1,5},{5,1},{9,13},{13,9},{2,6},{6,2},{1... | collective-permute-start | bytes 61448 | tf_op jit(solution)/shard_map/ppermute | solution.py:209
  53.3 3.8 %collective-permute-start.23 = (f32[40,128]{1,0:T(8,128)S(1)}, f32[40,128]{1,0:T(8,128)S(1)}, u32[]{:S(2)}, u32[]{:S(2)}) collective-permute-start(f32[40,128]{1,0:T(8,128)S(1)} %shard_map.44.a_ref), channel_id=1, source_target_pairs={{0,8},{4,12},{8,0},{12,4},{1,9},{5,13},{9,1},{13,5},{2,10},{6,14},... | collective-permute-start | bytes 61448 | tf_op jit(solution)/shard_map/ppermute | solution.py:209
  57.2 4.4 %collective-permute-start.24 = (f32[40,128]{1,0:T(8,128)S(1)}, f32[40,128]{1,0:T(8,128)S(1)}, u32[]{:S(2)}, u32[]{:S(2)}) collective-permute-start(f32[40,128]{1,0:T(8,128)S(1)} %shard_map.45.share_ref), channel_id=1, source_target_pairs={{0,1},{1,0},{2,3},{3,2},{4,5},{5,4},{6,7},{7,6},{8,9},{9,8},{10,11... | collective-permute-start | bytes 61448 | tf_op jit(solution)/shard_map/ppermute | solution.py:209
  57.3 4.7 %collective-permute-start.25 = (f32[40,128]{1,0:T(8,128)S(1)}, f32[40,128]{1,0:T(8,128)S(1)}, u32[]{:S(2)}, u32[]{:S(2)}) collective-permute-start(f32[40,128]{1,0:T(8,128)S(1)} %shard_map.45.share_ref), channel_id=1, source_target_pairs={{0,2},{1,3},{2,0},{3,1},{4,6},{5,7},{6,4},{7,5},{8,10},{9,11},{10,... | collective-permute-start | bytes 61448 | tf_op jit(solution)/shard_map/ppermute | solution.py:209
  60.2 5.6 %collective-permute-start.26 = (f32[40,128]{1,0:T(8,128)S(1)}, f32[40,128]{1,0:T(8,128)S(1)}, u32[]{:S(2)}, u32[]{:S(2)}) collective-permute-start(f32[40,128]{1,0:T(8,128)S(1)} %shard_map.45.share_ref), channel_id=1, source_target_pairs={{0,3},{1,2},{2,1},{3,0},{4,7},{5,6},{6,5},{7,4},{8,11},{9,10},{10,... | collective-permute-start | bytes 61448 | tf_op jit(solution)/shard_map/ppermute | solution.py:209

commit v5 on v4

--- a/solution.py
+++ b/solution.py
@@ -11,7 +11,7 @@
 ITERS = 2
 REACH = 20.0
 UNIT = REACH / 32767.0
-FIXED = 2.0**28
+FIXED, RANGE = 2.0**28, 2.0**26
 HIGHEST = lax.Precision.HIGHEST
 BF16, F32 = jnp.bfloat16, jnp.float32
 VMEM = pl.BlockSpec(memory_space=pltpu.VMEM)
@@ -21,15 +21,45 @@
     return lax.dot_general(a, b, ((contract[:1], contract[1:]), ((), ())), precision=precision, preferred_element_type=F32)
 
 
-def encode(landmarks, initial):
-    half = landmarks.shape[0] // 2
-    code = jnp.round(landmarks * (1.0 / UNIT)).astype(jnp.int32)
-    packed = (code[:half] << 16) | (code[half:] & 0xFFFF)
-    return jnp.concatenate([packed, jnp.round(initial * FIXED).astype(jnp.int32)], axis=0)
+def pair(high, low):
+    return (high << 16) | (low & 0xFFFF)
+
+
+def unpair(words):
+    return words >> 16, (words << 16) >> 16
+
+
+def encode(initial_ref, out_ref):
+    initial = initial_ref[...]
+    vecs, size = initial.shape
+    half = size // 2
+    mean = jnp.round(jnp.sum(initial, axis=1, keepdims=True) * (FIXED / size)).astype(jnp.int32)
+    apart = initial - mean.astype(F32) * (1.0 / FIXED)
+    reach = jnp.ceil(jnp.max(jnp.abs(apart), axis=1, keepdims=True) * RANGE).astype(jnp.int32) + 1
+    step = reach.astype(F32) * (1.0 / (RANGE * 32767.0))
+    level = jnp.round(apart / step).astype(jnp.int32)
+    words = pair(level[:, :half], level[:, half:])
+    row = lax.broadcasted_iota(jnp.int32, (vecs, size), 0)
+    lane = lax.broadcasted_iota(jnp.int32, (vecs, size), 1)
+    header = jnp.where(lane == row, mean, jnp.where(lane == row + vecs, reach, 0))
+    out_ref[: vecs // 2] = jnp.concatenate([words[: vecs // 2], words[vecs // 2 :]], axis=1)
+    out_ref[vecs // 2 :] = jnp.broadcast_to(jnp.sum(header, axis=0, keepdims=True), (8, size))
+
+
+def decode(block, half):
+    words = block[half : block.shape[0] - 8]
+    vecs = 2 * words.shape[0]
+    level = jnp.concatenate([jnp.concatenate(unpair(part), axis=1) for part in (words[:, :half], words[:, half:])], axis=0)
+    header = block[block.shape[0] - 8 :].astype(F32)[:1, : 2 * vecs]
+    row = lax.broadcasted_iota(jnp.int32, (vecs, 2 * vecs), 0)
+    lane = lax.broadcasted_iota(jnp.int32, (vecs, 2 * vecs), 1)
+    mean = jnp.sum(jnp.where(lane == row, header, 0.0), axis=1, keepdims=True) * (1.0 / FIXED)
+    step = jnp.sum(jnp.where(lane == row + vecs, header, 0.0), axis=1, keepdims=True) * (1.0 / (RANGE * 32767.0))
+    return level.astype(F32) * step + mean
 
 
 def split_codes(words):
-    code = jnp.concatenate([words >> 16, (words << 16) >> 16], axis=0)
+    code = jnp.concatenate(unpair(words), axis=0)
     high = ((code + 128) >> 8) << 8
     return high.astype(F32).astype(BF16), (code - high).astype(F32).astype(BF16)
 
@@ -51,31 +81,32 @@
     return high, low, scale * norms
 
 
+def side_kernel(half, scale, own_ref, outer_ref, high_ref, low_ref, norms_ref):
+    high_ref[...], low_ref[...], norms_ref[...] = own_side((own_ref, outer_ref), half, scale)
+
+
 def build_kernel(half, scale, *refs):
-    own, blocks, out_ref = refs[:2], refs[2:-1], refs[-1]
-    own_high, own_low, own_norms = own_side(own, half, scale)
+    side, blocks, (tile_ref, start_ref) = refs[:3], refs[3:-2], refs[-2:]
     for b, block in enumerate(blocks):
-        out_ref[pl.ds(b * 2 * half, 2 * half), :] = kernel_rows(block[:half], own_high, own_low, own_norms, scale)
-
-
-def first_kernel(counts, half, scale, total, *refs):
-    count = sum(counts)
-    own, blocks, parts = refs[:2], refs[2 : 2 + count], refs[2 + count : -2]
+        place = pl.ds(b * 2 * half, 2 * half)
+        tile_ref[place, :] = kernel_rows(block[:half], *(ref[...] for ref in side), scale)
+        start_ref[:, place] = decode(block[...], half)
+
+
+def first_kernel(count, half, scale, total, *refs):
+    side, block, tiles, parts = refs[:3], refs[3], refs[4 : 4 + count], refs[4 + count : -2]
     out_ref, tile_ref = refs[-2:]
     size = 2 * half
-    own_high, own_low, own_norms = own_side(own, half, scale)
-    for b, block in enumerate(blocks[count - counts[-1] :]):
-        tile_ref[pl.ds(b * size, size), :] = kernel_rows(block[:half], own_high, own_low, own_norms, scale)
-    starts = [block[half:].astype(F32) * (1.0 / FIXED) for block in blocks]
-    sums = starts[0]
-    for start in starts[1:]:
-        sums = sums + start
+    tile_ref[...] = kernel_rows(block[:half], *(ref[...] for ref in side), scale)
+    starts = [part[...] for part in parts] + [decode(block[...], half)]
+    pieces = [start[:, b : b + size] for start in starts for b in range(0, start.shape[1], size)]
+    sums = pieces[0]
+    for piece in pieces[1:]:
+        sums = sums + piece
     mean = jnp.sum(sums, axis=1, keepdims=True) / total
-    rounded = [(start - mean).astype(BF16) for start in starts]
     images = None
-    for tile in (*parts, tile_ref):
-        group, rounded = rounded[: tile.shape[0] // size], rounded[tile.shape[0] // size :]
-        term = matmul(jnp.concatenate(group, axis=1), tile[...], (1, 0))
+    for start, tile in zip(starts, (*tiles, tile_ref)):
+        term = matmul((start - mean).astype(BF16), tile[...], (1, 0))
         images = term if images is None else images + term
     out_ref[...] = images
 
@@ -230,6 +261,7 @@
     count = 16
     total = float(size * count)
     scale = UNIT * UNIT / (2.0 * corpus.shape[1])
+    levels = call(encode, [initial], jax.ShapeDtypeStruct((vecs // 2 + 8, size), jnp.int32))
     landmarks = lax.gather(
         corpus,
         sample_rows[:, None],
@@ -237,30 +269,35 @@
         (1, corpus.shape[1]),
         mode="promise_in_bounds",
     )
-    own = encode(landmarks, initial)
+    code = jnp.round(landmarks * (1.0 / UNIT)).astype(jnp.int32)
+    own = jnp.concatenate([pair(code[:half], code[half:]), levels], axis=0)
 
     def build(*blocks):
-        shape = jax.ShapeDtypeStruct((len(blocks) * size, 2 * size), BF16)
-        return call(functools.partial(build_kernel, half, scale), [own, outer, *blocks], shape)
+        shapes = jax.ShapeDtypeStruct((len(blocks) * size, 2 * size), BF16), jax.ShapeDtypeStruct((vecs, len(blocks) * size), F32)
+        tile, start = call(functools.partial(build_kernel, half, scale), [*side, *blocks], shapes)
+        tiles.append(tile)
+        starts.append(start)
 
     outer, partner, chip = NEAR(own), middle(own), CHIP(own)
+    tiles, starts = [], []
     groups = [[own, outer, CORE(own), CORE(outer)]]
-    tiles = [build(*groups[0])]
+    codes = jax.ShapeDtypeStruct((2 * size, corpus.shape[1]), BF16)
+    side = call(functools.partial(side_kernel, half, scale), [own, outer], (codes, codes, jax.ShapeDtypeStruct((1, 2 * size), F32)))
+    build(*groups[0])
     partner_outer, chip_outer, chip_partner = middle(outer), NEAR(chip), CHIP(partner)
     groups.append([partner, CORE(partner), chip, CORE(chip)])
-    tiles.append(build(*groups[1]))
+    build(*groups[1])
     chip_partner_outer = CHIP(after(partner_outer, tiles[0]))
     groups.append([partner_outer, CORE(partner_outer), chip_outer, CORE(chip_outer)])
-    tiles.append(build(*groups[2]))
+    build(*groups[2])
     groups.append([chip_partner, CORE(chip_partner)])
-    tiles.append(build(*groups[3]))
+    build(*groups[3])
     final = CORE(after(chip_partner_outer, *tiles[1:4]))
     groups.append([chip_partner_outer])
-    tiles.append(build(*groups[4]))
-    groups.append([final])
+    build(*groups[4])
     images, tile = call(
-        functools.partial(first_kernel, [len(group) for group in groups], half, scale, total),
-        [own, outer] + [block for group in groups for block in group] + tiles,
+        functools.partial(first_kernel, len(tiles), half, scale, total),
+        [*side, final, *tiles, *starts],
         (jax.ShapeDtypeStruct((vecs, 2 * size), F32), jax.ShapeDtypeStruct((size, 2 * size), BF16)),
     )
     tiles.append(tile)

time: 68.6 us -> 66.6 us (0.971)
  Pallas kernels: 18.3 us -> 15.8 us
    pallas_call x10 -> x12, Pallas kernels: 18.3 us -> 15.8 us  [call(): pl.pallas_call(kernel, out_shape=out_shape, in_specs=in_specs or [VMEM] *...]
  transfers between devices with their start and end apart: 28 -> 28, of which waited for: 11 -> 11; matrix products, arithmetic and copies ran while one was open for 0% -> 0% of each run, Pallas kernels for 13% -> 10%
where the time goes in v5:
time: 66.6 us; the launch traced here: 66.4 us
  starting transfers between devices  28.9 us (43%)
  waiting for transfers between devices  18.8 us (28%)
  Pallas kernels  15.8 us (24%)
  local copies, waits for them, and re-layouts  1.74 us (3%)
  other arithmetic  0.89 us (1%)
    ppermute x24, starting transfers between devices, exchange(): lax.ppermute(value, axis, [(i, i ^ offset) for i in range(size)])  26.1 us
    ppermute x24, waiting for transfers between devices, exchange(): lax.ppermute(value, axis, [(i, i ^ offset) for i in range(size)])  18.8 us
    pallas_call x12, Pallas kernels, call(): pl.pallas_call(kernel, out_shape=out_shape, in_specs=in_specs or [VMEM] *...  15.8 us
    ppermute x3, starting transfers between devices, middle(): return lax.ppermute(value, 'col', MIDDLE)  1.99 us
  transfers between devices with their start and end apart: 28, of which 11 were waited for; matrix products, arithmetic and copies ran while one was open for 0% of the time, Pallas kernels for 10%

profile of v5, /device:TPU:0, one launch (start us, length us, event | category | flops | bytes accessed | tf_op | source)
XLA Modules:
  0.0 66.4 jit_solution(12207489910846827094)
XLA Ops:
  0.0 0.8 %pad_clamp_fusion = s32[1024]{0:T(1024)S(1)} fusion(s32[256]{0:T(256)} %param.4), kind=kLoop, calls=%fused_computation.6 | loop fusion | flops 1024 | bytes 5120 | tf_op jit(solution)/shard_map/gather | solution.py:265
  0.8 0.8 %copy-done = f32[2048,256]{1,0:T(8,128)S(1)} copy-done((f32[2048,256]{1,0:T(8,128)S(1)}, f32[2048,256]{1,0:T(8,128)}, u32[]{:S(2)}) %copy-start) | copy-done | bytes 2097176
  1.6 1.0 %gather_fusion = f32[256,256]{1,0:T(8,128)S(1)} fusion(f32[2048,256]{1,0:T(8,128)S(1)} %copy-done, s32[1024]{0:T(1024)S(1)} %pad_clamp_fusion), kind=kCustom, calls=%fused_computation | custom fusion | bytes 525312 | tf_op jit(solution)/shard_map/gather | solution.py:265
  2.6 0.2 shard_map.37
  2.9 3.1 %collective-permute-start = (s32[168,256]{1,0:T(8,128)S(1)}, s32[168,256]{1,0:T(8,128)S(1)}, u32[]{:S(2)}, u32[]{:S(2)}) collective-permute-start(s32[168,256]{1,0:T(8,128)S(1)} %pad_add_fusion.own_ref.refs_3_), channel_id=1, source_target_pairs={{0,1},{1,0},{2,3},{3,2},{4,5},{5,4},{6,7},{7,6},{8,9},{9,8},{10,11... | collective-permute-start | bytes 516104 | tf_op jit(solution)/shard_map/ppermute | solution.py:240
  5.9 0.7 collective-permute-start.5
  6.6 1.6 %collective-permute-start.7 = (s32[168,256]{1,0:T(8,128)S(1)}, s32[168,256]{1,0:T(8,128)S(1)}, u32[]{:S(2)}, u32[]{:S(2)}) collective-permute-start(s32[168,256]{1,0:T(8,128)S(1)} %pad_add_fusion.own_ref.refs_3_), channel_id=1, source_target_pairs={{0,8},{4,12},{8,0},{12,4},{1,9},{5,13},{9,1},{13,5},{2,10},{6,14},... | collective-permute-start | bytes 516104 | tf_op jit(solution)/shard_map/ppermute | solution.py:240
  8.2 0.0 collective-permute-start.2
  8.2 2.1 %collective-permute-done.outer_ref.refs_4_ = s32[168,256]{1,0:T(8,128)S(1)} collective-permute-done((s32[168,256]{1,0:T(8,128)S(1)}, s32[168,256]{1,0:T(8,128)S(1)}, u32[]{:S(2)}, u32[]{:S(2)}) %collective-permute-start) | collective-permute-done | bytes 172064 | tf_op jit(solution)/shard_map/ppermute | solution.py:240
  10.3 0.0 collective-permute-start.3
  10.3 0.7 collective-permute-start.1
  11.0 0.0 collective-permute-done.5.refs_3_
  11.0 1.7 %collective-permute-start.12 = (s32[168,256]{1,0:T(8,128)S(1)}, s32[168,256]{1,0:T(8,128)S(1)}, u32[]{:S(2)}, u32[]{:S(2)}) collective-permute-start(s32[168,256]{1,0:T(8,128)S(1)} %collective-permute-done.5.refs_3_), channel_id=1, source_target_pairs={{0,8},{4,12},{8,0},{12,4},{1,9},{5,13},{9,1},{13,5},{2,10},{6,14},... | collective-permute-start | bytes 516104 | tf_op jit(solution)/shard_map/ppermute | solution.py:240
  12.7 0.0 collective-permute-done.7.refs_5_
  12.7 4.4 %collective-permute-start.10 = (s32[168,256]{1,0:T(8,128)S(1)}, s32[168,256]{1,0:T(8,128)S(1)}, u32[]{:S(2)}, u32[]{:S(2)}) collective-permute-start(s32[168,256]{1,0:T(8,128)S(1)} %collective-permute-done.7.refs_5_), channel_id=1, source_target_pairs={{0,1},{1,0},{2,3},{3,2},{4,5},{5,4},{6,7},{7,6},{8,9},{9,8},{10,11... | collective-permute-start | bytes 516104 | tf_op jit(solution)/shard_map/ppermute | solution.py:240
  17.1 0.0 collective-permute-done.2.refs_5_
  17.1 0.0 collective-permute-start.6
  17.1 0.7 %shard_map.38 = (bf16[512,256]{1,0:T(8,128)(2,1)S(1)}, bf16[512,256]{1,0:T(8,128)(2,1)S(1)}, f32[1,512]{1,0:T(1,128)S(1)}) custom-call(s32[168,256]{1,0:T(8,128)S(1)} %pad_add_fusion.own_ref.refs_3_, s32[168,256]{1,0:T(8,128)S(1)} %collective-permute-done.outer_ref.refs_4_), custom_call_target="tpu_custom_call" | custom-call | tf_op jit(solution)/shard_map/pallas_call | solution.py:226
  17.8 0.0 collective-permute-done.3.refs_6_
  17.9 0.6 collective-permute-start.8
  18.4 1.5 %shard_map.39 = (bf16[1024,512]{1,0:T(8,128)(2,1)S(1)}, f32[64,1024]{1,0:T(8,128)S(1)}) custom-call(bf16[512,256]{1,0:T(8,128)(2,1)S(1)} %get-tuple-element.25.refs_0_, bf16[512,256]{1,0:T(8,128)(2,1)S(1)} %get-tuple-element.26.refs_1_, f32[1,512]{1,0:T(1,128)S(1)} %get-tuple-element.27.refs_2_, s32[168,256]{1,0:T(8,128)S(1)} %pad_add_fusion.own_ref.refs_3_, ...), custom_call_target="tpu_custom_call" | custom-call | tf_op jit(solution)/shard_map/pallas_call | solution.py:226
  20.0 0.0 collective-permute-done.1.refs_3_
  20.0 0.1 collective-permute-start.9
  20.1 0.0 collective-permute-done.12.refs_3_
  20.1 0.5 collective-permute-start.13
  20.6 1.0 %collective-permute-done.10.refs_5_ = s32[168,256]{1,0:T(8,128)S(1)} collective-permute-done((s32[168,256]{1,0:T(8,128)S(1)}, s32[168,256]{1,0:T(8,128)S(1)}, u32[]{:S(2)}, u32[]{:S(2)}) %collective-permute-start.10) | collective-permute-done | bytes 172064 | tf_op jit(solution)/shard_map/ppermute | solution.py:240
  21.6 0.0 collective-permute-start.11
  21.6 0.0 collective-permute-done.6.refs_4_
  21.6 0.5 collective-permute-start.4
  22.1 0.0 collective-permute-done.8.refs_6_
  22.2 1.5 %shard_map.40 = (bf16[1024,512]{1,0:T(8,128)(2,1)S(1)}, f32[64,1024]{1,0:T(8,128)S(1)}) custom-call(bf16[512,256]{1,0:T(8,128)(2,1)S(1)} %get-tuple-element.25.refs_0_, bf16[512,256]{1,0:T(8,128)(2,1)S(1)} %get-tuple-element.26.refs_1_, f32[1,512]{1,0:T(1,128)S(1)} %get-tuple-element.27.refs_2_, s32[168,256]{1,0:T(8,128)S(1)} %collective-permute-done.5.refs_3_, ...), custom_call_target="tpu_custom_call" | custom-call | tf_op jit(solution)/shard_map/pallas_call | solution.py:226
  23.7 0.8 %shard_map.42 = (bf16[512,512]{1,0:T(8,128)(2,1)S(1)}, f32[64,512]{1,0:T(8,128)S(1)}) custom-call(bf16[512,256]{1,0:T(8,128)(2,1)S(1)} %get-tuple-element.25.refs_0_, bf16[512,256]{1,0:T(8,128)(2,1)S(1)} %get-tuple-element.26.refs_1_, f32[1,512]{1,0:T(1,128)S(1)} %get-tuple-element.27.refs_2_, s32[168,256]{1,0:T(8,128)S(1)} %collective-permute-done.12.refs_3_, ...), custom_call_target="tpu_custom_call" | custom-call | tf_op jit(solution)/shard_map/pallas_call | solution.py:226
  24.5 0.0 collective-permute-done.9.refs_4_
  24.5 0.0 collective-permute-done.11.refs_6_
  24.5 1.5 %shard_map.41 = (bf16[1024,512]{1,0:T(8,128)(2,1)S(1)}, f32[64,1024]{1,0:T(8,128)S(1)}) custom-call(bf16[512,256]{1,0:T(8,128)(2,1)S(1)} %get-tuple-element.25.refs_0_, bf16[512,256]{1,0:T(8,128)(2,1)S(1)} %get-tuple-element.26.refs_1_, f32[1,512]{1,0:T(1,128)S(1)} %get-tuple-element.27.refs_2_, s32[168,256]{1,0:T(8,128)S(1)} %collective-permute-done.1.refs_3_, ...), custom_call_target="tpu_custom_call" | custom-call | tf_op jit(solution)/shard_map/pallas_call | solution.py:226
  26.1 2.3 %collective-permute-done.4.refs_3_ = s32[168,256]{1,0:T(8,128)S(1)} collective-permute-done((s32[168,256]{1,0:T(8,128)S(1)}, s32[168,256]{1,0:T(8,128)S(1)}, u32[]{:S(2)}, u32[]{:S(2)}) %collective-permute-start.4) | collective-permute-done | bytes 172064 | tf_op jit(solution)/shard_map/ppermute | solution.py:240
  28.4 0.0 collective-permute-start.14
  28.4 0.5 shard_map.43
  28.9 0.9 %collective-permute-done.14.refs_3_ = s32[168,256]{1,0:T(8,128)S(1)} collective-permute-done((s32[168,256]{1,0:T(8,128)S(1)}, s32[168,256]{1,0:T(8,128)S(1)}, u32[]{:S(2)}, u32[]{:S(2)}) %collective-permute-start.14) | collective-permute-done | bytes 172064 | tf_op jit(solution)/shard_map/ppermute | solution.py:240
  29.8 1.3 %shard_map.44 = (f32[64,512]{1,0:T(8,128)S(1)}, bf16[256,512]{1,0:T(8,128)(2,1)S(1)}) custom-call(bf16[512,256]{1,0:T(8,128)(2,1)S(1)} %get-tuple-element.25.refs_0_, bf16[512,256]{1,0:T(8,128)(2,1)S(1)} %get-tuple-element.26.refs_1_, f32[1,512]{1,0:T(1,128)S(1)} %get-tuple-element.27.refs_2_, s32[168,256]{1,0:T(8,128)S(1)} %collective-permute-done.14.refs_3_, ...), custom_call_target="tpu_custom_call" | custom-call | tf_op jit(solution)/shard_map/pallas_call | solution.py:226
  31.1 0.7 %collective-permute-start.15 = (f32[64,512]{1,0:T(8,128)S(1)}, f32[64,512]{1,0:T(8,128)S(1)}, u32[]{:S(2)}, u32[]{:S(2)}) collective-permute-start(f32[64,512]{1,0:T(8,128)S(1)} %get-tuple-element.40.refs_0_), channel_id=1, source_target_pairs={{1,2},{2,1},{5,6},{6,5},{9,10},{10,9},{13,14},{14,13},{17,18},{18,... | collective-permute-start | bytes 393224 | tf_op jit(solution)/shard_map/ppermute | solution.py:248
  31.7 0.6 collective-permute-start.16
  32.3 0.8 %collective-permute-start.17 = (f32[64,512]{1,0:T(8,128)S(1)}, f32[64,512]{1,0:T(8,128)S(1)}, u32[]{:S(2)}, u32[]{:S(2)}) collective-permute-start(f32[64,512]{1,0:T(8,128)S(1)} %get-tuple-element.40.refs_0_), channel_id=1, source_target_pairs={{1,10},{2,9},{5,14},{6,13},{9,2},{10,1},{13,6},{14,5},{17,26},{18,... | collective-permute-start | bytes 393224 | tf_op jit(solution)/shard_map/ppermute | solution.py:252
  33.2 0.1 collective-permute-start.18
  33.3 0.5 collective-permute-start.19
  33.8 3.6 %collective-permute-done.16.refs_2_ = f32[64,512]{1,0:T(8,128)S(1)} collective-permute-done((f32[64,512]{1,0:T(8,128)S(1)}, f32[64,512]{1,0:T(8,128)S(1)}, u32[]{:S(2)}, u32[]{:S(2)}) %collective-permute-start.16) | collective-permute-done | bytes 131104 | tf_op jit(solution)/shard_map/ppermute | solution.py:240
  37.3 0.0 collective-permute-start.20
  37.3 0.0 collective-permute-done.17.refs_3_
  37.4 0.5 collective-permute-start.21
  37.9 0.8 %collective-permute-done.20.refs_6_ = f32[64,512]{1,0:T(8,128)S(1)} collective-permute-done((f32[64,512]{1,0:T(8,128)S(1)}, f32[64,512]{1,0:T(8,128)S(1)}, u32[]{:S(2)}, u32[]{:S(2)}) %collective-permute-start.20) | collective-permute-done | bytes 131104 | tf_op jit(solution)/shard_map/ppermute | solution.py:240
  38.7 0.2 collective-permute-done.21.refs_7_
  38.9 5.1 %shard_map.45 = (f32[64,256]{1,0:T(8,128)S(1)}, f32[64,256]{1,0:T(8,128)S(1)}, f32[40,128]{1,0:T(8,128)S(1)}) custom-call(f32[64,512]{1,0:T(8,128)S(1)} %get-tuple-element.40.refs_0_, f32[64,512]{1,0:T(8,128)S(1)} %collective-permute-done.15.refs_1_, f32[64,512]{1,0:T(8,128)S(1)} %collective-permute-done.16.refs_2_, ...), custom_call_target="tpu_custom_call" | custom-call | tf_op jit(solution)/shard_map/pallas_call | solution.py:226
  44.0 6.6 %collective-permute-start.27 = (f32[64,256]{1,0:T(8,128)S(1)}, f32[64,256]{1,0:T(8,128)S(1)}, u32[]{:S(2)}, u32[]{:S(2)}) collective-permute-start(f32[64,256]{1,0:T(8,128)S(1)} %get-tuple-element.44), channel_id=1, source_target_pairs={{0,1},{1,0},{2,3},{3,2},{4,5},{5,4},{6,7},{7,6},{8,9},{9,8},{10,11... | collective-permute-start | bytes 196616 | tf_op jit(solution)/shard_map/ppermute | solution.py:240
  50.5 1.2 %collective-permute-done.22.b_ref = f32[40,128]{1,0:T(8,128)S(1)} collective-permute-done((f32[40,128]{1,0:T(8,128)S(1)}, f32[40,128]{1,0:T(8,128)S(1)}, u32[]{:S(2)}, u32[]{:S(2)}) %collective-permute-start.22) | collective-permute-done | bytes 20512 | tf_op jit(solution)/shard_map/ppermute | solution.py:240
  51.7 0.1 shard_map.46.a_ref
  51.8 1.0 %collective-permute-start.23 = (f32[40,128]{1,0:T(8,128)S(1)}, f32[40,128]{1,0:T(8,128)S(1)}, u32[]{:S(2)}, u32[]{:S(2)}) collective-permute-start(f32[40,128]{1,0:T(8,128)S(1)} %shard_map.46.a_ref), channel_id=1, source_target_pairs={{0,8},{4,12},{8,0},{12,4},{1,9},{5,13},{9,1},{13,5},{2,10},{6,14},... | collective-permute-start | bytes 61448 | tf_op jit(solution)/shard_map/ppermute | solution.py:240
  52.8 2.8 %collective-permute-done.23.b_ref = f32[40,128]{1,0:T(8,128)S(1)} collective-permute-done((f32[40,128]{1,0:T(8,128)S(1)}, f32[40,128]{1,0:T(8,128)S(1)}, u32[]{:S(2)}, u32[]{:S(2)}) %collective-permute-start.23) | collective-permute-done | bytes 20512 | tf_op jit(solution)/shard_map/ppermute | solution.py:240
  55.6 0.1 shard_map.47.share_ref
  55.7 0.1 collective-permute-start.24
  55.7 2.5 %collective-permute-start.25 = (f32[40,128]{1,0:T(8,128)S(1)}, f32[40,128]{1,0:T(8,128)S(1)}, u32[]{:S(2)}, u32[]{:S(2)}) collective-permute-start(f32[40,128]{1,0:T(8,128)S(1)} %shard_map.47.share_ref), channel_id=1, source_target_pairs={{0,2},{1,3},{2,0},{3,1},{4,6},{5,7},{6,4},{7,5},{8,10},{9,11},{10,... | collective-permute-start | bytes 61448 | tf_op jit(solution)/shard_map/ppermute | solution.py:240
  58.2 1.8 %collective-permute-start.26 = (f32[40,128]{1,0:T(8,128)S(1)}, f32[40,128]{1,0:T(8,128)S(1)}, u32[]{:S(2)}, u32[]{:S(2)}) collective-permute-start(f32[40,128]{1,0:T(8,128)S(1)} %shard_map.47.share_ref), channel_id=1, source_target_pairs={{0,3},{1,2},{2,1},{3,0},{4,7},{5,6},{6,5},{7,4},{8,11},{9,10},{10,... | collective-permute-start | bytes 61448 | tf_op jit(solution)/shard_map/ppermute | solution.py:240
  60.1 0.4 collective-permute-done.25.far_ref
  60.4 3.4 %collective-permute-done.26.across_ref = f32[40,128]{1,0:T(8,128)S(1)} collective-permute-done((f32[40,128]{1,0:T(8,128)S(1)}, f32[40,128]{1,0:T(8,128)S(1)}, u32[]{:S(2)}, u32[]{:S(2)}) %collective-permute-start.26) | collective-permute-done | bytes 20512 | tf_op jit(solution)/shard_map/ppermute | solution.py:240
  63.8 2.6 %shard_map.48 = f32[64,256]{1,0:T(8,128)} custom-call(s32[1]{0:T(128)} %bitcast.outer_ref, f32[40,128]{1,0:T(8,128)S(1)} %shard_map.47.share_ref, f32[40,128]{1,0:T(8,128)S(1)} %collective-permute-done.24.near_ref, f32[40,128]{1,0:T(8,128)S(1)} %collective-permute-done.25.far_ref, f32[40,128]{1,0:T(8,128)S(1)} %collective-permute-done.26.across_ref, ...), custom_call_target="tpu_custom_call" | custom-call | tf_op jit(solution)/shard_map/pallas_call | solution.py:226
  (13 shorter events, 0.1 us)
Async XLA Ops:
  0.0 1.6 %copy-start = (f32[2048,256]{1,0:T(8,128)S(1)}, f32[2048,256]{1,0:T(8,128)}, u32[]{:S(2)}) copy-start(f32[2048,256]{1,0:T(8,128)} %param.3) | copy-start | bytes 6291460
  0.0 2.6 %copy-start.1 = (f32[64,256]{1,0:T(8,128)S(1)}, f32[64,256]{1,0:T(8,128)}, u32[]{:S(2)}) copy-start(f32[64,256]{1,0:T(8,128)} %initial_ref.1) | copy-start | bytes 196612
  2.9 7.5 %collective-permute-start = (s32[168,256]{1,0:T(8,128)S(1)}, s32[168,256]{1,0:T(8,128)S(1)}, u32[]{:S(2)}, u32[]{:S(2)}) collective-permute-start(s32[168,256]{1,0:T(8,128)S(1)} %pad_add_fusion.own_ref.refs_3_), channel_id=1, source_target_pairs={{0,1},{1,0},{2,3},{3,2},{4,5},{5,4},{6,7},{7,6},{8,9},{9,8},{10,11... | collective-permute-start | bytes 516104 | tf_op jit(solution)/shard_map/ppermute | solution.py:240
  5.9 5.0 %collective-permute-start.5 = (s32[168,256]{1,0:T(8,128)S(1)}, s32[168,256]{1,0:T(8,128)S(1)}, u32[]{:S(2)}, u32[]{:S(2)}) collective-permute-start(s32[168,256]{1,0:T(8,128)S(1)} %pad_add_fusion.own_ref.refs_3_), channel_id=1, source_target_pairs={{1,2},{2,1},{5,6},{6,5},{9,10},{10,9},{13,14},{14,13},{17,18},{18,... | collective-permute-start | bytes 516104 | tf_op jit(solution)/shard_map/ppermute | solution.py:248
  6.6 6.1 %collective-permute-start.7 = (s32[168,256]{1,0:T(8,128)S(1)}, s32[168,256]{1,0:T(8,128)S(1)}, u32[]{:S(2)}, u32[]{:S(2)}) collective-permute-start(s32[168,256]{1,0:T(8,128)S(1)} %pad_add_fusion.own_ref.refs_3_), channel_id=1, source_target_pairs={{0,8},{4,12},{8,0},{12,4},{1,9},{5,13},{9,1},{13,5},{2,10},{6,14},... | collective-permute-start | bytes 516104 | tf_op jit(solution)/shard_map/ppermute | solution.py:240
  8.2 8.9 %collective-permute-start.2 = (s32[168,256]{1,0:T(8,128)S(1)}, s32[168,256]{1,0:T(8,128)S(1)}, u32[]{:S(2)}, u32[]{:S(2)}) collective-permute-start(s32[168,256]{1,0:T(8,128)S(1)} %pad_add_fusion.own_ref.refs_3_), channel_id=1, source_target_pairs={{0,4},{4,0},{8,12},{12,8},{1,5},{5,1},{9,13},{13,9},{2,6},{6,2},{1... | collective-permute-start | bytes 516104 | tf_op jit(solution)/shard_map/ppermute | solution.py:240
  10.3 7.5 %collective-permute-start.3 = (s32[168,256]{1,0:T(8,128)S(1)}, s32[168,256]{1,0:T(8,128)S(1)}, u32[]{:S(2)}, u32[]{:S(2)}) collective-permute-start(s32[168,256]{1,0:T(8,128)S(1)} %collective-permute-done.outer_ref.refs_4_), channel_id=1, source_target_pairs={{0,4},{4,0},{8,12},{12,8},{1,5},{5,1},{9,13},{13,9},{2,6},{6,2},{1... | collective-permute-start | bytes 516104 | tf_op jit(solution)/shard_map/ppermute | solution.py:240
  10.3 9.6 %collective-permute-start.1 = (s32[168,256]{1,0:T(8,128)S(1)}, s32[168,256]{1,0:T(8,128)S(1)}, u32[]{:S(2)}, u32[]{:S(2)}) collective-permute-start(s32[168,256]{1,0:T(8,128)S(1)} %collective-permute-done.outer_ref.refs_4_), channel_id=1, source_target_pairs={{1,2},{2,1},{5,6},{6,5},{9,10},{10,9},{13,14},{14,13},{17,18},{18,... | collective-permute-start | bytes 516104 | tf_op jit(solution)/shard_map/ppermute | solution.py:248
  11.0 9.1 %collective-permute-start.12 = (s32[168,256]{1,0:T(8,128)S(1)}, s32[168,256]{1,0:T(8,128)S(1)}, u32[]{:S(2)}, u32[]{:S(2)}) collective-permute-start(s32[168,256]{1,0:T(8,128)S(1)} %collective-permute-done.5.refs_3_), channel_id=1, source_target_pairs={{0,8},{4,12},{8,0},{12,4},{1,9},{5,13},{9,1},{13,5},{2,10},{6,14},... | collective-permute-start | bytes 516104 | tf_op jit(solution)/shard_map/ppermute | solution.py:240
  12.7 8.9 %collective-permute-start.10 = (s32[168,256]{1,0:T(8,128)S(1)}, s32[168,256]{1,0:T(8,128)S(1)}, u32[]{:S(2)}, u32[]{:S(2)}) collective-permute-start(s32[168,256]{1,0:T(8,128)S(1)} %collective-permute-done.7.refs_5_), channel_id=1, source_target_pairs={{0,1},{1,0},{2,3},{3,2},{4,5},{5,4},{6,7},{7,6},{8,9},{9,8},{10,11... | collective-permute-start | bytes 516104 | tf_op jit(solution)/shard_map/ppermute | solution.py:240
  17.1 4.5 %collective-permute-start.6 = (s32[168,256]{1,0:T(8,128)S(1)}, s32[168,256]{1,0:T(8,128)S(1)}, u32[]{:S(2)}, u32[]{:S(2)}) collective-permute-start(s32[168,256]{1,0:T(8,128)S(1)} %collective-permute-done.5.refs_3_), channel_id=1, source_target_pairs={{0,4},{4,0},{8,12},{12,8},{1,5},{5,1},{9,13},{13,9},{2,6},{6,2},{1... | collective-permute-start | bytes 516104 | tf_op jit(solution)/shard_map/ppermute | solution.py:240
  17.9 4.3 %collective-permute-start.8 = (s32[168,256]{1,0:T(8,128)S(1)}, s32[168,256]{1,0:T(8,128)S(1)}, u32[]{:S(2)}, u32[]{:S(2)}) collective-permute-start(s32[168,256]{1,0:T(8,128)S(1)} %collective-permute-done.7.refs_5_), channel_id=1, source_target_pairs={{0,4},{4,0},{8,12},{12,8},{1,5},{5,1},{9,13},{13,9},{2,6},{6,2},{1... | collective-permute-start | bytes 516104 | tf_op jit(solution)/shard_map/ppermute | solution.py:240
  20.0 4.5 %collective-permute-start.9 = (s32[168,256]{1,0:T(8,128)S(1)}, s32[168,256]{1,0:T(8,128)S(1)}, u32[]{:S(2)}, u32[]{:S(2)}) collective-permute-start(s32[168,256]{1,0:T(8,128)S(1)} %collective-permute-done.1.refs_3_), channel_id=1, source_target_pairs={{0,4},{4,0},{8,12},{12,8},{1,5},{5,1},{9,13},{13,9},{2,6},{6,2},{1... | collective-permute-start | bytes 516104 | tf_op jit(solution)/shard_map/ppermute | solution.py:240
  20.1 3.6 %collective-permute-start.13 = (s32[168,256]{1,0:T(8,128)S(1)}, s32[168,256]{1,0:T(8,128)S(1)}, u32[]{:S(2)}, u32[]{:S(2)}) collective-permute-start(s32[168,256]{1,0:T(8,128)S(1)} %collective-permute-done.12.refs_3_), channel_id=1, source_target_pairs={{0,4},{4,0},{8,12},{12,8},{1,5},{5,1},{9,13},{13,9},{2,6},{6,2},{1... | collective-permute-start | bytes 516104 | tf_op jit(solution)/shard_map/ppermute | solution.py:240
  21.6 2.9 %collective-permute-start.11 = (s32[168,256]{1,0:T(8,128)S(1)}, s32[168,256]{1,0:T(8,128)S(1)}, u32[]{:S(2)}, u32[]{:S(2)}) collective-permute-start(s32[168,256]{1,0:T(8,128)S(1)} %collective-permute-done.10.refs_5_), channel_id=1, source_target_pairs={{0,4},{4,0},{8,12},{12,8},{1,5},{5,1},{9,13},{13,9},{2,6},{6,2},{1... | collective-permute-start | bytes 516104 | tf_op jit(solution)/shard_map/ppermute | solution.py:240
  21.6 6.8 %collective-permute-start.4 = (s32[168,256]{1,0:T(8,128)S(1)}, s32[168,256]{1,0:T(8,128)S(1)}, u32[]{:S(2)}, u32[]{:S(2)}) collective-permute-start(s32[168,256]{1,0:T(8,128)S(1)} %collective-permute-done.1.refs_3_), channel_id=1, source_target_pairs={{0,8},{4,12},{8,0},{12,4},{1,9},{5,13},{9,1},{13,5},{2,10},{6,14},... | collective-permute-start | bytes 516104 | tf_op jit(solution)/shard_map/ppermute | solution.py:240
  28.4 1.4 %collective-permute-start.14 = (s32[168,256]{1,0:T(8,128)S(1)}, s32[168,256]{1,0:T(8,128)S(1)}, u32[]{:S(2)}, u32[]{:S(2)}) collective-permute-start(s32[168,256]{1,0:T(8,128)S(1)} %collective-permute-done.4.refs_3_), channel_id=1, source_target_pairs={{0,4},{4,0},{8,12},{12,8},{1,5},{5,1},{9,13},{13,9},{2,6},{6,2},{1... | collective-permute-start | bytes 516104 | tf_op jit(solution)/shard_map/ppermute | solution.py:240
  31.1 2.2 %collective-permute-start.15 = (f32[64,512]{1,0:T(8,128)S(1)}, f32[64,512]{1,0:T(8,128)S(1)}, u32[]{:S(2)}, u32[]{:S(2)}) collective-permute-start(f32[64,512]{1,0:T(8,128)S(1)} %get-tuple-element.40.refs_0_), channel_id=1, source_target_pairs={{1,2},{2,1},{5,6},{6,5},{9,10},{10,9},{13,14},{14,13},{17,18},{18,... | collective-permute-start | bytes 393224 | tf_op jit(solution)/shard_map/ppermute | solution.py:248
  31.7 5.6 %collective-permute-start.16 = (f32[64,512]{1,0:T(8,128)S(1)}, f32[64,512]{1,0:T(8,128)S(1)}, u32[]{:S(2)}, u32[]{:S(2)}) collective-permute-start(f32[64,512]{1,0:T(8,128)S(1)} %get-tuple-element.40.refs_0_), channel_id=1, source_target_pairs={{0,8},{4,12},{8,0},{12,4},{1,9},{5,13},{9,1},{13,5},{2,10},{6,14},... | collective-permute-start | bytes 393224 | tf_op jit(solution)/shard_map/ppermute | solution.py:240
  32.3 5.0 %collective-permute-start.17 = (f32[64,512]{1,0:T(8,128)S(1)}, f32[64,512]{1,0:T(8,128)S(1)}, u32[]{:S(2)}, u32[]{:S(2)}) collective-permute-start(f32[64,512]{1,0:T(8,128)S(1)} %get-tuple-element.40.refs_0_), channel_id=1, source_target_pairs={{1,10},{2,9},{5,14},{6,13},{9,2},{10,1},{13,6},{14,5},{17,26},{18,... | collective-permute-start | bytes 393224 | tf_op jit(solution)/shard_map/ppermute | solution.py:252
  33.2 4.7 %collective-permute-start.18 = (f32[64,512]{1,0:T(8,128)S(1)}, f32[64,512]{1,0:T(8,128)S(1)}, u32[]{:S(2)}, u32[]{:S(2)}) collective-permute-start(f32[64,512]{1,0:T(8,128)S(1)} %get-tuple-element.40.refs_0_), channel_id=1, source_target_pairs={{0,4},{4,0},{8,12},{12,8},{1,5},{5,1},{9,13},{13,9},{2,6},{6,2},{1... | collective-permute-start | bytes 393224 | tf_op jit(solution)/shard_map/ppermute | solution.py:240
  33.3 4.6 %collective-permute-start.19 = (f32[64,512]{1,0:T(8,128)S(1)}, f32[64,512]{1,0:T(8,128)S(1)}, u32[]{:S(2)}, u32[]{:S(2)}) collective-permute-start(f32[64,512]{1,0:T(8,128)S(1)} %collective-permute-done.15.refs_1_), channel_id=1, source_target_pairs={{0,4},{4,0},{8,12},{12,8},{1,5},{5,1},{9,13},{13,9},{2,6},{6,2},{1... | collective-permute-start | bytes 393224 | tf_op jit(solution)/shard_map/ppermute | solution.py:240
  37.3 1.3 %collective-permute-start.20 = (f32[64,512]{1,0:T(8,128)S(1)}, f32[64,512]{1,0:T(8,128)S(1)}, u32[]{:S(2)}, u32[]{:S(2)}) collective-permute-start(f32[64,512]{1,0:T(8,128)S(1)} %collective-permute-done.16.refs_2_), channel_id=1, source_target_pairs={{0,4},{4,0},{8,12},{12,8},{1,5},{5,1},{9,13},{13,9},{2,6},{6,2},{1... | collective-permute-start | bytes 393224 | tf_op jit(solution)/shard_map/ppermute | solution.py:240
  37.4 1.5 %collective-permute-start.21 = (f32[64,512]{1,0:T(8,128)S(1)}, f32[64,512]{1,0:T(8,128)S(1)}, u32[]{:S(2)}, u32[]{:S(2)}) collective-permute-start(f32[64,512]{1,0:T(8,128)S(1)} %collective-permute-done.17.refs_3_), channel_id=1, source_target_pairs={{0,4},{4,0},{8,12},{12,8},{1,5},{5,1},{9,13},{13,9},{2,6},{6,2},{1... | collective-permute-start | bytes 393224 | tf_op jit(solution)/shard_map/ppermute | solution.py:240
  44.0 19.8 %collective-permute-start.27 = (f32[64,256]{1,0:T(8,128)S(1)}, f32[64,256]{1,0:T(8,128)S(1)}, u32[]{:S(2)}, u32[]{:S(2)}) collective-permute-start(f32[64,256]{1,0:T(8,128)S(1)} %get-tuple-element.44), channel_id=1, source_target_pairs={{0,1},{1,0},{2,3},{3,2},{4,5},{5,4},{6,7},{7,6},{8,9},{9,8},{10,11... | collective-permute-start | bytes 196616 | tf_op jit(solution)/shard_map/ppermute | solution.py:240
  50.5 1.2 %collective-permute-start.22 = (f32[40,128]{1,0:T(8,128)S(1)}, f32[40,128]{1,0:T(8,128)S(1)}, u32[]{:S(2)}, u32[]{:S(2)}) collective-permute-start(f32[40,128]{1,0:T(8,128)S(1)} %get-tuple-element.42.a_ref), channel_id=1, source_target_pairs={{0,4},{4,0},{8,12},{12,8},{1,5},{5,1},{9,13},{13,9},{2,6},{6,2},{1... | collective-permute-start | bytes 61448 | tf_op jit(solution)/shard_map/ppermute | solution.py:240
  51.8 3.8 %collective-permute-start.23 = (f32[40,128]{1,0:T(8,128)S(1)}, f32[40,128]{1,0:T(8,128)S(1)}, u32[]{:S(2)}, u32[]{:S(2)}) collective-permute-start(f32[40,128]{1,0:T(8,128)S(1)} %shard_map.46.a_ref), channel_id=1, source_target_pairs={{0,8},{4,12},{8,0},{12,4},{1,9},{5,13},{9,1},{13,5},{2,10},{6,14},... | collective-permute-start | bytes 61448 | tf_op jit(solution)/shard_map/ppermute | solution.py:240
  55.7 4.4 %collective-permute-start.24 = (f32[40,128]{1,0:T(8,128)S(1)}, f32[40,128]{1,0:T(8,128)S(1)}, u32[]{:S(2)}, u32[]{:S(2)}) collective-permute-start(f32[40,128]{1,0:T(8,128)S(1)} %shard_map.47.share_ref), channel_id=1, source_target_pairs={{0,1},{1,0},{2,3},{3,2},{4,5},{5,4},{6,7},{7,6},{8,9},{9,8},{10,11... | collective-permute-start | bytes 61448 | tf_op jit(solution)/shard_map/ppermute | solution.py:240
  55.7 4.7 %collective-permute-start.25 = (f32[40,128]{1,0:T(8,128)S(1)}, f32[40,128]{1,0:T(8,128)S(1)}, u32[]{:S(2)}, u32[]{:S(2)}) collective-permute-start(f32[40,128]{1,0:T(8,128)S(1)} %shard_map.47.share_ref), channel_id=1, source_target_pairs={{0,2},{1,3},{2,0},{3,1},{4,6},{5,7},{6,4},{7,5},{8,10},{9,11},{10,... | collective-permute-start | bytes 61448 | tf_op jit(solution)/shard_map/ppermute | solution.py:240
  58.2 5.6 %collective-permute-start.26 = (f32[40,128]{1,0:T(8,128)S(1)}, f32[40,128]{1,0:T(8,128)S(1)}, u32[]{:S(2)}, u32[]{:S(2)}) collective-permute-start(f32[40,128]{1,0:T(8,128)S(1)} %shard_map.47.share_ref), channel_id=1, source_target_pairs={{0,3},{1,2},{2,1},{3,0},{4,7},{5,6},{6,5},{7,4},{8,11},{9,10},{10,... | collective-permute-start | bytes 61448 | tf_op jit(solution)/shard_map/ppermute | solution.py:240

commit v6 on v5

--- a/solution.py
+++ b/solution.py
@@ -164,19 +164,44 @@
     return p[:n] + (p[n : 2 * n] + p[2 * n :])
 
 
-def second_kernel(pieces, total, *refs):
-    count = 1 + max(piece[0] for piece in pieces)
-    images, tiles = refs[:count], refs[count:-3]
+def partial_kernel(count, *refs):
+    shift_ref, images = refs[0], refs[1 : 1 + count]
+    stack_ref, gram_ref, sum_ref = refs[-3:]
+    value = jnp.concatenate([image[...] for image in images], axis=1) - shift_of(shift_ref)
+    stack = thirds(value)
+    stack_ref[...] = stack
+    gram_ref[...] = gram_of(stack)
+    sum_ref[...] = jnp.broadcast_to(jnp.sum(value, axis=1, keepdims=True), sum_ref.shape)
+
+
+def shift_of(ref):
+    return jnp.sum(ref[...], axis=1, keepdims=True) * (1.0 / ref.shape[1])
+
+
+def second_kernel(parts, pieces, total, *refs):
+    shift_ref, images = refs[0], refs[1:3]
+    stacks, grams, sums = (refs[3 + i * parts : 3 + (i + 1) * parts] for i in range(3))
+    tiles = refs[3 + 3 * parts : -3]
     own_ref, other_ref, share_ref = refs[-3:]
     size = own_ref.shape[1]
-    values = [images[i][:, b * size : (b + 1) * size] for i, b in pieces]
-    sums = values[0]
-    for value in values[1:]:
-        sums = sums + value
-    mean = jnp.sum(sums, axis=1, keepdims=True) / total
-    stack = thirds(jnp.concatenate([value - mean for value in values], axis=1))
-    solve = math.sqrt(total) * inverse_factor(gram_of(stack))
-    vectors = times(solve, stack).astype(BF16)
+    value = jnp.concatenate([image[...] for image in images], axis=1) - shift_of(shift_ref)
+    stack = thirds(value)
+    gram = gram_of(stack)
+    far = jnp.sum(value, axis=1, keepdims=True)
+    for part, sum_part in zip(grams, sums):
+        gram, far = gram + part[...], far + sum_part[:, :1]
+    far = far * (1.0 / total)
+    n = gram.shape[0]
+    eye = lax.broadcasted_iota(jnp.int32, (n, n), 0) == lax.broadcasted_iota(jnp.int32, (n, n), 1)
+    gram = gram - (total * far) * jnp.sum(jnp.where(eye, far, 0.0), axis=0, keepdims=True)
+    solve = math.sqrt(total) * inverse_factor(gram)
+    level = times(solve, thirds(jnp.broadcast_to(far, (n, 2 * n))))[:, :1]
+    vectors = []
+    for part in (*stacks, None):
+        whole = stack if part is None else part[...]
+        vectors.append((times(solve, whole) - level).astype(BF16))
+    vectors = jnp.concatenate(vectors, axis=1)
+    vectors = jnp.concatenate([vectors[:, p * size : (p + 1) * size] for p in pieces], axis=1)
     result, begin = None, 0
     for tile in tiles:
         end = begin + tile.shape[0]
@@ -186,9 +211,7 @@
     other_ref[...] = result[:, size:]
     local_mean = jnp.sum(result, axis=1, keepdims=True) / (2 * size)
     gram = gram_of(thirds(result - local_mean))
-    n = gram.shape[0]
     h = n // 2
-    eye = lax.broadcasted_iota(jnp.int32, (n, n), 0) == lax.broadcasted_iota(jnp.int32, (n, n), 1)
     across = jnp.sum(jnp.where(eye, local_mean, 0.0), axis=0, keepdims=True)
     share_ref[:h] = jnp.concatenate([gram[:h], gram[h:, h:], local_mean[:h], local_mean[h:], jnp.zeros((h, h - 2), F32)], axis=1)
     share_ref[h:] = jnp.broadcast_to(jnp.concatenate([across, across[:, h:], jnp.zeros((1, h), F32)], axis=1), (8, 4 * h))
@@ -288,29 +311,33 @@
     groups.append([partner, CORE(partner), chip, CORE(chip)])
     build(*groups[1])
     chip_partner_outer = CHIP(after(partner_outer, tiles[0]))
-    groups.append([partner_outer, CORE(partner_outer), chip_outer, CORE(chip_outer)])
-    build(*groups[2])
-    groups.append([chip_partner, CORE(chip_partner)])
-    build(*groups[3])
-    final = CORE(after(chip_partner_outer, *tiles[1:4]))
-    groups.append([chip_partner_outer])
-    build(*groups[4])
+    build(partner_outer, CORE(partner_outer))
+    build(chip_partner, CORE(chip_partner))
+    final = CORE(after(chip_partner_outer, *tiles[1:3]))
+    build(chip_outer, CORE(chip_outer))
+    build(chip_partner_outer)
     images, tile = call(
         functools.partial(first_kernel, len(tiles), half, scale, total),
         [*side, final, *tiles, *starts],
         (jax.ShapeDtypeStruct((vecs, 2 * size), F32), jax.ShapeDtypeStruct((size, 2 * size), BF16)),
     )
     tiles.append(tile)
-    there, beside = middle(images), CHIP(images)
-    beyond = diagonal(images)
-    gathered = [images, there, beside, beyond]
-    gathered += [CORE(value) for value in gathered]
-    here, part, chip, far = 0, 1, 2, 3
-    pieces = [(here, 0), (here, 1), (here + 4, 0), (here + 4, 1), (part, 0), (part + 4, 0), (chip, 0), (chip + 4, 0)]
-    pieces += [(part, 1), (part + 4, 1), (chip, 1), (chip + 4, 1), (far, 0), (far + 4, 0), (far, 1), (far + 4, 1)]
+    places = [images, middle(images), CHIP(images), diagonal(images)]
+    pairs = [[value, CORE(value)] for value in places]
     block = jax.ShapeDtypeStruct((vecs, size), F32)
+    parts = []
+    for group in ([0, 1, 2],):
+        values = [value for p in group for value in pairs[p]]
+        shapes = jax.ShapeDtypeStruct((3 * vecs, len(values) * 2 * size), BF16), jax.ShapeDtypeStruct((vecs, vecs), F32)
+        parts.append(call(functools.partial(partial_kernel, len(values)), [images, *values], (*shapes, jax.ShapeDtypeStruct((vecs, 128), F32))))
+    here, part, chip, far = (4 * p for p in range(4))
+    pieces = [here, here + 1, here + 2, here + 3, part, part + 2, chip, chip + 2]
+    pieces += [part + 1, part + 3, far, far + 2, chip + 1, chip + 3, far + 1, far + 3]
     packed = jax.ShapeDtypeStruct((vecs // 2 + 8, 2 * vecs), F32)
-    images, other, share = call(functools.partial(second_kernel, pieces, total), gathered + tiles, (block, block, packed))
+    known = [part[i] for i in range(3) for part in parts]
+    images, other, share = call(
+        functools.partial(second_kernel, len(parts), pieces, total), [images, *pairs[3], *known, *tiles], (block, block, packed)
+    )
     given = NEAR(other)
     for step, swap in enumerate((CORE, CHIP)):
         share = call(functools.partial(merge_kernel, 2.0 * size * 2**step), [share, swap(share)], packed)

time: 66.6 us -> 65.4 us (0.982)
  waiting for transfers between devices: 18.8 us -> 17.4 us
    ppermute x24, waiting for transfers between devices: 18.8 us -> 17.4 us  [exchange(): lax.ppermute(value, axis, [(i, i ^ offset) for i in range(size)])]
    pallas_call x12 -> x14, Pallas kernels: 15.8 us -> 16.1 us  [call(): pl.pallas_call(kernel, out_shape=out_shape, in_specs=in_specs or [VMEM] *...]
  transfers between devices with their start and end apart: 28 -> 28, of which waited for: 11 -> 11; matrix products, arithmetic and copies ran while one was open for 0% -> 0% of each run, Pallas kernels for 10% -> 12%
where the time goes in v6:
time: 65.4 us; the launch traced here: 65.2 us
  starting transfers between devices  28.9 us (44%)
  waiting for transfers between devices  17.4 us (27%)
  Pallas kernels  16.1 us (25%)
  local copies, waits for them, and re-layouts  1.74 us (3%)
  other arithmetic  0.89 us (1%)
    ppermute x24, starting transfers between devices, exchange(): lax.ppermute(value, axis, [(i, i ^ offset) for i in range(size)])  26 us
    ppermute x24, waiting for transfers between devices, exchange(): lax.ppermute(value, axis, [(i, i ^ offset) for i in range(size)])  17.4 us
    pallas_call x14, Pallas kernels, call(): pl.pallas_call(kernel, out_shape=out_shape, in_specs=in_specs or [VMEM] *...  16.1 us
    ppermute x3, starting transfers between devices, middle(): return lax.ppermute(value, 'col', MIDDLE)  1.99 us
  transfers between devices with their start and end apart: 28, of which 11 were waited for; matrix products, arithmetic and copies ran while one was open for 0% of the time, Pallas kernels for 12%

profile of v6, /device:TPU:0, one launch (start us, length us, event | category | flops | bytes accessed | tf_op | source)
XLA Modules:
  0.0 65.2 jit_solution(11836114967044801897)
XLA Ops:
  0.0 0.8 %pad_clamp_fusion = s32[1024]{0:T(1024)S(1)} fusion(s32[256]{0:T(256)} %param.4), kind=kLoop, calls=%fused_computation.6 | loop fusion | flops 1024 | bytes 5120 | tf_op jit(solution)/shard_map/gather | solution.py:288
  0.8 0.8 %copy-done = f32[2048,256]{1,0:T(8,128)S(1)} copy-done((f32[2048,256]{1,0:T(8,128)S(1)}, f32[2048,256]{1,0:T(8,128)}, u32[]{:S(2)}) %copy-start) | copy-done | bytes 2097176
  1.6 1.0 %gather_fusion = f32[256,256]{1,0:T(8,128)S(1)} fusion(f32[2048,256]{1,0:T(8,128)S(1)} %copy-done, s32[1024]{0:T(1024)S(1)} %pad_clamp_fusion), kind=kCustom, calls=%fused_computation | custom fusion | bytes 525312 | tf_op jit(solution)/shard_map/gather | solution.py:288
  2.6 0.2 shard_map.37
  2.9 3.1 %collective-permute-start = (s32[168,256]{1,0:T(8,128)S(1)}, s32[168,256]{1,0:T(8,128)S(1)}, u32[]{:S(2)}, u32[]{:S(2)}) collective-permute-start(s32[168,256]{1,0:T(8,128)S(1)} %pad_add_fusion.own_ref.refs_3_), channel_id=1, source_target_pairs={{0,1},{1,0},{2,3},{3,2},{4,5},{5,4},{6,7},{7,6},{8,9},{9,8},{10,11... | collective-permute-start | bytes 516104 | tf_op jit(solution)/shard_map/ppermute | solution.py:263
  5.9 0.7 %collective-permute-start.5 = (s32[168,256]{1,0:T(8,128)S(1)}, s32[168,256]{1,0:T(8,128)S(1)}, u32[]{:S(2)}, u32[]{:S(2)}) collective-permute-start(s32[168,256]{1,0:T(8,128)S(1)} %pad_add_fusion.own_ref.refs_3_), channel_id=1, source_target_pairs={{1,2},{2,1},{5,6},{6,5},{9,10},{10,9},{13,14},{14,13},{17,18},{18,... | collective-permute-start | bytes 516104 | tf_op jit(solution)/shard_map/ppermute | solution.py:271
  6.6 1.6 %collective-permute-start.7 = (s32[168,256]{1,0:T(8,128)S(1)}, s32[168,256]{1,0:T(8,128)S(1)}, u32[]{:S(2)}, u32[]{:S(2)}) collective-permute-start(s32[168,256]{1,0:T(8,128)S(1)} %pad_add_fusion.own_ref.refs_3_), channel_id=1, source_target_pairs={{0,8},{4,12},{8,0},{12,4},{1,9},{5,13},{9,1},{13,5},{2,10},{6,14},... | collective-permute-start | bytes 516104 | tf_op jit(solution)/shard_map/ppermute | solution.py:263
  8.2 0.0 collective-permute-start.2
  8.2 2.1 %collective-permute-done.outer_ref.refs_4_ = s32[168,256]{1,0:T(8,128)S(1)} collective-permute-done((s32[168,256]{1,0:T(8,128)S(1)}, s32[168,256]{1,0:T(8,128)S(1)}, u32[]{:S(2)}, u32[]{:S(2)}) %collective-permute-start) | collective-permute-done | bytes 172064 | tf_op jit(solution)/shard_map/ppermute | solution.py:263
  10.3 0.0 collective-permute-start.3
  10.3 0.7 %collective-permute-start.1 = (s32[168,256]{1,0:T(8,128)S(1)}, s32[168,256]{1,0:T(8,128)S(1)}, u32[]{:S(2)}, u32[]{:S(2)}) collective-permute-start(s32[168,256]{1,0:T(8,128)S(1)} %collective-permute-done.outer_ref.refs_4_), channel_id=1, source_target_pairs={{1,2},{2,1},{5,6},{6,5},{9,10},{10,9},{13,14},{14,13},{17,18},{18,... | collective-permute-start | bytes 516104 | tf_op jit(solution)/shard_map/ppermute | solution.py:271
  11.0 0.0 collective-permute-done.5.refs_3_
  11.0 0.6 collective-permute-start.6
  11.6 0.7 %shard_map.38 = (bf16[512,256]{1,0:T(8,128)(2,1)S(1)}, bf16[512,256]{1,0:T(8,128)(2,1)S(1)}, f32[1,512]{1,0:T(1,128)S(1)}) custom-call(s32[168,256]{1,0:T(8,128)S(1)} %pad_add_fusion.own_ref.refs_3_, s32[168,256]{1,0:T(8,128)S(1)} %collective-permute-done.outer_ref.refs_4_), custom_call_target="tpu_custom_call" | custom-call | tf_op jit(solution)/shard_map/pallas_call | solution.py:249
  12.3 0.2 collective-permute-done.7.refs_5_
  12.5 0.0 collective-permute-start.8
  12.5 0.0 collective-permute-done.2.refs_5_
  12.5 4.4 %collective-permute-start.13 = (s32[168,256]{1,0:T(8,128)S(1)}, s32[168,256]{1,0:T(8,128)S(1)}, u32[]{:S(2)}, u32[]{:S(2)}) collective-permute-start(s32[168,256]{1,0:T(8,128)S(1)} %collective-permute-done.7.refs_5_), channel_id=1, source_target_pairs={{0,1},{1,0},{2,3},{3,2},{4,5},{5,4},{6,7},{7,6},{8,9},{9,8},{10,11... | collective-permute-start | bytes 516104 | tf_op jit(solution)/shard_map/ppermute | solution.py:263
  17.0 0.0 collective-permute-done.3.refs_6_
  17.0 1.5 %collective-permute-start.11 = (s32[168,256]{1,0:T(8,128)S(1)}, s32[168,256]{1,0:T(8,128)S(1)}, u32[]{:S(2)}, u32[]{:S(2)}) collective-permute-start(s32[168,256]{1,0:T(8,128)S(1)} %collective-permute-done.5.refs_3_), channel_id=1, source_target_pairs={{0,8},{4,12},{8,0},{12,4},{1,9},{5,13},{9,1},{13,5},{2,10},{6,14},... | collective-permute-start | bytes 516104 | tf_op jit(solution)/shard_map/ppermute | solution.py:263
  18.4 1.5 %shard_map.39 = (bf16[1024,512]{1,0:T(8,128)(2,1)S(1)}, f32[64,1024]{1,0:T(8,128)S(1)}) custom-call(bf16[512,256]{1,0:T(8,128)(2,1)S(1)} %get-tuple-element.30.refs_0_, bf16[512,256]{1,0:T(8,128)(2,1)S(1)} %get-tuple-element.31.refs_1_, f32[1,512]{1,0:T(1,128)S(1)} %get-tuple-element.32.refs_2_, s32[168,256]{1,0:T(8,128)S(1)} %pad_add_fusion.own_ref.refs_3_, ...), custom_call_target="tpu_custom_call" | custom-call | tf_op jit(solution)/shard_map/pallas_call | solution.py:249
  20.0 0.0 collective-permute-done.1.refs_3_
  20.0 0.1 collective-permute-start.9
  20.1 0.0 collective-permute-done.6.refs_4_
  20.1 0.6 collective-permute-start.4
  20.7 1.0 %collective-permute-done.13.refs_3_ = s32[168,256]{1,0:T(8,128)S(1)} collective-permute-done((s32[168,256]{1,0:T(8,128)S(1)}, s32[168,256]{1,0:T(8,128)S(1)}, u32[]{:S(2)}, u32[]{:S(2)}) %collective-permute-start.13) | collective-permute-done | bytes 172064 | tf_op jit(solution)/shard_map/ppermute | solution.py:263
  21.7 0.0 collective-permute-start.14
  21.7 1.5 %collective-permute-done.11.refs_3_ = s32[168,256]{1,0:T(8,128)S(1)} collective-permute-done((s32[168,256]{1,0:T(8,128)S(1)}, s32[168,256]{1,0:T(8,128)S(1)}, u32[]{:S(2)}, u32[]{:S(2)}) %collective-permute-start.11) | collective-permute-done | bytes 172064 | tf_op jit(solution)/shard_map/ppermute | solution.py:263
  23.2 0.0 collective-permute-start.12
  23.2 0.0 collective-permute-done.8.refs_6_
  23.2 1.5 %shard_map.40 = (bf16[1024,512]{1,0:T(8,128)(2,1)S(1)}, f32[64,1024]{1,0:T(8,128)S(1)}) custom-call(bf16[512,256]{1,0:T(8,128)(2,1)S(1)} %get-tuple-element.30.refs_0_, bf16[512,256]{1,0:T(8,128)(2,1)S(1)} %get-tuple-element.31.refs_1_, f32[1,512]{1,0:T(1,128)S(1)} %get-tuple-element.32.refs_2_, s32[168,256]{1,0:T(8,128)S(1)} %collective-permute-done.5.refs_3_, ...), custom_call_target="tpu_custom_call" | custom-call | tf_op jit(solution)/shard_map/pallas_call | solution.py:249
  24.7 0.0 collective-permute-done.9.refs_4_
  24.7 0.8 %shard_map.41 = (bf16[512,512]{1,0:T(8,128)(2,1)S(1)}, f32[64,512]{1,0:T(8,128)S(1)}) custom-call(bf16[512,256]{1,0:T(8,128)(2,1)S(1)} %get-tuple-element.30.refs_0_, bf16[512,256]{1,0:T(8,128)(2,1)S(1)} %get-tuple-element.31.refs_1_, f32[1,512]{1,0:T(1,128)S(1)} %get-tuple-element.32.refs_2_, s32[168,256]{1,0:T(8,128)S(1)} %collective-permute-done.1.refs_3_, ...), custom_call_target="tpu_custom_call" | custom-call | tf_op jit(solution)/shard_map/pallas_call | solution.py:249
  25.6 1.3 %collective-permute-done.4.refs_3_ = s32[168,256]{1,0:T(8,128)S(1)} collective-permute-done((s32[168,256]{1,0:T(8,128)S(1)}, s32[168,256]{1,0:T(8,128)S(1)}, u32[]{:S(2)}, u32[]{:S(2)}) %collective-permute-start.4) | collective-permute-done | bytes 172064 | tf_op jit(solution)/shard_map/ppermute | solution.py:263
  26.9 0.5 shard_map.44
  27.4 0.8 %shard_map.43 = (bf16[512,512]{1,0:T(8,128)(2,1)S(1)}, f32[64,512]{1,0:T(8,128)S(1)}) custom-call(bf16[512,256]{1,0:T(8,128)(2,1)S(1)} %get-tuple-element.30.refs_0_, bf16[512,256]{1,0:T(8,128)(2,1)S(1)} %get-tuple-element.31.refs_1_, f32[1,512]{1,0:T(1,128)S(1)} %get-tuple-element.32.refs_2_, s32[168,256]{1,0:T(8,128)S(1)} %collective-permute-done.13.refs_3_, ...), custom_call_target="tpu_custom_call" | custom-call | tf_op jit(solution)/shard_map/pallas_call | solution.py:249
  28.2 0.0 collective-permute-done.12.refs_4_
  28.3 0.8 %shard_map.42 = (bf16[512,512]{1,0:T(8,128)(2,1)S(1)}, f32[64,512]{1,0:T(8,128)S(1)}) custom-call(bf16[512,256]{1,0:T(8,128)(2,1)S(1)} %get-tuple-element.30.refs_0_, bf16[512,256]{1,0:T(8,128)(2,1)S(1)} %get-tuple-element.31.refs_1_, f32[1,512]{1,0:T(1,128)S(1)} %get-tuple-element.32.refs_2_, s32[168,256]{1,0:T(8,128)S(1)} %collective-permute-done.11.refs_3_, ...), custom_call_target="tpu_custom_call" | custom-call | tf_op jit(solution)/shard_map/pallas_call | solution.py:249
  29.1 1.3 %shard_map.45 = (f32[64,512]{1,0:T(8,128)S(1)}, bf16[256,512]{1,0:T(8,128)(2,1)S(1)}) custom-call(bf16[512,256]{1,0:T(8,128)(2,1)S(1)} %get-tuple-element.30.refs_0_, bf16[512,256]{1,0:T(8,128)(2,1)S(1)} %get-tuple-element.31.refs_1_, f32[1,512]{1,0:T(1,128)S(1)} %get-tuple-element.32.refs_2_, s32[168,256]{1,0:T(8,128)S(1)} %collective-permute-done.10.refs_3_, ...), custom_call_target="tpu_custom_call" | custom-call | tf_op jit(solution)/shard_map/pallas_call | solution.py:249
  30.4 0.7 %collective-permute-start.18 = (f32[64,512]{1,0:T(8,128)S(1)}, f32[64,512]{1,0:T(8,128)S(1)}, u32[]{:S(2)}, u32[]{:S(2)}) collective-permute-start(f32[64,512]{1,0:T(8,128)S(1)} %get-tuple-element.47.refs_0_.refs_1_), channel_id=1, source_target_pairs={{1,2},{2,1},{5,6},{6,5},{9,10},{10,9},{13,14},{14,13},{17,18},{18,... | collective-permute-start | bytes 393224 | tf_op jit(solution)/shard_map/ppermute | solution.py:271
  31.1 1.7 %collective-permute-start.20 = (f32[64,512]{1,0:T(8,128)S(1)}, f32[64,512]{1,0:T(8,128)S(1)}, u32[]{:S(2)}, u32[]{:S(2)}) collective-permute-start(f32[64,512]{1,0:T(8,128)S(1)} %get-tuple-element.47.refs_0_.refs_1_), channel_id=1, source_target_pairs={{0,8},{4,12},{8,0},{12,4},{1,9},{5,13},{9,1},{13,5},{2,10},{6,14},... | collective-permute-start | bytes 393224 | tf_op jit(solution)/shard_map/ppermute | solution.py:263
  32.8 0.8 %collective-permute-start.15 = (f32[64,512]{1,0:T(8,128)S(1)}, f32[64,512]{1,0:T(8,128)S(1)}, u32[]{:S(2)}, u32[]{:S(2)}) collective-permute-start(f32[64,512]{1,0:T(8,128)S(1)} %get-tuple-element.47.refs_0_.refs_1_), channel_id=1, source_target_pairs={{1,10},{2,9},{5,14},{6,13},{9,2},{10,1},{13,6},{14,5},{17,26},{18,... | collective-permute-start | bytes 393224 | tf_op jit(solution)/shard_map/ppermute | solution.py:275
  33.7 0.1 collective-permute-start.17
  33.8 0.0 collective-permute-done.18.refs_3_
  33.8 0.5 collective-permute-start.19
  34.2 2.8 %collective-permute-done.20.refs_5_ = f32[64,512]{1,0:T(8,128)S(1)} collective-permute-done((f32[64,512]{1,0:T(8,128)S(1)}, f32[64,512]{1,0:T(8,128)S(1)}, u32[]{:S(2)}, u32[]{:S(2)}) %collective-permute-start.20) | collective-permute-done | bytes 131104 | tf_op jit(solution)/shard_map/ppermute | solution.py:263
  37.0 0.5 collective-permute-start.16
  37.6 0.0 collective-permute-done.19.refs_4_
  37.6 0.8 %collective-permute-done.21.refs_6_ = f32[64,512]{1,0:T(8,128)S(1)} collective-permute-done((f32[64,512]{1,0:T(8,128)S(1)}, f32[64,512]{1,0:T(8,128)S(1)}, u32[]{:S(2)}, u32[]{:S(2)}) %collective-permute-start.21) | collective-permute-done | bytes 131104 | tf_op jit(solution)/shard_map/ppermute | solution.py:263
  38.4 0.8 %shard_map.46 = (bf16[192,3072]{1,0:T(8,128)(2,1)S(1)}, f32[64,64]{1,0:T(8,128)S(1)}, f32[64,128]{1,0:T(8,128)S(1)}) custom-call(f32[64,512]{1,0:T(8,128)S(1)} %get-tuple-element.47.refs_0_.refs_1_, f32[64,512]{1,0:T(8,128)S(1)} %get-tuple-element.47.refs_0_.refs_1_, f32[64,512]{1,0:T(8,128)S(1)} %collective-permute-done.17.refs_2_, ...), custom_call_target="tpu_custom_call" | custom-call | tf_op jit(solution)/shard_map/pallas_call | solution.py:249
  39.2 4.3 %shard_map.47 = (f32[64,256]{1,0:T(8,128)S(1)}, f32[64,256]{1,0:T(8,128)S(1)}, f32[40,128]{1,0:T(8,128)S(1)}) custom-call(f32[64,512]{1,0:T(8,128)S(1)} %get-tuple-element.47.refs_0_.refs_1_, f32[64,512]{1,0:T(8,128)S(1)} %collective-permute-done.15.refs_1_, f32[64,512]{1,0:T(8,128)S(1)} %collective-permute-done.16.refs_2_, ...), custom_call_target="tpu_custom_call" | custom-call | tf_op jit(solution)/shard_map/pallas_call | solution.py:249
  43.5 6.4 %collective-permute-start.27 = (f32[64,256]{1,0:T(8,128)S(1)}, f32[64,256]{1,0:T(8,128)S(1)}, u32[]{:S(2)}, u32[]{:S(2)}) collective-permute-start(f32[64,256]{1,0:T(8,128)S(1)} %get-tuple-element.54), channel_id=1, source_target_pairs={{0,1},{1,0},{2,3},{3,2},{4,5},{5,4},{6,7},{7,6},{8,9},{9,8},{10,11... | collective-permute-start | bytes 196616 | tf_op jit(solution)/shard_map/ppermute | solution.py:263
  49.9 0.0 collective-permute-start.22
  49.9 1.2 %collective-permute-done.22.b_ref = f32[40,128]{1,0:T(8,128)S(1)} collective-permute-done((f32[40,128]{1,0:T(8,128)S(1)}, f32[40,128]{1,0:T(8,128)S(1)}, u32[]{:S(2)}, u32[]{:S(2)}) %collective-permute-start.22) | collective-permute-done | bytes 20512 | tf_op jit(solution)/shard_map/ppermute | solution.py:263
  51.1 0.1 shard_map.48.a_ref
  51.2 0.6 collective-permute-start.23
  51.8 3.2 %collective-permute-done.23.b_ref = f32[40,128]{1,0:T(8,128)S(1)} collective-permute-done((f32[40,128]{1,0:T(8,128)S(1)}, f32[40,128]{1,0:T(8,128)S(1)}, u32[]{:S(2)}, u32[]{:S(2)}) %collective-permute-start.23) | collective-permute-done | bytes 20512 | tf_op jit(solution)/shard_map/ppermute | solution.py:263
  55.0 0.1 shard_map.49.share_ref
  55.1 0.1 collective-permute-start.24
  55.2 1.8 %collective-permute-start.25 = (f32[40,128]{1,0:T(8,128)S(1)}, f32[40,128]{1,0:T(8,128)S(1)}, u32[]{:S(2)}, u32[]{:S(2)}) collective-permute-start(f32[40,128]{1,0:T(8,128)S(1)} %shard_map.49.share_ref), channel_id=1, source_target_pairs={{0,2},{1,3},{2,0},{3,1},{4,6},{5,7},{6,4},{7,5},{8,10},{9,11},{10,... | collective-permute-start | bytes 61448 | tf_op jit(solution)/shard_map/ppermute | solution.py:263
  57.0 2.5 %collective-permute-start.26 = (f32[40,128]{1,0:T(8,128)S(1)}, f32[40,128]{1,0:T(8,128)S(1)}, u32[]{:S(2)}, u32[]{:S(2)}) collective-permute-start(f32[40,128]{1,0:T(8,128)S(1)} %shard_map.49.share_ref), channel_id=1, source_target_pairs={{0,3},{1,2},{2,1},{3,0},{4,7},{5,6},{6,5},{7,4},{8,11},{9,10},{10,... | collective-permute-start | bytes 61448 | tf_op jit(solution)/shard_map/ppermute | solution.py:263
  59.5 0.4 collective-permute-done.25.far_ref
  59.8 2.7 %collective-permute-done.26.across_ref = f32[40,128]{1,0:T(8,128)S(1)} collective-permute-done((f32[40,128]{1,0:T(8,128)S(1)}, f32[40,128]{1,0:T(8,128)S(1)}, u32[]{:S(2)}, u32[]{:S(2)}) %collective-permute-start.26) | collective-permute-done | bytes 20512 | tf_op jit(solution)/shard_map/ppermute | solution.py:263
  62.6 2.6 %shard_map.50 = f32[64,256]{1,0:T(8,128)} custom-call(s32[1]{0:T(128)} %bitcast.outer_ref, f32[40,128]{1,0:T(8,128)S(1)} %shard_map.49.share_ref, f32[40,128]{1,0:T(8,128)S(1)} %collective-permute-done.24.near_ref, f32[40,128]{1,0:T(8,128)S(1)} %collective-permute-done.25.far_ref, f32[40,128]{1,0:T(8,128)S(1)} %collective-permute-done.26.across_ref, ...), custom_call_target="tpu_custom_call" | custom-call | tf_op jit(solution)/shard_map/pallas_call | solution.py:249
  (15 shorter events, 0.1 us)
Async XLA Ops:
  0.0 1.6 %copy-start = (f32[2048,256]{1,0:T(8,128)S(1)}, f32[2048,256]{1,0:T(8,128)}, u32[]{:S(2)}) copy-start(f32[2048,256]{1,0:T(8,128)} %param.3) | copy-start | bytes 6291460
  0.0 2.6 %copy-start.1 = (f32[64,256]{1,0:T(8,128)S(1)}, f32[64,256]{1,0:T(8,128)}, u32[]{:S(2)}) copy-start(f32[64,256]{1,0:T(8,128)} %initial_ref.1) | copy-start | bytes 196612
  2.9 7.5 %collective-permute-start = (s32[168,256]{1,0:T(8,128)S(1)}, s32[168,256]{1,0:T(8,128)S(1)}, u32[]{:S(2)}, u32[]{:S(2)}) collective-permute-start(s32[168,256]{1,0:T(8,128)S(1)} %pad_add_fusion.own_ref.refs_3_), channel_id=1, source_target_pairs={{0,1},{1,0},{2,3},{3,2},{4,5},{5,4},{6,7},{7,6},{8,9},{9,8},{10,11... | collective-permute-start | bytes 516104 | tf_op jit(solution)/shard_map/ppermute | solution.py:263
  5.9 5.0 %collective-permute-start.5 = (s32[168,256]{1,0:T(8,128)S(1)}, s32[168,256]{1,0:T(8,128)S(1)}, u32[]{:S(2)}, u32[]{:S(2)}) collective-permute-start(s32[168,256]{1,0:T(8,128)S(1)} %pad_add_fusion.own_ref.refs_3_), channel_id=1, source_target_pairs={{1,2},{2,1},{5,6},{6,5},{9,10},{10,9},{13,14},{14,13},{17,18},{18,... | collective-permute-start | bytes 516104 | tf_op jit(solution)/shard_map/ppermute | solution.py:271
  6.6 5.9 %collective-permute-start.7 = (s32[168,256]{1,0:T(8,128)S(1)}, s32[168,256]{1,0:T(8,128)S(1)}, u32[]{:S(2)}, u32[]{:S(2)}) collective-permute-start(s32[168,256]{1,0:T(8,128)S(1)} %pad_add_fusion.own_ref.refs_3_), channel_id=1, source_target_pairs={{0,8},{4,12},{8,0},{12,4},{1,9},{5,13},{9,1},{13,5},{2,10},{6,14},... | collective-permute-start | bytes 516104 | tf_op jit(solution)/shard_map/ppermute | solution.py:263
  8.2 4.3 %collective-permute-start.2 = (s32[168,256]{1,0:T(8,128)S(1)}, s32[168,256]{1,0:T(8,128)S(1)}, u32[]{:S(2)}, u32[]{:S(2)}) collective-permute-start(s32[168,256]{1,0:T(8,128)S(1)} %pad_add_fusion.own_ref.refs_3_), channel_id=1, source_target_pairs={{0,4},{4,0},{8,12},{12,8},{1,5},{5,1},{9,13},{13,9},{2,6},{6,2},{1... | collective-permute-start | bytes 516104 | tf_op jit(solution)/shard_map/ppermute | solution.py:263
  10.3 6.6 %collective-permute-start.3 = (s32[168,256]{1,0:T(8,128)S(1)}, s32[168,256]{1,0:T(8,128)S(1)}, u32[]{:S(2)}, u32[]{:S(2)}) collective-permute-start(s32[168,256]{1,0:T(8,128)S(1)} %collective-permute-done.outer_ref.refs_4_), channel_id=1, source_target_pairs={{0,4},{4,0},{8,12},{12,8},{1,5},{5,1},{9,13},{13,9},{2,6},{6,2},{1... | collective-permute-start | bytes 516104 | tf_op jit(solution)/shard_map/ppermute | solution.py:263
  10.3 9.7 %collective-permute-start.1 = (s32[168,256]{1,0:T(8,128)S(1)}, s32[168,256]{1,0:T(8,128)S(1)}, u32[]{:S(2)}, u32[]{:S(2)}) collective-permute-start(s32[168,256]{1,0:T(8,128)S(1)} %collective-permute-done.outer_ref.refs_4_), channel_id=1, source_target_pairs={{1,2},{2,1},{5,6},{6,5},{9,10},{10,9},{13,14},{14,13},{17,18},{18,... | collective-permute-start | bytes 516104 | tf_op jit(solution)/shard_map/ppermute | solution.py:271
  11.0 9.1 %collective-permute-start.6 = (s32[168,256]{1,0:T(8,128)S(1)}, s32[168,256]{1,0:T(8,128)S(1)}, u32[]{:S(2)}, u32[]{:S(2)}) collective-permute-start(s32[168,256]{1,0:T(8,128)S(1)} %collective-permute-done.5.refs_3_), channel_id=1, source_target_pairs={{0,4},{4,0},{8,12},{12,8},{1,5},{5,1},{9,13},{13,9},{2,6},{6,2},{1... | collective-permute-start | bytes 516104 | tf_op jit(solution)/shard_map/ppermute | solution.py:263
  12.5 10.7 %collective-permute-start.8 = (s32[168,256]{1,0:T(8,128)S(1)}, s32[168,256]{1,0:T(8,128)S(1)}, u32[]{:S(2)}, u32[]{:S(2)}) collective-permute-start(s32[168,256]{1,0:T(8,128)S(1)} %collective-permute-done.7.refs_5_), channel_id=1, source_target_pairs={{0,4},{4,0},{8,12},{12,8},{1,5},{5,1},{9,13},{13,9},{2,6},{6,2},{1... | collective-permute-start | bytes 516104 | tf_op jit(solution)/shard_map/ppermute | solution.py:263
  12.5 9.2 %collective-permute-start.13 = (s32[168,256]{1,0:T(8,128)S(1)}, s32[168,256]{1,0:T(8,128)S(1)}, u32[]{:S(2)}, u32[]{:S(2)}) collective-permute-start(s32[168,256]{1,0:T(8,128)S(1)} %collective-permute-done.7.refs_5_), channel_id=1, source_target_pairs={{0,1},{1,0},{2,3},{3,2},{4,5},{5,4},{6,7},{7,6},{8,9},{9,8},{10,11... | collective-permute-start | bytes 516104 | tf_op jit(solution)/shard_map/ppermute | solution.py:263
  17.0 6.2 %collective-permute-start.11 = (s32[168,256]{1,0:T(8,128)S(1)}, s32[168,256]{1,0:T(8,128)S(1)}, u32[]{:S(2)}, u32[]{:S(2)}) collective-permute-start(s32[168,256]{1,0:T(8,128)S(1)} %collective-permute-done.5.refs_3_), channel_id=1, source_target_pairs={{0,8},{4,12},{8,0},{12,4},{1,9},{5,13},{9,1},{13,5},{2,10},{6,14},... | collective-permute-start | bytes 516104 | tf_op jit(solution)/shard_map/ppermute | solution.py:263
  20.0 4.7 %collective-permute-start.9 = (s32[168,256]{1,0:T(8,128)S(1)}, s32[168,256]{1,0:T(8,128)S(1)}, u32[]{:S(2)}, u32[]{:S(2)}) collective-permute-start(s32[168,256]{1,0:T(8,128)S(1)} %collective-permute-done.1.refs_3_), channel_id=1, source_target_pairs={{0,4},{4,0},{8,12},{12,8},{1,5},{5,1},{9,13},{13,9},{2,6},{6,2},{1... | collective-permute-start | bytes 516104 | tf_op jit(solution)/shard_map/ppermute | solution.py:263
  20.1 6.8 %collective-permute-start.4 = (s32[168,256]{1,0:T(8,128)S(1)}, s32[168,256]{1,0:T(8,128)S(1)}, u32[]{:S(2)}, u32[]{:S(2)}) collective-permute-start(s32[168,256]{1,0:T(8,128)S(1)} %collective-permute-done.1.refs_3_), channel_id=1, source_target_pairs={{0,8},{4,12},{8,0},{12,4},{1,9},{5,13},{9,1},{13,5},{2,10},{6,14},... | collective-permute-start | bytes 516104 | tf_op jit(solution)/shard_map/ppermute | solution.py:263
  21.7 5.7 %collective-permute-start.14 = (s32[168,256]{1,0:T(8,128)S(1)}, s32[168,256]{1,0:T(8,128)S(1)}, u32[]{:S(2)}, u32[]{:S(2)}) collective-permute-start(s32[168,256]{1,0:T(8,128)S(1)} %collective-permute-done.13.refs_3_), channel_id=1, source_target_pairs={{0,4},{4,0},{8,12},{12,8},{1,5},{5,1},{9,13},{13,9},{2,6},{6,2},{1... | collective-permute-start | bytes 516104 | tf_op jit(solution)/shard_map/ppermute | solution.py:263
  23.2 5.1 %collective-permute-start.12 = (s32[168,256]{1,0:T(8,128)S(1)}, s32[168,256]{1,0:T(8,128)S(1)}, u32[]{:S(2)}, u32[]{:S(2)}) collective-permute-start(s32[168,256]{1,0:T(8,128)S(1)} %collective-permute-done.11.refs_3_), channel_id=1, source_target_pairs={{0,4},{4,0},{8,12},{12,8},{1,5},{5,1},{9,13},{13,9},{2,6},{6,2},{1... | collective-permute-start | bytes 516104 | tf_op jit(solution)/shard_map/ppermute | solution.py:263
  26.9 2.2 %collective-permute-start.10 = (s32[168,256]{1,0:T(8,128)S(1)}, s32[168,256]{1,0:T(8,128)S(1)}, u32[]{:S(2)}, u32[]{:S(2)}) collective-permute-start(s32[168,256]{1,0:T(8,128)S(1)} %collective-permute-done.4.refs_3_), channel_id=1, source_target_pairs={{0,4},{4,0},{8,12},{12,8},{1,5},{5,1},{9,13},{13,9},{2,6},{6,2},{1... | collective-permute-start | bytes 516104 | tf_op jit(solution)/shard_map/ppermute | solution.py:263
  30.4 3.4 %collective-permute-start.18 = (f32[64,512]{1,0:T(8,128)S(1)}, f32[64,512]{1,0:T(8,128)S(1)}, u32[]{:S(2)}, u32[]{:S(2)}) collective-permute-start(f32[64,512]{1,0:T(8,128)S(1)} %get-tuple-element.47.refs_0_.refs_1_), channel_id=1, source_target_pairs={{1,2},{2,1},{5,6},{6,5},{9,10},{10,9},{13,14},{14,13},{17,18},{18,... | collective-permute-start | bytes 393224 | tf_op jit(solution)/shard_map/ppermute | solution.py:271
  31.1 6.0 %collective-permute-start.20 = (f32[64,512]{1,0:T(8,128)S(1)}, f32[64,512]{1,0:T(8,128)S(1)}, u32[]{:S(2)}, u32[]{:S(2)}) collective-permute-start(f32[64,512]{1,0:T(8,128)S(1)} %get-tuple-element.47.refs_0_.refs_1_), channel_id=1, source_target_pairs={{0,8},{4,12},{8,0},{12,4},{1,9},{5,13},{9,1},{13,5},{2,10},{6,14},... | collective-permute-start | bytes 393224 | tf_op jit(solution)/shard_map/ppermute | solution.py:263
  32.8 4.2 %collective-permute-start.15 = (f32[64,512]{1,0:T(8,128)S(1)}, f32[64,512]{1,0:T(8,128)S(1)}, u32[]{:S(2)}, u32[]{:S(2)}) collective-permute-start(f32[64,512]{1,0:T(8,128)S(1)} %get-tuple-element.47.refs_0_.refs_1_), channel_id=1, source_target_pairs={{1,10},{2,9},{5,14},{6,13},{9,2},{10,1},{13,6},{14,5},{17,26},{18,... | collective-permute-start | bytes 393224 | tf_op jit(solution)/shard_map/ppermute | solution.py:275
  33.7 3.9 %collective-permute-start.17 = (f32[64,512]{1,0:T(8,128)S(1)}, f32[64,512]{1,0:T(8,128)S(1)}, u32[]{:S(2)}, u32[]{:S(2)}) collective-permute-start(f32[64,512]{1,0:T(8,128)S(1)} %get-tuple-element.47.refs_0_.refs_1_), channel_id=1, source_target_pairs={{0,4},{4,0},{8,12},{12,8},{1,5},{5,1},{9,13},{13,9},{2,6},{6,2},{1... | collective-permute-start | bytes 393224 | tf_op jit(solution)/shard_map/ppermute | solution.py:263
  33.8 3.8 %collective-permute-start.19 = (f32[64,512]{1,0:T(8,128)S(1)}, f32[64,512]{1,0:T(8,128)S(1)}, u32[]{:S(2)}, u32[]{:S(2)}) collective-permute-start(f32[64,512]{1,0:T(8,128)S(1)} %collective-permute-done.18.refs_3_), channel_id=1, source_target_pairs={{0,4},{4,0},{8,12},{12,8},{1,5},{5,1},{9,13},{13,9},{2,6},{6,2},{1... | collective-permute-start | bytes 393224 | tf_op jit(solution)/shard_map/ppermute | solution.py:263
  37.0 1.3 %collective-permute-start.21 = (f32[64,512]{1,0:T(8,128)S(1)}, f32[64,512]{1,0:T(8,128)S(1)}, u32[]{:S(2)}, u32[]{:S(2)}) collective-permute-start(f32[64,512]{1,0:T(8,128)S(1)} %collective-permute-done.20.refs_5_), channel_id=1, source_target_pairs={{0,4},{4,0},{8,12},{12,8},{1,5},{5,1},{9,13},{13,9},{2,6},{6,2},{1... | collective-permute-start | bytes 393224 | tf_op jit(solution)/shard_map/ppermute | solution.py:263
  37.0 2.1 %collective-permute-start.16 = (f32[64,512]{1,0:T(8,128)S(1)}, f32[64,512]{1,0:T(8,128)S(1)}, u32[]{:S(2)}, u32[]{:S(2)}) collective-permute-start(f32[64,512]{1,0:T(8,128)S(1)} %collective-permute-done.15.refs_1_), channel_id=1, source_target_pairs={{0,4},{4,0},{8,12},{12,8},{1,5},{5,1},{9,13},{13,9},{2,6},{6,2},{1... | collective-permute-start | bytes 393224 | tf_op jit(solution)/shard_map/ppermute | solution.py:263
  43.5 19.1 %collective-permute-start.27 = (f32[64,256]{1,0:T(8,128)S(1)}, f32[64,256]{1,0:T(8,128)S(1)}, u32[]{:S(2)}, u32[]{:S(2)}) collective-permute-start(f32[64,256]{1,0:T(8,128)S(1)} %get-tuple-element.54), channel_id=1, source_target_pairs={{0,1},{1,0},{2,3},{3,2},{4,5},{5,4},{6,7},{7,6},{8,9},{9,8},{10,11... | collective-permute-start | bytes 196616 | tf_op jit(solution)/shard_map/ppermute | solution.py:263
  49.9 1.2 %collective-permute-start.22 = (f32[40,128]{1,0:T(8,128)S(1)}, f32[40,128]{1,0:T(8,128)S(1)}, u32[]{:S(2)}, u32[]{:S(2)}) collective-permute-start(f32[40,128]{1,0:T(8,128)S(1)} %get-tuple-element.52.a_ref), channel_id=1, source_target_pairs={{0,4},{4,0},{8,12},{12,8},{1,5},{5,1},{9,13},{13,9},{2,6},{6,2},{1... | collective-permute-start | bytes 61448 | tf_op jit(solution)/shard_map/ppermute | solution.py:263
  51.2 3.8 %collective-permute-start.23 = (f32[40,128]{1,0:T(8,128)S(1)}, f32[40,128]{1,0:T(8,128)S(1)}, u32[]{:S(2)}, u32[]{:S(2)}) collective-permute-start(f32[40,128]{1,0:T(8,128)S(1)} %shard_map.48.a_ref), channel_id=1, source_target_pairs={{0,8},{4,12},{8,0},{12,4},{1,9},{5,13},{9,1},{13,5},{2,10},{6,14},... | collective-permute-start | bytes 61448 | tf_op jit(solution)/shard_map/ppermute | solution.py:263
  55.1 4.4 %collective-permute-start.24 = (f32[40,128]{1,0:T(8,128)S(1)}, f32[40,128]{1,0:T(8,128)S(1)}, u32[]{:S(2)}, u32[]{:S(2)}) collective-permute-start(f32[40,128]{1,0:T(8,128)S(1)} %shard_map.49.share_ref), channel_id=1, source_target_pairs={{0,1},{1,0},{2,3},{3,2},{4,5},{5,4},{6,7},{7,6},{8,9},{9,8},{10,11... | collective-permute-start | bytes 61448 | tf_op jit(solution)/shard_map/ppermute | solution.py:263
  55.2 4.7 %collective-permute-start.25 = (f32[40,128]{1,0:T(8,128)S(1)}, f32[40,128]{1,0:T(8,128)S(1)}, u32[]{:S(2)}, u32[]{:S(2)}) collective-permute-start(f32[40,128]{1,0:T(8,128)S(1)} %shard_map.49.share_ref), channel_id=1, source_target_pairs={{0,2},{1,3},{2,0},{3,1},{4,6},{5,7},{6,4},{7,5},{8,10},{9,11},{10,... | collective-permute-start | bytes 61448 | tf_op jit(solution)/shard_map/ppermute | solution.py:263
  57.0 5.6 %collective-permute-start.26 = (f32[40,128]{1,0:T(8,128)S(1)}, f32[40,128]{1,0:T(8,128)S(1)}, u32[]{:S(2)}, u32[]{:S(2)}) collective-permute-start(f32[40,128]{1,0:T(8,128)S(1)} %shard_map.49.share_ref), channel_id=1, source_target_pairs={{0,3},{1,2},{2,1},{3,0},{4,7},{5,6},{6,5},{7,4},{8,11},{9,10},{10,... | collective-permute-start | bytes 61448 | tf_op jit(solution)/shard_map/ppermute | solution.py:263

commit v7 on v6

--- a/solution.py
+++ b/solution.py
@@ -231,12 +231,15 @@
     out_ref[...] = merge(a_ref[...], b_ref[...], each)
 
 
-def last_kernel(total, outer_ref, share_ref, near_ref, far_ref, across_ref, own_ref, given_ref, out_ref):
+def column_kernel(each, outer_ref, share_ref, near_ref, far_ref, across_ref, out_ref):
     outer = outer_ref[0] == 1
     first = jnp.where(outer, near_ref[...], share_ref[...])
-    second = jnp.where(outer, far_ref[...], across_ref[...])
-    images = jnp.where(outer, given_ref[...], own_ref[...])
-    share = merge(first, second, 0.5 * total)
+    out_ref[...] = merge(first, jnp.where(outer, far_ref[...], across_ref[...]), each)
+
+
+def last_kernel(total, outer_ref, share_ref, beside_ref, own_ref, given_ref, out_ref):
+    images = jnp.where(outer_ref[0] == 1, given_ref[...], own_ref[...])
+    share = merge(share_ref[...], beside_ref[...], 0.5 * total)
     h = share.shape[0] - 8
     mean = jnp.concatenate([share[:h, 3 * h : 3 * h + 1], share[:h, 3 * h + 1 : 3 * h + 2]], axis=0)
     top = share[:h, : 2 * h]
@@ -339,16 +342,17 @@
         functools.partial(second_kernel, len(parts), pieces, total), [images, *pairs[3], *known, *tiles], (block, block, packed)
     )
     given = NEAR(other)
-    for step, swap in enumerate((CORE, CHIP)):
-        share = call(functools.partial(merge_kernel, 2.0 * size * 2**step), [share, swap(share)], packed)
     place = lax.axis_index("col")
     flag = ((place == 0) | (place == 3)).astype(jnp.int32).reshape(1)
-    return call(
-        functools.partial(last_kernel, total),
-        [flag, share, NEAR(share), FAR(share), OPPOSITE(share), images, given],
-        block,
-        [pl.BlockSpec(memory_space=pltpu.SMEM)] + [VMEM] * 6,
-    )
+    share = call(functools.partial(merge_kernel, 2.0 * size), [share, CORE(share)], packed)
+    smem = pl.BlockSpec(memory_space=pltpu.SMEM)
+    share = call(
+        functools.partial(column_kernel, 4.0 * size),
+        [flag, share, NEAR(share), FAR(share), middle(share)],
+        packed,
+        [smem] + [VMEM] * 4,
+    )
+    return call(functools.partial(last_kernel, total), [flag, share, CHIP(share), images, given], block, [smem] + [VMEM] * 4)
 
 
 def local_large(corpus, sample_rows, initial):

time: 65.4 us -> 62.7 us (0.959)
  starting transfers between devices: 28.9 us -> 27 us
  waiting for transfers between devices: 17.4 us -> 16.4 us
    ppermute x24 -> x23, starting transfers between devices: 26 us -> 23.6 us  [exchange(): lax.ppermute(value, axis, [(i, i ^ offset) for i in range(size)])]
    ppermute x24 -> x23, waiting for transfers between devices: 17.4 us -> 16.4 us  [exchange(): lax.ppermute(value, axis, [(i, i ^ offset) for i in range(size)])]
    ppermute x3 -> x4, starting transfers between devices: 1.99 us -> 2.64 us  [middle(): return lax.ppermute(value, 'col', MIDDLE)]
where the time goes in v7:
time: 62.7 us; the launch traced here: 62.4 us
  starting transfers between devices  27 us (43%)
  waiting for transfers between devices  16.4 us (26%)
  Pallas kernels  16.1 us (26%)
  local copies, waits for them, and re-layouts  1.74 us (3%)
  other arithmetic  0.89 us (1%)
    ppermute x23, starting transfers between devices, exchange(): lax.ppermute(value, axis, [(i, i ^ offset) for i in range(size)])  23.6 us
    ppermute x23, waiting for transfers between devices, exchange(): lax.ppermute(value, axis, [(i, i ^ offset) for i in range(size)])  16.4 us
    pallas_call x14, Pallas kernels, call(): pl.pallas_call(kernel, out_shape=out_shape, in_specs=in_specs or [VMEM] *...  16.1 us
    ppermute x4, starting transfers between devices, middle(): return lax.ppermute(value, 'col', MIDDLE)  2.64 us
  transfers between devices with their start and end apart: 28, of which 11 were waited for; matrix products, arithmetic and copies ran while one was open for 0% of the time, Pallas kernels for 12%

profile of v7, /device:TPU:0, one launch (start us, length us, event | category | flops | bytes accessed | tf_op | source)
XLA Modules:
  0.0 62.4 jit_solution(15602888178325849042)
XLA Ops:
  0.0 0.8 %pad_clamp_fusion = s32[1024]{0:T(1024)S(1)} fusion(s32[256]{0:T(256)} %param.4), kind=kLoop, calls=%fused_computation.6 | loop fusion | flops 1024 | bytes 5120 | tf_op jit(solution)/shard_map/gather | solution.py:291
  0.8 0.8 %copy-done = f32[2048,256]{1,0:T(8,128)S(1)} copy-done((f32[2048,256]{1,0:T(8,128)S(1)}, f32[2048,256]{1,0:T(8,128)}, u32[]{:S(2)}) %copy-start) | copy-done | bytes 2097176
  1.6 1.0 %gather_fusion = f32[256,256]{1,0:T(8,128)S(1)} fusion(f32[2048,256]{1,0:T(8,128)S(1)} %copy-done, s32[1024]{0:T(1024)S(1)} %pad_clamp_fusion), kind=kCustom, calls=%fused_computation | custom fusion | bytes 525312 | tf_op jit(solution)/shard_map/gather | solution.py:291
  2.6 0.2 shard_map.37
  2.9 3.1 %collective-permute-start = (s32[168,256]{1,0:T(8,128)S(1)}, s32[168,256]{1,0:T(8,128)S(1)}, u32[]{:S(2)}, u32[]{:S(2)}) collective-permute-start(s32[168,256]{1,0:T(8,128)S(1)} %pad_add_fusion.own_ref.refs_3_), channel_id=1, source_target_pairs={{0,1},{1,0},{2,3},{3,2},{4,5},{5,4},{6,7},{7,6},{8,9},{9,8},{10,11... | collective-permute-start | bytes 516104 | tf_op jit(solution)/shard_map/ppermute | solution.py:266
  5.9 0.7 %collective-permute-start.5 = (s32[168,256]{1,0:T(8,128)S(1)}, s32[168,256]{1,0:T(8,128)S(1)}, u32[]{:S(2)}, u32[]{:S(2)}) collective-permute-start(s32[168,256]{1,0:T(8,128)S(1)} %pad_add_fusion.own_ref.refs_3_), channel_id=1, source_target_pairs={{1,2},{2,1},{5,6},{6,5},{9,10},{10,9},{13,14},{14,13},{17,18},{18,... | collective-permute-start | bytes 516104 | tf_op jit(solution)/shard_map/ppermute | solution.py:274
  6.6 1.6 %collective-permute-start.7 = (s32[168,256]{1,0:T(8,128)S(1)}, s32[168,256]{1,0:T(8,128)S(1)}, u32[]{:S(2)}, u32[]{:S(2)}) collective-permute-start(s32[168,256]{1,0:T(8,128)S(1)} %pad_add_fusion.own_ref.refs_3_), channel_id=1, source_target_pairs={{0,8},{4,12},{8,0},{12,4},{1,9},{5,13},{9,1},{13,5},{2,10},{6,14},... | collective-permute-start | bytes 516104 | tf_op jit(solution)/shard_map/ppermute | solution.py:266
  8.2 0.0 collective-permute-start.2
  8.2 2.1 %collective-permute-done.outer_ref.refs_4_ = s32[168,256]{1,0:T(8,128)S(1)} collective-permute-done((s32[168,256]{1,0:T(8,128)S(1)}, s32[168,256]{1,0:T(8,128)S(1)}, u32[]{:S(2)}, u32[]{:S(2)}) %collective-permute-start) | collective-permute-done | bytes 172064 | tf_op jit(solution)/shard_map/ppermute | solution.py:266
  10.3 0.0 collective-permute-start.3
  10.3 0.7 %collective-permute-start.1 = (s32[168,256]{1,0:T(8,128)S(1)}, s32[168,256]{1,0:T(8,128)S(1)}, u32[]{:S(2)}, u32[]{:S(2)}) collective-permute-start(s32[168,256]{1,0:T(8,128)S(1)} %collective-permute-done.outer_ref.refs_4_), channel_id=1, source_target_pairs={{1,2},{2,1},{5,6},{6,5},{9,10},{10,9},{13,14},{14,13},{17,18},{18,... | collective-permute-start | bytes 516104 | tf_op jit(solution)/shard_map/ppermute | solution.py:274
  11.0 0.0 collective-permute-done.5.refs_3_
  11.0 0.6 collective-permute-start.6
  11.6 0.7 %shard_map.38 = (bf16[512,256]{1,0:T(8,128)(2,1)S(1)}, bf16[512,256]{1,0:T(8,128)(2,1)S(1)}, f32[1,512]{1,0:T(1,128)S(1)}) custom-call(s32[168,256]{1,0:T(8,128)S(1)} %pad_add_fusion.own_ref.refs_3_, s32[168,256]{1,0:T(8,128)S(1)} %collective-permute-done.outer_ref.refs_4_), custom_call_target="tpu_custom_call" | custom-call | tf_op jit(solution)/shard_map/pallas_call | solution.py:252
  12.3 0.2 collective-permute-done.7.refs_5_
  12.5 0.0 collective-permute-start.8
  12.5 0.0 collective-permute-done.2.refs_5_
  12.5 4.4 %collective-permute-start.13 = (s32[168,256]{1,0:T(8,128)S(1)}, s32[168,256]{1,0:T(8,128)S(1)}, u32[]{:S(2)}, u32[]{:S(2)}) collective-permute-start(s32[168,256]{1,0:T(8,128)S(1)} %collective-permute-done.7.refs_5_), channel_id=1, source_target_pairs={{0,1},{1,0},{2,3},{3,2},{4,5},{5,4},{6,7},{7,6},{8,9},{9,8},{10,11... | collective-permute-start | bytes 516104 | tf_op jit(solution)/shard_map/ppermute | solution.py:266
  17.0 0.0 collective-permute-done.3.refs_6_
  17.0 1.5 %collective-permute-start.11 = (s32[168,256]{1,0:T(8,128)S(1)}, s32[168,256]{1,0:T(8,128)S(1)}, u32[]{:S(2)}, u32[]{:S(2)}) collective-permute-start(s32[168,256]{1,0:T(8,128)S(1)} %collective-permute-done.5.refs_3_), channel_id=1, source_target_pairs={{0,8},{4,12},{8,0},{12,4},{1,9},{5,13},{9,1},{13,5},{2,10},{6,14},... | collective-permute-start | bytes 516104 | tf_op jit(solution)/shard_map/ppermute | solution.py:266
  18.4 1.5 %shard_map.39 = (bf16[1024,512]{1,0:T(8,128)(2,1)S(1)}, f32[64,1024]{1,0:T(8,128)S(1)}) custom-call(bf16[512,256]{1,0:T(8,128)(2,1)S(1)} %get-tuple-element.30.refs_0_, bf16[512,256]{1,0:T(8,128)(2,1)S(1)} %get-tuple-element.31.refs_1_, f32[1,512]{1,0:T(1,128)S(1)} %get-tuple-element.32.refs_2_, s32[168,256]{1,0:T(8,128)S(1)} %pad_add_fusion.own_ref.refs_3_, ...), custom_call_target="tpu_custom_call" | custom-call | tf_op jit(solution)/shard_map/pallas_call | solution.py:252
  20.0 0.0 collective-permute-done.1.refs_3_
  20.0 0.1 collective-permute-start.9
  20.1 0.0 collective-permute-done.6.refs_4_
  20.1 0.6 collective-permute-start.4
  20.7 1.0 %collective-permute-done.13.refs_3_ = s32[168,256]{1,0:T(8,128)S(1)} collective-permute-done((s32[168,256]{1,0:T(8,128)S(1)}, s32[168,256]{1,0:T(8,128)S(1)}, u32[]{:S(2)}, u32[]{:S(2)}) %collective-permute-start.13) | collective-permute-done | bytes 172064 | tf_op jit(solution)/shard_map/ppermute | solution.py:266
  21.7 0.0 collective-permute-start.14
  21.7 1.5 %collective-permute-done.11.refs_3_ = s32[168,256]{1,0:T(8,128)S(1)} collective-permute-done((s32[168,256]{1,0:T(8,128)S(1)}, s32[168,256]{1,0:T(8,128)S(1)}, u32[]{:S(2)}, u32[]{:S(2)}) %collective-permute-start.11) | collective-permute-done | bytes 172064 | tf_op jit(solution)/shard_map/ppermute | solution.py:266
  23.2 0.0 collective-permute-start.12
  23.2 0.0 collective-permute-done.8.refs_6_
  23.2 1.5 %shard_map.40 = (bf16[1024,512]{1,0:T(8,128)(2,1)S(1)}, f32[64,1024]{1,0:T(8,128)S(1)}) custom-call(bf16[512,256]{1,0:T(8,128)(2,1)S(1)} %get-tuple-element.30.refs_0_, bf16[512,256]{1,0:T(8,128)(2,1)S(1)} %get-tuple-element.31.refs_1_, f32[1,512]{1,0:T(1,128)S(1)} %get-tuple-element.32.refs_2_, s32[168,256]{1,0:T(8,128)S(1)} %collective-permute-done.5.refs_3_, ...), custom_call_target="tpu_custom_call" | custom-call | tf_op jit(solution)/shard_map/pallas_call | solution.py:252
  24.7 0.0 collective-permute-done.9.refs_4_
  24.7 0.8 %shard_map.41 = (bf16[512,512]{1,0:T(8,128)(2,1)S(1)}, f32[64,512]{1,0:T(8,128)S(1)}) custom-call(bf16[512,256]{1,0:T(8,128)(2,1)S(1)} %get-tuple-element.30.refs_0_, bf16[512,256]{1,0:T(8,128)(2,1)S(1)} %get-tuple-element.31.refs_1_, f32[1,512]{1,0:T(1,128)S(1)} %get-tuple-element.32.refs_2_, s32[168,256]{1,0:T(8,128)S(1)} %collective-permute-done.1.refs_3_, ...), custom_call_target="tpu_custom_call" | custom-call | tf_op jit(solution)/shard_map/pallas_call | solution.py:252
  25.6 1.3 %collective-permute-done.4.refs_3_ = s32[168,256]{1,0:T(8,128)S(1)} collective-permute-done((s32[168,256]{1,0:T(8,128)S(1)}, s32[168,256]{1,0:T(8,128)S(1)}, u32[]{:S(2)}, u32[]{:S(2)}) %collective-permute-start.4) | collective-permute-done | bytes 172064 | tf_op jit(solution)/shard_map/ppermute | solution.py:266
  26.9 0.0 collective-permute-start.10
  26.9 0.5 shard_map.44
  27.4 0.8 %shard_map.43 = (bf16[512,512]{1,0:T(8,128)(2,1)S(1)}, f32[64,512]{1,0:T(8,128)S(1)}) custom-call(bf16[512,256]{1,0:T(8,128)(2,1)S(1)} %get-tuple-element.30.refs_0_, bf16[512,256]{1,0:T(8,128)(2,1)S(1)} %get-tuple-element.31.refs_1_, f32[1,512]{1,0:T(1,128)S(1)} %get-tuple-element.32.refs_2_, s32[168,256]{1,0:T(8,128)S(1)} %collective-permute-done.13.refs_3_, ...), custom_call_target="tpu_custom_call" | custom-call | tf_op jit(solution)/shard_map/pallas_call | solution.py:252
  28.2 0.0 collective-permute-done.12.refs_4_
  28.3 0.8 %shard_map.42 = (bf16[512,512]{1,0:T(8,128)(2,1)S(1)}, f32[64,512]{1,0:T(8,128)S(1)}) custom-call(bf16[512,256]{1,0:T(8,128)(2,1)S(1)} %get-tuple-element.30.refs_0_, bf16[512,256]{1,0:T(8,128)(2,1)S(1)} %get-tuple-element.31.refs_1_, f32[1,512]{1,0:T(1,128)S(1)} %get-tuple-element.32.refs_2_, s32[168,256]{1,0:T(8,128)S(1)} %collective-permute-done.11.refs_3_, ...), custom_call_target="tpu_custom_call" | custom-call | tf_op jit(solution)/shard_map/pallas_call | solution.py:252
  29.1 1.3 %shard_map.45 = (f32[64,512]{1,0:T(8,128)S(1)}, bf16[256,512]{1,0:T(8,128)(2,1)S(1)}) custom-call(bf16[512,256]{1,0:T(8,128)(2,1)S(1)} %get-tuple-element.30.refs_0_, bf16[512,256]{1,0:T(8,128)(2,1)S(1)} %get-tuple-element.31.refs_1_, f32[1,512]{1,0:T(1,128)S(1)} %get-tuple-element.32.refs_2_, s32[168,256]{1,0:T(8,128)S(1)} %collective-permute-done.10.refs_3_, ...), custom_call_target="tpu_custom_call" | custom-call | tf_op jit(solution)/shard_map/pallas_call | solution.py:252
  30.4 0.7 %collective-permute-start.18 = (f32[64,512]{1,0:T(8,128)S(1)}, f32[64,512]{1,0:T(8,128)S(1)}, u32[]{:S(2)}, u32[]{:S(2)}) collective-permute-start(f32[64,512]{1,0:T(8,128)S(1)} %get-tuple-element.47.refs_0_.refs_1_), channel_id=1, source_target_pairs={{1,2},{2,1},{5,6},{6,5},{9,10},{10,9},{13,14},{14,13},{17,18},{18,... | collective-permute-start | bytes 393224 | tf_op jit(solution)/shard_map/ppermute | solution.py:274
  31.1 1.7 %collective-permute-start.20 = (f32[64,512]{1,0:T(8,128)S(1)}, f32[64,512]{1,0:T(8,128)S(1)}, u32[]{:S(2)}, u32[]{:S(2)}) collective-permute-start(f32[64,512]{1,0:T(8,128)S(1)} %get-tuple-element.47.refs_0_.refs_1_), channel_id=1, source_target_pairs={{0,8},{4,12},{8,0},{12,4},{1,9},{5,13},{9,1},{13,5},{2,10},{6,14},... | collective-permute-start | bytes 393224 | tf_op jit(solution)/shard_map/ppermute | solution.py:266
  32.8 0.8 %collective-permute-start.15 = (f32[64,512]{1,0:T(8,128)S(1)}, f32[64,512]{1,0:T(8,128)S(1)}, u32[]{:S(2)}, u32[]{:S(2)}) collective-permute-start(f32[64,512]{1,0:T(8,128)S(1)} %get-tuple-element.47.refs_0_.refs_1_), channel_id=1, source_target_pairs={{1,10},{2,9},{5,14},{6,13},{9,2},{10,1},{13,6},{14,5},{17,26},{18,... | collective-permute-start | bytes 393224 | tf_op jit(solution)/shard_map/ppermute | solution.py:278
  33.7 0.1 collective-permute-start.17
  33.8 0.5 collective-permute-start.19
  34.2 2.8 %collective-permute-done.20.refs_5_ = f32[64,512]{1,0:T(8,128)S(1)} collective-permute-done((f32[64,512]{1,0:T(8,128)S(1)}, f32[64,512]{1,0:T(8,128)S(1)}, u32[]{:S(2)}, u32[]{:S(2)}) %collective-permute-start.20) | collective-permute-done | bytes 131104 | tf_op jit(solution)/shard_map/ppermute | solution.py:266
  37.0 0.5 collective-permute-start.16
  37.6 0.8 %collective-permute-done.21.refs_6_ = f32[64,512]{1,0:T(8,128)S(1)} collective-permute-done((f32[64,512]{1,0:T(8,128)S(1)}, f32[64,512]{1,0:T(8,128)S(1)}, u32[]{:S(2)}, u32[]{:S(2)}) %collective-permute-start.21) | collective-permute-done | bytes 131104 | tf_op jit(solution)/shard_map/ppermute | solution.py:266
  38.4 0.8 %shard_map.46 = (bf16[192,3072]{1,0:T(8,128)(2,1)S(1)}, f32[64,64]{1,0:T(8,128)S(1)}, f32[64,128]{1,0:T(8,128)S(1)}) custom-call(f32[64,512]{1,0:T(8,128)S(1)} %get-tuple-element.47.refs_0_.refs_1_, f32[64,512]{1,0:T(8,128)S(1)} %get-tuple-element.47.refs_0_.refs_1_, f32[64,512]{1,0:T(8,128)S(1)} %collective-permute-done.17.refs_2_, ...), custom_call_target="tpu_custom_call" | custom-call | tf_op jit(solution)/shard_map/pallas_call | solution.py:252
  39.2 4.3 %shard_map.47 = (f32[64,256]{1,0:T(8,128)S(1)}, f32[64,256]{1,0:T(8,128)S(1)}, f32[40,128]{1,0:T(8,128)S(1)}) custom-call(f32[64,512]{1,0:T(8,128)S(1)} %get-tuple-element.47.refs_0_.refs_1_, f32[64,512]{1,0:T(8,128)S(1)} %collective-permute-done.15.refs_1_, f32[64,512]{1,0:T(8,128)S(1)} %collective-permute-done.16.refs_2_, ...), custom_call_target="tpu_custom_call" | custom-call | tf_op jit(solution)/shard_map/pallas_call | solution.py:252
  43.5 6.4 %collective-permute-start.27 = (f32[64,256]{1,0:T(8,128)S(1)}, f32[64,256]{1,0:T(8,128)S(1)}, u32[]{:S(2)}, u32[]{:S(2)}) collective-permute-start(f32[64,256]{1,0:T(8,128)S(1)} %get-tuple-element.54), channel_id=1, source_target_pairs={{0,1},{1,0},{2,3},{3,2},{4,5},{5,4},{6,7},{7,6},{8,9},{9,8},{10,11... | collective-permute-start | bytes 196616 | tf_op jit(solution)/shard_map/ppermute | solution.py:266
  49.9 0.0 collective-permute-start.22
  49.9 1.2 %collective-permute-done.22.b_ref = f32[40,128]{1,0:T(8,128)S(1)} collective-permute-done((f32[40,128]{1,0:T(8,128)S(1)}, f32[40,128]{1,0:T(8,128)S(1)}, u32[]{:S(2)}, u32[]{:S(2)}) %collective-permute-start.22) | collective-permute-done | bytes 20512 | tf_op jit(solution)/shard_map/ppermute | solution.py:266
  51.1 0.1 shard_map.48.share_ref
  51.2 0.1 collective-permute-start.23
  51.3 1.8 %collective-permute-start.24 = (f32[40,128]{1,0:T(8,128)S(1)}, f32[40,128]{1,0:T(8,128)S(1)}, u32[]{:S(2)}, u32[]{:S(2)}) collective-permute-start(f32[40,128]{1,0:T(8,128)S(1)} %shard_map.48.share_ref), channel_id=1, source_target_pairs={{0,2},{1,3},{2,0},{3,1},{4,6},{5,7},{6,4},{7,5},{8,10},{9,11},{10,... | collective-permute-start | bytes 61448 | tf_op jit(solution)/shard_map/ppermute | solution.py:266
  53.1 0.7 %collective-permute-start.25 = (f32[40,128]{1,0:T(8,128)S(1)}, f32[40,128]{1,0:T(8,128)S(1)}, u32[]{:S(2)}, u32[]{:S(2)}) collective-permute-start(f32[40,128]{1,0:T(8,128)S(1)} %shard_map.48.share_ref), channel_id=1, source_target_pairs={{1,2},{2,1},{5,6},{6,5},{9,10},{10,9},{13,14},{14,13},{17,18},{18,... | collective-permute-start | bytes 61448 | tf_op jit(solution)/shard_map/ppermute | solution.py:274
  53.8 1.2 %collective-permute-done.23.near_ref = f32[40,128]{1,0:T(8,128)S(1)} collective-permute-done((f32[40,128]{1,0:T(8,128)S(1)}, f32[40,128]{1,0:T(8,128)S(1)}, u32[]{:S(2)}, u32[]{:S(2)}) %collective-permute-start.23) | collective-permute-done | bytes 20512 | tf_op jit(solution)/shard_map/ppermute | solution.py:266
  55.0 1.0 %collective-permute-done.24.far_ref = f32[40,128]{1,0:T(8,128)S(1)} collective-permute-done((f32[40,128]{1,0:T(8,128)S(1)}, f32[40,128]{1,0:T(8,128)S(1)}, u32[]{:S(2)}, u32[]{:S(2)}) %collective-permute-start.24) | collective-permute-done | bytes 20512 | tf_op jit(solution)/shard_map/ppermute | solution.py:266
  56.0 0.0 collective-permute-done.25.across_ref
  56.0 0.1 shard_map.49.share_ref
  56.1 0.6 collective-permute-start.26
  56.6 3.2 %collective-permute-done.26.beside_ref = f32[40,128]{1,0:T(8,128)S(1)} collective-permute-done((f32[40,128]{1,0:T(8,128)S(1)}, f32[40,128]{1,0:T(8,128)S(1)}, u32[]{:S(2)}, u32[]{:S(2)}) %collective-permute-start.26) | collective-permute-done | bytes 20512 | tf_op jit(solution)/shard_map/ppermute | solution.py:266
  59.9 2.6 %shard_map.50 = f32[64,256]{1,0:T(8,128)} custom-call(s32[1]{0:T(128)} %bitcast.outer_ref, f32[40,128]{1,0:T(8,128)S(1)} %shard_map.49.share_ref, f32[40,128]{1,0:T(8,128)S(1)} %collective-permute-done.26.beside_ref, f32[64,256]{1,0:T(8,128)S(1)} %get-tuple-element.53.own_ref, f32[64,256]{1,0:T(8,128)S(1)} %collective-permute-done.27.given_ref), custom_call_target="tpu_custom_call" | custom-call | tf_op jit(solution)/shard_map/pallas_call | solution.py:252
  (15 shorter events, 0.1 us)
Async XLA Ops:
  0.0 1.6 %copy-start = (f32[2048,256]{1,0:T(8,128)S(1)}, f32[2048,256]{1,0:T(8,128)}, u32[]{:S(2)}) copy-start(f32[2048,256]{1,0:T(8,128)} %param.3) | copy-start | bytes 6291460
  0.0 2.6 %copy-start.1 = (f32[64,256]{1,0:T(8,128)S(1)}, f32[64,256]{1,0:T(8,128)}, u32[]{:S(2)}) copy-start(f32[64,256]{1,0:T(8,128)} %initial_ref.1) | copy-start | bytes 196612
  2.9 7.5 %collective-permute-start = (s32[168,256]{1,0:T(8,128)S(1)}, s32[168,256]{1,0:T(8,128)S(1)}, u32[]{:S(2)}, u32[]{:S(2)}) collective-permute-start(s32[168,256]{1,0:T(8,128)S(1)} %pad_add_fusion.own_ref.refs_3_), channel_id=1, source_target_pairs={{0,1},{1,0},{2,3},{3,2},{4,5},{5,4},{6,7},{7,6},{8,9},{9,8},{10,11... | collective-permute-start | bytes 516104 | tf_op jit(solution)/shard_map/ppermute | solution.py:266
  5.9 5.0 %collective-permute-start.5 = (s32[168,256]{1,0:T(8,128)S(1)}, s32[168,256]{1,0:T(8,128)S(1)}, u32[]{:S(2)}, u32[]{:S(2)}) collective-permute-start(s32[168,256]{1,0:T(8,128)S(1)} %pad_add_fusion.own_ref.refs_3_), channel_id=1, source_target_pairs={{1,2},{2,1},{5,6},{6,5},{9,10},{10,9},{13,14},{14,13},{17,18},{18,... | collective-permute-start | bytes 516104 | tf_op jit(solution)/shard_map/ppermute | solution.py:274
  6.6 5.9 %collective-permute-start.7 = (s32[168,256]{1,0:T(8,128)S(1)}, s32[168,256]{1,0:T(8,128)S(1)}, u32[]{:S(2)}, u32[]{:S(2)}) collective-permute-start(s32[168,256]{1,0:T(8,128)S(1)} %pad_add_fusion.own_ref.refs_3_), channel_id=1, source_target_pairs={{0,8},{4,12},{8,0},{12,4},{1,9},{5,13},{9,1},{13,5},{2,10},{6,14},... | collective-permute-start | bytes 516104 | tf_op jit(solution)/shard_map/ppermute | solution.py:266
  8.2 4.3 %collective-permute-start.2 = (s32[168,256]{1,0:T(8,128)S(1)}, s32[168,256]{1,0:T(8,128)S(1)}, u32[]{:S(2)}, u32[]{:S(2)}) collective-permute-start(s32[168,256]{1,0:T(8,128)S(1)} %pad_add_fusion.own_ref.refs_3_), channel_id=1, source_target_pairs={{0,4},{4,0},{8,12},{12,8},{1,5},{5,1},{9,13},{13,9},{2,6},{6,2},{1... | collective-permute-start | bytes 516104 | tf_op jit(solution)/shard_map/ppermute | solution.py:266
  10.3 6.6 %collective-permute-start.3 = (s32[168,256]{1,0:T(8,128)S(1)}, s32[168,256]{1,0:T(8,128)S(1)}, u32[]{:S(2)}, u32[]{:S(2)}) collective-permute-start(s32[168,256]{1,0:T(8,128)S(1)} %collective-permute-done.outer_ref.refs_4_), channel_id=1, source_target_pairs={{0,4},{4,0},{8,12},{12,8},{1,5},{5,1},{9,13},{13,9},{2,6},{6,2},{1... | collective-permute-start | bytes 516104 | tf_op jit(solution)/shard_map/ppermute | solution.py:266
  10.3 9.7 %collective-permute-start.1 = (s32[168,256]{1,0:T(8,128)S(1)}, s32[168,256]{1,0:T(8,128)S(1)}, u32[]{:S(2)}, u32[]{:S(2)}) collective-permute-start(s32[168,256]{1,0:T(8,128)S(1)} %collective-permute-done.outer_ref.refs_4_), channel_id=1, source_target_pairs={{1,2},{2,1},{5,6},{6,5},{9,10},{10,9},{13,14},{14,13},{17,18},{18,... | collective-permute-start | bytes 516104 | tf_op jit(solution)/shard_map/ppermute | solution.py:274
  11.0 9.1 %collective-permute-start.6 = (s32[168,256]{1,0:T(8,128)S(1)}, s32[168,256]{1,0:T(8,128)S(1)}, u32[]{:S(2)}, u32[]{:S(2)}) collective-permute-start(s32[168,256]{1,0:T(8,128)S(1)} %collective-permute-done.5.refs_3_), channel_id=1, source_target_pairs={{0,4},{4,0},{8,12},{12,8},{1,5},{5,1},{9,13},{13,9},{2,6},{6,2},{1... | collective-permute-start | bytes 516104 | tf_op jit(solution)/shard_map/ppermute | solution.py:266
  12.5 10.7 %collective-permute-start.8 = (s32[168,256]{1,0:T(8,128)S(1)}, s32[168,256]{1,0:T(8,128)S(1)}, u32[]{:S(2)}, u32[]{:S(2)}) collective-permute-start(s32[168,256]{1,0:T(8,128)S(1)} %collective-permute-done.7.refs_5_), channel_id=1, source_target_pairs={{0,4},{4,0},{8,12},{12,8},{1,5},{5,1},{9,13},{13,9},{2,6},{6,2},{1... | collective-permute-start | bytes 516104 | tf_op jit(solution)/shard_map/ppermute | solution.py:266
  12.5 9.2 %collective-permute-start.13 = (s32[168,256]{1,0:T(8,128)S(1)}, s32[168,256]{1,0:T(8,128)S(1)}, u32[]{:S(2)}, u32[]{:S(2)}) collective-permute-start(s32[168,256]{1,0:T(8,128)S(1)} %collective-permute-done.7.refs_5_), channel_id=1, source_target_pairs={{0,1},{1,0},{2,3},{3,2},{4,5},{5,4},{6,7},{7,6},{8,9},{9,8},{10,11... | collective-permute-start | bytes 516104 | tf_op jit(solution)/shard_map/ppermute | solution.py:266
  17.0 6.2 %collective-permute-start.11 = (s32[168,256]{1,0:T(8,128)S(1)}, s32[168,256]{1,0:T(8,128)S(1)}, u32[]{:S(2)}, u32[]{:S(2)}) collective-permute-start(s32[168,256]{1,0:T(8,128)S(1)} %collective-permute-done.5.refs_3_), channel_id=1, source_target_pairs={{0,8},{4,12},{8,0},{12,4},{1,9},{5,13},{9,1},{13,5},{2,10},{6,14},... | collective-permute-start | bytes 516104 | tf_op jit(solution)/shard_map/ppermute | solution.py:266
  20.0 4.7 %collective-permute-start.9 = (s32[168,256]{1,0:T(8,128)S(1)}, s32[168,256]{1,0:T(8,128)S(1)}, u32[]{:S(2)}, u32[]{:S(2)}) collective-permute-start(s32[168,256]{1,0:T(8,128)S(1)} %collective-permute-done.1.refs_3_), channel_id=1, source_target_pairs={{0,4},{4,0},{8,12},{12,8},{1,5},{5,1},{9,13},{13,9},{2,6},{6,2},{1... | collective-permute-start | bytes 516104 | tf_op jit(solution)/shard_map/ppermute | solution.py:266
  20.1 6.8 %collective-permute-start.4 = (s32[168,256]{1,0:T(8,128)S(1)}, s32[168,256]{1,0:T(8,128)S(1)}, u32[]{:S(2)}, u32[]{:S(2)}) collective-permute-start(s32[168,256]{1,0:T(8,128)S(1)} %collective-permute-done.1.refs_3_), channel_id=1, source_target_pairs={{0,8},{4,12},{8,0},{12,4},{1,9},{5,13},{9,1},{13,5},{2,10},{6,14},... | collective-permute-start | bytes 516104 | tf_op jit(solution)/shard_map/ppermute | solution.py:266
  21.7 5.7 %collective-permute-start.14 = (s32[168,256]{1,0:T(8,128)S(1)}, s32[168,256]{1,0:T(8,128)S(1)}, u32[]{:S(2)}, u32[]{:S(2)}) collective-permute-start(s32[168,256]{1,0:T(8,128)S(1)} %collective-permute-done.13.refs_3_), channel_id=1, source_target_pairs={{0,4},{4,0},{8,12},{12,8},{1,5},{5,1},{9,13},{13,9},{2,6},{6,2},{1... | collective-permute-start | bytes 516104 | tf_op jit(solution)/shard_map/ppermute | solution.py:266
  23.2 5.1 %collective-permute-start.12 = (s32[168,256]{1,0:T(8,128)S(1)}, s32[168,256]{1,0:T(8,128)S(1)}, u32[]{:S(2)}, u32[]{:S(2)}) collective-permute-start(s32[168,256]{1,0:T(8,128)S(1)} %collective-permute-done.11.refs_3_), channel_id=1, source_target_pairs={{0,4},{4,0},{8,12},{12,8},{1,5},{5,1},{9,13},{13,9},{2,6},{6,2},{1... | collective-permute-start | bytes 516104 | tf_op jit(solution)/shard_map/ppermute | solution.py:266
  26.9 2.2 %collective-permute-start.10 = (s32[168,256]{1,0:T(8,128)S(1)}, s32[168,256]{1,0:T(8,128)S(1)}, u32[]{:S(2)}, u32[]{:S(2)}) collective-permute-start(s32[168,256]{1,0:T(8,128)S(1)} %collective-permute-done.4.refs_3_), channel_id=1, source_target_pairs={{0,4},{4,0},{8,12},{12,8},{1,5},{5,1},{9,13},{13,9},{2,6},{6,2},{1... | collective-permute-start | bytes 516104 | tf_op jit(solution)/shard_map/ppermute | solution.py:266
  30.4 3.4 %collective-permute-start.18 = (f32[64,512]{1,0:T(8,128)S(1)}, f32[64,512]{1,0:T(8,128)S(1)}, u32[]{:S(2)}, u32[]{:S(2)}) collective-permute-start(f32[64,512]{1,0:T(8,128)S(1)} %get-tuple-element.47.refs_0_.refs_1_), channel_id=1, source_target_pairs={{1,2},{2,1},{5,6},{6,5},{9,10},{10,9},{13,14},{14,13},{17,18},{18,... | collective-permute-start | bytes 393224 | tf_op jit(solution)/shard_map/ppermute | solution.py:274
  31.1 6.0 %collective-permute-start.20 = (f32[64,512]{1,0:T(8,128)S(1)}, f32[64,512]{1,0:T(8,128)S(1)}, u32[]{:S(2)}, u32[]{:S(2)}) collective-permute-start(f32[64,512]{1,0:T(8,128)S(1)} %get-tuple-element.47.refs_0_.refs_1_), channel_id=1, source_target_pairs={{0,8},{4,12},{8,0},{12,4},{1,9},{5,13},{9,1},{13,5},{2,10},{6,14},... | collective-permute-start | bytes 393224 | tf_op jit(solution)/shard_map/ppermute | solution.py:266
  32.8 4.2 %collective-permute-start.15 = (f32[64,512]{1,0:T(8,128)S(1)}, f32[64,512]{1,0:T(8,128)S(1)}, u32[]{:S(2)}, u32[]{:S(2)}) collective-permute-start(f32[64,512]{1,0:T(8,128)S(1)} %get-tuple-element.47.refs_0_.refs_1_), channel_id=1, source_target_pairs={{1,10},{2,9},{5,14},{6,13},{9,2},{10,1},{13,6},{14,5},{17,26},{18,... | collective-permute-start | bytes 393224 | tf_op jit(solution)/shard_map/ppermute | solution.py:278
  33.7 3.9 %collective-permute-start.17 = (f32[64,512]{1,0:T(8,128)S(1)}, f32[64,512]{1,0:T(8,128)S(1)}, u32[]{:S(2)}, u32[]{:S(2)}) collective-permute-start(f32[64,512]{1,0:T(8,128)S(1)} %get-tuple-element.47.refs_0_.refs_1_), channel_id=1, source_target_pairs={{0,4},{4,0},{8,12},{12,8},{1,5},{5,1},{9,13},{13,9},{2,6},{6,2},{1... | collective-permute-start | bytes 393224 | tf_op jit(solution)/shard_map/ppermute | solution.py:266
  33.8 3.8 %collective-permute-start.19 = (f32[64,512]{1,0:T(8,128)S(1)}, f32[64,512]{1,0:T(8,128)S(1)}, u32[]{:S(2)}, u32[]{:S(2)}) collective-permute-start(f32[64,512]{1,0:T(8,128)S(1)} %collective-permute-done.18.refs_3_), channel_id=1, source_target_pairs={{0,4},{4,0},{8,12},{12,8},{1,5},{5,1},{9,13},{13,9},{2,6},{6,2},{1... | collective-permute-start | bytes 393224 | tf_op jit(solution)/shard_map/ppermute | solution.py:266
  37.0 1.3 %collective-permute-start.21 = (f32[64,512]{1,0:T(8,128)S(1)}, f32[64,512]{1,0:T(8,128)S(1)}, u32[]{:S(2)}, u32[]{:S(2)}) collective-permute-start(f32[64,512]{1,0:T(8,128)S(1)} %collective-permute-done.20.refs_5_), channel_id=1, source_target_pairs={{0,4},{4,0},{8,12},{12,8},{1,5},{5,1},{9,13},{13,9},{2,6},{6,2},{1... | collective-permute-start | bytes 393224 | tf_op jit(solution)/shard_map/ppermute | solution.py:266
  37.0 2.1 %collective-permute-start.16 = (f32[64,512]{1,0:T(8,128)S(1)}, f32[64,512]{1,0:T(8,128)S(1)}, u32[]{:S(2)}, u32[]{:S(2)}) collective-permute-start(f32[64,512]{1,0:T(8,128)S(1)} %collective-permute-done.15.refs_1_), channel_id=1, source_target_pairs={{0,4},{4,0},{8,12},{12,8},{1,5},{5,1},{9,13},{13,9},{2,6},{6,2},{1... | collective-permute-start | bytes 393224 | tf_op jit(solution)/shard_map/ppermute | solution.py:266
  43.5 16.3 %collective-permute-start.27 = (f32[64,256]{1,0:T(8,128)S(1)}, f32[64,256]{1,0:T(8,128)S(1)}, u32[]{:S(2)}, u32[]{:S(2)}) collective-permute-start(f32[64,256]{1,0:T(8,128)S(1)} %get-tuple-element.54), channel_id=1, source_target_pairs={{0,1},{1,0},{2,3},{3,2},{4,5},{5,4},{6,7},{7,6},{8,9},{9,8},{10,11... | collective-permute-start | bytes 196616 | tf_op jit(solution)/shard_map/ppermute | solution.py:266
  49.9 1.2 %collective-permute-start.22 = (f32[40,128]{1,0:T(8,128)S(1)}, f32[40,128]{1,0:T(8,128)S(1)}, u32[]{:S(2)}, u32[]{:S(2)}) collective-permute-start(f32[40,128]{1,0:T(8,128)S(1)} %get-tuple-element.52.a_ref), channel_id=1, source_target_pairs={{0,4},{4,0},{8,12},{12,8},{1,5},{5,1},{9,13},{13,9},{2,6},{6,2},{1... | collective-permute-start | bytes 61448 | tf_op jit(solution)/shard_map/ppermute | solution.py:266
  51.2 3.8 %collective-permute-start.23 = (f32[40,128]{1,0:T(8,128)S(1)}, f32[40,128]{1,0:T(8,128)S(1)}, u32[]{:S(2)}, u32[]{:S(2)}) collective-permute-start(f32[40,128]{1,0:T(8,128)S(1)} %shard_map.48.share_ref), channel_id=1, source_target_pairs={{0,1},{1,0},{2,3},{3,2},{4,5},{5,4},{6,7},{7,6},{8,9},{9,8},{10,11... | collective-permute-start | bytes 61448 | tf_op jit(solution)/shard_map/ppermute | solution.py:266
  51.3 4.7 %collective-permute-start.24 = (f32[40,128]{1,0:T(8,128)S(1)}, f32[40,128]{1,0:T(8,128)S(1)}, u32[]{:S(2)}, u32[]{:S(2)}) collective-permute-start(f32[40,128]{1,0:T(8,128)S(1)} %shard_map.48.share_ref), channel_id=1, source_target_pairs={{0,2},{1,3},{2,0},{3,1},{4,6},{5,7},{6,4},{7,5},{8,10},{9,11},{10,... | collective-permute-start | bytes 61448 | tf_op jit(solution)/shard_map/ppermute | solution.py:266
  53.1 2.9 %collective-permute-start.25 = (f32[40,128]{1,0:T(8,128)S(1)}, f32[40,128]{1,0:T(8,128)S(1)}, u32[]{:S(2)}, u32[]{:S(2)}) collective-permute-start(f32[40,128]{1,0:T(8,128)S(1)} %shard_map.48.share_ref), channel_id=1, source_target_pairs={{1,2},{2,1},{5,6},{6,5},{9,10},{10,9},{13,14},{14,13},{17,18},{18,... | collective-permute-start | bytes 61448 | tf_op jit(solution)/shard_map/ppermute | solution.py:274
  56.1 3.8 %collective-permute-start.26 = (f32[40,128]{1,0:T(8,128)S(1)}, f32[40,128]{1,0:T(8,128)S(1)}, u32[]{:S(2)}, u32[]{:S(2)}) collective-permute-start(f32[40,128]{1,0:T(8,128)S(1)} %shard_map.49.share_ref), channel_id=1, source_target_pairs={{0,8},{4,12},{8,0},{12,4},{1,9},{5,13},{9,1},{13,5},{2,10},{6,14},... | collective-permute-start | bytes 61448 | tf_op jit(solution)/shard_map/ppermute | solution.py:266

commit v8 on v7

--- a/solution.py
+++ b/solution.py
@@ -271,11 +271,11 @@
 
 
 def middle(value):
-    return lax.ppermute(value, "col", MIDDLE)
+    return lax.ppermute(value, ("row", "col"), [(4 * r + c, 4 * (r ^ 0) + 3 - c) if c in (1, 2) else (4 * r + c, 4 * (r ^ 1) + c) for r in range(4) for c in range(4)])
 
 
 def diagonal(value):
-    return lax.ppermute(value, ("row", "col"), [(4 * r + c, 4 * (r ^ 2) + 3 - c) for r in range(4) for c in (1, 2)])
+    return lax.ppermute(value, ("row", "col"), [(4 * r + c, 4 * (r ^ 2) + 3 - c) if c in (1, 2) else (4 * r + c, 4 * (r ^ 1) + c) for r in range(4) for c in range(4)])
 
 
 MIDDLE = [(1, 2), (2, 1)]

time: 62.7 us -> 58.4 us (0.931)
  starting transfers between devices: 27 us -> 21 us
  waiting for transfers between devices: 16.4 us -> 18.3 us
    ppermute x23, starting transfers between devices: 23.6 us -> 20 us  [exchange(): lax.ppermute(value, axis, [(i, i ^ offset) for i in range(size)])]
    ppermute x5, starting transfers between devices: 3.48 us -> 1.09 us  [the longest x4 1.09 us: middle(): lax.ppermute(value, ('row', 'col'), [(4 * r + c, 4 * (r ^ 0) + 3 - c) if...]
    ppermute x23, waiting for transfers between devices: 16.4 us -> 18.3 us  [exchange(): lax.ppermute(value, axis, [(i, i ^ offset) for i in range(size)])]
  transfers between devices with their start and end apart: 28 -> 28, of which waited for: 11 -> 11; matrix products, arithmetic and copies ran while one was open for 0% -> 0% of each run, Pallas kernels for 12% -> 13%
where the time goes in v8:
time: 58.4 us; the launch traced here: 58.3 us
  starting transfers between devices  21 us (36%)
  waiting for transfers between devices  18.3 us (31%)
  Pallas kernels  16.1 us (28%)
  local copies, waits for them, and re-layouts  1.74 us (3%)
  other arithmetic  0.89 us (2%)
    ppermute x23, starting transfers between devices, exchange(): lax.ppermute(value, axis, [(i, i ^ offset) for i in range(size)])  20 us
    ppermute x23, waiting for transfers between devices, exchange(): lax.ppermute(value, axis, [(i, i ^ offset) for i in range(size)])  18.3 us
    pallas_call x14, Pallas kernels, call(): pl.pallas_call(kernel, out_shape=out_shape, in_specs=in_specs or [VMEM] *...  16.1 us
  transfers between devices with their start and end apart: 28, of which 11 were waited for; matrix products, arithmetic and copies ran while one was open for 0% of the time, Pallas kernels for 13%

profile of v8, /device:TPU:0, one launch (start us, length us, event | category | flops | bytes accessed | tf_op | source)
XLA Modules:
  0.0 58.3 jit_solution(7969247343247484704)
XLA Ops:
  0.0 0.8 %pad_clamp_fusion = s32[1024]{0:T(1024)S(1)} fusion(s32[256]{0:T(256)} %param.4), kind=kLoop, calls=%fused_computation.6 | loop fusion | flops 1024 | bytes 5120 | tf_op jit(solution)/shard_map/gather | solution.py:291
  0.8 0.8 %copy-done = f32[2048,256]{1,0:T(8,128)S(1)} copy-done((f32[2048,256]{1,0:T(8,128)S(1)}, f32[2048,256]{1,0:T(8,128)}, u32[]{:S(2)}) %copy-start) | copy-done | bytes 2097176
  1.6 1.0 %gather_fusion = f32[256,256]{1,0:T(8,128)S(1)} fusion(f32[2048,256]{1,0:T(8,128)S(1)} %copy-done, s32[1024]{0:T(1024)S(1)} %pad_clamp_fusion), kind=kCustom, calls=%fused_computation | custom fusion | bytes 525312 | tf_op jit(solution)/shard_map/gather | solution.py:291
  2.6 0.2 shard_map.37
  2.9 3.1 %collective-permute-start = (s32[168,256]{1,0:T(8,128)S(1)}, s32[168,256]{1,0:T(8,128)S(1)}, u32[]{:S(2)}, u32[]{:S(2)}) collective-permute-start(s32[168,256]{1,0:T(8,128)S(1)} %pad_add_fusion.own_ref.refs_3_), channel_id=1, source_target_pairs={{0,1},{1,0},{2,3},{3,2},{4,5},{5,4},{6,7},{7,6},{8,9},{9,8},{10,11... | collective-permute-start | bytes 516104 | tf_op jit(solution)/shard_map/ppermute | solution.py:266
  5.9 0.0 collective-permute-start.5
  6.0 1.5 %collective-permute-start.7 = (s32[168,256]{1,0:T(8,128)S(1)}, s32[168,256]{1,0:T(8,128)S(1)}, u32[]{:S(2)}, u32[]{:S(2)}) collective-permute-start(s32[168,256]{1,0:T(8,128)S(1)} %pad_add_fusion.own_ref.refs_3_), channel_id=1, source_target_pairs={{0,8},{4,12},{8,0},{12,4},{1,9},{5,13},{9,1},{13,5},{2,10},{6,14},... | collective-permute-start | bytes 516104 | tf_op jit(solution)/shard_map/ppermute | solution.py:266
  7.4 0.2 collective-permute-start.2
  7.7 2.7 %collective-permute-done.outer_ref.refs_4_ = s32[168,256]{1,0:T(8,128)S(1)} collective-permute-done((s32[168,256]{1,0:T(8,128)S(1)}, s32[168,256]{1,0:T(8,128)S(1)}, u32[]{:S(2)}, u32[]{:S(2)}) %collective-permute-start) | collective-permute-done | bytes 172064 | tf_op jit(solution)/shard_map/ppermute | solution.py:266
  10.3 0.0 collective-permute-start.3
  10.3 0.5 collective-permute-start.1
  10.8 0.0 collective-permute-done.5.refs_3_
  10.8 0.0 collective-permute-start.6
  10.8 0.7 %shard_map.38 = (bf16[512,256]{1,0:T(8,128)(2,1)S(1)}, bf16[512,256]{1,0:T(8,128)(2,1)S(1)}, f32[1,512]{1,0:T(1,128)S(1)}) custom-call(s32[168,256]{1,0:T(8,128)S(1)} %pad_add_fusion.own_ref.refs_3_, s32[168,256]{1,0:T(8,128)S(1)} %collective-permute-done.outer_ref.refs_4_), custom_call_target="tpu_custom_call" | custom-call | tf_op jit(solution)/shard_map/pallas_call | solution.py:252
  11.6 1.2 %collective-permute-done.7.refs_5_ = s32[168,256]{1,0:T(8,128)S(1)} collective-permute-done((s32[168,256]{1,0:T(8,128)S(1)}, s32[168,256]{1,0:T(8,128)S(1)}, u32[]{:S(2)}, u32[]{:S(2)}) %collective-permute-start.7) | collective-permute-done | bytes 172064 | tf_op jit(solution)/shard_map/ppermute | solution.py:266
  12.7 0.0 collective-permute-start.8
  12.7 0.0 collective-permute-done.2.refs_5_
  12.7 2.2 %collective-permute-start.13 = (s32[168,256]{1,0:T(8,128)S(1)}, s32[168,256]{1,0:T(8,128)S(1)}, u32[]{:S(2)}, u32[]{:S(2)}) collective-permute-start(s32[168,256]{1,0:T(8,128)S(1)} %collective-permute-done.7.refs_5_), channel_id=1, source_target_pairs={{0,1},{1,0},{2,3},{3,2},{4,5},{5,4},{6,7},{7,6},{8,9},{9,8},{10,11... | collective-permute-start | bytes 516104 | tf_op jit(solution)/shard_map/ppermute | solution.py:266
  15.0 0.0 collective-permute-done.3.refs_6_
  15.0 1.5 %collective-permute-start.11 = (s32[168,256]{1,0:T(8,128)S(1)}, s32[168,256]{1,0:T(8,128)S(1)}, u32[]{:S(2)}, u32[]{:S(2)}) collective-permute-start(s32[168,256]{1,0:T(8,128)S(1)} %collective-permute-done.5.refs_3_), channel_id=1, source_target_pairs={{0,8},{4,12},{8,0},{12,4},{1,9},{5,13},{9,1},{13,5},{2,10},{6,14},... | collective-permute-start | bytes 516104 | tf_op jit(solution)/shard_map/ppermute | solution.py:266
  16.5 1.5 %shard_map.39 = (bf16[1024,512]{1,0:T(8,128)(2,1)S(1)}, f32[64,1024]{1,0:T(8,128)S(1)}) custom-call(bf16[512,256]{1,0:T(8,128)(2,1)S(1)} %get-tuple-element.30.refs_0_, bf16[512,256]{1,0:T(8,128)(2,1)S(1)} %get-tuple-element.31.refs_1_, f32[1,512]{1,0:T(1,128)S(1)} %get-tuple-element.32.refs_2_, s32[168,256]{1,0:T(8,128)S(1)} %pad_add_fusion.own_ref.refs_3_, ...), custom_call_target="tpu_custom_call" | custom-call | tf_op jit(solution)/shard_map/pallas_call | solution.py:252
  18.0 0.0 collective-permute-done.1.refs_3_
  18.0 0.1 collective-permute-start.9
  18.1 0.0 collective-permute-done.6.refs_4_
  18.1 0.6 %collective-permute-start.4 = (s32[168,256]{1,0:T(8,128)S(1)}, s32[168,256]{1,0:T(8,128)S(1)}, u32[]{:S(2)}, u32[]{:S(2)}) collective-permute-start(s32[168,256]{1,0:T(8,128)S(1)} %collective-permute-done.1.refs_3_), channel_id=1, source_target_pairs={{0,8},{4,12},{8,0},{12,4},{1,9},{5,13},{9,1},{13,5},{2,10},{6,14},... | collective-permute-start | bytes 516104 | tf_op jit(solution)/shard_map/ppermute | solution.py:266
  18.7 1.0 %collective-permute-done.13.refs_3_ = s32[168,256]{1,0:T(8,128)S(1)} collective-permute-done((s32[168,256]{1,0:T(8,128)S(1)}, s32[168,256]{1,0:T(8,128)S(1)}, u32[]{:S(2)}, u32[]{:S(2)}) %collective-permute-start.13) | collective-permute-done | bytes 172064 | tf_op jit(solution)/shard_map/ppermute | solution.py:266
  19.7 1.5 %collective-permute-done.11.refs_3_ = s32[168,256]{1,0:T(8,128)S(1)} collective-permute-done((s32[168,256]{1,0:T(8,128)S(1)}, s32[168,256]{1,0:T(8,128)S(1)}, u32[]{:S(2)}, u32[]{:S(2)}) %collective-permute-start.11) | collective-permute-done | bytes 172064 | tf_op jit(solution)/shard_map/ppermute | solution.py:266
  21.2 1.5 %shard_map.40 = (bf16[1024,512]{1,0:T(8,128)(2,1)S(1)}, f32[64,1024]{1,0:T(8,128)S(1)}) custom-call(bf16[512,256]{1,0:T(8,128)(2,1)S(1)} %get-tuple-element.30.refs_0_, bf16[512,256]{1,0:T(8,128)(2,1)S(1)} %get-tuple-element.31.refs_1_, f32[1,512]{1,0:T(1,128)S(1)} %get-tuple-element.32.refs_2_, s32[168,256]{1,0:T(8,128)S(1)} %collective-permute-done.5.refs_3_, ...), custom_call_target="tpu_custom_call" | custom-call | tf_op jit(solution)/shard_map/pallas_call | solution.py:252
  22.8 0.0 collective-permute-done.9.refs_4_
  22.8 0.8 %shard_map.41 = (bf16[512,512]{1,0:T(8,128)(2,1)S(1)}, f32[64,512]{1,0:T(8,128)S(1)}) custom-call(bf16[512,256]{1,0:T(8,128)(2,1)S(1)} %get-tuple-element.30.refs_0_, bf16[512,256]{1,0:T(8,128)(2,1)S(1)} %get-tuple-element.31.refs_1_, f32[1,512]{1,0:T(1,128)S(1)} %get-tuple-element.32.refs_2_, s32[168,256]{1,0:T(8,128)S(1)} %collective-permute-done.1.refs_3_, ...), custom_call_target="tpu_custom_call" | custom-call | tf_op jit(solution)/shard_map/pallas_call | solution.py:252
  23.6 1.3 %collective-permute-done.4.refs_3_ = s32[168,256]{1,0:T(8,128)S(1)} collective-permute-done((s32[168,256]{1,0:T(8,128)S(1)}, s32[168,256]{1,0:T(8,128)S(1)}, u32[]{:S(2)}, u32[]{:S(2)}) %collective-permute-start.4) | collective-permute-done | bytes 172064 | tf_op jit(solution)/shard_map/ppermute | solution.py:266
  24.9 0.0 collective-permute-start.10
  24.9 0.5 shard_map.44
  25.4 0.8 %shard_map.43 = (bf16[512,512]{1,0:T(8,128)(2,1)S(1)}, f32[64,512]{1,0:T(8,128)S(1)}) custom-call(bf16[512,256]{1,0:T(8,128)(2,1)S(1)} %get-tuple-element.30.refs_0_, bf16[512,256]{1,0:T(8,128)(2,1)S(1)} %get-tuple-element.31.refs_1_, f32[1,512]{1,0:T(1,128)S(1)} %get-tuple-element.32.refs_2_, s32[168,256]{1,0:T(8,128)S(1)} %collective-permute-done.13.refs_3_, ...), custom_call_target="tpu_custom_call" | custom-call | tf_op jit(solution)/shard_map/pallas_call | solution.py:252
  26.3 0.0 collective-permute-done.12.refs_4_
  26.3 0.8 %shard_map.42 = (bf16[512,512]{1,0:T(8,128)(2,1)S(1)}, f32[64,512]{1,0:T(8,128)S(1)}) custom-call(bf16[512,256]{1,0:T(8,128)(2,1)S(1)} %get-tuple-element.30.refs_0_, bf16[512,256]{1,0:T(8,128)(2,1)S(1)} %get-tuple-element.31.refs_1_, f32[1,512]{1,0:T(1,128)S(1)} %get-tuple-element.32.refs_2_, s32[168,256]{1,0:T(8,128)S(1)} %collective-permute-done.11.refs_3_, ...), custom_call_target="tpu_custom_call" | custom-call | tf_op jit(solution)/shard_map/pallas_call | solution.py:252
  27.1 1.3 %shard_map.45 = (f32[64,512]{1,0:T(8,128)S(1)}, bf16[256,512]{1,0:T(8,128)(2,1)S(1)}) custom-call(bf16[512,256]{1,0:T(8,128)(2,1)S(1)} %get-tuple-element.30.refs_0_, bf16[512,256]{1,0:T(8,128)(2,1)S(1)} %get-tuple-element.31.refs_1_, f32[1,512]{1,0:T(1,128)S(1)} %get-tuple-element.32.refs_2_, s32[168,256]{1,0:T(8,128)S(1)} %collective-permute-done.10.refs_3_, ...), custom_call_target="tpu_custom_call" | custom-call | tf_op jit(solution)/shard_map/pallas_call | solution.py:252
  28.4 0.6 collective-permute-start.18
  29.0 1.5 %collective-permute-start.20 = (f32[64,512]{1,0:T(8,128)S(1)}, f32[64,512]{1,0:T(8,128)S(1)}, u32[]{:S(2)}, u32[]{:S(2)}) collective-permute-start(f32[64,512]{1,0:T(8,128)S(1)} %get-tuple-element.47.refs_0_.refs_1_), channel_id=1, source_target_pairs={{0,8},{4,12},{8,0},{12,4},{1,9},{5,13},{9,1},{13,5},{2,10},{6,14},... | collective-permute-start | bytes 393224 | tf_op jit(solution)/shard_map/ppermute | solution.py:266
  30.5 0.5 collective-permute-start.17
  31.0 0.0 collective-permute-done.18.refs_3_
  31.0 0.0 collective-permute-start.19
  31.0 3.5 %collective-permute-done.20.refs_5_ = f32[64,512]{1,0:T(8,128)S(1)} collective-permute-done((f32[64,512]{1,0:T(8,128)S(1)}, f32[64,512]{1,0:T(8,128)S(1)}, u32[]{:S(2)}, u32[]{:S(2)}) %collective-permute-start.20) | collective-permute-done | bytes 131104 | tf_op jit(solution)/shard_map/ppermute | solution.py:266
  34.5 0.0 collective-permute-start.21
  34.5 0.0 collective-permute-done.15.refs_1_
  34.5 0.5 collective-permute-start.16
  35.0 0.0 collective-permute-done.17.refs_2_
  35.0 0.0 collective-permute-done.19.refs_4_
  35.0 0.8 %collective-permute-done.21.refs_6_ = f32[64,512]{1,0:T(8,128)S(1)} collective-permute-done((f32[64,512]{1,0:T(8,128)S(1)}, f32[64,512]{1,0:T(8,128)S(1)}, u32[]{:S(2)}, u32[]{:S(2)}) %collective-permute-start.21) | collective-permute-done | bytes 131104 | tf_op jit(solution)/shard_map/ppermute | solution.py:266
  35.8 0.8 %shard_map.46 = (bf16[192,3072]{1,0:T(8,128)(2,1)S(1)}, f32[64,64]{1,0:T(8,128)S(1)}, f32[64,128]{1,0:T(8,128)S(1)}) custom-call(f32[64,512]{1,0:T(8,128)S(1)} %get-tuple-element.47.refs_0_.refs_1_, f32[64,512]{1,0:T(8,128)S(1)} %get-tuple-element.47.refs_0_.refs_1_, f32[64,512]{1,0:T(8,128)S(1)} %collective-permute-done.17.refs_2_, ...), custom_call_target="tpu_custom_call" | custom-call | tf_op jit(solution)/shard_map/pallas_call | solution.py:252
  36.6 4.3 %shard_map.47 = (f32[64,256]{1,0:T(8,128)S(1)}, f32[64,256]{1,0:T(8,128)S(1)}, f32[40,128]{1,0:T(8,128)S(1)}) custom-call(f32[64,512]{1,0:T(8,128)S(1)} %get-tuple-element.47.refs_0_.refs_1_, f32[64,512]{1,0:T(8,128)S(1)} %collective-permute-done.15.refs_1_, f32[64,512]{1,0:T(8,128)S(1)} %collective-permute-done.16.refs_2_, ...), custom_call_target="tpu_custom_call" | custom-call | tf_op jit(solution)/shard_map/pallas_call | solution.py:252
  40.9 4.8 %collective-permute-start.27 = (f32[64,256]{1,0:T(8,128)S(1)}, f32[64,256]{1,0:T(8,128)S(1)}, u32[]{:S(2)}, u32[]{:S(2)}) collective-permute-start(f32[64,256]{1,0:T(8,128)S(1)} %get-tuple-element.54), channel_id=1, source_target_pairs={{0,1},{1,0},{2,3},{3,2},{4,5},{5,4},{6,7},{7,6},{8,9},{9,8},{10,11... | collective-permute-start | bytes 196616 | tf_op jit(solution)/shard_map/ppermute | solution.py:266
  45.8 0.0 collective-permute-start.22
  45.8 1.2 %collective-permute-done.22.b_ref = f32[40,128]{1,0:T(8,128)S(1)} collective-permute-done((f32[40,128]{1,0:T(8,128)S(1)}, f32[40,128]{1,0:T(8,128)S(1)}, u32[]{:S(2)}, u32[]{:S(2)}) %collective-permute-start.22) | collective-permute-done | bytes 20512 | tf_op jit(solution)/shard_map/ppermute | solution.py:266
  47.0 0.1 shard_map.48.share_ref
  47.0 0.1 collective-permute-start.23
  47.1 1.8 %collective-permute-start.24 = (f32[40,128]{1,0:T(8,128)S(1)}, f32[40,128]{1,0:T(8,128)S(1)}, u32[]{:S(2)}, u32[]{:S(2)}) collective-permute-start(f32[40,128]{1,0:T(8,128)S(1)} %shard_map.48.share_ref), channel_id=1, source_target_pairs={{0,2},{1,3},{2,0},{3,1},{4,6},{5,7},{6,4},{7,5},{8,10},{9,11},{10,... | collective-permute-start | bytes 61448 | tf_op jit(solution)/shard_map/ppermute | solution.py:266
  48.9 1.9 %collective-permute-done.23.near_ref = f32[40,128]{1,0:T(8,128)S(1)} collective-permute-done((f32[40,128]{1,0:T(8,128)S(1)}, f32[40,128]{1,0:T(8,128)S(1)}, u32[]{:S(2)}, u32[]{:S(2)}) %collective-permute-start.23) | collective-permute-done | bytes 20512 | tf_op jit(solution)/shard_map/ppermute | solution.py:266
  50.8 1.0 %collective-permute-done.24.far_ref = f32[40,128]{1,0:T(8,128)S(1)} collective-permute-done((f32[40,128]{1,0:T(8,128)S(1)}, f32[40,128]{1,0:T(8,128)S(1)}, u32[]{:S(2)}, u32[]{:S(2)}) %collective-permute-start.24) | collective-permute-done | bytes 20512 | tf_op jit(solution)/shard_map/ppermute | solution.py:266
  51.8 0.0 collective-permute-done.25.across_ref
  51.8 0.1 shard_map.49.share_ref
  51.9 1.5 %collective-permute-start.26 = (f32[40,128]{1,0:T(8,128)S(1)}, f32[40,128]{1,0:T(8,128)S(1)}, u32[]{:S(2)}, u32[]{:S(2)}) collective-permute-start(f32[40,128]{1,0:T(8,128)S(1)} %shard_map.49.share_ref), channel_id=1, source_target_pairs={{0,8},{4,12},{8,0},{12,4},{1,9},{5,13},{9,1},{13,5},{2,10},{6,14},... | collective-permute-start | bytes 61448 | tf_op jit(solution)/shard_map/ppermute | solution.py:266
  53.4 2.3 %collective-permute-done.26.beside_ref = f32[40,128]{1,0:T(8,128)S(1)} collective-permute-done((f32[40,128]{1,0:T(8,128)S(1)}, f32[40,128]{1,0:T(8,128)S(1)}, u32[]{:S(2)}, u32[]{:S(2)}) %collective-permute-start.26) | collective-permute-done | bytes 20512 | tf_op jit(solution)/shard_map/ppermute | solution.py:266
  55.7 2.6 %shard_map.50 = f32[64,256]{1,0:T(8,128)} custom-call(s32[1]{0:T(128)} %bitcast.outer_ref, f32[40,128]{1,0:T(8,128)S(1)} %shard_map.49.share_ref, f32[40,128]{1,0:T(8,128)S(1)} %collective-permute-done.26.beside_ref, f32[64,256]{1,0:T(8,128)S(1)} %get-tuple-element.53.own_ref, f32[64,256]{1,0:T(8,128)S(1)} %collective-permute-done.27.given_ref), custom_call_target="tpu_custom_call" | custom-call | tf_op jit(solution)/shard_map/pallas_call | solution.py:252
  (15 shorter events, 0.1 us)
Async XLA Ops:
  0.0 1.6 %copy-start = (f32[2048,256]{1,0:T(8,128)S(1)}, f32[2048,256]{1,0:T(8,128)}, u32[]{:S(2)}) copy-start(f32[2048,256]{1,0:T(8,128)} %param.3) | copy-start | bytes 6291460
  0.0 2.6 %copy-start.1 = (f32[64,256]{1,0:T(8,128)S(1)}, f32[64,256]{1,0:T(8,128)}, u32[]{:S(2)}) copy-start(f32[64,256]{1,0:T(8,128)} %initial_ref.1) | copy-start | bytes 196612
  2.9 7.5 %collective-permute-start = (s32[168,256]{1,0:T(8,128)S(1)}, s32[168,256]{1,0:T(8,128)S(1)}, u32[]{:S(2)}, u32[]{:S(2)}) collective-permute-start(s32[168,256]{1,0:T(8,128)S(1)} %pad_add_fusion.own_ref.refs_3_), channel_id=1, source_target_pairs={{0,1},{1,0},{2,3},{3,2},{4,5},{5,4},{6,7},{7,6},{8,9},{9,8},{10,11... | collective-permute-start | bytes 516104 | tf_op jit(solution)/shard_map/ppermute | solution.py:266
  5.9 4.9 %collective-permute-start.5 = (s32[168,256]{1,0:T(8,128)S(1)}, s32[168,256]{1,0:T(8,128)S(1)}, u32[]{:S(2)}, u32[]{:S(2)}) collective-permute-start(s32[168,256]{1,0:T(8,128)S(1)} %pad_add_fusion.own_ref.refs_3_), channel_id=1, source_target_pairs={{0,4},{1,2},{2,1},{3,7},{4,0},{5,6},{6,5},{7,3},{8,12},{9,10},{10,... | collective-permute-start | bytes 516104 | tf_op jit(solution)/shard_map/ppermute | solution.py:274
  6.0 6.8 %collective-permute-start.7 = (s32[168,256]{1,0:T(8,128)S(1)}, s32[168,256]{1,0:T(8,128)S(1)}, u32[]{:S(2)}, u32[]{:S(2)}) collective-permute-start(s32[168,256]{1,0:T(8,128)S(1)} %pad_add_fusion.own_ref.refs_3_), channel_id=1, source_target_pairs={{0,8},{4,12},{8,0},{12,4},{1,9},{5,13},{9,1},{13,5},{2,10},{6,14},... | collective-permute-start | bytes 516104 | tf_op jit(solution)/shard_map/ppermute | solution.py:266
  7.4 5.3 %collective-permute-start.2 = (s32[168,256]{1,0:T(8,128)S(1)}, s32[168,256]{1,0:T(8,128)S(1)}, u32[]{:S(2)}, u32[]{:S(2)}) collective-permute-start(s32[168,256]{1,0:T(8,128)S(1)} %pad_add_fusion.own_ref.refs_3_), channel_id=1, source_target_pairs={{0,4},{4,0},{8,12},{12,8},{1,5},{5,1},{9,13},{13,9},{2,6},{6,2},{1... | collective-permute-start | bytes 516104 | tf_op jit(solution)/shard_map/ppermute | solution.py:266
  10.3 4.7 %collective-permute-start.3 = (s32[168,256]{1,0:T(8,128)S(1)}, s32[168,256]{1,0:T(8,128)S(1)}, u32[]{:S(2)}, u32[]{:S(2)}) collective-permute-start(s32[168,256]{1,0:T(8,128)S(1)} %collective-permute-done.outer_ref.refs_4_), channel_id=1, source_target_pairs={{0,4},{4,0},{8,12},{12,8},{1,5},{5,1},{9,13},{13,9},{2,6},{6,2},{1... | collective-permute-start | bytes 516104 | tf_op jit(solution)/shard_map/ppermute | solution.py:266
  10.3 7.7 %collective-permute-start.1 = (s32[168,256]{1,0:T(8,128)S(1)}, s32[168,256]{1,0:T(8,128)S(1)}, u32[]{:S(2)}, u32[]{:S(2)}) collective-permute-start(s32[168,256]{1,0:T(8,128)S(1)} %collective-permute-done.outer_ref.refs_4_), channel_id=1, source_target_pairs={{0,4},{1,2},{2,1},{3,7},{4,0},{5,6},{6,5},{7,3},{8,12},{9,10},{10,... | collective-permute-start | bytes 516104 | tf_op jit(solution)/shard_map/ppermute | solution.py:274
  10.8 7.3 %collective-permute-start.6 = (s32[168,256]{1,0:T(8,128)S(1)}, s32[168,256]{1,0:T(8,128)S(1)}, u32[]{:S(2)}, u32[]{:S(2)}) collective-permute-start(s32[168,256]{1,0:T(8,128)S(1)} %collective-permute-done.5.refs_3_), channel_id=1, source_target_pairs={{0,4},{4,0},{8,12},{12,8},{1,5},{5,1},{9,13},{13,9},{2,6},{6,2},{1... | collective-permute-start | bytes 516104 | tf_op jit(solution)/shard_map/ppermute | solution.py:266
  12.7 8.5 %collective-permute-start.8 = (s32[168,256]{1,0:T(8,128)S(1)}, s32[168,256]{1,0:T(8,128)S(1)}, u32[]{:S(2)}, u32[]{:S(2)}) collective-permute-start(s32[168,256]{1,0:T(8,128)S(1)} %collective-permute-done.7.refs_5_), channel_id=1, source_target_pairs={{0,4},{4,0},{8,12},{12,8},{1,5},{5,1},{9,13},{13,9},{2,6},{6,2},{1... | collective-permute-start | bytes 516104 | tf_op jit(solution)/shard_map/ppermute | solution.py:266
  12.7 7.0 %collective-permute-start.13 = (s32[168,256]{1,0:T(8,128)S(1)}, s32[168,256]{1,0:T(8,128)S(1)}, u32[]{:S(2)}, u32[]{:S(2)}) collective-permute-start(s32[168,256]{1,0:T(8,128)S(1)} %collective-permute-done.7.refs_5_), channel_id=1, source_target_pairs={{0,1},{1,0},{2,3},{3,2},{4,5},{5,4},{6,7},{7,6},{8,9},{9,8},{10,11... | collective-permute-start | bytes 516104 | tf_op jit(solution)/shard_map/ppermute | solution.py:266
  15.0 6.2 %collective-permute-start.11 = (s32[168,256]{1,0:T(8,128)S(1)}, s32[168,256]{1,0:T(8,128)S(1)}, u32[]{:S(2)}, u32[]{:S(2)}) collective-permute-start(s32[168,256]{1,0:T(8,128)S(1)} %collective-permute-done.5.refs_3_), channel_id=1, source_target_pairs={{0,8},{4,12},{8,0},{12,4},{1,9},{5,13},{9,1},{13,5},{2,10},{6,14},... | collective-permute-start | bytes 516104 | tf_op jit(solution)/shard_map/ppermute | solution.py:266
  18.0 4.7 %collective-permute-start.9 = (s32[168,256]{1,0:T(8,128)S(1)}, s32[168,256]{1,0:T(8,128)S(1)}, u32[]{:S(2)}, u32[]{:S(2)}) collective-permute-start(s32[168,256]{1,0:T(8,128)S(1)} %collective-permute-done.1.refs_3_), channel_id=1, source_target_pairs={{0,4},{4,0},{8,12},{12,8},{1,5},{5,1},{9,13},{13,9},{2,6},{6,2},{1... | collective-permute-start | bytes 516104 | tf_op jit(solution)/shard_map/ppermute | solution.py:266
  18.1 6.8 %collective-permute-start.4 = (s32[168,256]{1,0:T(8,128)S(1)}, s32[168,256]{1,0:T(8,128)S(1)}, u32[]{:S(2)}, u32[]{:S(2)}) collective-permute-start(s32[168,256]{1,0:T(8,128)S(1)} %collective-permute-done.1.refs_3_), channel_id=1, source_target_pairs={{0,8},{4,12},{8,0},{12,4},{1,9},{5,13},{9,1},{13,5},{2,10},{6,14},... | collective-permute-start | bytes 516104 | tf_op jit(solution)/shard_map/ppermute | solution.py:266
  19.7 5.7 %collective-permute-start.14 = (s32[168,256]{1,0:T(8,128)S(1)}, s32[168,256]{1,0:T(8,128)S(1)}, u32[]{:S(2)}, u32[]{:S(2)}) collective-permute-start(s32[168,256]{1,0:T(8,128)S(1)} %collective-permute-done.13.refs_3_), channel_id=1, source_target_pairs={{0,4},{4,0},{8,12},{12,8},{1,5},{5,1},{9,13},{13,9},{2,6},{6,2},{1... | collective-permute-start | bytes 516104 | tf_op jit(solution)/shard_map/ppermute | solution.py:266
  21.2 5.1 %collective-permute-start.12 = (s32[168,256]{1,0:T(8,128)S(1)}, s32[168,256]{1,0:T(8,128)S(1)}, u32[]{:S(2)}, u32[]{:S(2)}) collective-permute-start(s32[168,256]{1,0:T(8,128)S(1)} %collective-permute-done.11.refs_3_), channel_id=1, source_target_pairs={{0,4},{4,0},{8,12},{12,8},{1,5},{5,1},{9,13},{13,9},{2,6},{6,2},{1... | collective-permute-start | bytes 516104 | tf_op jit(solution)/shard_map/ppermute | solution.py:266
  24.9 2.2 %collective-permute-start.10 = (s32[168,256]{1,0:T(8,128)S(1)}, s32[168,256]{1,0:T(8,128)S(1)}, u32[]{:S(2)}, u32[]{:S(2)}) collective-permute-start(s32[168,256]{1,0:T(8,128)S(1)} %collective-permute-done.4.refs_3_), channel_id=1, source_target_pairs={{0,4},{4,0},{8,12},{12,8},{1,5},{5,1},{9,13},{13,9},{2,6},{6,2},{1... | collective-permute-start | bytes 516104 | tf_op jit(solution)/shard_map/ppermute | solution.py:266
  28.4 2.6 %collective-permute-start.18 = (f32[64,512]{1,0:T(8,128)S(1)}, f32[64,512]{1,0:T(8,128)S(1)}, u32[]{:S(2)}, u32[]{:S(2)}) collective-permute-start(f32[64,512]{1,0:T(8,128)S(1)} %get-tuple-element.47.refs_0_.refs_1_), channel_id=1, source_target_pairs={{0,4},{1,2},{2,1},{3,7},{4,0},{5,6},{6,5},{7,3},{8,12},{9,10},{10,... | collective-permute-start | bytes 393224 | tf_op jit(solution)/shard_map/ppermute | solution.py:274
  29.0 5.5 %collective-permute-start.20 = (f32[64,512]{1,0:T(8,128)S(1)}, f32[64,512]{1,0:T(8,128)S(1)}, u32[]{:S(2)}, u32[]{:S(2)}) collective-permute-start(f32[64,512]{1,0:T(8,128)S(1)} %get-tuple-element.47.refs_0_.refs_1_), channel_id=1, source_target_pairs={{0,8},{4,12},{8,0},{12,4},{1,9},{5,13},{9,1},{13,5},{2,10},{6,14},... | collective-permute-start | bytes 393224 | tf_op jit(solution)/shard_map/ppermute | solution.py:266
  30.5 4.0 %collective-permute-start.15 = (f32[64,512]{1,0:T(8,128)S(1)}, f32[64,512]{1,0:T(8,128)S(1)}, u32[]{:S(2)}, u32[]{:S(2)}) collective-permute-start(f32[64,512]{1,0:T(8,128)S(1)} %get-tuple-element.47.refs_0_.refs_1_), channel_id=1, source_target_pairs={{0,4},{1,10},{2,9},{3,7},{4,0},{5,14},{6,13},{7,3},{8,12},{9,2},{1... | collective-permute-start | bytes 393224 | tf_op jit(solution)/shard_map/ppermute | solution.py:278
  30.5 4.5 %collective-permute-start.17 = (f32[64,512]{1,0:T(8,128)S(1)}, f32[64,512]{1,0:T(8,128)S(1)}, u32[]{:S(2)}, u32[]{:S(2)}) collective-permute-start(f32[64,512]{1,0:T(8,128)S(1)} %get-tuple-element.47.refs_0_.refs_1_), channel_id=1, source_target_pairs={{0,4},{4,0},{8,12},{12,8},{1,5},{5,1},{9,13},{13,9},{2,6},{6,2},{1... | collective-permute-start | bytes 393224 | tf_op jit(solution)/shard_map/ppermute | solution.py:266
  31.0 4.0 %collective-permute-start.19 = (f32[64,512]{1,0:T(8,128)S(1)}, f32[64,512]{1,0:T(8,128)S(1)}, u32[]{:S(2)}, u32[]{:S(2)}) collective-permute-start(f32[64,512]{1,0:T(8,128)S(1)} %collective-permute-done.18.refs_3_), channel_id=1, source_target_pairs={{0,4},{4,0},{8,12},{12,8},{1,5},{5,1},{9,13},{13,9},{2,6},{6,2},{1... | collective-permute-start | bytes 393224 | tf_op jit(solution)/shard_map/ppermute | solution.py:266
  34.5 1.3 %collective-permute-start.21 = (f32[64,512]{1,0:T(8,128)S(1)}, f32[64,512]{1,0:T(8,128)S(1)}, u32[]{:S(2)}, u32[]{:S(2)}) collective-permute-start(f32[64,512]{1,0:T(8,128)S(1)} %collective-permute-done.20.refs_5_), channel_id=1, source_target_pairs={{0,4},{4,0},{8,12},{12,8},{1,5},{5,1},{9,13},{13,9},{2,6},{6,2},{1... | collective-permute-start | bytes 393224 | tf_op jit(solution)/shard_map/ppermute | solution.py:266
  34.5 2.1 %collective-permute-start.16 = (f32[64,512]{1,0:T(8,128)S(1)}, f32[64,512]{1,0:T(8,128)S(1)}, u32[]{:S(2)}, u32[]{:S(2)}) collective-permute-start(f32[64,512]{1,0:T(8,128)S(1)} %collective-permute-done.15.refs_1_), channel_id=1, source_target_pairs={{0,4},{4,0},{8,12},{12,8},{1,5},{5,1},{9,13},{13,9},{2,6},{6,2},{1... | collective-permute-start | bytes 393224 | tf_op jit(solution)/shard_map/ppermute | solution.py:266
  40.9 14.8 %collective-permute-start.27 = (f32[64,256]{1,0:T(8,128)S(1)}, f32[64,256]{1,0:T(8,128)S(1)}, u32[]{:S(2)}, u32[]{:S(2)}) collective-permute-start(f32[64,256]{1,0:T(8,128)S(1)} %get-tuple-element.54), channel_id=1, source_target_pairs={{0,1},{1,0},{2,3},{3,2},{4,5},{5,4},{6,7},{7,6},{8,9},{9,8},{10,11... | collective-permute-start | bytes 196616 | tf_op jit(solution)/shard_map/ppermute | solution.py:266
  45.8 1.2 %collective-permute-start.22 = (f32[40,128]{1,0:T(8,128)S(1)}, f32[40,128]{1,0:T(8,128)S(1)}, u32[]{:S(2)}, u32[]{:S(2)}) collective-permute-start(f32[40,128]{1,0:T(8,128)S(1)} %get-tuple-element.52.a_ref), channel_id=1, source_target_pairs={{0,4},{4,0},{8,12},{12,8},{1,5},{5,1},{9,13},{13,9},{2,6},{6,2},{1... | collective-permute-start | bytes 61448 | tf_op jit(solution)/shard_map/ppermute | solution.py:266
  47.0 3.8 %collective-permute-start.23 = (f32[40,128]{1,0:T(8,128)S(1)}, f32[40,128]{1,0:T(8,128)S(1)}, u32[]{:S(2)}, u32[]{:S(2)}) collective-permute-start(f32[40,128]{1,0:T(8,128)S(1)} %shard_map.48.share_ref), channel_id=1, source_target_pairs={{0,1},{1,0},{2,3},{3,2},{4,5},{5,4},{6,7},{7,6},{8,9},{9,8},{10,11... | collective-permute-start | bytes 61448 | tf_op jit(solution)/shard_map/ppermute | solution.py:266
  47.1 4.7 %collective-permute-start.24 = (f32[40,128]{1,0:T(8,128)S(1)}, f32[40,128]{1,0:T(8,128)S(1)}, u32[]{:S(2)}, u32[]{:S(2)}) collective-permute-start(f32[40,128]{1,0:T(8,128)S(1)} %shard_map.48.share_ref), channel_id=1, source_target_pairs={{0,2},{1,3},{2,0},{3,1},{4,6},{5,7},{6,4},{7,5},{8,10},{9,11},{10,... | collective-permute-start | bytes 61448 | tf_op jit(solution)/shard_map/ppermute | solution.py:266
  48.9 2.9 %collective-permute-start.25 = (f32[40,128]{1,0:T(8,128)S(1)}, f32[40,128]{1,0:T(8,128)S(1)}, u32[]{:S(2)}, u32[]{:S(2)}) collective-permute-start(f32[40,128]{1,0:T(8,128)S(1)} %shard_map.48.share_ref), channel_id=1, source_target_pairs={{0,4},{1,2},{2,1},{3,7},{4,0},{5,6},{6,5},{7,3},{8,12},{9,10},{10,... | collective-permute-start | bytes 61448 | tf_op jit(solution)/shard_map/ppermute | solution.py:274
  51.9 3.8 %collective-permute-start.26 = (f32[40,128]{1,0:T(8,128)S(1)}, f32[40,128]{1,0:T(8,128)S(1)}, u32[]{:S(2)}, u32[]{:S(2)}) collective-permute-start(f32[40,128]{1,0:T(8,128)S(1)} %shard_map.49.share_ref), channel_id=1, source_target_pairs={{0,8},{4,12},{8,0},{12,4},{1,9},{5,13},{9,1},{13,5},{2,10},{6,14},... | collective-permute-start | bytes 61448 | tf_op jit(solution)/shard_map/ppermute | solution.py:266

commit v9 on v8

--- a/solution.py
+++ b/solution.py
@@ -316,7 +316,7 @@
     chip_partner_outer = CHIP(after(partner_outer, tiles[0]))
     build(partner_outer, CORE(partner_outer))
     build(chip_partner, CORE(chip_partner))
-    final = CORE(after(chip_partner_outer, *tiles[1:3]))
+    final = CORE(after(chip_partner_outer, *tiles[1:5]))
     build(chip_outer, CORE(chip_outer))
     build(chip_partner_outer)
     images, tile = call(
@@ -348,7 +348,7 @@
     smem = pl.BlockSpec(memory_space=pltpu.SMEM)
     share = call(
         functools.partial(column_kernel, 4.0 * size),
-        [flag, share, NEAR(share), FAR(share), middle(share)],
+        [flag, share, NEAR(share), lax.ppermute(share, "col", [(0, 1), (1, 3), (2, 0), (3, 2)]), middle(share)],
         packed,
         [smem] + [VMEM] * 4,
     )

time: 58.4 us -> 57.8 us (0.990)
  waiting for transfers between devices: 18.3 us -> 15.7 us
  starting transfers between devices: 21 us -> 23 us
    ppermute x23 -> x22, waiting for transfers between devices: 18.3 us -> 14.6 us  [exchange(): lax.ppermute(value, axis, [(i, i ^ offset) for i in range(size)])]
    ppermute x0 -> x1, starting transfers between devices: none -> 1.95 us  [local(): lax.ppermute(share, 'col', [(0, 1), (1, 3), (2, 0), (3, 2)])]
    ppermute x0 -> x1, waiting for transfers between devices: none -> 1.08 us  [local(): lax.ppermute(share, 'col', [(0, 1), (1, 3), (2, 0), (3, 2)])]
    ppermute x23 -> x22, starting transfers between devices: 20 us -> 20 us  [exchange(): lax.ppermute(value, axis, [(i, i ^ offset) for i in range(size)])]
  transfers between devices with their start and end apart: 28 -> 28, of which waited for: 11 -> 9; matrix products, arithmetic and copies ran while one was open for 0% -> 0% of each run, Pallas kernels for 13% -> 13%
where the time goes in v9:
time: 57.8 us; the launch traced here: 57.6 us
  starting transfers between devices  23 us (40%)
  Pallas kernels  16.1 us (28%)
  waiting for transfers between devices  15.7 us (27%)
  local copies, waits for them, and re-layouts  1.74 us (3%)
  other arithmetic  0.89 us (2%)
    ppermute x22, starting transfers between devices, exchange(): lax.ppermute(value, axis, [(i, i ^ offset) for i in range(size)])  20 us
    pallas_call x14, Pallas kernels, call(): pl.pallas_call(kernel, out_shape=out_shape, in_specs=in_specs or [VMEM] *...  16.1 us
    ppermute x22, waiting for transfers between devices, exchange(): lax.ppermute(value, axis, [(i, i ^ offset) for i in range(size)])  14.6 us
    ppermute x1, starting transfers between devices, local(): lax.ppermute(share, 'col', [(0, 1), (1, 3), (2, 0), (3, 2)])  1.95 us
  transfers between devices with their start and end apart: 28, of which 9 were waited for; matrix products, arithmetic and copies ran while one was open for 0% of the time, Pallas kernels for 13%

profile of v9, /device:TPU:0, one launch (start us, length us, event | category | flops | bytes accessed | tf_op | source)
XLA Modules:
  0.0 57.6 jit_solution(5312247020336136407)
XLA Ops:
  0.0 0.8 %pad_clamp_fusion = s32[1024]{0:T(1024)S(1)} fusion(s32[256]{0:T(256)} %param.4), kind=kLoop, calls=%fused_computation.6 | loop fusion | flops 1024 | bytes 5120 | tf_op jit(solution)/shard_map/gather | solution.py:291
  0.8 0.8 %copy-done = f32[2048,256]{1,0:T(8,128)S(1)} copy-done((f32[2048,256]{1,0:T(8,128)S(1)}, f32[2048,256]{1,0:T(8,128)}, u32[]{:S(2)}) %copy-start) | copy-done | bytes 2097176
  1.6 1.0 %gather_fusion = f32[256,256]{1,0:T(8,128)S(1)} fusion(f32[2048,256]{1,0:T(8,128)S(1)} %copy-done, s32[1024]{0:T(1024)S(1)} %pad_clamp_fusion), kind=kCustom, calls=%fused_computation | custom fusion | bytes 525312 | tf_op jit(solution)/shard_map/gather | solution.py:291
  2.6 0.2 shard_map.37
  2.9 3.1 %collective-permute-start = (s32[168,256]{1,0:T(8,128)S(1)}, s32[168,256]{1,0:T(8,128)S(1)}, u32[]{:S(2)}, u32[]{:S(2)}) collective-permute-start(s32[168,256]{1,0:T(8,128)S(1)} %pad_add_fusion.own_ref.refs_3_), channel_id=1, source_target_pairs={{0,1},{1,0},{2,3},{3,2},{4,5},{5,4},{6,7},{7,6},{8,9},{9,8},{10,11... | collective-permute-start | bytes 516104 | tf_op jit(solution)/shard_map/ppermute | solution.py:266
  5.9 0.0 collective-permute-start.5
  6.0 0.5 collective-permute-start.2
  6.5 1.5 %collective-permute-start.7 = (s32[168,256]{1,0:T(8,128)S(1)}, s32[168,256]{1,0:T(8,128)S(1)}, u32[]{:S(2)}, u32[]{:S(2)}) collective-permute-start(s32[168,256]{1,0:T(8,128)S(1)} %pad_add_fusion.own_ref.refs_3_), channel_id=1, source_target_pairs={{0,8},{4,12},{8,0},{12,4},{1,9},{5,13},{9,1},{13,5},{2,10},{6,14},... | collective-permute-start | bytes 516104 | tf_op jit(solution)/shard_map/ppermute | solution.py:266
  8.0 2.4 %collective-permute-done.outer_ref.refs_4_ = s32[168,256]{1,0:T(8,128)S(1)} collective-permute-done((s32[168,256]{1,0:T(8,128)S(1)}, s32[168,256]{1,0:T(8,128)S(1)}, u32[]{:S(2)}, u32[]{:S(2)}) %collective-permute-start) | collective-permute-done | bytes 172064 | tf_op jit(solution)/shard_map/ppermute | solution.py:266
  10.3 0.0 collective-permute-start.3
  10.3 0.5 collective-permute-start.1
  10.8 0.0 collective-permute-done.5.refs_3_
  10.8 1.7 %collective-permute-start.10 = (s32[168,256]{1,0:T(8,128)S(1)}, s32[168,256]{1,0:T(8,128)S(1)}, u32[]{:S(2)}, u32[]{:S(2)}) collective-permute-start(s32[168,256]{1,0:T(8,128)S(1)} %collective-permute-done.5.refs_3_), channel_id=1, source_target_pairs={{0,8},{4,12},{8,0},{12,4},{1,9},{5,13},{9,1},{13,5},{2,10},{6,14},... | collective-permute-start | bytes 516104 | tf_op jit(solution)/shard_map/ppermute | solution.py:266
  12.5 0.0 collective-permute-done.2.refs_5_
  12.5 0.7 %shard_map.38 = (bf16[512,256]{1,0:T(8,128)(2,1)S(1)}, bf16[512,256]{1,0:T(8,128)(2,1)S(1)}, f32[1,512]{1,0:T(1,128)S(1)}) custom-call(s32[168,256]{1,0:T(8,128)S(1)} %pad_add_fusion.own_ref.refs_3_, s32[168,256]{1,0:T(8,128)S(1)} %collective-permute-done.outer_ref.refs_4_), custom_call_target="tpu_custom_call" | custom-call | tf_op jit(solution)/shard_map/pallas_call | solution.py:252
  13.2 0.0 collective-permute-done.7.refs_5_
  13.2 0.6 collective-permute-start.8
  13.8 0.0 collective-permute-done.3.refs_6_
  13.8 2.6 %collective-permute-start.13 = (s32[168,256]{1,0:T(8,128)S(1)}, s32[168,256]{1,0:T(8,128)S(1)}, u32[]{:S(2)}, u32[]{:S(2)}) collective-permute-start(s32[168,256]{1,0:T(8,128)S(1)} %collective-permute-done.7.refs_5_), channel_id=1, source_target_pairs={{0,1},{1,0},{2,3},{3,2},{4,5},{5,4},{6,7},{7,6},{8,9},{9,8},{10,11... | collective-permute-start | bytes 516104 | tf_op jit(solution)/shard_map/ppermute | solution.py:266
  16.5 1.5 %shard_map.39 = (bf16[1024,512]{1,0:T(8,128)(2,1)S(1)}, f32[64,1024]{1,0:T(8,128)S(1)}) custom-call(bf16[512,256]{1,0:T(8,128)(2,1)S(1)} %get-tuple-element.30.refs_0_, bf16[512,256]{1,0:T(8,128)(2,1)S(1)} %get-tuple-element.31.refs_1_, f32[1,512]{1,0:T(1,128)S(1)} %get-tuple-element.32.refs_2_, s32[168,256]{1,0:T(8,128)S(1)} %pad_add_fusion.own_ref.refs_3_, ...), custom_call_target="tpu_custom_call" | custom-call | tf_op jit(solution)/shard_map/pallas_call | solution.py:252
  18.0 0.1 collective-permute-start.9
  18.1 0.0 collective-permute-done.10.refs_3_
  18.1 0.5 collective-permute-start.11
  18.6 0.0 collective-permute-done.6.refs_4_
  18.6 0.9 %collective-permute-start.4 = (s32[168,256]{1,0:T(8,128)S(1)}, s32[168,256]{1,0:T(8,128)S(1)}, u32[]{:S(2)}, u32[]{:S(2)}) collective-permute-start(s32[168,256]{1,0:T(8,128)S(1)} %collective-permute-done.1.refs_3_), channel_id=1, source_target_pairs={{0,8},{4,12},{8,0},{12,4},{1,9},{5,13},{9,1},{13,5},{2,10},{6,14},... | collective-permute-start | bytes 516104 | tf_op jit(solution)/shard_map/ppermute | solution.py:266
  19.5 1.6 %collective-permute-done.13.refs_3_ = s32[168,256]{1,0:T(8,128)S(1)} collective-permute-done((s32[168,256]{1,0:T(8,128)S(1)}, s32[168,256]{1,0:T(8,128)S(1)}, u32[]{:S(2)}, u32[]{:S(2)}) %collective-permute-start.13) | collective-permute-done | bytes 172064 | tf_op jit(solution)/shard_map/ppermute | solution.py:266
  21.1 0.0 collective-permute-start.14
  21.1 0.0 collective-permute-done.8.refs_6_
  21.1 1.5 %shard_map.40 = (bf16[1024,512]{1,0:T(8,128)(2,1)S(1)}, f32[64,1024]{1,0:T(8,128)S(1)}) custom-call(bf16[512,256]{1,0:T(8,128)(2,1)S(1)} %get-tuple-element.30.refs_0_, bf16[512,256]{1,0:T(8,128)(2,1)S(1)} %get-tuple-element.31.refs_1_, f32[1,512]{1,0:T(1,128)S(1)} %get-tuple-element.32.refs_2_, s32[168,256]{1,0:T(8,128)S(1)} %collective-permute-done.5.refs_3_, ...), custom_call_target="tpu_custom_call" | custom-call | tf_op jit(solution)/shard_map/pallas_call | solution.py:252
  22.6 0.0 collective-permute-done.9.refs_4_
  22.7 0.8 %shard_map.41 = (bf16[512,512]{1,0:T(8,128)(2,1)S(1)}, f32[64,512]{1,0:T(8,128)S(1)}) custom-call(bf16[512,256]{1,0:T(8,128)(2,1)S(1)} %get-tuple-element.30.refs_0_, bf16[512,256]{1,0:T(8,128)(2,1)S(1)} %get-tuple-element.31.refs_1_, f32[1,512]{1,0:T(1,128)S(1)} %get-tuple-element.32.refs_2_, s32[168,256]{1,0:T(8,128)S(1)} %collective-permute-done.1.refs_3_, ...), custom_call_target="tpu_custom_call" | custom-call | tf_op jit(solution)/shard_map/pallas_call | solution.py:252
  23.5 0.0 collective-permute-done.11.refs_4_
  23.5 0.8 %shard_map.42 = (bf16[512,512]{1,0:T(8,128)(2,1)S(1)}, f32[64,512]{1,0:T(8,128)S(1)}) custom-call(bf16[512,256]{1,0:T(8,128)(2,1)S(1)} %get-tuple-element.30.refs_0_, bf16[512,256]{1,0:T(8,128)(2,1)S(1)} %get-tuple-element.31.refs_1_, f32[1,512]{1,0:T(1,128)S(1)} %get-tuple-element.32.refs_2_, s32[168,256]{1,0:T(8,128)S(1)} %collective-permute-done.10.refs_3_, ...), custom_call_target="tpu_custom_call" | custom-call | tf_op jit(solution)/shard_map/pallas_call | solution.py:252
  24.4 0.6 %collective-permute-done.4.refs_3_ = s32[168,256]{1,0:T(8,128)S(1)} collective-permute-done((s32[168,256]{1,0:T(8,128)S(1)}, s32[168,256]{1,0:T(8,128)S(1)}, u32[]{:S(2)}, u32[]{:S(2)}) %collective-permute-start.4) | collective-permute-done | bytes 172064 | tf_op jit(solution)/shard_map/ppermute | solution.py:266
  25.0 0.5 shard_map.44
  25.5 0.8 %shard_map.43 = (bf16[512,512]{1,0:T(8,128)(2,1)S(1)}, f32[64,512]{1,0:T(8,128)S(1)}) custom-call(bf16[512,256]{1,0:T(8,128)(2,1)S(1)} %get-tuple-element.30.refs_0_, bf16[512,256]{1,0:T(8,128)(2,1)S(1)} %get-tuple-element.31.refs_1_, f32[1,512]{1,0:T(1,128)S(1)} %get-tuple-element.32.refs_2_, s32[168,256]{1,0:T(8,128)S(1)} %collective-permute-done.13.refs_3_, ...), custom_call_target="tpu_custom_call" | custom-call | tf_op jit(solution)/shard_map/pallas_call | solution.py:252
  26.4 0.0 collective-permute-done.12.refs_3_
  26.4 1.3 %shard_map.45 = (f32[64,512]{1,0:T(8,128)S(1)}, bf16[256,512]{1,0:T(8,128)(2,1)S(1)}) custom-call(bf16[512,256]{1,0:T(8,128)(2,1)S(1)} %get-tuple-element.30.refs_0_, bf16[512,256]{1,0:T(8,128)(2,1)S(1)} %get-tuple-element.31.refs_1_, f32[1,512]{1,0:T(1,128)S(1)} %get-tuple-element.32.refs_2_, s32[168,256]{1,0:T(8,128)S(1)} %collective-permute-done.12.refs_3_, ...), custom_call_target="tpu_custom_call" | custom-call | tf_op jit(solution)/shard_map/pallas_call | solution.py:252
  27.6 0.6 collective-permute-start.18
  28.2 1.1 %collective-permute-start.20 = (f32[64,512]{1,0:T(8,128)S(1)}, f32[64,512]{1,0:T(8,128)S(1)}, u32[]{:S(2)}, u32[]{:S(2)}) collective-permute-start(f32[64,512]{1,0:T(8,128)S(1)} %get-tuple-element.47.refs_0_.refs_1_), channel_id=1, source_target_pairs={{0,8},{4,12},{8,0},{12,4},{1,9},{5,13},{9,1},{13,5},{2,10},{6,14},... | collective-permute-start | bytes 393224 | tf_op jit(solution)/shard_map/ppermute | solution.py:266
  29.3 0.0 collective-permute-start.15
  29.3 0.5 collective-permute-start.17
  29.8 0.0 collective-permute-start.19
  29.8 3.9 %collective-permute-done.20.refs_5_ = f32[64,512]{1,0:T(8,128)S(1)} collective-permute-done((f32[64,512]{1,0:T(8,128)S(1)}, f32[64,512]{1,0:T(8,128)S(1)}, u32[]{:S(2)}, u32[]{:S(2)}) %collective-permute-start.20) | collective-permute-done | bytes 131104 | tf_op jit(solution)/shard_map/ppermute | solution.py:266
  33.7 0.0 collective-permute-done.15.refs_1_
  33.7 0.5 collective-permute-start.16
  34.2 0.0 collective-permute-done.17.refs_2_
  34.2 0.0 collective-permute-done.19.refs_4_
  34.2 0.8 %collective-permute-done.21.refs_6_ = f32[64,512]{1,0:T(8,128)S(1)} collective-permute-done((f32[64,512]{1,0:T(8,128)S(1)}, f32[64,512]{1,0:T(8,128)S(1)}, u32[]{:S(2)}, u32[]{:S(2)}) %collective-permute-start.21) | collective-permute-done | bytes 131104 | tf_op jit(solution)/shard_map/ppermute | solution.py:266
  35.0 0.8 %shard_map.46 = (bf16[192,3072]{1,0:T(8,128)(2,1)S(1)}, f32[64,64]{1,0:T(8,128)S(1)}, f32[64,128]{1,0:T(8,128)S(1)}) custom-call(f32[64,512]{1,0:T(8,128)S(1)} %get-tuple-element.47.refs_0_.refs_1_, f32[64,512]{1,0:T(8,128)S(1)} %get-tuple-element.47.refs_0_.refs_1_, f32[64,512]{1,0:T(8,128)S(1)} %collective-permute-done.17.refs_2_, ...), custom_call_target="tpu_custom_call" | custom-call | tf_op jit(solution)/shard_map/pallas_call | solution.py:252
  35.8 4.3 %shard_map.47 = (f32[64,256]{1,0:T(8,128)S(1)}, f32[64,256]{1,0:T(8,128)S(1)}, f32[40,128]{1,0:T(8,128)S(1)}) custom-call(f32[64,512]{1,0:T(8,128)S(1)} %get-tuple-element.47.refs_0_.refs_1_, f32[64,512]{1,0:T(8,128)S(1)} %collective-permute-done.15.refs_1_, f32[64,512]{1,0:T(8,128)S(1)} %collective-permute-done.16.refs_2_, ...), custom_call_target="tpu_custom_call" | custom-call | tf_op jit(solution)/shard_map/pallas_call | solution.py:252
  40.2 4.9 %collective-permute-start.27 = (f32[64,256]{1,0:T(8,128)S(1)}, f32[64,256]{1,0:T(8,128)S(1)}, u32[]{:S(2)}, u32[]{:S(2)}) collective-permute-start(f32[64,256]{1,0:T(8,128)S(1)} %get-tuple-element.54), channel_id=1, source_target_pairs={{0,1},{1,0},{2,3},{3,2},{4,5},{5,4},{6,7},{7,6},{8,9},{9,8},{10,11... | collective-permute-start | bytes 196616 | tf_op jit(solution)/shard_map/ppermute | solution.py:266
  45.0 1.2 %collective-permute-done.22.b_ref = f32[40,128]{1,0:T(8,128)S(1)} collective-permute-done((f32[40,128]{1,0:T(8,128)S(1)}, f32[40,128]{1,0:T(8,128)S(1)}, u32[]{:S(2)}, u32[]{:S(2)}) %collective-permute-start.22) | collective-permute-done | bytes 20512 | tf_op jit(solution)/shard_map/ppermute | solution.py:266
  46.2 0.1 shard_map.48.share_ref
  46.3 0.1 collective-permute-start.23
  46.4 1.9 %collective-permute-start.24 = (f32[40,128]{1,0:T(8,128)S(1)}, f32[40,128]{1,0:T(8,128)S(1)}, u32[]{:S(2)}, u32[]{:S(2)}) collective-permute-start(f32[40,128]{1,0:T(8,128)S(1)} %shard_map.48.share_ref), channel_id=1, source_target_pairs={{0,1},{1,3},{2,0},{3,2},{4,5},{5,7},{6,4},{7,6},{8,9},{9,11},{10,8... | collective-permute-start | bytes 61448 | tf_op jit(solution)/shard_map/ppermute | solution.py:351
  48.3 0.0 collective-permute-start.25
  48.3 1.8 %collective-permute-done.23.near_ref = f32[40,128]{1,0:T(8,128)S(1)} collective-permute-done((f32[40,128]{1,0:T(8,128)S(1)}, f32[40,128]{1,0:T(8,128)S(1)}, u32[]{:S(2)}, u32[]{:S(2)}) %collective-permute-start.23) | collective-permute-done | bytes 20512 | tf_op jit(solution)/shard_map/ppermute | solution.py:266
  50.1 1.1 %collective-permute-done.24.far_ref = f32[40,128]{1,0:T(8,128)S(1)} collective-permute-done((f32[40,128]{1,0:T(8,128)S(1)}, f32[40,128]{1,0:T(8,128)S(1)}, u32[]{:S(2)}, u32[]{:S(2)}) %collective-permute-start.24) | collective-permute-done | bytes 20512 | tf_op jit(solution)/shard_map/ppermute | solution.py:351
  51.2 0.1 shard_map.49.share_ref
  51.3 1.5 %collective-permute-start.26 = (f32[40,128]{1,0:T(8,128)S(1)}, f32[40,128]{1,0:T(8,128)S(1)}, u32[]{:S(2)}, u32[]{:S(2)}) collective-permute-start(f32[40,128]{1,0:T(8,128)S(1)} %shard_map.49.share_ref), channel_id=1, source_target_pairs={{0,8},{4,12},{8,0},{12,4},{1,9},{5,13},{9,1},{13,5},{2,10},{6,14},... | collective-permute-start | bytes 61448 | tf_op jit(solution)/shard_map/ppermute | solution.py:266
  52.7 2.3 %collective-permute-done.26.beside_ref = f32[40,128]{1,0:T(8,128)S(1)} collective-permute-done((f32[40,128]{1,0:T(8,128)S(1)}, f32[40,128]{1,0:T(8,128)S(1)}, u32[]{:S(2)}, u32[]{:S(2)}) %collective-permute-start.26) | collective-permute-done | bytes 20512 | tf_op jit(solution)/shard_map/ppermute | solution.py:266
  55.0 0.0 collective-permute-done.27.given_ref
  55.0 2.6 %shard_map.50 = f32[64,256]{1,0:T(8,128)} custom-call(s32[1]{0:T(128)} %bitcast.outer_ref, f32[40,128]{1,0:T(8,128)S(1)} %shard_map.49.share_ref, f32[40,128]{1,0:T(8,128)S(1)} %collective-permute-done.26.beside_ref, f32[64,256]{1,0:T(8,128)S(1)} %get-tuple-element.53.own_ref, f32[64,256]{1,0:T(8,128)S(1)} %collective-permute-done.27.given_ref), custom_call_target="tpu_custom_call" | custom-call | tf_op jit(solution)/shard_map/pallas_call | solution.py:252
  (15 shorter events, 0.1 us)
Async XLA Ops:
  0.0 1.6 %copy-start = (f32[2048,256]{1,0:T(8,128)S(1)}, f32[2048,256]{1,0:T(8,128)}, u32[]{:S(2)}) copy-start(f32[2048,256]{1,0:T(8,128)} %param.3) | copy-start | bytes 6291460
  0.0 2.6 %copy-start.1 = (f32[64,256]{1,0:T(8,128)S(1)}, f32[64,256]{1,0:T(8,128)}, u32[]{:S(2)}) copy-start(f32[64,256]{1,0:T(8,128)} %initial_ref.1) | copy-start | bytes 196612
  2.9 7.5 %collective-permute-start = (s32[168,256]{1,0:T(8,128)S(1)}, s32[168,256]{1,0:T(8,128)S(1)}, u32[]{:S(2)}, u32[]{:S(2)}) collective-permute-start(s32[168,256]{1,0:T(8,128)S(1)} %pad_add_fusion.own_ref.refs_3_), channel_id=1, source_target_pairs={{0,1},{1,0},{2,3},{3,2},{4,5},{5,4},{6,7},{7,6},{8,9},{9,8},{10,11... | collective-permute-start | bytes 516104 | tf_op jit(solution)/shard_map/ppermute | solution.py:266
  5.9 4.9 %collective-permute-start.5 = (s32[168,256]{1,0:T(8,128)S(1)}, s32[168,256]{1,0:T(8,128)S(1)}, u32[]{:S(2)}, u32[]{:S(2)}) collective-permute-start(s32[168,256]{1,0:T(8,128)S(1)} %pad_add_fusion.own_ref.refs_3_), channel_id=1, source_target_pairs={{0,4},{1,2},{2,1},{3,7},{4,0},{5,6},{6,5},{7,3},{8,12},{9,10},{10,... | collective-permute-start | bytes 516104 | tf_op jit(solution)/shard_map/ppermute | solution.py:274
  6.0 6.5 %collective-permute-start.2 = (s32[168,256]{1,0:T(8,128)S(1)}, s32[168,256]{1,0:T(8,128)S(1)}, u32[]{:S(2)}, u32[]{:S(2)}) collective-permute-start(s32[168,256]{1,0:T(8,128)S(1)} %pad_add_fusion.own_ref.refs_3_), channel_id=1, source_target_pairs={{0,4},{4,0},{8,12},{12,8},{1,5},{5,1},{9,13},{13,9},{2,6},{6,2},{1... | collective-permute-start | bytes 516104 | tf_op jit(solution)/shard_map/ppermute | solution.py:266
  6.5 6.8 %collective-permute-start.7 = (s32[168,256]{1,0:T(8,128)S(1)}, s32[168,256]{1,0:T(8,128)S(1)}, u32[]{:S(2)}, u32[]{:S(2)}) collective-permute-start(s32[168,256]{1,0:T(8,128)S(1)} %pad_add_fusion.own_ref.refs_3_), channel_id=1, source_target_pairs={{0,8},{4,12},{8,0},{12,4},{1,9},{5,13},{9,1},{13,5},{2,10},{6,14},... | collective-permute-start | bytes 516104 | tf_op jit(solution)/shard_map/ppermute | solution.py:266
  10.3 3.5 %collective-permute-start.3 = (s32[168,256]{1,0:T(8,128)S(1)}, s32[168,256]{1,0:T(8,128)S(1)}, u32[]{:S(2)}, u32[]{:S(2)}) collective-permute-start(s32[168,256]{1,0:T(8,128)S(1)} %collective-permute-done.outer_ref.refs_4_), channel_id=1, source_target_pairs={{0,4},{4,0},{8,12},{12,8},{1,5},{5,1},{9,13},{13,9},{2,6},{6,2},{1... | collective-permute-start | bytes 516104 | tf_op jit(solution)/shard_map/ppermute | solution.py:266
  10.3 7.7 %collective-permute-start.1 = (s32[168,256]{1,0:T(8,128)S(1)}, s32[168,256]{1,0:T(8,128)S(1)}, u32[]{:S(2)}, u32[]{:S(2)}) collective-permute-start(s32[168,256]{1,0:T(8,128)S(1)} %collective-permute-done.outer_ref.refs_4_), channel_id=1, source_target_pairs={{0,4},{1,2},{2,1},{3,7},{4,0},{5,6},{6,5},{7,3},{8,12},{9,10},{10,... | collective-permute-start | bytes 516104 | tf_op jit(solution)/shard_map/ppermute | solution.py:274
  10.8 7.3 %collective-permute-start.10 = (s32[168,256]{1,0:T(8,128)S(1)}, s32[168,256]{1,0:T(8,128)S(1)}, u32[]{:S(2)}, u32[]{:S(2)}) collective-permute-start(s32[168,256]{1,0:T(8,128)S(1)} %collective-permute-done.5.refs_3_), channel_id=1, source_target_pairs={{0,8},{4,12},{8,0},{12,4},{1,9},{5,13},{9,1},{13,5},{2,10},{6,14},... | collective-permute-start | bytes 516104 | tf_op jit(solution)/shard_map/ppermute | solution.py:266
  12.5 6.1 %collective-permute-start.6 = (s32[168,256]{1,0:T(8,128)S(1)}, s32[168,256]{1,0:T(8,128)S(1)}, u32[]{:S(2)}, u32[]{:S(2)}) collective-permute-start(s32[168,256]{1,0:T(8,128)S(1)} %collective-permute-done.5.refs_3_), channel_id=1, source_target_pairs={{0,4},{4,0},{8,12},{12,8},{1,5},{5,1},{9,13},{13,9},{2,6},{6,2},{1... | collective-permute-start | bytes 516104 | tf_op jit(solution)/shard_map/ppermute | solution.py:266
  13.2 7.9 %collective-permute-start.8 = (s32[168,256]{1,0:T(8,128)S(1)}, s32[168,256]{1,0:T(8,128)S(1)}, u32[]{:S(2)}, u32[]{:S(2)}) collective-permute-start(s32[168,256]{1,0:T(8,128)S(1)} %collective-permute-done.7.refs_5_), channel_id=1, source_target_pairs={{0,4},{4,0},{8,12},{12,8},{1,5},{5,1},{9,13},{13,9},{2,6},{6,2},{1... | collective-permute-start | bytes 516104 | tf_op jit(solution)/shard_map/ppermute | solution.py:266
  13.8 7.3 %collective-permute-start.13 = (s32[168,256]{1,0:T(8,128)S(1)}, s32[168,256]{1,0:T(8,128)S(1)}, u32[]{:S(2)}, u32[]{:S(2)}) collective-permute-start(s32[168,256]{1,0:T(8,128)S(1)} %collective-permute-done.7.refs_5_), channel_id=1, source_target_pairs={{0,1},{1,0},{2,3},{3,2},{4,5},{5,4},{6,7},{7,6},{8,9},{9,8},{10,11... | collective-permute-start | bytes 516104 | tf_op jit(solution)/shard_map/ppermute | solution.py:266
  18.0 4.6 %collective-permute-start.9 = (s32[168,256]{1,0:T(8,128)S(1)}, s32[168,256]{1,0:T(8,128)S(1)}, u32[]{:S(2)}, u32[]{:S(2)}) collective-permute-start(s32[168,256]{1,0:T(8,128)S(1)} %collective-permute-done.1.refs_3_), channel_id=1, source_target_pairs={{0,4},{4,0},{8,12},{12,8},{1,5},{5,1},{9,13},{13,9},{2,6},{6,2},{1... | collective-permute-start | bytes 516104 | tf_op jit(solution)/shard_map/ppermute | solution.py:266
  18.1 5.4 %collective-permute-start.11 = (s32[168,256]{1,0:T(8,128)S(1)}, s32[168,256]{1,0:T(8,128)S(1)}, u32[]{:S(2)}, u32[]{:S(2)}) collective-permute-start(s32[168,256]{1,0:T(8,128)S(1)} %collective-permute-done.10.refs_3_), channel_id=1, source_target_pairs={{0,4},{4,0},{8,12},{12,8},{1,5},{5,1},{9,13},{13,9},{2,6},{6,2},{1... | collective-permute-start | bytes 516104 | tf_op jit(solution)/shard_map/ppermute | solution.py:266
  18.6 6.4 %collective-permute-start.4 = (s32[168,256]{1,0:T(8,128)S(1)}, s32[168,256]{1,0:T(8,128)S(1)}, u32[]{:S(2)}, u32[]{:S(2)}) collective-permute-start(s32[168,256]{1,0:T(8,128)S(1)} %collective-permute-done.1.refs_3_), channel_id=1, source_target_pairs={{0,8},{4,12},{8,0},{12,4},{1,9},{5,13},{9,1},{13,5},{2,10},{6,14},... | collective-permute-start | bytes 516104 | tf_op jit(solution)/shard_map/ppermute | solution.py:266
  21.1 4.4 %collective-permute-start.14 = (s32[168,256]{1,0:T(8,128)S(1)}, s32[168,256]{1,0:T(8,128)S(1)}, u32[]{:S(2)}, u32[]{:S(2)}) collective-permute-start(s32[168,256]{1,0:T(8,128)S(1)} %collective-permute-done.13.refs_3_), channel_id=1, source_target_pairs={{0,4},{4,0},{8,12},{12,8},{1,5},{5,1},{9,13},{13,9},{2,6},{6,2},{1... | collective-permute-start | bytes 516104 | tf_op jit(solution)/shard_map/ppermute | solution.py:266
  25.0 1.4 %collective-permute-start.12 = (s32[168,256]{1,0:T(8,128)S(1)}, s32[168,256]{1,0:T(8,128)S(1)}, u32[]{:S(2)}, u32[]{:S(2)}) collective-permute-start(s32[168,256]{1,0:T(8,128)S(1)} %collective-permute-done.4.refs_3_), channel_id=1, source_target_pairs={{0,4},{4,0},{8,12},{12,8},{1,5},{5,1},{9,13},{13,9},{2,6},{6,2},{1... | collective-permute-start | bytes 516104 | tf_op jit(solution)/shard_map/ppermute | solution.py:266
  27.6 2.2 %collective-permute-start.18 = (f32[64,512]{1,0:T(8,128)S(1)}, f32[64,512]{1,0:T(8,128)S(1)}, u32[]{:S(2)}, u32[]{:S(2)}) collective-permute-start(f32[64,512]{1,0:T(8,128)S(1)} %get-tuple-element.47.refs_0_.refs_1_), channel_id=1, source_target_pairs={{0,4},{1,2},{2,1},{3,7},{4,0},{5,6},{6,5},{7,3},{8,12},{9,10},{10,... | collective-permute-start | bytes 393224 | tf_op jit(solution)/shard_map/ppermute | solution.py:274
  28.2 5.5 %collective-permute-start.20 = (f32[64,512]{1,0:T(8,128)S(1)}, f32[64,512]{1,0:T(8,128)S(1)}, u32[]{:S(2)}, u32[]{:S(2)}) collective-permute-start(f32[64,512]{1,0:T(8,128)S(1)} %get-tuple-element.47.refs_0_.refs_1_), channel_id=1, source_target_pairs={{0,8},{4,12},{8,0},{12,4},{1,9},{5,13},{9,1},{13,5},{2,10},{6,14},... | collective-permute-start | bytes 393224 | tf_op jit(solution)/shard_map/ppermute | solution.py:266
  29.3 4.4 %collective-permute-start.15 = (f32[64,512]{1,0:T(8,128)S(1)}, f32[64,512]{1,0:T(8,128)S(1)}, u32[]{:S(2)}, u32[]{:S(2)}) collective-permute-start(f32[64,512]{1,0:T(8,128)S(1)} %get-tuple-element.47.refs_0_.refs_1_), channel_id=1, source_target_pairs={{0,4},{1,10},{2,9},{3,7},{4,0},{5,14},{6,13},{7,3},{8,12},{9,2},{1... | collective-permute-start | bytes 393224 | tf_op jit(solution)/shard_map/ppermute | solution.py:278
  29.3 4.9 %collective-permute-start.17 = (f32[64,512]{1,0:T(8,128)S(1)}, f32[64,512]{1,0:T(8,128)S(1)}, u32[]{:S(2)}, u32[]{:S(2)}) collective-permute-start(f32[64,512]{1,0:T(8,128)S(1)} %get-tuple-element.47.refs_0_.refs_1_), channel_id=1, source_target_pairs={{0,4},{4,0},{8,12},{12,8},{1,5},{5,1},{9,13},{13,9},{2,6},{6,2},{1... | collective-permute-start | bytes 393224 | tf_op jit(solution)/shard_map/ppermute | solution.py:266
  29.8 4.4 %collective-permute-start.19 = (f32[64,512]{1,0:T(8,128)S(1)}, f32[64,512]{1,0:T(8,128)S(1)}, u32[]{:S(2)}, u32[]{:S(2)}) collective-permute-start(f32[64,512]{1,0:T(8,128)S(1)} %collective-permute-done.18.refs_3_), channel_id=1, source_target_pairs={{0,4},{4,0},{8,12},{12,8},{1,5},{5,1},{9,13},{13,9},{2,6},{6,2},{1... | collective-permute-start | bytes 393224 | tf_op jit(solution)/shard_map/ppermute | solution.py:266
  33.7 1.3 %collective-permute-start.21 = (f32[64,512]{1,0:T(8,128)S(1)}, f32[64,512]{1,0:T(8,128)S(1)}, u32[]{:S(2)}, u32[]{:S(2)}) collective-permute-start(f32[64,512]{1,0:T(8,128)S(1)} %collective-permute-done.20.refs_5_), channel_id=1, source_target_pairs={{0,4},{4,0},{8,12},{12,8},{1,5},{5,1},{9,13},{13,9},{2,6},{6,2},{1... | collective-permute-start | bytes 393224 | tf_op jit(solution)/shard_map/ppermute | solution.py:266
  33.7 2.1 %collective-permute-start.16 = (f32[64,512]{1,0:T(8,128)S(1)}, f32[64,512]{1,0:T(8,128)S(1)}, u32[]{:S(2)}, u32[]{:S(2)}) collective-permute-start(f32[64,512]{1,0:T(8,128)S(1)} %collective-permute-done.15.refs_1_), channel_id=1, source_target_pairs={{0,4},{4,0},{8,12},{12,8},{1,5},{5,1},{9,13},{13,9},{2,6},{6,2},{1... | collective-permute-start | bytes 393224 | tf_op jit(solution)/shard_map/ppermute | solution.py:266
  40.2 14.9 %collective-permute-start.27 = (f32[64,256]{1,0:T(8,128)S(1)}, f32[64,256]{1,0:T(8,128)S(1)}, u32[]{:S(2)}, u32[]{:S(2)}) collective-permute-start(f32[64,256]{1,0:T(8,128)S(1)} %get-tuple-element.54), channel_id=1, source_target_pairs={{0,1},{1,0},{2,3},{3,2},{4,5},{5,4},{6,7},{7,6},{8,9},{9,8},{10,11... | collective-permute-start | bytes 196616 | tf_op jit(solution)/shard_map/ppermute | solution.py:266
  45.0 1.2 %collective-permute-start.22 = (f32[40,128]{1,0:T(8,128)S(1)}, f32[40,128]{1,0:T(8,128)S(1)}, u32[]{:S(2)}, u32[]{:S(2)}) collective-permute-start(f32[40,128]{1,0:T(8,128)S(1)} %get-tuple-element.52.a_ref), channel_id=1, source_target_pairs={{0,4},{4,0},{8,12},{12,8},{1,5},{5,1},{9,13},{13,9},{2,6},{6,2},{1... | collective-permute-start | bytes 61448 | tf_op jit(solution)/shard_map/ppermute | solution.py:266
  46.3 3.8 %collective-permute-start.23 = (f32[40,128]{1,0:T(8,128)S(1)}, f32[40,128]{1,0:T(8,128)S(1)}, u32[]{:S(2)}, u32[]{:S(2)}) collective-permute-start(f32[40,128]{1,0:T(8,128)S(1)} %shard_map.48.share_ref), channel_id=1, source_target_pairs={{0,1},{1,0},{2,3},{3,2},{4,5},{5,4},{6,7},{7,6},{8,9},{9,8},{10,11... | collective-permute-start | bytes 61448 | tf_op jit(solution)/shard_map/ppermute | solution.py:266
  46.4 4.8 %collective-permute-start.24 = (f32[40,128]{1,0:T(8,128)S(1)}, f32[40,128]{1,0:T(8,128)S(1)}, u32[]{:S(2)}, u32[]{:S(2)}) collective-permute-start(f32[40,128]{1,0:T(8,128)S(1)} %shard_map.48.share_ref), channel_id=1, source_target_pairs={{0,1},{1,3},{2,0},{3,2},{4,5},{5,7},{6,4},{7,6},{8,9},{9,11},{10,8... | collective-permute-start | bytes 61448 | tf_op jit(solution)/shard_map/ppermute | solution.py:351
  48.3 2.8 %collective-permute-start.25 = (f32[40,128]{1,0:T(8,128)S(1)}, f32[40,128]{1,0:T(8,128)S(1)}, u32[]{:S(2)}, u32[]{:S(2)}) collective-permute-start(f32[40,128]{1,0:T(8,128)S(1)} %shard_map.48.share_ref), channel_id=1, source_target_pairs={{0,4},{1,2},{2,1},{3,7},{4,0},{5,6},{6,5},{7,3},{8,12},{9,10},{10,... | collective-permute-start | bytes 61448 | tf_op jit(solution)/shard_map/ppermute | solution.py:274
  51.3 3.8 %collective-permute-start.26 = (f32[40,128]{1,0:T(8,128)S(1)}, f32[40,128]{1,0:T(8,128)S(1)}, u32[]{:S(2)}, u32[]{:S(2)}) collective-permute-start(f32[40,128]{1,0:T(8,128)S(1)} %shard_map.49.share_ref), channel_id=1, source_target_pairs={{0,8},{4,12},{8,0},{12,4},{1,9},{5,13},{9,1},{13,5},{2,10},{6,14},... | collective-permute-start | bytes 61448 | tf_op jit(solution)/shard_map/ppermute | solution.py:266

commit v10 on v9

--- a/solution.py
+++ b/solution.py
@@ -193,14 +193,12 @@
     far = far * (1.0 / total)
     n = gram.shape[0]
     eye = lax.broadcasted_iota(jnp.int32, (n, n), 0) == lax.broadcasted_iota(jnp.int32, (n, n), 1)
-    gram = gram - (total * far) * jnp.sum(jnp.where(eye, far, 0.0), axis=0, keepdims=True)
+    row = jnp.sum(jnp.where(eye, far, 0.0), axis=0, keepdims=True)
+    gram = gram - (total * far) * row
     solve = math.sqrt(total) * inverse_factor(gram)
-    level = times(solve, thirds(jnp.broadcast_to(far, (n, 2 * n))))[:, :1]
-    vectors = []
-    for part in (*stacks, None):
-        whole = stack if part is None else part[...]
-        vectors.append((times(solve, whole) - level).astype(BF16))
-    vectors = jnp.concatenate(vectors, axis=1)
+    level = jnp.sum(solve * row, axis=1, keepdims=True)
+    whole = jnp.concatenate([*(part[...] for part in stacks), stack], axis=1)
+    vectors = (times(solve, whole) - level).astype(BF16)
     vectors = jnp.concatenate([vectors[:, p * size : (p + 1) * size] for p in pieces], axis=1)
     result, begin = None, 0
     for tile in tiles:

time: 57.8 us -> 57.6 us (level)
  no operation moved by 1% of the time
where the time goes in v10:
time: 57.6 us; the launch traced here: 57.5 us
  starting transfers between devices  23.1 us (40%)
  Pallas kernels  16 us (28%)
  waiting for transfers between devices  15.7 us (27%)
  local copies, waits for them, and re-layouts  1.74 us (3%)
  other arithmetic  0.89 us (2%)
    ppermute x22, starting transfers between devices, exchange(): lax.ppermute(value, axis, [(i, i ^ offset) for i in range(size)])  20 us
    pallas_call x14, Pallas kernels, call(): pl.pallas_call(kernel, out_shape=out_shape, in_specs=in_specs or [VMEM] *...  16 us
    ppermute x22, waiting for transfers between devices, exchange(): lax.ppermute(value, axis, [(i, i ^ offset) for i in range(size)])  14.6 us
    ppermute x1, starting transfers between devices, local(): lax.ppermute(share, 'col', [(0, 1), (1, 3), (2, 0), (3, 2)])  1.95 us
  transfers between devices with their start and end apart: 28, of which 9 were waited for; matrix products, arithmetic and copies ran while one was open for 0% of the time, Pallas kernels for 13%

profile of v10, /device:TPU:0, one launch (start us, length us, event | category | flops | bytes accessed | tf_op | source)
XLA Modules:
  0.0 57.5 jit_solution(7101147417977011301)
XLA Ops:
  0.0 0.8 %pad_clamp_fusion = s32[1024]{0:T(1024)S(1)} fusion(s32[256]{0:T(256)} %param.4), kind=kLoop, calls=%fused_computation.6 | loop fusion | flops 1024 | bytes 5120 | tf_op jit(solution)/shard_map/gather | solution.py:289
  0.8 0.8 %copy-done = f32[2048,256]{1,0:T(8,128)S(1)} copy-done((f32[2048,256]{1,0:T(8,128)S(1)}, f32[2048,256]{1,0:T(8,128)}, u32[]{:S(2)}) %copy-start) | copy-done | bytes 2097176
  1.6 1.0 %gather_fusion = f32[256,256]{1,0:T(8,128)S(1)} fusion(f32[2048,256]{1,0:T(8,128)S(1)} %copy-done, s32[1024]{0:T(1024)S(1)} %pad_clamp_fusion), kind=kCustom, calls=%fused_computation | custom fusion | bytes 525312 | tf_op jit(solution)/shard_map/gather | solution.py:289
  2.6 0.2 shard_map.37
  2.9 3.1 %collective-permute-start = (s32[168,256]{1,0:T(8,128)S(1)}, s32[168,256]{1,0:T(8,128)S(1)}, u32[]{:S(2)}, u32[]{:S(2)}) collective-permute-start(s32[168,256]{1,0:T(8,128)S(1)} %pad_add_fusion.own_ref.refs_3_), channel_id=1, source_target_pairs={{0,1},{1,0},{2,3},{3,2},{4,5},{5,4},{6,7},{7,6},{8,9},{9,8},{10,11... | collective-permute-start | bytes 516104 | tf_op jit(solution)/shard_map/ppermute | solution.py:264
  5.9 0.0 collective-permute-start.5
  6.0 0.5 collective-permute-start.2
  6.5 1.5 %collective-permute-start.7 = (s32[168,256]{1,0:T(8,128)S(1)}, s32[168,256]{1,0:T(8,128)S(1)}, u32[]{:S(2)}, u32[]{:S(2)}) collective-permute-start(s32[168,256]{1,0:T(8,128)S(1)} %pad_add_fusion.own_ref.refs_3_), channel_id=1, source_target_pairs={{0,8},{4,12},{8,0},{12,4},{1,9},{5,13},{9,1},{13,5},{2,10},{6,14},... | collective-permute-start | bytes 516104 | tf_op jit(solution)/shard_map/ppermute | solution.py:264
  8.0 2.4 %collective-permute-done.outer_ref.refs_4_ = s32[168,256]{1,0:T(8,128)S(1)} collective-permute-done((s32[168,256]{1,0:T(8,128)S(1)}, s32[168,256]{1,0:T(8,128)S(1)}, u32[]{:S(2)}, u32[]{:S(2)}) %collective-permute-start) | collective-permute-done | bytes 172064 | tf_op jit(solution)/shard_map/ppermute | solution.py:264
  10.3 0.0 collective-permute-start.3
  10.3 0.5 collective-permute-start.1
  10.8 1.7 %collective-permute-start.10 = (s32[168,256]{1,0:T(8,128)S(1)}, s32[168,256]{1,0:T(8,128)S(1)}, u32[]{:S(2)}, u32[]{:S(2)}) collective-permute-start(s32[168,256]{1,0:T(8,128)S(1)} %collective-permute-done.5.refs_3_), channel_id=1, source_target_pairs={{0,8},{4,12},{8,0},{12,4},{1,9},{5,13},{9,1},{13,5},{2,10},{6,14},... | collective-permute-start | bytes 516104 | tf_op jit(solution)/shard_map/ppermute | solution.py:264
  12.5 0.7 %shard_map.38 = (bf16[512,256]{1,0:T(8,128)(2,1)S(1)}, bf16[512,256]{1,0:T(8,128)(2,1)S(1)}, f32[1,512]{1,0:T(1,128)S(1)}) custom-call(s32[168,256]{1,0:T(8,128)S(1)} %pad_add_fusion.own_ref.refs_3_, s32[168,256]{1,0:T(8,128)S(1)} %collective-permute-done.outer_ref.refs_4_), custom_call_target="tpu_custom_call" | custom-call | tf_op jit(solution)/shard_map/pallas_call | solution.py:250
  13.2 0.0 collective-permute-done.7.refs_5_
  13.2 0.6 collective-permute-start.8
  13.8 0.0 collective-permute-done.3.refs_6_
  13.8 2.6 %collective-permute-start.13 = (s32[168,256]{1,0:T(8,128)S(1)}, s32[168,256]{1,0:T(8,128)S(1)}, u32[]{:S(2)}, u32[]{:S(2)}) collective-permute-start(s32[168,256]{1,0:T(8,128)S(1)} %collective-permute-done.7.refs_5_), channel_id=1, source_target_pairs={{0,1},{1,0},{2,3},{3,2},{4,5},{5,4},{6,7},{7,6},{8,9},{9,8},{10,11... | collective-permute-start | bytes 516104 | tf_op jit(solution)/shard_map/ppermute | solution.py:264
  16.5 1.5 %shard_map.39 = (bf16[1024,512]{1,0:T(8,128)(2,1)S(1)}, f32[64,1024]{1,0:T(8,128)S(1)}) custom-call(bf16[512,256]{1,0:T(8,128)(2,1)S(1)} %get-tuple-element.30.refs_0_, bf16[512,256]{1,0:T(8,128)(2,1)S(1)} %get-tuple-element.31.refs_1_, f32[1,512]{1,0:T(1,128)S(1)} %get-tuple-element.32.refs_2_, s32[168,256]{1,0:T(8,128)S(1)} %pad_add_fusion.own_ref.refs_3_, ...), custom_call_target="tpu_custom_call" | custom-call | tf_op jit(solution)/shard_map/pallas_call | solution.py:250
  18.0 0.1 collective-permute-start.9
  18.1 0.0 collective-permute-done.10.refs_3_
  18.1 0.5 collective-permute-start.11
  18.6 0.0 collective-permute-done.6.refs_4_
  18.6 0.9 %collective-permute-start.4 = (s32[168,256]{1,0:T(8,128)S(1)}, s32[168,256]{1,0:T(8,128)S(1)}, u32[]{:S(2)}, u32[]{:S(2)}) collective-permute-start(s32[168,256]{1,0:T(8,128)S(1)} %collective-permute-done.1.refs_3_), channel_id=1, source_target_pairs={{0,8},{4,12},{8,0},{12,4},{1,9},{5,13},{9,1},{13,5},{2,10},{6,14},... | collective-permute-start | bytes 516104 | tf_op jit(solution)/shard_map/ppermute | solution.py:264
  19.5 1.6 %collective-permute-done.13.refs_3_ = s32[168,256]{1,0:T(8,128)S(1)} collective-permute-done((s32[168,256]{1,0:T(8,128)S(1)}, s32[168,256]{1,0:T(8,128)S(1)}, u32[]{:S(2)}, u32[]{:S(2)}) %collective-permute-start.13) | collective-permute-done | bytes 172064 | tf_op jit(solution)/shard_map/ppermute | solution.py:264
  21.1 0.0 collective-permute-start.14
  21.1 0.0 collective-permute-done.8.refs_6_
  21.1 1.5 %shard_map.40 = (bf16[1024,512]{1,0:T(8,128)(2,1)S(1)}, f32[64,1024]{1,0:T(8,128)S(1)}) custom-call(bf16[512,256]{1,0:T(8,128)(2,1)S(1)} %get-tuple-element.30.refs_0_, bf16[512,256]{1,0:T(8,128)(2,1)S(1)} %get-tuple-element.31.refs_1_, f32[1,512]{1,0:T(1,128)S(1)} %get-tuple-element.32.refs_2_, s32[168,256]{1,0:T(8,128)S(1)} %collective-permute-done.5.refs_3_, ...), custom_call_target="tpu_custom_call" | custom-call | tf_op jit(solution)/shard_map/pallas_call | solution.py:250
  22.6 0.0 collective-permute-done.9.refs_4_
  22.7 0.8 %shard_map.41 = (bf16[512,512]{1,0:T(8,128)(2,1)S(1)}, f32[64,512]{1,0:T(8,128)S(1)}) custom-call(bf16[512,256]{1,0:T(8,128)(2,1)S(1)} %get-tuple-element.30.refs_0_, bf16[512,256]{1,0:T(8,128)(2,1)S(1)} %get-tuple-element.31.refs_1_, f32[1,512]{1,0:T(1,128)S(1)} %get-tuple-element.32.refs_2_, s32[168,256]{1,0:T(8,128)S(1)} %collective-permute-done.1.refs_3_, ...), custom_call_target="tpu_custom_call" | custom-call | tf_op jit(solution)/shard_map/pallas_call | solution.py:250
  23.5 0.0 collective-permute-done.11.refs_4_
  23.5 0.8 %shard_map.42 = (bf16[512,512]{1,0:T(8,128)(2,1)S(1)}, f32[64,512]{1,0:T(8,128)S(1)}) custom-call(bf16[512,256]{1,0:T(8,128)(2,1)S(1)} %get-tuple-element.30.refs_0_, bf16[512,256]{1,0:T(8,128)(2,1)S(1)} %get-tuple-element.31.refs_1_, f32[1,512]{1,0:T(1,128)S(1)} %get-tuple-element.32.refs_2_, s32[168,256]{1,0:T(8,128)S(1)} %collective-permute-done.10.refs_3_, ...), custom_call_target="tpu_custom_call" | custom-call | tf_op jit(solution)/shard_map/pallas_call | solution.py:250
  24.4 0.6 %collective-permute-done.4.refs_3_ = s32[168,256]{1,0:T(8,128)S(1)} collective-permute-done((s32[168,256]{1,0:T(8,128)S(1)}, s32[168,256]{1,0:T(8,128)S(1)}, u32[]{:S(2)}, u32[]{:S(2)}) %collective-permute-start.4) | collective-permute-done | bytes 172064 | tf_op jit(solution)/shard_map/ppermute | solution.py:264
  25.0 0.5 shard_map.44
  25.5 0.8 %shard_map.43 = (bf16[512,512]{1,0:T(8,128)(2,1)S(1)}, f32[64,512]{1,0:T(8,128)S(1)}) custom-call(bf16[512,256]{1,0:T(8,128)(2,1)S(1)} %get-tuple-element.30.refs_0_, bf16[512,256]{1,0:T(8,128)(2,1)S(1)} %get-tuple-element.31.refs_1_, f32[1,512]{1,0:T(1,128)S(1)} %get-tuple-element.32.refs_2_, s32[168,256]{1,0:T(8,128)S(1)} %collective-permute-done.13.refs_3_, ...), custom_call_target="tpu_custom_call" | custom-call | tf_op jit(solution)/shard_map/pallas_call | solution.py:250
  26.4 0.0 collective-permute-done.12.refs_3_
  26.4 1.3 %shard_map.45 = (f32[64,512]{1,0:T(8,128)S(1)}, bf16[256,512]{1,0:T(8,128)(2,1)S(1)}) custom-call(bf16[512,256]{1,0:T(8,128)(2,1)S(1)} %get-tuple-element.30.refs_0_, bf16[512,256]{1,0:T(8,128)(2,1)S(1)} %get-tuple-element.31.refs_1_, f32[1,512]{1,0:T(1,128)S(1)} %get-tuple-element.32.refs_2_, s32[168,256]{1,0:T(8,128)S(1)} %collective-permute-done.12.refs_3_, ...), custom_call_target="tpu_custom_call" | custom-call | tf_op jit(solution)/shard_map/pallas_call | solution.py:250
  27.6 0.6 collective-permute-start.18
  28.2 1.1 %collective-permute-start.20 = (f32[64,512]{1,0:T(8,128)S(1)}, f32[64,512]{1,0:T(8,128)S(1)}, u32[]{:S(2)}, u32[]{:S(2)}) collective-permute-start(f32[64,512]{1,0:T(8,128)S(1)} %get-tuple-element.47.refs_0_.refs_1_), channel_id=1, source_target_pairs={{0,8},{4,12},{8,0},{12,4},{1,9},{5,13},{9,1},{13,5},{2,10},{6,14},... | collective-permute-start | bytes 393224 | tf_op jit(solution)/shard_map/ppermute | solution.py:264
  29.3 0.0 collective-permute-start.15
  29.3 0.5 collective-permute-start.17
  29.8 0.0 collective-permute-start.19
  29.8 3.9 %collective-permute-done.20.refs_5_ = f32[64,512]{1,0:T(8,128)S(1)} collective-permute-done((f32[64,512]{1,0:T(8,128)S(1)}, f32[64,512]{1,0:T(8,128)S(1)}, u32[]{:S(2)}, u32[]{:S(2)}) %collective-permute-start.20) | collective-permute-done | bytes 131104 | tf_op jit(solution)/shard_map/ppermute | solution.py:264
  33.7 0.0 collective-permute-done.15.refs_1_
  33.7 0.5 collective-permute-start.16
  34.2 0.0 collective-permute-done.17.refs_2_
  34.2 0.0 collective-permute-done.19.refs_4_
  34.2 0.8 %collective-permute-done.21.refs_6_ = f32[64,512]{1,0:T(8,128)S(1)} collective-permute-done((f32[64,512]{1,0:T(8,128)S(1)}, f32[64,512]{1,0:T(8,128)S(1)}, u32[]{:S(2)}, u32[]{:S(2)}) %collective-permute-start.21) | collective-permute-done | bytes 131104 | tf_op jit(solution)/shard_map/ppermute | solution.py:264
  35.0 0.8 %shard_map.46 = (bf16[192,3072]{1,0:T(8,128)(2,1)S(1)}, f32[64,64]{1,0:T(8,128)S(1)}, f32[64,128]{1,0:T(8,128)S(1)}) custom-call(f32[64,512]{1,0:T(8,128)S(1)} %get-tuple-element.47.refs_0_.refs_1_, f32[64,512]{1,0:T(8,128)S(1)} %get-tuple-element.47.refs_0_.refs_1_, f32[64,512]{1,0:T(8,128)S(1)} %collective-permute-done.17.refs_2_, ...), custom_call_target="tpu_custom_call" | custom-call | tf_op jit(solution)/shard_map/pallas_call | solution.py:250
  35.8 4.2 %shard_map.47 = (f32[64,256]{1,0:T(8,128)S(1)}, f32[64,256]{1,0:T(8,128)S(1)}, f32[40,128]{1,0:T(8,128)S(1)}) custom-call(f32[64,512]{1,0:T(8,128)S(1)} %get-tuple-element.47.refs_0_.refs_1_, f32[64,512]{1,0:T(8,128)S(1)} %collective-permute-done.15.refs_1_, f32[64,512]{1,0:T(8,128)S(1)} %collective-permute-done.16.refs_2_, ...), custom_call_target="tpu_custom_call" | custom-call | tf_op jit(solution)/shard_map/pallas_call | solution.py:250
  40.0 4.9 %collective-permute-start.27 = (f32[64,256]{1,0:T(8,128)S(1)}, f32[64,256]{1,0:T(8,128)S(1)}, u32[]{:S(2)}, u32[]{:S(2)}) collective-permute-start(f32[64,256]{1,0:T(8,128)S(1)} %get-tuple-element.54), channel_id=1, source_target_pairs={{0,1},{1,0},{2,3},{3,2},{4,5},{5,4},{6,7},{7,6},{8,9},{9,8},{10,11... | collective-permute-start | bytes 196616 | tf_op jit(solution)/shard_map/ppermute | solution.py:264
  44.9 0.0 collective-permute-start.22
  44.9 1.2 %collective-permute-done.22.b_ref = f32[40,128]{1,0:T(8,128)S(1)} collective-permute-done((f32[40,128]{1,0:T(8,128)S(1)}, f32[40,128]{1,0:T(8,128)S(1)}, u32[]{:S(2)}, u32[]{:S(2)}) %collective-permute-start.22) | collective-permute-done | bytes 20512 | tf_op jit(solution)/shard_map/ppermute | solution.py:264
  46.1 0.1 shard_map.48.share_ref
  46.2 0.1 collective-permute-start.23
  46.3 1.9 %collective-permute-start.24 = (f32[40,128]{1,0:T(8,128)S(1)}, f32[40,128]{1,0:T(8,128)S(1)}, u32[]{:S(2)}, u32[]{:S(2)}) collective-permute-start(f32[40,128]{1,0:T(8,128)S(1)} %shard_map.48.share_ref), channel_id=1, source_target_pairs={{0,1},{1,3},{2,0},{3,2},{4,5},{5,7},{6,4},{7,6},{8,9},{9,11},{10,8... | collective-permute-start | bytes 61448 | tf_op jit(solution)/shard_map/ppermute | solution.py:349
  48.2 0.0 collective-permute-start.25
  48.2 1.8 %collective-permute-done.23.near_ref = f32[40,128]{1,0:T(8,128)S(1)} collective-permute-done((f32[40,128]{1,0:T(8,128)S(1)}, f32[40,128]{1,0:T(8,128)S(1)}, u32[]{:S(2)}, u32[]{:S(2)}) %collective-permute-start.23) | collective-permute-done | bytes 20512 | tf_op jit(solution)/shard_map/ppermute | solution.py:264
  50.0 1.1 %collective-permute-done.24.far_ref = f32[40,128]{1,0:T(8,128)S(1)} collective-permute-done((f32[40,128]{1,0:T(8,128)S(1)}, f32[40,128]{1,0:T(8,128)S(1)}, u32[]{:S(2)}, u32[]{:S(2)}) %collective-permute-start.24) | collective-permute-done | bytes 20512 | tf_op jit(solution)/shard_map/ppermute | solution.py:349
  51.0 0.0 collective-permute-done.25.across_ref
  51.0 0.1 shard_map.49.share_ref
  51.1 1.5 %collective-permute-start.26 = (f32[40,128]{1,0:T(8,128)S(1)}, f32[40,128]{1,0:T(8,128)S(1)}, u32[]{:S(2)}, u32[]{:S(2)}) collective-permute-start(f32[40,128]{1,0:T(8,128)S(1)} %shard_map.49.share_ref), channel_id=1, source_target_pairs={{0,8},{4,12},{8,0},{12,4},{1,9},{5,13},{9,1},{13,5},{2,10},{6,14},... | collective-permute-start | bytes 61448 | tf_op jit(solution)/shard_map/ppermute | solution.py:264
  52.6 2.3 %collective-permute-done.26.beside_ref = f32[40,128]{1,0:T(8,128)S(1)} collective-permute-done((f32[40,128]{1,0:T(8,128)S(1)}, f32[40,128]{1,0:T(8,128)S(1)}, u32[]{:S(2)}, u32[]{:S(2)}) %collective-permute-start.26) | collective-permute-done | bytes 20512 | tf_op jit(solution)/shard_map/ppermute | solution.py:264
  54.9 0.0 collective-permute-done.27.given_ref
  54.9 2.6 %shard_map.50 = f32[64,256]{1,0:T(8,128)} custom-call(s32[1]{0:T(128)} %bitcast.outer_ref, f32[40,128]{1,0:T(8,128)S(1)} %shard_map.49.share_ref, f32[40,128]{1,0:T(8,128)S(1)} %collective-permute-done.26.beside_ref, f32[64,256]{1,0:T(8,128)S(1)} %get-tuple-element.53.own_ref, f32[64,256]{1,0:T(8,128)S(1)} %collective-permute-done.27.given_ref), custom_call_target="tpu_custom_call" | custom-call | tf_op jit(solution)/shard_map/pallas_call | solution.py:250
  (15 shorter events, 0.1 us)
Async XLA Ops:
  0.0 1.6 %copy-start = (f32[2048,256]{1,0:T(8,128)S(1)}, f32[2048,256]{1,0:T(8,128)}, u32[]{:S(2)}) copy-start(f32[2048,256]{1,0:T(8,128)} %param.3) | copy-start | bytes 6291460
  0.0 2.6 %copy-start.1 = (f32[64,256]{1,0:T(8,128)S(1)}, f32[64,256]{1,0:T(8,128)}, u32[]{:S(2)}) copy-start(f32[64,256]{1,0:T(8,128)} %initial_ref.1) | copy-start | bytes 196612
  2.9 7.5 %collective-permute-start = (s32[168,256]{1,0:T(8,128)S(1)}, s32[168,256]{1,0:T(8,128)S(1)}, u32[]{:S(2)}, u32[]{:S(2)}) collective-permute-start(s32[168,256]{1,0:T(8,128)S(1)} %pad_add_fusion.own_ref.refs_3_), channel_id=1, source_target_pairs={{0,1},{1,0},{2,3},{3,2},{4,5},{5,4},{6,7},{7,6},{8,9},{9,8},{10,11... | collective-permute-start | bytes 516104 | tf_op jit(solution)/shard_map/ppermute | solution.py:264
  5.9 4.9 %collective-permute-start.5 = (s32[168,256]{1,0:T(8,128)S(1)}, s32[168,256]{1,0:T(8,128)S(1)}, u32[]{:S(2)}, u32[]{:S(2)}) collective-permute-start(s32[168,256]{1,0:T(8,128)S(1)} %pad_add_fusion.own_ref.refs_3_), channel_id=1, source_target_pairs={{0,4},{1,2},{2,1},{3,7},{4,0},{5,6},{6,5},{7,3},{8,12},{9,10},{10,... | collective-permute-start | bytes 516104 | tf_op jit(solution)/shard_map/ppermute | solution.py:272
  6.0 6.5 %collective-permute-start.2 = (s32[168,256]{1,0:T(8,128)S(1)}, s32[168,256]{1,0:T(8,128)S(1)}, u32[]{:S(2)}, u32[]{:S(2)}) collective-permute-start(s32[168,256]{1,0:T(8,128)S(1)} %pad_add_fusion.own_ref.refs_3_), channel_id=1, source_target_pairs={{0,4},{4,0},{8,12},{12,8},{1,5},{5,1},{9,13},{13,9},{2,6},{6,2},{1... | collective-permute-start | bytes 516104 | tf_op jit(solution)/shard_map/ppermute | solution.py:264
  6.5 6.8 %collective-permute-start.7 = (s32[168,256]{1,0:T(8,128)S(1)}, s32[168,256]{1,0:T(8,128)S(1)}, u32[]{:S(2)}, u32[]{:S(2)}) collective-permute-start(s32[168,256]{1,0:T(8,128)S(1)} %pad_add_fusion.own_ref.refs_3_), channel_id=1, source_target_pairs={{0,8},{4,12},{8,0},{12,4},{1,9},{5,13},{9,1},{13,5},{2,10},{6,14},... | collective-permute-start | bytes 516104 | tf_op jit(solution)/shard_map/ppermute | solution.py:264
  10.3 3.5 %collective-permute-start.3 = (s32[168,256]{1,0:T(8,128)S(1)}, s32[168,256]{1,0:T(8,128)S(1)}, u32[]{:S(2)}, u32[]{:S(2)}) collective-permute-start(s32[168,256]{1,0:T(8,128)S(1)} %collective-permute-done.outer_ref.refs_4_), channel_id=1, source_target_pairs={{0,4},{4,0},{8,12},{12,8},{1,5},{5,1},{9,13},{13,9},{2,6},{6,2},{1... | collective-permute-start | bytes 516104 | tf_op jit(solution)/shard_map/ppermute | solution.py:264
  10.3 7.7 %collective-permute-start.1 = (s32[168,256]{1,0:T(8,128)S(1)}, s32[168,256]{1,0:T(8,128)S(1)}, u32[]{:S(2)}, u32[]{:S(2)}) collective-permute-start(s32[168,256]{1,0:T(8,128)S(1)} %collective-permute-done.outer_ref.refs_4_), channel_id=1, source_target_pairs={{0,4},{1,2},{2,1},{3,7},{4,0},{5,6},{6,5},{7,3},{8,12},{9,10},{10,... | collective-permute-start | bytes 516104 | tf_op jit(solution)/shard_map/ppermute | solution.py:272
  10.8 7.3 %collective-permute-start.10 = (s32[168,256]{1,0:T(8,128)S(1)}, s32[168,256]{1,0:T(8,128)S(1)}, u32[]{:S(2)}, u32[]{:S(2)}) collective-permute-start(s32[168,256]{1,0:T(8,128)S(1)} %collective-permute-done.5.refs_3_), channel_id=1, source_target_pairs={{0,8},{4,12},{8,0},{12,4},{1,9},{5,13},{9,1},{13,5},{2,10},{6,14},... | collective-permute-start | bytes 516104 | tf_op jit(solution)/shard_map/ppermute | solution.py:264
  12.5 6.1 %collective-permute-start.6 = (s32[168,256]{1,0:T(8,128)S(1)}, s32[168,256]{1,0:T(8,128)S(1)}, u32[]{:S(2)}, u32[]{:S(2)}) collective-permute-start(s32[168,256]{1,0:T(8,128)S(1)} %collective-permute-done.5.refs_3_), channel_id=1, source_target_pairs={{0,4},{4,0},{8,12},{12,8},{1,5},{5,1},{9,13},{13,9},{2,6},{6,2},{1... | collective-permute-start | bytes 516104 | tf_op jit(solution)/shard_map/ppermute | solution.py:264
  13.2 7.9 %collective-permute-start.8 = (s32[168,256]{1,0:T(8,128)S(1)}, s32[168,256]{1,0:T(8,128)S(1)}, u32[]{:S(2)}, u32[]{:S(2)}) collective-permute-start(s32[168,256]{1,0:T(8,128)S(1)} %collective-permute-done.7.refs_5_), channel_id=1, source_target_pairs={{0,4},{4,0},{8,12},{12,8},{1,5},{5,1},{9,13},{13,9},{2,6},{6,2},{1... | collective-permute-start | bytes 516104 | tf_op jit(solution)/shard_map/ppermute | solution.py:264
  13.8 7.3 %collective-permute-start.13 = (s32[168,256]{1,0:T(8,128)S(1)}, s32[168,256]{1,0:T(8,128)S(1)}, u32[]{:S(2)}, u32[]{:S(2)}) collective-permute-start(s32[168,256]{1,0:T(8,128)S(1)} %collective-permute-done.7.refs_5_), channel_id=1, source_target_pairs={{0,1},{1,0},{2,3},{3,2},{4,5},{5,4},{6,7},{7,6},{8,9},{9,8},{10,11... | collective-permute-start | bytes 516104 | tf_op jit(solution)/shard_map/ppermute | solution.py:264
  18.0 4.6 %collective-permute-start.9 = (s32[168,256]{1,0:T(8,128)S(1)}, s32[168,256]{1,0:T(8,128)S(1)}, u32[]{:S(2)}, u32[]{:S(2)}) collective-permute-start(s32[168,256]{1,0:T(8,128)S(1)} %collective-permute-done.1.refs_3_), channel_id=1, source_target_pairs={{0,4},{4,0},{8,12},{12,8},{1,5},{5,1},{9,13},{13,9},{2,6},{6,2},{1... | collective-permute-start | bytes 516104 | tf_op jit(solution)/shard_map/ppermute | solution.py:264
  18.1 5.4 %collective-permute-start.11 = (s32[168,256]{1,0:T(8,128)S(1)}, s32[168,256]{1,0:T(8,128)S(1)}, u32[]{:S(2)}, u32[]{:S(2)}) collective-permute-start(s32[168,256]{1,0:T(8,128)S(1)} %collective-permute-done.10.refs_3_), channel_id=1, source_target_pairs={{0,4},{4,0},{8,12},{12,8},{1,5},{5,1},{9,13},{13,9},{2,6},{6,2},{1... | collective-permute-start | bytes 516104 | tf_op jit(solution)/shard_map/ppermute | solution.py:264
  18.6 6.4 %collective-permute-start.4 = (s32[168,256]{1,0:T(8,128)S(1)}, s32[168,256]{1,0:T(8,128)S(1)}, u32[]{:S(2)}, u32[]{:S(2)}) collective-permute-start(s32[168,256]{1,0:T(8,128)S(1)} %collective-permute-done.1.refs_3_), channel_id=1, source_target_pairs={{0,8},{4,12},{8,0},{12,4},{1,9},{5,13},{9,1},{13,5},{2,10},{6,14},... | collective-permute-start | bytes 516104 | tf_op jit(solution)/shard_map/ppermute | solution.py:264
  21.1 4.4 %collective-permute-start.14 = (s32[168,256]{1,0:T(8,128)S(1)}, s32[168,256]{1,0:T(8,128)S(1)}, u32[]{:S(2)}, u32[]{:S(2)}) collective-permute-start(s32[168,256]{1,0:T(8,128)S(1)} %collective-permute-done.13.refs_3_), channel_id=1, source_target_pairs={{0,4},{4,0},{8,12},{12,8},{1,5},{5,1},{9,13},{13,9},{2,6},{6,2},{1... | collective-permute-start | bytes 516104 | tf_op jit(solution)/shard_map/ppermute | solution.py:264
  25.0 1.4 %collective-permute-start.12 = (s32[168,256]{1,0:T(8,128)S(1)}, s32[168,256]{1,0:T(8,128)S(1)}, u32[]{:S(2)}, u32[]{:S(2)}) collective-permute-start(s32[168,256]{1,0:T(8,128)S(1)} %collective-permute-done.4.refs_3_), channel_id=1, source_target_pairs={{0,4},{4,0},{8,12},{12,8},{1,5},{5,1},{9,13},{13,9},{2,6},{6,2},{1... | collective-permute-start | bytes 516104 | tf_op jit(solution)/shard_map/ppermute | solution.py:264
  27.6 2.2 %collective-permute-start.18 = (f32[64,512]{1,0:T(8,128)S(1)}, f32[64,512]{1,0:T(8,128)S(1)}, u32[]{:S(2)}, u32[]{:S(2)}) collective-permute-start(f32[64,512]{1,0:T(8,128)S(1)} %get-tuple-element.47.refs_0_.refs_1_), channel_id=1, source_target_pairs={{0,4},{1,2},{2,1},{3,7},{4,0},{5,6},{6,5},{7,3},{8,12},{9,10},{10,... | collective-permute-start | bytes 393224 | tf_op jit(solution)/shard_map/ppermute | solution.py:272
  28.2 5.5 %collective-permute-start.20 = (f32[64,512]{1,0:T(8,128)S(1)}, f32[64,512]{1,0:T(8,128)S(1)}, u32[]{:S(2)}, u32[]{:S(2)}) collective-permute-start(f32[64,512]{1,0:T(8,128)S(1)} %get-tuple-element.47.refs_0_.refs_1_), channel_id=1, source_target_pairs={{0,8},{4,12},{8,0},{12,4},{1,9},{5,13},{9,1},{13,5},{2,10},{6,14},... | collective-permute-start | bytes 393224 | tf_op jit(solution)/shard_map/ppermute | solution.py:264
  29.3 4.4 %collective-permute-start.15 = (f32[64,512]{1,0:T(8,128)S(1)}, f32[64,512]{1,0:T(8,128)S(1)}, u32[]{:S(2)}, u32[]{:S(2)}) collective-permute-start(f32[64,512]{1,0:T(8,128)S(1)} %get-tuple-element.47.refs_0_.refs_1_), channel_id=1, source_target_pairs={{0,4},{1,10},{2,9},{3,7},{4,0},{5,14},{6,13},{7,3},{8,12},{9,2},{1... | collective-permute-start | bytes 393224 | tf_op jit(solution)/shard_map/ppermute | solution.py:276
  29.3 4.9 %collective-permute-start.17 = (f32[64,512]{1,0:T(8,128)S(1)}, f32[64,512]{1,0:T(8,128)S(1)}, u32[]{:S(2)}, u32[]{:S(2)}) collective-permute-start(f32[64,512]{1,0:T(8,128)S(1)} %get-tuple-element.47.refs_0_.refs_1_), channel_id=1, source_target_pairs={{0,4},{4,0},{8,12},{12,8},{1,5},{5,1},{9,13},{13,9},{2,6},{6,2},{1... | collective-permute-start | bytes 393224 | tf_op jit(solution)/shard_map/ppermute | solution.py:264
  29.8 4.4 %collective-permute-start.19 = (f32[64,512]{1,0:T(8,128)S(1)}, f32[64,512]{1,0:T(8,128)S(1)}, u32[]{:S(2)}, u32[]{:S(2)}) collective-permute-start(f32[64,512]{1,0:T(8,128)S(1)} %collective-permute-done.18.refs_3_), channel_id=1, source_target_pairs={{0,4},{4,0},{8,12},{12,8},{1,5},{5,1},{9,13},{13,9},{2,6},{6,2},{1... | collective-permute-start | bytes 393224 | tf_op jit(solution)/shard_map/ppermute | solution.py:264
  33.7 1.3 %collective-permute-start.21 = (f32[64,512]{1,0:T(8,128)S(1)}, f32[64,512]{1,0:T(8,128)S(1)}, u32[]{:S(2)}, u32[]{:S(2)}) collective-permute-start(f32[64,512]{1,0:T(8,128)S(1)} %collective-permute-done.20.refs_5_), channel_id=1, source_target_pairs={{0,4},{4,0},{8,12},{12,8},{1,5},{5,1},{9,13},{13,9},{2,6},{6,2},{1... | collective-permute-start | bytes 393224 | tf_op jit(solution)/shard_map/ppermute | solution.py:264
  33.7 2.1 %collective-permute-start.16 = (f32[64,512]{1,0:T(8,128)S(1)}, f32[64,512]{1,0:T(8,128)S(1)}, u32[]{:S(2)}, u32[]{:S(2)}) collective-permute-start(f32[64,512]{1,0:T(8,128)S(1)} %collective-permute-done.15.refs_1_), channel_id=1, source_target_pairs={{0,4},{4,0},{8,12},{12,8},{1,5},{5,1},{9,13},{13,9},{2,6},{6,2},{1... | collective-permute-start | bytes 393224 | tf_op jit(solution)/shard_map/ppermute | solution.py:264
  40.0 14.9 %collective-permute-start.27 = (f32[64,256]{1,0:T(8,128)S(1)}, f32[64,256]{1,0:T(8,128)S(1)}, u32[]{:S(2)}, u32[]{:S(2)}) collective-permute-start(f32[64,256]{1,0:T(8,128)S(1)} %get-tuple-element.54), channel_id=1, source_target_pairs={{0,1},{1,0},{2,3},{3,2},{4,5},{5,4},{6,7},{7,6},{8,9},{9,8},{10,11... | collective-permute-start | bytes 196616 | tf_op jit(solution)/shard_map/ppermute | solution.py:264
  44.9 1.2 %collective-permute-start.22 = (f32[40,128]{1,0:T(8,128)S(1)}, f32[40,128]{1,0:T(8,128)S(1)}, u32[]{:S(2)}, u32[]{:S(2)}) collective-permute-start(f32[40,128]{1,0:T(8,128)S(1)} %get-tuple-element.52.a_ref), channel_id=1, source_target_pairs={{0,4},{4,0},{8,12},{12,8},{1,5},{5,1},{9,13},{13,9},{2,6},{6,2},{1... | collective-permute-start | bytes 61448 | tf_op jit(solution)/shard_map/ppermute | solution.py:264
  46.2 3.8 %collective-permute-start.23 = (f32[40,128]{1,0:T(8,128)S(1)}, f32[40,128]{1,0:T(8,128)S(1)}, u32[]{:S(2)}, u32[]{:S(2)}) collective-permute-start(f32[40,128]{1,0:T(8,128)S(1)} %shard_map.48.share_ref), channel_id=1, source_target_pairs={{0,1},{1,0},{2,3},{3,2},{4,5},{5,4},{6,7},{7,6},{8,9},{9,8},{10,11... | collective-permute-start | bytes 61448 | tf_op jit(solution)/shard_map/ppermute | solution.py:264
  46.3 4.8 %collective-permute-start.24 = (f32[40,128]{1,0:T(8,128)S(1)}, f32[40,128]{1,0:T(8,128)S(1)}, u32[]{:S(2)}, u32[]{:S(2)}) collective-permute-start(f32[40,128]{1,0:T(8,128)S(1)} %shard_map.48.share_ref), channel_id=1, source_target_pairs={{0,1},{1,3},{2,0},{3,2},{4,5},{5,7},{6,4},{7,6},{8,9},{9,11},{10,8... | collective-permute-start | bytes 61448 | tf_op jit(solution)/shard_map/ppermute | solution.py:349
  48.2 2.8 %collective-permute-start.25 = (f32[40,128]{1,0:T(8,128)S(1)}, f32[40,128]{1,0:T(8,128)S(1)}, u32[]{:S(2)}, u32[]{:S(2)}) collective-permute-start(f32[40,128]{1,0:T(8,128)S(1)} %shard_map.48.share_ref), channel_id=1, source_target_pairs={{0,4},{1,2},{2,1},{3,7},{4,0},{5,6},{6,5},{7,3},{8,12},{9,10},{10,... | collective-permute-start | bytes 61448 | tf_op jit(solution)/shard_map/ppermute | solution.py:272
  51.1 3.8 %collective-permute-start.26 = (f32[40,128]{1,0:T(8,128)S(1)}, f32[40,128]{1,0:T(8,128)S(1)}, u32[]{:S(2)}, u32[]{:S(2)}) collective-permute-start(f32[40,128]{1,0:T(8,128)S(1)} %shard_map.49.share_ref), channel_id=1, source_target_pairs={{0,8},{4,12},{8,0},{12,4},{1,9},{5,13},{9,1},{13,5},{2,10},{6,14},... | collective-permute-start | bytes 61448 | tf_op jit(solution)/shard_map/ppermute | solution.py:264

commit v11 on v10

--- a/solution.py
+++ b/solution.py
@@ -313,8 +313,9 @@
     build(*groups[1])
     chip_partner_outer = CHIP(after(partner_outer, tiles[0]))
     build(partner_outer, CORE(partner_outer))
-    build(chip_partner, CORE(chip_partner))
-    final = CORE(after(chip_partner_outer, *tiles[1:5]))
+    build(chip_partner)
+    build(CORE(chip_partner))
+    final = CORE(after(chip_partner_outer, *tiles[1:6]))
     build(chip_outer, CORE(chip_outer))
     build(chip_partner_outer)
     images, tile = call(

time: 57.6 us -> 57.6 us (level)
    pallas_call x14 -> x15, Pallas kernels: 16 us -> 16.1 us  [call(): pl.pallas_call(kernel, out_shape=out_shape, in_specs=in_specs or [VMEM] *...]
  transfers between devices with their start and end apart: 28 -> 28, of which waited for: 9 -> 9; matrix products, arithmetic and copies ran while one was open for 0% -> 0% of each run, Pallas kernels for 13% -> 14%
where the time goes in v11:
time: 57.6 us; the launch traced here: 57.5 us
  starting transfers between devices  23.1 us (40%)
  Pallas kernels  16.1 us (28%)
  waiting for transfers between devices  15.5 us (27%)
  local copies, waits for them, and re-layouts  1.74 us (3%)
  other arithmetic  0.89 us (2%)
    ppermute x22, starting transfers between devices, exchange(): lax.ppermute(value, axis, [(i, i ^ offset) for i in range(size)])  20.1 us
    pallas_call x15, Pallas kernels, call(): pl.pallas_call(kernel, out_shape=out_shape, in_specs=in_specs or [VMEM] *...  16.1 us
    ppermute x22, waiting for transfers between devices, exchange(): lax.ppermute(value, axis, [(i, i ^ offset) for i in range(size)])  14.4 us
    ppermute x1, starting transfers between devices, local(): lax.ppermute(share, 'col', [(0, 1), (1, 3), (2, 0), (3, 2)])  1.95 us
  transfers between devices with their start and end apart: 28, of which 9 were waited for; matrix products, arithmetic and copies ran while one was open for 0% of the time, Pallas kernels for 14%

profile of v11, /device:TPU:0, one launch (start us, length us, event | category | flops | bytes accessed | tf_op | source)
XLA Modules:
  0.0 57.5 jit_solution(810502350919735701)
XLA Ops:
  0.0 0.8 %pad_clamp_fusion = s32[1024]{0:T(1024)S(1)} fusion(s32[256]{0:T(256)} %param.4), kind=kLoop, calls=%fused_computation.6 | loop fusion | flops 1024 | bytes 5120 | tf_op jit(solution)/shard_map/gather | solution.py:289
  0.8 0.8 %copy-done = f32[2048,256]{1,0:T(8,128)S(1)} copy-done((f32[2048,256]{1,0:T(8,128)S(1)}, f32[2048,256]{1,0:T(8,128)}, u32[]{:S(2)}) %copy-start) | copy-done | bytes 2097176
  1.6 1.0 %gather_fusion = f32[256,256]{1,0:T(8,128)S(1)} fusion(f32[2048,256]{1,0:T(8,128)S(1)} %copy-done, s32[1024]{0:T(1024)S(1)} %pad_clamp_fusion), kind=kCustom, calls=%fused_computation | custom fusion | bytes 525312 | tf_op jit(solution)/shard_map/gather | solution.py:289
  2.6 0.2 shard_map.37
  2.9 3.1 %collective-permute-start = (s32[168,256]{1,0:T(8,128)S(1)}, s32[168,256]{1,0:T(8,128)S(1)}, u32[]{:S(2)}, u32[]{:S(2)}) collective-permute-start(s32[168,256]{1,0:T(8,128)S(1)} %pad_add_fusion.own_ref.refs_3_), channel_id=1, source_target_pairs={{0,1},{1,0},{2,3},{3,2},{4,5},{5,4},{6,7},{7,6},{8,9},{9,8},{10,11... | collective-permute-start | bytes 516104 | tf_op jit(solution)/shard_map/ppermute | solution.py:264
  5.9 0.0 collective-permute-start.5
  6.0 0.5 collective-permute-start.2
  6.5 1.5 %collective-permute-start.7 = (s32[168,256]{1,0:T(8,128)S(1)}, s32[168,256]{1,0:T(8,128)S(1)}, u32[]{:S(2)}, u32[]{:S(2)}) collective-permute-start(s32[168,256]{1,0:T(8,128)S(1)} %pad_add_fusion.own_ref.refs_3_), channel_id=1, source_target_pairs={{0,8},{4,12},{8,0},{12,4},{1,9},{5,13},{9,1},{13,5},{2,10},{6,14},... | collective-permute-start | bytes 516104 | tf_op jit(solution)/shard_map/ppermute | solution.py:264
  8.0 2.4 %collective-permute-done.outer_ref.refs_4_ = s32[168,256]{1,0:T(8,128)S(1)} collective-permute-done((s32[168,256]{1,0:T(8,128)S(1)}, s32[168,256]{1,0:T(8,128)S(1)}, u32[]{:S(2)}, u32[]{:S(2)}) %collective-permute-start) | collective-permute-done | bytes 172064 | tf_op jit(solution)/shard_map/ppermute | solution.py:264
  10.3 0.0 collective-permute-start.3
  10.3 0.5 collective-permute-start.1
  10.8 0.0 collective-permute-done.5.refs_3_
  10.8 1.7 %collective-permute-start.10 = (s32[168,256]{1,0:T(8,128)S(1)}, s32[168,256]{1,0:T(8,128)S(1)}, u32[]{:S(2)}, u32[]{:S(2)}) collective-permute-start(s32[168,256]{1,0:T(8,128)S(1)} %collective-permute-done.5.refs_3_), channel_id=1, source_target_pairs={{0,8},{4,12},{8,0},{12,4},{1,9},{5,13},{9,1},{13,5},{2,10},{6,14},... | collective-permute-start | bytes 516104 | tf_op jit(solution)/shard_map/ppermute | solution.py:264
  12.5 0.0 collective-permute-done.2.refs_5_
  12.5 0.0 collective-permute-start.6
  12.5 0.7 %shard_map.38 = (bf16[512,256]{1,0:T(8,128)(2,1)S(1)}, bf16[512,256]{1,0:T(8,128)(2,1)S(1)}, f32[1,512]{1,0:T(1,128)S(1)}) custom-call(s32[168,256]{1,0:T(8,128)S(1)} %pad_add_fusion.own_ref.refs_3_, s32[168,256]{1,0:T(8,128)S(1)} %collective-permute-done.outer_ref.refs_4_), custom_call_target="tpu_custom_call" | custom-call | tf_op jit(solution)/shard_map/pallas_call | solution.py:250
  13.2 0.0 collective-permute-done.7.refs_5_
  13.2 0.6 collective-permute-start.8
  13.8 0.0 collective-permute-done.3.refs_6_
  13.8 2.6 %collective-permute-start.13 = (s32[168,256]{1,0:T(8,128)S(1)}, s32[168,256]{1,0:T(8,128)S(1)}, u32[]{:S(2)}, u32[]{:S(2)}) collective-permute-start(s32[168,256]{1,0:T(8,128)S(1)} %collective-permute-done.7.refs_5_), channel_id=1, source_target_pairs={{0,1},{1,0},{2,3},{3,2},{4,5},{5,4},{6,7},{7,6},{8,9},{9,8},{10,11... | collective-permute-start | bytes 516104 | tf_op jit(solution)/shard_map/ppermute | solution.py:264
  16.5 1.5 %shard_map.39 = (bf16[1024,512]{1,0:T(8,128)(2,1)S(1)}, f32[64,1024]{1,0:T(8,128)S(1)}) custom-call(bf16[512,256]{1,0:T(8,128)(2,1)S(1)} %get-tuple-element.32.refs_0_, bf16[512,256]{1,0:T(8,128)(2,1)S(1)} %get-tuple-element.33.refs_1_, f32[1,512]{1,0:T(1,128)S(1)} %get-tuple-element.34.refs_2_, s32[168,256]{1,0:T(8,128)S(1)} %pad_add_fusion.own_ref.refs_3_, ...), custom_call_target="tpu_custom_call" | custom-call | tf_op jit(solution)/shard_map/pallas_call | solution.py:250
  18.0 0.0 collective-permute-done.1.refs_3_
  18.0 0.1 collective-permute-start.9
  18.1 0.5 collective-permute-start.11
  18.6 0.0 collective-permute-done.6.refs_4_
  18.6 0.9 %collective-permute-start.4 = (s32[168,256]{1,0:T(8,128)S(1)}, s32[168,256]{1,0:T(8,128)S(1)}, u32[]{:S(2)}, u32[]{:S(2)}) collective-permute-start(s32[168,256]{1,0:T(8,128)S(1)} %collective-permute-done.1.refs_3_), channel_id=1, source_target_pairs={{0,8},{4,12},{8,0},{12,4},{1,9},{5,13},{9,1},{13,5},{2,10},{6,14},... | collective-permute-start | bytes 516104 | tf_op jit(solution)/shard_map/ppermute | solution.py:264
  19.5 0.5 shard_map.42
  20.0 1.1 %collective-permute-done.13.refs_3_ = s32[168,256]{1,0:T(8,128)S(1)} collective-permute-done((s32[168,256]{1,0:T(8,128)S(1)}, s32[168,256]{1,0:T(8,128)S(1)}, u32[]{:S(2)}, u32[]{:S(2)}) %collective-permute-start.13) | collective-permute-done | bytes 172064 | tf_op jit(solution)/shard_map/ppermute | solution.py:264
  21.1 1.5 %shard_map.40 = (bf16[1024,512]{1,0:T(8,128)(2,1)S(1)}, f32[64,1024]{1,0:T(8,128)S(1)}) custom-call(bf16[512,256]{1,0:T(8,128)(2,1)S(1)} %get-tuple-element.32.refs_0_, bf16[512,256]{1,0:T(8,128)(2,1)S(1)} %get-tuple-element.33.refs_1_, f32[1,512]{1,0:T(1,128)S(1)} %get-tuple-element.34.refs_2_, s32[168,256]{1,0:T(8,128)S(1)} %collective-permute-done.5.refs_3_, ...), custom_call_target="tpu_custom_call" | custom-call | tf_op jit(solution)/shard_map/pallas_call | solution.py:250
  22.6 0.8 %shard_map.41 = (bf16[512,512]{1,0:T(8,128)(2,1)S(1)}, f32[64,512]{1,0:T(8,128)S(1)}) custom-call(bf16[512,256]{1,0:T(8,128)(2,1)S(1)} %get-tuple-element.32.refs_0_, bf16[512,256]{1,0:T(8,128)(2,1)S(1)} %get-tuple-element.33.refs_1_, f32[1,512]{1,0:T(1,128)S(1)} %get-tuple-element.34.refs_2_, s32[168,256]{1,0:T(8,128)S(1)} %collective-permute-done.1.refs_3_, ...), custom_call_target="tpu_custom_call" | custom-call | tf_op jit(solution)/shard_map/pallas_call | solution.py:250
  23.5 0.0 collective-permute-done.11.refs_3_
  23.5 0.5 shard_map.43
  24.0 1.0 %collective-permute-done.4.refs_3_ = s32[168,256]{1,0:T(8,128)S(1)} collective-permute-done((s32[168,256]{1,0:T(8,128)S(1)}, s32[168,256]{1,0:T(8,128)S(1)}, u32[]{:S(2)}, u32[]{:S(2)}) %collective-permute-start.4) | collective-permute-done | bytes 172064 | tf_op jit(solution)/shard_map/ppermute | solution.py:264
  25.0 0.5 shard_map.45
  25.5 0.0 collective-permute-done.14.refs_4_
  25.5 0.8 %shard_map.44 = (bf16[512,512]{1,0:T(8,128)(2,1)S(1)}, f32[64,512]{1,0:T(8,128)S(1)}) custom-call(bf16[512,256]{1,0:T(8,128)(2,1)S(1)} %get-tuple-element.32.refs_0_, bf16[512,256]{1,0:T(8,128)(2,1)S(1)} %get-tuple-element.33.refs_1_, f32[1,512]{1,0:T(1,128)S(1)} %get-tuple-element.34.refs_2_, s32[168,256]{1,0:T(8,128)S(1)} %collective-permute-done.13.refs_3_, ...), custom_call_target="tpu_custom_call" | custom-call | tf_op jit(solution)/shard_map/pallas_call | solution.py:250
  26.3 0.0 collective-permute-done.12.refs_3_
  26.4 1.3 %shard_map.46 = (f32[64,512]{1,0:T(8,128)S(1)}, bf16[256,512]{1,0:T(8,128)(2,1)S(1)}) custom-call(bf16[512,256]{1,0:T(8,128)(2,1)S(1)} %get-tuple-element.32.refs_0_, bf16[512,256]{1,0:T(8,128)(2,1)S(1)} %get-tuple-element.33.refs_1_, f32[1,512]{1,0:T(1,128)S(1)} %get-tuple-element.34.refs_2_, s32[168,256]{1,0:T(8,128)S(1)} %collective-permute-done.12.refs_3_, ...), custom_call_target="tpu_custom_call" | custom-call | tf_op jit(solution)/shard_map/pallas_call | solution.py:250
  27.6 0.6 collective-permute-start.18
  28.2 1.1 %collective-permute-start.20 = (f32[64,512]{1,0:T(8,128)S(1)}, f32[64,512]{1,0:T(8,128)S(1)}, u32[]{:S(2)}, u32[]{:S(2)}) collective-permute-start(f32[64,512]{1,0:T(8,128)S(1)} %get-tuple-element.51.refs_0_.refs_1_), channel_id=1, source_target_pairs={{0,8},{4,12},{8,0},{12,4},{1,9},{5,13},{9,1},{13,5},{2,10},{6,14},... | collective-permute-start | bytes 393224 | tf_op jit(solution)/shard_map/ppermute | solution.py:264
  29.3 0.0 collective-permute-start.15
  29.3 0.5 collective-permute-start.17
  29.8 0.0 collective-permute-done.18.refs_3_
  29.8 0.0 collective-permute-start.19
  29.8 3.9 %collective-permute-done.20.refs_5_ = f32[64,512]{1,0:T(8,128)S(1)} collective-permute-done((f32[64,512]{1,0:T(8,128)S(1)}, f32[64,512]{1,0:T(8,128)S(1)}, u32[]{:S(2)}, u32[]{:S(2)}) %collective-permute-start.20) | collective-permute-done | bytes 131104 | tf_op jit(solution)/shard_map/ppermute | solution.py:264
  33.7 0.5 collective-permute-start.16
  34.2 0.8 %collective-permute-done.21.refs_6_ = f32[64,512]{1,0:T(8,128)S(1)} collective-permute-done((f32[64,512]{1,0:T(8,128)S(1)}, f32[64,512]{1,0:T(8,128)S(1)}, u32[]{:S(2)}, u32[]{:S(2)}) %collective-permute-start.21) | collective-permute-done | bytes 131104 | tf_op jit(solution)/shard_map/ppermute | solution.py:264
  35.0 0.8 %shard_map.47 = (bf16[192,3072]{1,0:T(8,128)(2,1)S(1)}, f32[64,64]{1,0:T(8,128)S(1)}, f32[64,128]{1,0:T(8,128)S(1)}) custom-call(f32[64,512]{1,0:T(8,128)S(1)} %get-tuple-element.51.refs_0_.refs_1_, f32[64,512]{1,0:T(8,128)S(1)} %get-tuple-element.51.refs_0_.refs_1_, f32[64,512]{1,0:T(8,128)S(1)} %collective-permute-done.17.refs_2_, ...), custom_call_target="tpu_custom_call" | custom-call | tf_op jit(solution)/shard_map/pallas_call | solution.py:250
  35.8 0.0 collective-permute-done.16.refs_2_
  35.8 4.2 %shard_map.48 = (f32[64,256]{1,0:T(8,128)S(1)}, f32[64,256]{1,0:T(8,128)S(1)}, f32[40,128]{1,0:T(8,128)S(1)}) custom-call(f32[64,512]{1,0:T(8,128)S(1)} %get-tuple-element.51.refs_0_.refs_1_, f32[64,512]{1,0:T(8,128)S(1)} %collective-permute-done.15.refs_1_, f32[64,512]{1,0:T(8,128)S(1)} %collective-permute-done.16.refs_2_, ...), custom_call_target="tpu_custom_call" | custom-call | tf_op jit(solution)/shard_map/pallas_call | solution.py:250
  40.0 4.9 %collective-permute-start.27 = (f32[64,256]{1,0:T(8,128)S(1)}, f32[64,256]{1,0:T(8,128)S(1)}, u32[]{:S(2)}, u32[]{:S(2)}) collective-permute-start(f32[64,256]{1,0:T(8,128)S(1)} %get-tuple-element.58), channel_id=1, source_target_pairs={{0,1},{1,0},{2,3},{3,2},{4,5},{5,4},{6,7},{7,6},{8,9},{9,8},{10,11... | collective-permute-start | bytes 196616 | tf_op jit(solution)/shard_map/ppermute | solution.py:264
  44.9 0.0 collective-permute-start.22
  44.9 1.2 %collective-permute-done.22.b_ref = f32[40,128]{1,0:T(8,128)S(1)} collective-permute-done((f32[40,128]{1,0:T(8,128)S(1)}, f32[40,128]{1,0:T(8,128)S(1)}, u32[]{:S(2)}, u32[]{:S(2)}) %collective-permute-start.22) | collective-permute-done | bytes 20512 | tf_op jit(solution)/shard_map/ppermute | solution.py:264
  46.1 0.1 shard_map.49.share_ref
  46.2 0.1 collective-permute-start.23
  46.3 1.9 %collective-permute-start.24 = (f32[40,128]{1,0:T(8,128)S(1)}, f32[40,128]{1,0:T(8,128)S(1)}, u32[]{:S(2)}, u32[]{:S(2)}) collective-permute-start(f32[40,128]{1,0:T(8,128)S(1)} %shard_map.49.share_ref), channel_id=1, source_target_pairs={{0,1},{1,3},{2,0},{3,2},{4,5},{5,7},{6,4},{7,6},{8,9},{9,11},{10,8... | collective-permute-start | bytes 61448 | tf_op jit(solution)/shard_map/ppermute | solution.py:350
  48.2 1.8 %collective-permute-done.23.near_ref = f32[40,128]{1,0:T(8,128)S(1)} collective-permute-done((f32[40,128]{1,0:T(8,128)S(1)}, f32[40,128]{1,0:T(8,128)S(1)}, u32[]{:S(2)}, u32[]{:S(2)}) %collective-permute-start.23) | collective-permute-done | bytes 20512 | tf_op jit(solution)/shard_map/ppermute | solution.py:264
  50.0 1.1 %collective-permute-done.24.far_ref = f32[40,128]{1,0:T(8,128)S(1)} collective-permute-done((f32[40,128]{1,0:T(8,128)S(1)}, f32[40,128]{1,0:T(8,128)S(1)}, u32[]{:S(2)}, u32[]{:S(2)}) %collective-permute-start.24) | collective-permute-done | bytes 20512 | tf_op jit(solution)/shard_map/ppermute | solution.py:350
  51.0 0.0 collective-permute-done.25.across_ref
  51.0 0.1 shard_map.50.share_ref
  51.1 1.5 %collective-permute-start.26 = (f32[40,128]{1,0:T(8,128)S(1)}, f32[40,128]{1,0:T(8,128)S(1)}, u32[]{:S(2)}, u32[]{:S(2)}) collective-permute-start(f32[40,128]{1,0:T(8,128)S(1)} %shard_map.50.share_ref), channel_id=1, source_target_pairs={{0,8},{4,12},{8,0},{12,4},{1,9},{5,13},{9,1},{13,5},{2,10},{6,14},... | collective-permute-start | bytes 61448 | tf_op jit(solution)/shard_map/ppermute | solution.py:264
  52.6 2.3 %collective-permute-done.26.beside_ref = f32[40,128]{1,0:T(8,128)S(1)} collective-permute-done((f32[40,128]{1,0:T(8,128)S(1)}, f32[40,128]{1,0:T(8,128)S(1)}, u32[]{:S(2)}, u32[]{:S(2)}) %collective-permute-start.26) | collective-permute-done | bytes 20512 | tf_op jit(solution)/shard_map/ppermute | solution.py:264
  54.9 0.0 collective-permute-done.27.given_ref
  54.9 2.6 %shard_map.51 = f32[64,256]{1,0:T(8,128)} custom-call(s32[1]{0:T(128)} %bitcast.outer_ref, f32[40,128]{1,0:T(8,128)S(1)} %shard_map.50.share_ref, f32[40,128]{1,0:T(8,128)S(1)} %collective-permute-done.26.beside_ref, f32[64,256]{1,0:T(8,128)S(1)} %get-tuple-element.57.own_ref, f32[64,256]{1,0:T(8,128)S(1)} %collective-permute-done.27.given_ref), custom_call_target="tpu_custom_call" | custom-call | tf_op jit(solution)/shard_map/pallas_call | solution.py:250
  (16 shorter events, 0.1 us)
Async XLA Ops:
  0.0 1.6 %copy-start = (f32[2048,256]{1,0:T(8,128)S(1)}, f32[2048,256]{1,0:T(8,128)}, u32[]{:S(2)}) copy-start(f32[2048,256]{1,0:T(8,128)} %param.3) | copy-start | bytes 6291460
  0.0 2.6 %copy-start.1 = (f32[64,256]{1,0:T(8,128)S(1)}, f32[64,256]{1,0:T(8,128)}, u32[]{:S(2)}) copy-start(f32[64,256]{1,0:T(8,128)} %initial_ref.1) | copy-start | bytes 196612
  2.9 7.5 %collective-permute-start = (s32[168,256]{1,0:T(8,128)S(1)}, s32[168,256]{1,0:T(8,128)S(1)}, u32[]{:S(2)}, u32[]{:S(2)}) collective-permute-start(s32[168,256]{1,0:T(8,128)S(1)} %pad_add_fusion.own_ref.refs_3_), channel_id=1, source_target_pairs={{0,1},{1,0},{2,3},{3,2},{4,5},{5,4},{6,7},{7,6},{8,9},{9,8},{10,11... | collective-permute-start | bytes 516104 | tf_op jit(solution)/shard_map/ppermute | solution.py:264
  5.9 4.9 %collective-permute-start.5 = (s32[168,256]{1,0:T(8,128)S(1)}, s32[168,256]{1,0:T(8,128)S(1)}, u32[]{:S(2)}, u32[]{:S(2)}) collective-permute-start(s32[168,256]{1,0:T(8,128)S(1)} %pad_add_fusion.own_ref.refs_3_), channel_id=1, source_target_pairs={{0,4},{1,2},{2,1},{3,7},{4,0},{5,6},{6,5},{7,3},{8,12},{9,10},{10,... | collective-permute-start | bytes 516104 | tf_op jit(solution)/shard_map/ppermute | solution.py:272
  6.0 6.5 %collective-permute-start.2 = (s32[168,256]{1,0:T(8,128)S(1)}, s32[168,256]{1,0:T(8,128)S(1)}, u32[]{:S(2)}, u32[]{:S(2)}) collective-permute-start(s32[168,256]{1,0:T(8,128)S(1)} %pad_add_fusion.own_ref.refs_3_), channel_id=1, source_target_pairs={{0,4},{4,0},{8,12},{12,8},{1,5},{5,1},{9,13},{13,9},{2,6},{6,2},{1... | collective-permute-start | bytes 516104 | tf_op jit(solution)/shard_map/ppermute | solution.py:264
  6.5 6.8 %collective-permute-start.7 = (s32[168,256]{1,0:T(8,128)S(1)}, s32[168,256]{1,0:T(8,128)S(1)}, u32[]{:S(2)}, u32[]{:S(2)}) collective-permute-start(s32[168,256]{1,0:T(8,128)S(1)} %pad_add_fusion.own_ref.refs_3_), channel_id=1, source_target_pairs={{0,8},{4,12},{8,0},{12,4},{1,9},{5,13},{9,1},{13,5},{2,10},{6,14},... | collective-permute-start | bytes 516104 | tf_op jit(solution)/shard_map/ppermute | solution.py:264
  10.3 3.5 %collective-permute-start.3 = (s32[168,256]{1,0:T(8,128)S(1)}, s32[168,256]{1,0:T(8,128)S(1)}, u32[]{:S(2)}, u32[]{:S(2)}) collective-permute-start(s32[168,256]{1,0:T(8,128)S(1)} %collective-permute-done.outer_ref.refs_4_), channel_id=1, source_target_pairs={{0,4},{4,0},{8,12},{12,8},{1,5},{5,1},{9,13},{13,9},{2,6},{6,2},{1... | collective-permute-start | bytes 516104 | tf_op jit(solution)/shard_map/ppermute | solution.py:264
  10.3 7.7 %collective-permute-start.1 = (s32[168,256]{1,0:T(8,128)S(1)}, s32[168,256]{1,0:T(8,128)S(1)}, u32[]{:S(2)}, u32[]{:S(2)}) collective-permute-start(s32[168,256]{1,0:T(8,128)S(1)} %collective-permute-done.outer_ref.refs_4_), channel_id=1, source_target_pairs={{0,4},{1,2},{2,1},{3,7},{4,0},{5,6},{6,5},{7,3},{8,12},{9,10},{10,... | collective-permute-start | bytes 516104 | tf_op jit(solution)/shard_map/ppermute | solution.py:272
  10.8 7.3 %collective-permute-start.10 = (s32[168,256]{1,0:T(8,128)S(1)}, s32[168,256]{1,0:T(8,128)S(1)}, u32[]{:S(2)}, u32[]{:S(2)}) collective-permute-start(s32[168,256]{1,0:T(8,128)S(1)} %collective-permute-done.5.refs_3_), channel_id=1, source_target_pairs={{0,8},{4,12},{8,0},{12,4},{1,9},{5,13},{9,1},{13,5},{2,10},{6,14},... | collective-permute-start | bytes 516104 | tf_op jit(solution)/shard_map/ppermute | solution.py:264
  12.5 6.1 %collective-permute-start.6 = (s32[168,256]{1,0:T(8,128)S(1)}, s32[168,256]{1,0:T(8,128)S(1)}, u32[]{:S(2)}, u32[]{:S(2)}) collective-permute-start(s32[168,256]{1,0:T(8,128)S(1)} %collective-permute-done.5.refs_3_), channel_id=1, source_target_pairs={{0,4},{4,0},{8,12},{12,8},{1,5},{5,1},{9,13},{13,9},{2,6},{6,2},{1... | collective-permute-start | bytes 516104 | tf_op jit(solution)/shard_map/ppermute | solution.py:264
  13.2 7.9 %collective-permute-start.8 = (s32[168,256]{1,0:T(8,128)S(1)}, s32[168,256]{1,0:T(8,128)S(1)}, u32[]{:S(2)}, u32[]{:S(2)}) collective-permute-start(s32[168,256]{1,0:T(8,128)S(1)} %collective-permute-done.7.refs_5_), channel_id=1, source_target_pairs={{0,4},{4,0},{8,12},{12,8},{1,5},{5,1},{9,13},{13,9},{2,6},{6,2},{1... | collective-permute-start | bytes 516104 | tf_op jit(solution)/shard_map/ppermute | solution.py:264
  13.8 7.3 %collective-permute-start.13 = (s32[168,256]{1,0:T(8,128)S(1)}, s32[168,256]{1,0:T(8,128)S(1)}, u32[]{:S(2)}, u32[]{:S(2)}) collective-permute-start(s32[168,256]{1,0:T(8,128)S(1)} %collective-permute-done.7.refs_5_), channel_id=1, source_target_pairs={{0,1},{1,0},{2,3},{3,2},{4,5},{5,4},{6,7},{7,6},{8,9},{9,8},{10,11... | collective-permute-start | bytes 516104 | tf_op jit(solution)/shard_map/ppermute | solution.py:264
  18.0 4.6 %collective-permute-start.9 = (s32[168,256]{1,0:T(8,128)S(1)}, s32[168,256]{1,0:T(8,128)S(1)}, u32[]{:S(2)}, u32[]{:S(2)}) collective-permute-start(s32[168,256]{1,0:T(8,128)S(1)} %collective-permute-done.1.refs_3_), channel_id=1, source_target_pairs={{0,4},{4,0},{8,12},{12,8},{1,5},{5,1},{9,13},{13,9},{2,6},{6,2},{1... | collective-permute-start | bytes 516104 | tf_op jit(solution)/shard_map/ppermute | solution.py:264
  18.1 5.4 %collective-permute-start.11 = (s32[168,256]{1,0:T(8,128)S(1)}, s32[168,256]{1,0:T(8,128)S(1)}, u32[]{:S(2)}, u32[]{:S(2)}) collective-permute-start(s32[168,256]{1,0:T(8,128)S(1)} %collective-permute-done.10.refs_3_), channel_id=1, source_target_pairs={{0,4},{4,0},{8,12},{12,8},{1,5},{5,1},{9,13},{13,9},{2,6},{6,2},{1... | collective-permute-start | bytes 516104 | tf_op jit(solution)/shard_map/ppermute | solution.py:264
  18.6 6.4 %collective-permute-start.4 = (s32[168,256]{1,0:T(8,128)S(1)}, s32[168,256]{1,0:T(8,128)S(1)}, u32[]{:S(2)}, u32[]{:S(2)}) collective-permute-start(s32[168,256]{1,0:T(8,128)S(1)} %collective-permute-done.1.refs_3_), channel_id=1, source_target_pairs={{0,8},{4,12},{8,0},{12,4},{1,9},{5,13},{9,1},{13,5},{2,10},{6,14},... | collective-permute-start | bytes 516104 | tf_op jit(solution)/shard_map/ppermute | solution.py:264
  21.1 4.4 %collective-permute-start.14 = (s32[168,256]{1,0:T(8,128)S(1)}, s32[168,256]{1,0:T(8,128)S(1)}, u32[]{:S(2)}, u32[]{:S(2)}) collective-permute-start(s32[168,256]{1,0:T(8,128)S(1)} %collective-permute-done.13.refs_3_), channel_id=1, source_target_pairs={{0,4},{4,0},{8,12},{12,8},{1,5},{5,1},{9,13},{13,9},{2,6},{6,2},{1... | collective-permute-start | bytes 516104 | tf_op jit(solution)/shard_map/ppermute | solution.py:264
  25.0 1.4 %collective-permute-start.12 = (s32[168,256]{1,0:T(8,128)S(1)}, s32[168,256]{1,0:T(8,128)S(1)}, u32[]{:S(2)}, u32[]{:S(2)}) collective-permute-start(s32[168,256]{1,0:T(8,128)S(1)} %collective-permute-done.4.refs_3_), channel_id=1, source_target_pairs={{0,4},{4,0},{8,12},{12,8},{1,5},{5,1},{9,13},{13,9},{2,6},{6,2},{1... | collective-permute-start | bytes 516104 | tf_op jit(solution)/shard_map/ppermute | solution.py:264
  27.6 2.2 %collective-permute-start.18 = (f32[64,512]{1,0:T(8,128)S(1)}, f32[64,512]{1,0:T(8,128)S(1)}, u32[]{:S(2)}, u32[]{:S(2)}) collective-permute-start(f32[64,512]{1,0:T(8,128)S(1)} %get-tuple-element.51.refs_0_.refs_1_), channel_id=1, source_target_pairs={{0,4},{1,2},{2,1},{3,7},{4,0},{5,6},{6,5},{7,3},{8,12},{9,10},{10,... | collective-permute-start | bytes 393224 | tf_op jit(solution)/shard_map/ppermute | solution.py:272
  28.2 5.5 %collective-permute-start.20 = (f32[64,512]{1,0:T(8,128)S(1)}, f32[64,512]{1,0:T(8,128)S(1)}, u32[]{:S(2)}, u32[]{:S(2)}) collective-permute-start(f32[64,512]{1,0:T(8,128)S(1)} %get-tuple-element.51.refs_0_.refs_1_), channel_id=1, source_target_pairs={{0,8},{4,12},{8,0},{12,4},{1,9},{5,13},{9,1},{13,5},{2,10},{6,14},... | collective-permute-start | bytes 393224 | tf_op jit(solution)/shard_map/ppermute | solution.py:264
  29.3 4.4 %collective-permute-start.15 = (f32[64,512]{1,0:T(8,128)S(1)}, f32[64,512]{1,0:T(8,128)S(1)}, u32[]{:S(2)}, u32[]{:S(2)}) collective-permute-start(f32[64,512]{1,0:T(8,128)S(1)} %get-tuple-element.51.refs_0_.refs_1_), channel_id=1, source_target_pairs={{0,4},{1,10},{2,9},{3,7},{4,0},{5,14},{6,13},{7,3},{8,12},{9,2},{1... | collective-permute-start | bytes 393224 | tf_op jit(solution)/shard_map/ppermute | solution.py:276
  29.3 4.9 %collective-permute-start.17 = (f32[64,512]{1,0:T(8,128)S(1)}, f32[64,512]{1,0:T(8,128)S(1)}, u32[]{:S(2)}, u32[]{:S(2)}) collective-permute-start(f32[64,512]{1,0:T(8,128)S(1)} %get-tuple-element.51.refs_0_.refs_1_), channel_id=1, source_target_pairs={{0,4},{4,0},{8,12},{12,8},{1,5},{5,1},{9,13},{13,9},{2,6},{6,2},{1... | collective-permute-start | bytes 393224 | tf_op jit(solution)/shard_map/ppermute | solution.py:264
  29.8 4.4 %collective-permute-start.19 = (f32[64,512]{1,0:T(8,128)S(1)}, f32[64,512]{1,0:T(8,128)S(1)}, u32[]{:S(2)}, u32[]{:S(2)}) collective-permute-start(f32[64,512]{1,0:T(8,128)S(1)} %collective-permute-done.18.refs_3_), channel_id=1, source_target_pairs={{0,4},{4,0},{8,12},{12,8},{1,5},{5,1},{9,13},{13,9},{2,6},{6,2},{1... | collective-permute-start | bytes 393224 | tf_op jit(solution)/shard_map/ppermute | solution.py:264
  33.7 1.3 %collective-permute-start.21 = (f32[64,512]{1,0:T(8,128)S(1)}, f32[64,512]{1,0:T(8,128)S(1)}, u32[]{:S(2)}, u32[]{:S(2)}) collective-permute-start(f32[64,512]{1,0:T(8,128)S(1)} %collective-permute-done.20.refs_5_), channel_id=1, source_target_pairs={{0,4},{4,0},{8,12},{12,8},{1,5},{5,1},{9,13},{13,9},{2,6},{6,2},{1... | collective-permute-start | bytes 393224 | tf_op jit(solution)/shard_map/ppermute | solution.py:264
  33.7 2.1 %collective-permute-start.16 = (f32[64,512]{1,0:T(8,128)S(1)}, f32[64,512]{1,0:T(8,128)S(1)}, u32[]{:S(2)}, u32[]{:S(2)}) collective-permute-start(f32[64,512]{1,0:T(8,128)S(1)} %collective-permute-done.15.refs_1_), channel_id=1, source_target_pairs={{0,4},{4,0},{8,12},{12,8},{1,5},{5,1},{9,13},{13,9},{2,6},{6,2},{1... | collective-permute-start | bytes 393224 | tf_op jit(solution)/shard_map/ppermute | solution.py:264
  40.0 14.9 %collective-permute-start.27 = (f32[64,256]{1,0:T(8,128)S(1)}, f32[64,256]{1,0:T(8,128)S(1)}, u32[]{:S(2)}, u32[]{:S(2)}) collective-permute-start(f32[64,256]{1,0:T(8,128)S(1)} %get-tuple-element.58), channel_id=1, source_target_pairs={{0,1},{1,0},{2,3},{3,2},{4,5},{5,4},{6,7},{7,6},{8,9},{9,8},{10,11... | collective-permute-start | bytes 196616 | tf_op jit(solution)/shard_map/ppermute | solution.py:264
  44.9 1.2 %collective-permute-start.22 = (f32[40,128]{1,0:T(8,128)S(1)}, f32[40,128]{1,0:T(8,128)S(1)}, u32[]{:S(2)}, u32[]{:S(2)}) collective-permute-start(f32[40,128]{1,0:T(8,128)S(1)} %get-tuple-element.56.a_ref), channel_id=1, source_target_pairs={{0,4},{4,0},{8,12},{12,8},{1,5},{5,1},{9,13},{13,9},{2,6},{6,2},{1... | collective-permute-start | bytes 61448 | tf_op jit(solution)/shard_map/ppermute | solution.py:264
  46.2 3.8 %collective-permute-start.23 = (f32[40,128]{1,0:T(8,128)S(1)}, f32[40,128]{1,0:T(8,128)S(1)}, u32[]{:S(2)}, u32[]{:S(2)}) collective-permute-start(f32[40,128]{1,0:T(8,128)S(1)} %shard_map.49.share_ref), channel_id=1, source_target_pairs={{0,1},{1,0},{2,3},{3,2},{4,5},{5,4},{6,7},{7,6},{8,9},{9,8},{10,11... | collective-permute-start | bytes 61448 | tf_op jit(solution)/shard_map/ppermute | solution.py:264
  46.3 4.8 %collective-permute-start.24 = (f32[40,128]{1,0:T(8,128)S(1)}, f32[40,128]{1,0:T(8,128)S(1)}, u32[]{:S(2)}, u32[]{:S(2)}) collective-permute-start(f32[40,128]{1,0:T(8,128)S(1)} %shard_map.49.share_ref), channel_id=1, source_target_pairs={{0,1},{1,3},{2,0},{3,2},{4,5},{5,7},{6,4},{7,6},{8,9},{9,11},{10,8... | collective-permute-start | bytes 61448 | tf_op jit(solution)/shard_map/ppermute | solution.py:350
  48.2 2.8 %collective-permute-start.25 = (f32[40,128]{1,0:T(8,128)S(1)}, f32[40,128]{1,0:T(8,128)S(1)}, u32[]{:S(2)}, u32[]{:S(2)}) collective-permute-start(f32[40,128]{1,0:T(8,128)S(1)} %shard_map.49.share_ref), channel_id=1, source_target_pairs={{0,4},{1,2},{2,1},{3,7},{4,0},{5,6},{6,5},{7,3},{8,12},{9,10},{10,... | collective-permute-start | bytes 61448 | tf_op jit(solution)/shard_map/ppermute | solution.py:272
  51.1 3.8 %collective-permute-start.26 = (f32[40,128]{1,0:T(8,128)S(1)}, f32[40,128]{1,0:T(8,128)S(1)}, u32[]{:S(2)}, u32[]{:S(2)}) collective-permute-start(f32[40,128]{1,0:T(8,128)S(1)} %shard_map.50.share_ref), channel_id=1, source_target_pairs={{0,8},{4,12},{8,0},{12,4},{1,9},{5,13},{9,1},{13,5},{2,10},{6,14},... | collective-permute-start | bytes 61448 | tf_op jit(solution)/shard_map/ppermute | solution.py:264
